TPU v7x, 256 devices: a whole 4x4x8 slice. The times are simulated.
256 devices in a mesh: lon: 16 (over z, core), lat: 8 (over y, x_hi), tp: 2 (over x_lo).
Axes of the slice: x: 4 (x_hi: 2, x_lo: 2; x = x_hi * 2 + x_lo), y: 4, z: 8, core: 2. Of those that a mesh axis runs over, the one named last changes fastest.
Arguments:
- latent: bfloat16 [192, 96, 4, 512], P('lon', 'lat'), may hold values from -6 to 6
- cotangent: bfloat16 [192, 96, 4, 512], P('lon', 'lat'), may hold values from -6 to 6
- ln_gain: float32 [512], replicated, may hold values from 0.1 to 1.9
- w_qkv: bfloat16 [3, 512, 512], P(None, None, 'tp'), may hold values from -0.25 to 0.25
- w_out: bfloat16 [512, 512], P('tp'), may hold values from -0.25 to 0.25
- bias_table: float32 [16, 2, 8, 3312], P('lat', None, 'tp'), may hold values from -3 to 360
Outputs:
- output: bfloat16 [192, 96, 4, 512], P('lon', 'lat')
- grad_latent: bfloat16 [192, 96, 4, 512], P('lon', 'lat')
- grad_gain: float32 [512], replicated
- grad_wqkv: float32 [3, 512, 512], P(None, None, 'tp')
- grad_wout: float32 [512, 512], P('tp')
- grad_bias: float32 [16, 2, 8, 3312], P('lat', None, 'tp')
All inputs are finite; a program needn't handle non-finite values.
Results may differ from a plain program's by a relative error of at most 0.023.
Values may be sent and summed in bfloat16 or wider, within the bound.
No kernel may reach another device: no remote copies, remote signals or barrier semaphores. Data moves between devices by JAX's collectives and lax.ppermute only.
A program may use at most 128 MiB of HBM per device.

v0:
```python
import math

import jax
import jax.numpy as jnp
import numpy as np
from jax import lax
from jax.sharding import PartitionSpec as P

HD = 64
WLON = 12
WLAT = 6
WLEV = 2
WTOK = 144
NREL = 3312


def passed_along(shard, axis, by):
    count = lax.axis_size(axis)
    return lax.ppermute(shard, axis, [(i, (i + by) % count) for i in range(count)])


def pair_layout():
    position = np.arange(WTOK)
    lon_pos = position // (WLAT * WLEV)
    lat_pos = position // WLEV % WLAT
    lev_pos = position % WLEV
    relative = lon_pos[None, :] - lon_pos[:, None] + WLON - 1
    entries = (
        (lev_pos[:, None] * WLEV + lev_pos[None, :]) * WLAT * WLAT
        + lat_pos[:, None] * WLAT
        + lat_pos[None, :]
    ) * (2 * WLON - 1) + relative
    return (entries.astype(np.int32), lat_pos, lev_pos)


def to_windows(values):
    lon_cells, lat_cells, lev_cells, channels = values.shape
    blocks = values.reshape(
        lon_cells // WLON, WLON, lat_cells // WLAT, WLAT, lev_cells // WLEV, WLEV, channels
    )
    blocks = blocks.transpose(2, 4, 0, 1, 3, 5, 6)
    return blocks.reshape(lat_cells // WLAT, lev_cells // WLEV, lon_cells // WLON, WTOK, channels)


def from_windows(values):
    lat_bands, lev_bands, lon_bands, window_len, channels = values.shape
    blocks = values.reshape(lat_bands, lev_bands, lon_bands, WLON, WLAT, WLEV, channels)
    blocks = blocks.transpose(2, 3, 0, 4, 1, 5, 6)
    return blocks.reshape(lon_bands * WLON, lat_bands * WLAT, lev_bands * WLEV, channels)


def allowed_pairs(last_lat, lev_bands, lat_pos, lev_pos):
    lat_edge = jnp.asarray(lat_pos >= WLAT - WLAT // 2)
    lev_edge = jnp.asarray(lev_pos >= WLEV - WLEV // 2)
    lev_last = jnp.arange(lev_bands) == lev_bands - 1
    lat_region = last_lat[:, None] & lat_edge[None, :]
    lev_region = lev_last[:, None] & lev_edge[None, :]
    same_lat = lat_region[:, :, None] == lat_region[:, None, :]
    same_lev = lev_region[:, :, None] == lev_region[:, None, :]
    return same_lat[:, None] & same_lev[None, :]


def layer_norm(values, scale_gain):
    values = values.astype(jnp.float32)
    centre = jnp.mean(values, -1, keepdims=True)
    shifted = values - centre
    inv_std = lax.rsqrt(jnp.mean(shifted * shifted, -1, keepdims=True) + 1e-05)
    normed = shifted * inv_std
    return (normed, inv_std, (normed * scale_gain).astype(jnp.bfloat16))


def enter(values, lon_move, lat_move):
    lon_half = WLON // 2
    lat_half = WLAT // 2
    arrived = lon_move(values[:lon_half])
    values = jnp.concatenate([values[lon_half:], arrived], 0)
    arrived = lat_move(values[:, :lat_half])
    values = jnp.concatenate([values[:, lat_half:], arrived], 1)
    return jnp.roll(values, -(WLEV // 2), axis=2)


def leave(values, lon_move, lat_move):
    lon_half = WLON // 2
    lat_half = WLAT // 2
    values = jnp.roll(values, WLEV // 2, axis=2)
    arrived = lat_move(values[:, values.shape[1] - lat_half :])
    values = jnp.concatenate([arrived, values[:, : values.shape[1] - lat_half]], 1)
    arrived = lon_move(values[values.shape[0] - lon_half :])
    values = jnp.concatenate([arrived, values[: values.shape[0] - lon_half]], 0)
    return values


def head_total(partial_value):
    return lax.psum(partial_value.astype(jnp.bfloat16), "tp").astype(jnp.float32)


def on_device(latent, cotangent, ln_gain, w_qkv, w_out, bias_table):
    lon_cells, lat_cells, lev_cells, model_width = latent.shape
    local_width = w_out.shape[0]
    head_count = local_width // HD
    lat_bands = lat_cells // WLAT
    lev_bands = lev_cells // WLEV
    lon_bands = lon_cells // WLON
    entries, lat_pos, lev_pos = pair_layout()
    entry_ids = jnp.asarray(entries)
    inv_scale = 1.0 / math.sqrt(HD)
    last_device = lax.axis_index("lat") == lax.axis_size("lat") - 1
    last_lat = last_device & (jnp.arange(lat_bands) == lat_bands - 1)
    allowed = allowed_pairs(last_lat, lev_bands, lat_pos, lev_pos)
    bias_full = jnp.take(bias_table, entry_ids, axis=3)
    head_shape = (lat_bands, lev_bands, lon_bands, WTOK, head_count, HD)
    win_shape = (lat_bands, lev_bands, lon_bands, WTOK, model_width)
    joined = jnp.concatenate([latent, cotangent], 3)
    rolled = enter(
        joined,
        lambda border: passed_along(border, "lon", -1),
        lambda border: passed_along(border, "lat", -1),
    )
    windows = to_windows(rolled)
    latent_win = windows[..., :model_width]
    upstream = windows[..., model_width:]
    hidden = layer_norm(latent_win, ln_gain)[2]
    hidden_flat = hidden.reshape(-1, model_width)
    projected = [
        jnp.dot(hidden_flat, w_qkv[member], preferred_element_type=jnp.float32).astype(jnp.bfloat16)
        for member in range(3)
    ]
    queries, key_rows, value_rows = [matrix.reshape(head_shape) for matrix in projected]
    scores = (
        jnp.einsum("abwqhe,abwkhe->abwhqk", queries, key_rows, preferred_element_type=jnp.float32)
        * inv_scale
        + bias_full[:, :, None]
    )
    scores = jnp.where(allowed[:, :, None, None], scores, -jnp.inf)
    row_max = jnp.max(scores, -1, keepdims=True)
    expsum = jnp.exp(scores - row_max)
    attn_weights = expsum / jnp.sum(expsum, -1, keepdims=True)
    attn_low = attn_weights.astype(jnp.bfloat16)
    attended = jnp.einsum(
        "abwhqk,abwkhe->abwqhe", attn_low, value_rows, preferred_element_type=jnp.float32
    ).astype(jnp.bfloat16)
    attended_flat = attended.reshape(-1, local_width)
    out_win = head_total(jnp.dot(attended_flat, w_out, preferred_element_type=jnp.float32)).astype(
        jnp.bfloat16
    )
    out_own = leave(
        from_windows(out_win.reshape(win_shape)),
        lambda border: passed_along(border, "lon", 1),
        lambda border: passed_along(border, "lat", 1),
    )
    cot_flat = upstream.reshape(-1, model_width)
    grad_out_local = jnp.dot(attended_flat.T, cot_flat, preferred_element_type=jnp.float32)
    down_heads = (
        jnp.dot(cot_flat, w_out.T, preferred_element_type=jnp.float32)
        .astype(jnp.bfloat16)
        .reshape(head_shape)
    )
    output = (latent.astype(jnp.float32) + out_own.astype(jnp.float32)).astype(jnp.bfloat16)
    down_scores = jnp.einsum(
        "abwqhe,abwkhe->abwhqk", down_heads, value_rows, preferred_element_type=jnp.float32
    )
    grad_values = jnp.einsum(
        "abwhqk,abwqhe->abwkhe", attn_low, down_heads, preferred_element_type=jnp.float32
    ).astype(jnp.bfloat16)
    centred = jnp.sum(down_scores * attn_weights, -1, keepdims=True)
    grad_scores = attn_weights * (down_scores - centred)
    bias_terms = jnp.sum(grad_scores, 2)
    grad_bias_local = jax.ops.segment_sum(
        bias_terms.reshape(-1, WTOK * WTOK).T, entry_ids.reshape(-1), num_segments=NREL
    ).T
    grad_bias_local = grad_bias_local.reshape(bias_table.shape)
    scores_low = grad_scores.astype(jnp.bfloat16)
    grad_queries = (
        jnp.einsum(
            "abwhqk,abwkhe->abwqhe", scores_low, key_rows, preferred_element_type=jnp.float32
        )
        * inv_scale
    ).astype(jnp.bfloat16)
    grad_keys = (
        jnp.einsum("abwhqk,abwqhe->abwkhe", scores_low, queries, preferred_element_type=jnp.float32)
        * inv_scale
    ).astype(jnp.bfloat16)
    grads_proj = [
        matrix.reshape(-1, local_width) for matrix in (grad_queries, grad_keys, grad_values)
    ]
    grad_qkv_local = jnp.stack(
        [
            jnp.dot(hidden_flat.T, matrix, preferred_element_type=jnp.float32)
            for matrix in grads_proj
        ]
    )
    input_partial = jnp.dot(grads_proj[0], w_qkv[0].T, preferred_element_type=jnp.float32)
    input_partial = input_partial + jnp.dot(
        grads_proj[1], w_qkv[1].T, preferred_element_type=jnp.float32
    )
    input_partial = input_partial + jnp.dot(
        grads_proj[2], w_qkv[2].T, preferred_element_type=jnp.float32
    )
    grad_hidden = lax.psum(input_partial.astype(jnp.bfloat16), "tp")
    grad_own = leave(
        from_windows(grad_hidden.reshape(win_shape)),
        lambda border: passed_along(border, "lon", 1),
        lambda border: passed_along(border, "lat", 1),
    )
    normed, inv_std, unused = layer_norm(latent, ln_gain)
    grad_float = grad_own.astype(jnp.float32)
    scaled = grad_float * ln_gain
    grad_latent = (
        cotangent.astype(jnp.float32)
        + inv_std
        * (
            scaled
            - jnp.mean(scaled, -1, keepdims=True)
            - normed * jnp.mean(scaled * normed, -1, keepdims=True)
        )
    ).astype(jnp.bfloat16)
    gain_local = jnp.sum((grad_float * normed).reshape(-1, model_width), 0)
    grad_wqkv, grad_wout, grad_gain = lax.psum(
        (grad_qkv_local, grad_out_local, gain_local), ("lon", "lat")
    )
    grad_bias = lax.psum(grad_bias_local.astype(jnp.bfloat16), "lon").astype(jnp.float32)
    return (output, grad_latent, grad_gain, grad_wqkv, grad_wout, grad_bias)


def solution(mesh):
    return jax.shard_map(
        on_device,
        mesh=mesh,
        in_specs=(
            P("lon", "lat", None, None),
            P("lon", "lat", None, None),
            P(),
            P(None, None, "tp"),
            P("tp", None),
            P("lat", None, "tp", None),
        ),
        out_specs=(
            P("lon", "lat", None, None),
            P("lon", "lat", None, None),
            P(),
            P(None, None, "tp"),
            P("tp", None),
            P("lat", None, "tp", None),
        ),
        check_vma=False,
    )
```

profile of v0, /device:TPU:1, one launch (start us, length us, event | category | flops | bytes accessed | tf_op | source)
XLA Modules:
  0.0 1765.5 jit_solution(11339824459877405426)
XLA Ops:
  7.2 1.4 constant_dynamic-update-slice_fusion.1
  9.0 1.5 fusion.51
  10.5 3.2 collective-permute-start
  13.7 6.9 copy.66
  20.6 78.5 %gather_fusion = f32[20736,2,2,4]{3,2,1,0:T(2,128)} fusion(f32[2,2,4,3312]{2,1,3,0:T(2,128)} %copy.66, s32[21504]{0:T(1024)S(1)} %pad_clamp_fusion), kind=kCustom, calls=%fused_computation | custom fusion | bytes 2737152 | tf_op jit(solution)/shard_map/jit(_take)/gather | solution.py:110
  99.1 59.7 %copy.68 = f32[144,144,2,2,4]{0,1,4,3,2:T(8,128)S(1)} copy(f32[144,144,2,2,4]{4,3,2,1,0:T(2,128)} %bitcast.93) | data formatting | bytes 2654208 | tf_op jit(solution)/shard_map/jit(_take)/gather | solution.py:110
  161.3 3.5 collective-permute-start.1
  166.1 1.6 fusion.29
  169.6 2.2 fusion.28
  171.8 4.2 reshape.284
  176.0 2.4 copy.59
  185.8 2.1 reshape.316
  187.9 2.1 copy.69
  190.0 2.1 reshape.317
  192.1 2.1 copy.64
  194.2 2.1 reshape.318
  196.3 2.1 copy.65
  198.4 1.8 fusion.1
  200.2 2.5 fusion.54
  204.8 2.1 reshape.319
  206.9 2.1 copy.75
  209.0 4.0 fusion.10
  213.0 1.8 multiply_reduce_fusion
  214.8 2.1 subtract_multiply_fusion
  218.1 1.3 fusion.12
  219.4 4.1 fusion.11
  223.4 2.5 copy.87
  226.0 1.6 copy.71
  231.1 1.4 fusion.40
  233.5 1.7 copy.85
  235.5 1.4 convolution_add_fusion.1
  237.0 1.3 fusion.7
  239.3 2.5 copy.86
  241.9 2.8 reshape.297
  244.6 3.0 reshape.298
  247.6 6.8 copy.88
  254.5 113.0 %scatter_custom_fusion = f32[3312,16]{1,0:T(8,128)S(1)} fusion(s32[20736]{0:T(1024)} %constant.67, f32[20736,16]{1,0:T(8,128)} %copy.88, f32[]{:T(128)} %constant.17.clone.1), kind=kCustom, calls=%fused_computation.64 | custom fusion | flops 331776 | bytes 212480 | tf_op jit(solution)/shard_map/scatter-add | solution.py:168
  372.9 1.5 slice.113
  375.5 1.9 collective-permute-start.4
  377.4 105.5 %all-reduce.6.cloned.1.call-done = bf16[2,2,4,3312]{3,2,1,0:T(4,128)(2,1)} async-done(((bf16[2,2,4,3312]{3,2,1,0:T(4,128)(2,1)}), bf16[2,2,4,3312]{3,2,1,0:T(4,128)(2,1)}) %all-reduce.6.cloned.1.call-update) | async-done | bytes 106000 | tf_op jit(solution)/shard_map/psum | solution.py:221
  482.9 1.6 convert_element_type.132
  485.0 2.8 collective-permute-start.2
  489.5 4.4 collective-permute-done.2
  495.3 1.5 fusion.26
  496.8 318.9 %psum.44 = f32[512]{0:T(512)} all-reduce(f32[512]{0:T(512)S(1)} %get-tuple-element.6), channel_id=1, replica_groups=mesh['lon'=16,'lat'=8,'tp'=2] {'lon','lat'}, use_global_device_ids=true, to_apply=%region_12.13 | all-reduce | flops 512 | bytes 4096 | tf_op jit(solution)/shard_map/psum | solution.py:218
  815.7 2.5 fusion.23
  818.2 937.0 %all-reduce.8.cloned.1.call-done = (f32[3,512,256]{2,1,0:T(8,128)}, f32[256,512]{1,0:T(8,128)}) async-done(((f32[3,512,256]{2,1,0:T(8,128)}, f32[256,512]{1,0:T(8,128)}), (f32[3,512,256]{2,1,0:T(8,128)}, f32[256,512]{1,0:T(8,128)})) %all-reduce.8.cloned.1.call-update) | async-done | bytes 2097168 | tf_op jit(solution)/shard_map/psum | solution.py:218
  1755.2 2.7 copy.110
  (142 shorter events, 33.1 us)
Async XLA Ops:
  7.2 196.6 %copy-start = (bf16[256,512]{1,0:T(8,128)(2,1)S(1)}, bf16[256,512]{1,0:T(8,128)(2,1)}, u32[]{:S(2)}) copy-start(bf16[256,512]{1,0:T(8,128)(2,1)} %param.13) | copy-start | bytes 786436
  7.2 1.5 copy-start.22
  7.2 365.7 %all-reduce.10.cloned.1.call-start = ((), (), s32[]{:S(2)}) async-start(), calls=%async_computation.2 | async-start | bytes 2359296 | tf_op jit(solution)/shard_map/psum | solution.py:94
  8.9 4.8 copy-start.31
  10.5 149.7 %collective-permute-start = (bf16[6,12,4,1024]{3,2,1,0:T(4,128)(2,1)}, bf16[6,12,4,1024]{3,2,1,0:T(4,128)(2,1)}, u32[]{:S(2)}, u32[]{:S(2)}) collective-permute-start(bf16[6,12,4,1024]{3,2,1,0:T(4,128)(2,1)} %get-tuple-element.14), channel_id=1, source_target_pairs={{0,240},{16,0},{32,16},{48,32},{64,48},{80,64},{96,80},{112,96},{1... | collective-permute-start | bytes 1769480 | tf_op jit(solution)/shard_map/ppermute | solution.py:19
  13.7 6.9 copy-start.32
  99.1 59.7 %copy-start.35 = (pred[144]{0:T(512)(128)(4,1)S(1)}, pred[144]{0:T(512)(128)(4,1)}, u32[]{:S(2)}) copy-start(pred[144]{0:T(512)(128)(4,1)} %constant.54.clone) | copy-start | bytes 436
  99.1 59.8 %copy-start.34 = (pred[144]{0:T(512)(128)(4,1)S(1)}, pred[144]{0:T(512)(128)(4,1)}, u32[]{:S(2)}) copy-start(pred[144]{0:T(512)(128)(4,1)} %constant.53.clone) | copy-start | bytes 436
  99.1 60.0 %copy-start.1 = (bf16[12,12,4,512]{3,2,1,0:T(4,128)(2,1)S(1)}, bf16[12,12,4,512]{3,2,1,0:T(4,128)(2,1)}, u32[]{:S(2)}) copy-start(bf16[12,12,4,512]{3,2,1,0:T(4,128)(2,1)} %param.9) | copy-start | bytes 1769476
  158.8 1.4 copy-start.9
  161.3 7.2 collective-permute-start.1
  178.4 2.0 copy-start.33
  180.4 1.1 copy-start.27
  181.4 2.2 copy-start.4
  194.2 4.2 copy-start.28
  200.2 2.6 copy-start.6
  200.2 2.6 copy-start.24
  202.8 10.3 copy-start.2
  202.8 0.9 copy-start.7
  214.8 2.1 copy-start.11
  216.9 1.1 copy-start.10
  227.9 0.8 copy-start.14
  228.6 1.6 copy-start.26
  231.1 2.0 copy-start.16
  231.1 1.5 copy-start.25
  233.4 3.5 copy-start.20
  235.5 1.5 copy-start.18
  239.3 5.3 copy-start.3
  254.4 228.4 %all-reduce.6.cloned.1.call-start = ((), (), s32[]{:S(2)}) async-start(), calls=%async_computation | async-start | bytes 212992 | tf_op jit(solution)/shard_map/psum | solution.py:221
  367.6 1.1 copy-start.5
  367.6 1.1 copy-start.19
  367.6 1.6 copy-start.21
  368.8 1.0 copy-start.17
  369.2 1.1 copy-start.8
  369.2 1.2 copy-start.15
  371.5 1383.7 %all-reduce.8.cloned.1.call-start = ((), (), s32[]{:S(2)}) async-start(), calls=%async_computation.1 | async-start | bytes 4194304 | tf_op jit(solution)/shard_map/psum | solution.py:218
  372.9 4.5 copy-start.30
  372.9 111.6 %copy-start.12 = (bf16[12,12,4,512]{3,2,1,0:T(4,128)(2,1)S(1)}, bf16[12,12,4,512]{3,2,1,0:T(4,128)(2,1)}, u32[]{:S(2)}) copy-start(bf16[12,12,4,512]{3,2,1,0:T(4,128)(2,1)} %get-tuple-element.11) | copy-start | bytes 1769476
  375.4 112.3 %copy-start.13 = (bf16[12,12,4,512]{3,2,1,0:T(4,128)(2,1)S(1)}, bf16[12,12,4,512]{3,2,1,0:T(4,128)(2,1)}, u32[]{:S(2)}) copy-start(bf16[12,12,4,512]{3,2,1,0:T(4,128)(2,1)} %get-tuple-element.12) | copy-start | bytes 1769476
  375.5 112.3 %collective-permute-start.4 = (bf16[12,3,4,512]{3,2,1,0:T(4,128)(2,1)S(1)}, bf16[12,3,4,512]{3,2,1,0:T(4,128)(2,1)S(1)}, u32[]{:S(2)}, u32[]{:S(2)}) collective-permute-start(bf16[12,3,4,512]{3,2,1,0:T(4,128)(2,1)S(1)} %pad_maximum_fusion.6), channel_id=1, source_target_pairs={{0,2},{2,4},{4,6},{6,8},{8,10},{10,12},{12,14},{14,0},{1,3},{3,5},... | collective-permute-start | bytes 442376 | tf_op jit(solution)/shard_map/ppermute | solution.py:19
  485.0 8.9 collective-permute-start.2
  488.5 6.7 collective-permute-start.5
  494.6 321.1 %copy-start.23 = (bf16[12,12,4,512]{3,2,1,0:T(4,128)(2,1)S(1)}, bf16[12,12,4,512]{3,2,1,0:T(4,128)(2,1)}, u32[]{:S(2)}) copy-start(bf16[12,12,4,512]{3,2,1,0:T(4,128)(2,1)} %param.10) | copy-start | bytes 1769476
  494.6 321.0 %collective-permute-start.3 = (bf16[6,12,4,512]{3,2,1,0:T(4,128)(2,1)S(1)}, bf16[6,12,4,512]{3,2,1,0:T(4,128)(2,1)S(1)}, u32[]{:S(2)}, u32[]{:S(2)}) collective-permute-start(bf16[6,12,4,512]{3,2,1,0:T(4,128)(2,1)S(1)} %get-tuple-element.19), channel_id=1, source_target_pairs={{0,16},{16,32},{32,48},{48,64},{64,80},{80,96},{96,112},{112,128},... | collective-permute-start | bytes 884744 | tf_op jit(solution)/shard_map/ppermute | solution.py:19
  1755.2 2.7 copy-start.29
Sparse Core Ops, SparseCore 0:
  254.5 61.0 all-reduce.9
  371.7 111.1 all-reduce.5
  486.1 1269.0 all-reduce.7
where the time goes:
time: 1780 us; the launch traced here: 1770 us
  waiting for transfers between devices  1050 us (59%)
  blocking collectives  319 us (18%)
  local copies, waits for them, and re-layouts  207 us (12%)
  other arithmetic  138 us (8%)
  matrix products  25.2 us (1%)
    psum x1, waiting for transfers between devices, on_device(): lax.psum((grad_qkv_local, grad_out_local, gain_local), ('lon', 'lat'))  937 us
    psum x1, blocking collectives, on_device(): lax.psum((grad_qkv_local, grad_out_local, gain_local), ('lon', 'lat'))  319 us
    gather x2, local copies, waits for them, and re-layouts, on_device(): bias_full = jnp.take(bias_table, entry_ids, axis=3)  138 us
    scatter-add x1, other arithmetic, on_device(): jax.ops.segment_sum(bias_terms.reshape(-1, WTOK * WTOK).T, entry_ids.resh...  113 us
    psum x1, waiting for transfers between devices, on_device(): lax.psum(grad_bias_local.astype(jnp.bfloat16), 'lon').astype(jnp.float32)  105 us
  transfers between devices with their start and end apart: 9, of which 4 were waited for; matrix products, arithmetic and copies ran while one was open for 16% of the time, Pallas kernels for 0%

commit v1 on v0

v1 whole, which is shorter than its diff:
```python
import jax
import jax.numpy as jnp
import numpy as np
from jax import lax
from jax.experimental import pallas as pl
from jax.experimental.pallas import tpu as pltpu
from jax.sharding import PartitionSpec as P

BF = jnp.bfloat16
F32 = jnp.float32
WTOK = 144
OFFS = 23
NT = (((1,), (1,)), ((), ()))
TN = (((0,), (0,)), ((), ()))
SECTIONS = (216, 216, 72, 72)


def section_rows(lon, lat, lev, low):
    lon_first, lat_first = lon < 6, lat < 9
    if low:
        lon_first, lat_first = lon >= 6, lat >= 3
        lon_at = lon - 6 if lon_first else lon
        lat_at = lat - 3 if lat_first else lat
    else:
        lon_at = lon if lon_first else lon - 6
        lat_at = lat if lat_first else lat - 9
    section = (0 if lon_first else 1) + (0 if lat_first else 2)
    return section, (lon_at * (9 if lat_first else 3) + lat_at) * 4 + lev


def placements():
    to_window = [np.zeros((576, n), np.float32) for n in SECTIONS]
    to_owner = [np.zeros((576, n), np.float32) for n in SECTIONS]
    for a in range(2):
        for b in range(2):
            for p in range(12):
                for s in range(2):
                    for r in range(6):
                        row = (a * 2 + b) * WTOK + p * 12 + s * 6 + r
                        section, at = section_rows(p, a * 6 + r, (b * 2 + s + 1) % 4, False)
                        to_window[section][row, at] = 1
    for lon in range(12):
        for lat in range(12):
            for lev in range(4):
                section, at = section_rows(lon, lat, lev, True)
                to_owner[section][(lon * 12 + lat) * 4 + lev, at] = 1
    return to_window, to_owner


def offset_matrix():
    spread = np.zeros((12, 12 * OFFS, WTOK), np.float32)
    for p_t in range(12):
        for p_u in range(12):
            for rs in range(12):
                spread[p_t, rs * OFFS + p_u - p_t + 11, p_u * 12 + rs] = 1
    return spread


TO_WINDOW, TO_OWNER = placements()
SPREAD = offset_matrix()


def dot(a, b, dims=(((1,), (0,)), ((), ()))):
    return lax.dot_general(a, b, dims, preferred_element_type=F32)


def call(body, outs, args, scratch=(), smem=1):
    vmem = pl.BlockSpec(memory_space=pltpu.VMEM)
    return pl.pallas_call(
        body,
        out_shape=[jax.ShapeDtypeStruct(s, t) for s, t in outs],
        in_specs=[pl.BlockSpec(memory_space=pltpu.SMEM)] * smem + [vmem] * (len(args) - smem),
        out_specs=[vmem] * len(outs),
        scratch_shapes=list(scratch),
        compiler_params=pltpu.CompilerParams(vmem_limit_bytes=50 * 1024 * 1024),
    )(*args)


def bias_kernel(info, table, spread, bias):
    full = table[...]
    high = full.astype(BF)
    rest = full - high.astype(F32)
    mid = rest.astype(BF)
    low = (rest - mid.astype(F32)).astype(BF)
    row = lax.broadcasted_iota(jnp.int32, (192, WTOK), 0)
    col = lax.broadcasted_iota(jnp.int32, (192, WTOK), 1)
    rs_t, rs_u = row % 12, col % 12
    s_t, s_u = (rs_t >= 6).astype(jnp.int32), (rs_u >= 6).astype(jnp.int32)
    edge_t = (rs_t - s_t * 6 >= 3).astype(jnp.int32)
    edge_u = (rs_u - s_u * 6 >= 3).astype(jnp.int32)
    last_lat = (row >= 96).astype(jnp.int32) * info[0]
    last_lev = ((row % 96) >= 48).astype(jnp.int32)
    barred = (last_lat * (edge_t - edge_u) != 0) | (last_lev * (s_t - s_u) != 0)
    for p in range(12):
        at = dot(low, spread[p]) + dot(mid, spread[p])
        at = at + dot(high, spread[p])
        at = jnp.where(barred, -jnp.inf, at)
        for i in range(16):
            bias[i * WTOK + p * 12 : i * WTOK + p * 12 + 12, :] = at[i * 12 : i * 12 + 12]


def main_kernel(info, own, lon, lat, cor, t0, t1, t2, t3, b0, b1, b2, b3, gain, w_qkv, w_out, bias,
                o_own, o_lon, o_lat, o_cor, keep, send, o_ds, att_s, gq_s, gk_s, gv_s):
    def gathered(which):
        return dot(t0[...], own[which]) + dot(t1[...], lon[which]) + dot(t2[...], lat[which]) + dot(t3[...], cor[which])

    values = gathered(0)
    cot = gathered(1).astype(BF)
    shifted = values - jnp.mean(values, -1, keepdims=True)
    normed = shifted * lax.rsqrt(jnp.mean(shifted * shifted, -1, keepdims=True) + 1e-05)
    hidden = (normed * gain[...]).astype(BF)
    q, k, v = [dot(hidden, w_qkv[j]).astype(BF) for j in range(3)]
    down = dot(cot, w_out[...], NT).astype(BF)
    head = lax.broadcasted_iota(jnp.int32, (WTOK, 256), 1) // 64

    def stacked(rows):
        return jnp.concatenate([jnp.where(head == h, rows, jnp.zeros_like(rows)) for h in range(4)], 0)

    def unstacked(rows):
        total = jnp.zeros((WTOK, 256), F32)
        for h in range(4):
            total = jnp.where(head == h, rows[h * WTOK : (h + 1) * WTOK], total)
        return total

    for w in range(4):
        rows = slice(w * WTOK, (w + 1) * WTOK)
        four = slice(w * 576, (w + 1) * 576)
        qs, ds_ = stacked(q[rows]), stacked(down[rows])
        scores = dot(qs, k[rows], NT) * 0.125 + bias[four, :]
        exps = jnp.exp(scores - jnp.max(scores, -1, keepdims=True))
        probs = exps / jnp.sum(exps, -1, keepdims=True)
        probs_low = probs.astype(BF)
        att_s[rows, :] = unstacked(dot(probs_low, v[rows])).astype(BF)
        dp = dot(ds_, v[rows], NT)
        gv_s[rows, :] = dot(probs_low, ds_, TN).astype(BF)
        grad = probs * (dp - jnp.sum(dp * probs, -1, keepdims=True))
        o_ds[four, :] = grad
        grad_low = grad.astype(BF)
        gq_s[rows, :] = unstacked(dot(grad_low, k[rows]) * 0.125).astype(BF)
        gk_s[rows, :] = (dot(grad_low, qs, TN) * 0.125).astype(BF)

    att, gq, gk, gv = att_s[...], gq_s[...], gk_s[...], gv_s[...]
    out_part = dot(att, w_out[...]).astype(BF)
    hid_part = (dot(gq, w_qkv[0], NT) + dot(gk, w_qkv[1], NT) + dot(gv, w_qkv[2], NT)).astype(BF)
    for back, ref in ((b0, o_own), (b1, o_lon), (b2, o_lat), (b3, o_cor)):
        ref[0] = dot(back[...], out_part).astype(BF)
        ref[1] = dot(back[...], hid_part).astype(BF)
    wo = dot(att, cot, TN)
    first = [dot(hidden, gq, TN), dot(hidden, gk, TN)]
    second = [dot(hidden, gv, TN), jnp.concatenate([wo[:, :256], wo[:, 256:]], 0)]
    core = info[1]
    for j in range(2):
        rows = slice(j * 512, (j + 1) * 512)
        keep[rows, :] = jnp.where(core == 0, first[j], second[j])
        send[rows, :] = jnp.where(core == 0, second[j], first[j]).astype(BF)

def core_sum_kernel(keep, recv, total):
    total[...] = (keep[...] + recv[...].astype(F32)).astype(BF)


def chip_sum_kernel(parts, out):
    total = parts[0].astype(F32)
    for j in range(1, 64):
        total = total + parts[j].astype(F32)
    total = total.astype(BF)
    for j in range(64):
        out[j] = total


def weights_kernel(info, mine, other, w_qkv, wqkv, wout, gain):
    first = jnp.where(info[1] == 0, mine[...], other[...]).astype(F32)
    second = jnp.where(info[1] == 0, other[...], mine[...]).astype(F32)
    wqkv[0] = first[:512]
    wqkv[1] = first[512:]
    wqkv[2] = second[:512]
    wout[:, 0:256] = second[512:768]
    wout[:, 256:512] = second[768:]
    total = first[:512] * w_qkv[0].astype(F32)
    total = total + first[512:] * w_qkv[1].astype(F32)
    total = total + second[:512] * w_qkv[2].astype(F32)
    gain[...] = jnp.sum(total, -1, keepdims=True)


def bias_grad_kernel(info, ds, spread, keep, send, part):
    total = jnp.zeros((192, 12 * OFFS), F32)
    for p in range(12):
        for i in range(16):
            part[i * 12 : i * 12 + 12, :] = ds[i * WTOK + p * 12 : i * WTOK + p * 12 + 12, :]
        rows = part[...]
        high = rows.astype(BF)
        low = (rows - high.astype(F32)).astype(BF)
        total = total + dot(high, spread[p], NT) + dot(low, spread[p], NT)
    keep[...] = jnp.where(info[1] == 0, total[:96], total[96:])
    send[...] = jnp.where(info[1] == 0, total[96:], total[:96]).astype(BF)


def pair_sum_kernel(a1, a2, a3, b1, b2, b3, o1, o2, o3):
    for a, b, o in ((a1, b1, o1), (a2, b2, o2), (a3, b3, o3)):
        o[...] = (a[...].astype(F32) + b[...].astype(F32)).astype(BF)


def final_kernel(latent, cot, gain, own_a, own_b, lon, lat, cor, t0, t1, t2, t3, output, grad):
    own = [(own_a[j].astype(F32) + own_b[j].astype(F32)).astype(BF) for j in range(2)]

    def placed(which):
        return dot(t0[...], own[which]) + dot(t1[...], lon[which]) + dot(t2[...], lat[which]) + dot(t3[...], cor[which])

    values = latent[...].astype(F32)
    output[...] = (values + placed(0)).astype(BF)
    shifted = values - jnp.mean(values, -1, keepdims=True)
    inv_std = lax.rsqrt(jnp.mean(shifted * shifted, -1, keepdims=True) + 1e-05)
    normed = shifted * inv_std
    scaled = placed(1) * gain[...]
    inner = scaled - jnp.mean(scaled, -1, keepdims=True) - normed * jnp.mean(scaled * normed, -1, keepdims=True)
    grad[...] = (cot[...].astype(F32) + inv_std * inner).astype(BF)


def moved(value, by_lon, by_lat):
    n_lon, n_lat = lax.axis_size("lon"), lax.axis_size("lat")
    pairs = [
        (i * n_lat + j, (i + by_lon) % n_lon * n_lat + (j + by_lat) % n_lat)
        for i in range(n_lon)
        for j in range(n_lat)
    ]
    return lax.ppermute(value, ("lon", "lat"), pairs)


def swapped(value, lon_bits, lat_bits):
    n_lon, n_lat = lax.axis_size("lon"), lax.axis_size("lat")
    pairs = [(i * n_lat + j, (i ^ lon_bits) * n_lat + (j ^ lat_bits)) for i in range(n_lon) for j in range(n_lat)]
    return lax.ppermute(value, ("lon", "lat"), pairs)


def chip_groups():
    n_lon, n_lat = lax.axis_size("lon"), lax.axis_size("lat")
    return [[i * n_lat + j for i in range(core, n_lon, 2) for j in range(n_lat)] for core in range(2)]


def other_group(value):
    return lax.ppermute(value, "tp", [(0, 1), (1, 0)])


def on_device(latent, cotangent, ln_gain, w_qkv, w_out, bias_table):
    to_window = [jnp.asarray(m, BF) for m in TO_WINDOW]
    to_section = [jnp.asarray(m.T, BF) for m in TO_WINDOW]
    to_owner = [jnp.asarray(m, BF) for m in TO_OWNER]
    spread = jnp.asarray(SPREAD, BF)
    i_lon, i_lat = lax.axis_index("lon"), lax.axis_index("lat")
    last = (i_lat == lax.axis_size("lat") - 1).astype(jnp.int32)
    core = i_lon % 2
    info = jnp.stack([last, core]).astype(jnp.int32)
    gain = ln_gain.reshape(1, 512)

    def section(lon, lat):
        return jnp.stack([latent[lon, lat].reshape(-1, 512), cotangent[lon, lat].reshape(-1, 512)])

    low_lon, low_lat, high_lon, high_lat = slice(0, 6), slice(0, 3), slice(6, 12), slice(3, 12)
    in_lon = moved(section(low_lon, high_lat), -1, 0)
    in_lat = moved(section(high_lon, low_lat), 0, -1)
    in_cor = moved(section(low_lon, low_lat), -1, -1)
    in_own = section(high_lon, high_lat)

    table = bias_table.reshape(16, 2, 2, 6, 6 * OFFS).transpose(0, 1, 3, 2, 4).reshape(192, 12 * OFFS)
    (bias,) = call(bias_kernel, [((16 * WTOK, WTOK), F32)], [info, table, spread])

    part = lambda n: ((2, n, 512), BF)
    p_own, p_lon, p_lat, p_cor, keep, send, ds = call(
        main_kernel,
        [part(216), part(216), part(72), part(72), ((1024, 256), F32), ((1024, 256), BF), ((16 * WTOK, WTOK), F32)],
        [info, in_own, in_lon, in_lat, in_cor, *to_window, *to_section, gain, w_qkv, w_out, bias],
        [pltpu.VMEM((576, 256), BF)] * 4,
    )

    recv = swapped(send, 1, 0)
    (total,) = call(core_sum_kernel, [((1024, 256), BF)], [keep, recv], smem=0)
    groups = chip_groups()
    parts = lax.all_to_all(total.reshape(64, 16, 256), ("lon", "lat"), 0, 0, axis_index_groups=groups)
    (copies,) = call(chip_sum_kernel, [((64, 16, 256), BF)], [parts], smem=0)
    mine = lax.all_to_all(copies, ("lon", "lat"), 0, 0, axis_index_groups=groups).reshape(1024, 256)
    grad_wqkv, grad_wout, gain_part = call(
        weights_kernel,
        [((3, 512, 256), F32), ((256, 512), F32), ((512, 1), F32)],
        [info, mine, swapped(mine, 1, 0), w_qkv],
    )
    gain_part = gain_part.reshape(512)
    grad_gain = (gain_part + other_group(gain_part)) / ln_gain

    b_keep, b_send = call(
        bias_grad_kernel,
        [((96, 12 * OFFS), F32), ((96, 12 * OFFS), BF)],
        [info, ds, spread],
        [pltpu.VMEM((192, WTOK), F32)],
    )
    b_sum = (b_keep + swapped(b_send, 1, 0).astype(F32)).astype(BF)
    for bits in (2, 4, 8):
        b_sum = (b_sum.astype(F32) + swapped(b_sum, bits, 0).astype(F32)).astype(BF)
    b_other = swapped(b_sum, 1, 0)
    b_all = jnp.where(core == 0, jnp.stack([b_sum, b_other]), jnp.stack([b_other, b_sum]))
    grad_bias = b_all.reshape(16, 2, 6, 2, 6 * OFFS).transpose(0, 1, 3, 2, 4).astype(F32)
    grad_bias = grad_bias.reshape(bias_table.shape)

    halves = [p_lon, p_lat, p_cor]
    others = [other_group(p) for p in halves]
    own_other = other_group(p_own)
    s_lon, s_lat, s_cor = call(pair_sum_kernel, [part(216), part(72), part(72)], halves + others, smem=0)
    r_lon, r_lat, r_cor = moved(s_lon, 1, 0), moved(s_lat, 0, 1), moved(s_cor, 1, 1)
    output, grad_latent = call(
        final_kernel,
        [((576, 512), BF), ((576, 512), BF)],
        [latent.reshape(576, 512), cotangent.reshape(576, 512), gain, p_own, own_other, r_lon, r_lat, r_cor, *to_owner],
        smem=0,
    )
    return (
        output.reshape(latent.shape),
        grad_latent.reshape(latent.shape),
        grad_gain,
        grad_wqkv,
        grad_wout,
        grad_bias,
    )


def solution(mesh):
    specs = (
        P("lon", "lat", None, None),
        P("lon", "lat", None, None),
        P(),
        P(None, None, "tp"),
        P("tp", None),
        P("lat", None, "tp", None),
    )
    return jax.shard_map(on_device, mesh=mesh, in_specs=specs, out_specs=specs, check_vma=False)
```

time: 1780 us -> 133 us (0.07)
  waiting for transfers between devices: 1050 us -> 10.8 us
  blocking collectives: 319 us -> 24.9 us
  local copies, waits for them, and re-layouts: 207 us -> 20.3 us
  other arithmetic: 138 us -> 5.32 us
  starting transfers between devices: 13.2 us -> 42.3 us
  Pallas kernels: 0 us -> 27.4 us
  matrix products: 25.2 us -> 0 us
    psum x3 -> x0, waiting for transfers between devices: 1040 us -> none  [the longest x1 937 us: on_device(): lax.psum((grad_qkv_local, grad_out_local, gain_local), ('lon', 'lat'))]
    psum x1 -> x0, blocking collectives: 319 us -> none  [on_device(): lax.psum((grad_qkv_local, grad_out_local, gain_local), ('lon', 'lat'))]
    gather x2 -> x0, local copies, waits for them, and re-layouts: 138 us -> none  [on_device(): bias_full = jnp.take(bias_table, entry_ids, axis=3)]
    scatter-add x1 -> x0, other arithmetic: 113 us -> none  [on_device(): jax.ops.segment_sum(bias_terms.reshape(-1, WTOK * WTOK).T, entry_ids.resh...]
    pallas_call x0 -> x8, Pallas kernels: none -> 27.4 us  [call(): pl.pallas_call(body, out_shape=[jax.ShapeDtypeStruct(s, t) for s, t in ou...]
    dot_general x18 -> x0, matrix products: 25.2 us -> none  [the longest x1 4.07 us: on_device(): jnp.einsum('abwhqk,abwqhe->abwkhe', attn_low, down_heads, preferred_eleme...]
    all_to_all x0 -> x1, blocking collectives: none -> 24.9 us  [on_device(): lax.all_to_all(total.reshape(64, 16, 256), ('lon', 'lat'), 0, 0, axis_ind...]
    ppermute x6 -> x18, starting transfers between devices: 13 us -> 35.1 us  [the longest x6 19.5 us: moved(): return lax.ppermute(value, ('lon', 'lat'), pairs)]
  transfers between devices with their start and end apart: 9 -> 19, of which waited for: 4 -> 5; matrix products, arithmetic and copies ran while one was open for 16% -> 13% of each run, Pallas kernels for 0% -> 11%
where the time goes in v1:
time: 133 us; the launch traced here: 132 us
  starting transfers between devices  42.3 us (32%)
  Pallas kernels  27.4 us (21%)
  blocking collectives  24.9 us (19%)
  local copies, waits for them, and re-layouts  20.3 us (15%)
  waiting for transfers between devices  10.8 us (8%)
  other arithmetic  5.32 us (4%)
    pallas_call x8, Pallas kernels, call(): pl.pallas_call(body, out_shape=[jax.ShapeDtypeStruct(s, t) for s, t in ou...  27.4 us
    all_to_all x1, blocking collectives, on_device(): lax.all_to_all(total.reshape(64, 16, 256), ('lon', 'lat'), 0, 0, axis_ind...  24.9 us
    ppermute x6, starting transfers between devices, moved(): return lax.ppermute(value, ('lon', 'lat'), pairs)  19.5 us
    ppermute x7, starting transfers between devices, swapped(): return lax.ppermute(value, ('lon', 'lat'), pairs)  12.6 us
    ppermute x7, waiting for transfers between devices, swapped(): return lax.ppermute(value, ('lon', 'lat'), pairs)  8.34 us
    all_to_all x1, starting transfers between devices, on_device(): lax.all_to_all(copies, ('lon', 'lat'), 0, 0, axis_index_groups=groups)  7.19 us
    unnamed x42, local copies, waits for them, and re-layouts  3.58 us
    ppermute x5, starting transfers between devices, other_group(): return lax.ppermute(value, 'tp', [(0, 1), (1, 0)])  3.06 us
  transfers between devices with their start and end apart: 19, of which 5 were waited for; matrix products, arithmetic and copies ran while one was open for 13% of the time, Pallas kernels for 11%

profile of v1, /device:TPU:1, one launch (start us, length us, event | category | flops | bytes accessed | tf_op | source)
XLA Modules:
  0.0 132.1 jit_solution(8271897412896096233)
XLA Ops:
  0.6 1.9 %fusion.3 = (bf16[6,9,4,512]{3,2,1,0:T(4,128)(2,1)S(1)}, bf16[6,9,4,512]{3,2,1,0:T(4,128)(2,1)}) fusion(bf16[12,12,4,512]{3,2,1,0:T(4,128)(2,1)} %param.19), kind=kLoop, calls=%fused_computation.14 | loop fusion | bytes 884736 | tf_op jit(solution)/shard_map/slice | solution.py:255
  2.6 1.9 %fusion.4 = (bf16[6,9,4,512]{3,2,1,0:T(4,128)(2,1)S(1)}, bf16[6,9,4,512]{3,2,1,0:T(4,128)(2,1)}) fusion(bf16[12,12,4,512]{3,2,1,0:T(4,128)(2,1)} %param.20), kind=kLoop, calls=%fused_computation.15 | loop fusion | bytes 884736 | tf_op jit(solution)/shard_map/slice | solution.py:255
  4.6 0.8 pad_maximum_fusion.1
  5.4 3.2 %collective-permute-start = (bf16[2,216,512]{2,1,0:T(8,128)(2,1)}, bf16[2,216,512]{2,1,0:T(8,128)(2,1)}, u32[]{:S(2)}, u32[]{:S(2)}) collective-permute-start(bf16[2,216,512]{2,1,0:T(8,128)(2,1)} %pad_maximum_fusion.1), channel_id=1, source_target_pairs={{0,240},{2,242},{4,244},{6,246},{8,248},{10,250},{12,252},{14,254}... | collective-permute-start | bytes 1327112 | tf_op jit(solution)/shard_map/ppermute | solution.py:225
  8.6 1.0 fusion.1
  9.6 1.1 fusion.2
  10.8 3.5 %collective-permute-start.1 = (bf16[2,72,512]{2,1,0:T(8,128)(2,1)S(1)}, bf16[2,72,512]{2,1,0:T(8,128)(2,1)S(1)}, u32[]{:S(2)}, u32[]{:S(2)}) collective-permute-start(bf16[2,72,512]{2,1,0:T(8,128)(2,1)S(1)} %pad_maximum_fusion.2), channel_id=1, source_target_pairs={{0,14},{2,0},{4,2},{6,4},{8,6},{10,8},{12,10},{14,12},{16,30},{18,... | collective-permute-start | bytes 442376 | tf_op jit(solution)/shard_map/ppermute | solution.py:225
  14.4 0.7 pad_maximum_fusion.3
  15.0 5.7 %collective-permute-start.2 = (bf16[2,72,512]{2,1,0:T(8,128)(2,1)}, bf16[2,72,512]{2,1,0:T(8,128)(2,1)S(1)}, u32[]{:S(2)}, u32[]{:S(2)}) collective-permute-start(bf16[2,72,512]{2,1,0:T(8,128)(2,1)} %pad_maximum_fusion.3), channel_id=1, source_target_pairs={{0,254},{2,240},{4,242},{6,244},{8,246},{10,248},{12,250},{14,252}... | collective-permute-start | bytes 442376 | tf_op jit(solution)/shard_map/ppermute | solution.py:225
  21.8 1.0 stack_reshape.24
  22.8 1.0 stack_reshape.25
  24.0 4.0 %shard_map.226.bias = f32[2304,144]{1,0:T(8,128)} custom-call(s32[2]{0:T(128)S(1)} %pad_add_fusion.info, f32[192,276]{1,0:T(8,128)S(1)} %reshape.59.table, bf16[12,276,144]{2,1,0:T(8,128)(2,1)S(1)} %copy-done), custom_call_target="tpu_custom_call" | custom-call | tf_op jit(solution)/shard_map/pallas_call | solution.py:69
  28.1 0.7 copy-done.15
  28.8 0.9 copy-done.16
  29.7 11.6 %shard_map.227 = (bf16[2,216,512]{2,1,0:T(8,128)(2,1)S(1)}, bf16[2,216,512]{2,1,0:T(8,128)(2,1)S(1)}, bf16[2,72,512]{2,1,0:T(8,128)(2,1)S(1)}, bf16[2,72,512]{2,...) custom-call(s32[2]{0:T(128)S(1)} %pad_add_fusion.info, ...), custom_call_target="tpu_custom_call" | custom-call | tf_op jit(solution)/shard_map/pallas_call | solution.py:69
  41.5 1.9 %collective-permute-done.10.recv = bf16[1024,256]{1,0:T(8,128)(2,1)S(1)} collective-permute-done((bf16[1024,256]{1,0:T(8,128)(2,1)}, bf16[1024,256]{1,0:T(8,128)(2,1)S(1)}, u32[]{:S(2)}, u32[]{:S(2)}) %collective-permute-start.10) | collective-permute-done | bytes 524320 | tf_op jit(solution)/shard_map/ppermute | solution.py:231
  43.4 1.2 copy-done.2
  44.8 24.9 %all_to_all.10.parts = bf16[64,16,256]{2,1,0:T(8,128)(2,1)S(1)} all-to-all(bf16[64,16,256]{2,1,0:T(8,128)(2,1)S(1)} %bitcast.11), channel_id=1, replica_groups={{0,2,4,6,8,10,12,14,32,34,36,38,40,42,44,46,64,66,68,70,72,74,76,78,96,..., dimensions={0} | all-to-all | bytes 1048576 | tf_op jit(solution)/shard_map/all_to_all | solution.py:277
  69.6 0.9 shard_map.231
  70.5 7.2 %all-to-all-start.1 = ((bf16[64,16,256]{2,1,0:T(8,128)(2,1)}), bf16[64,16,256]{2,1,0:T(8,128)(2,1)S(1)}, u32[]{:S(2)}, u32[]{:S(2)}) async-start(bf16[64,16,256]{2,1,0:T(8,128)(2,1)} %shard_map.231), calls=%async_computation.1 | async-start | bytes 1048576 | tf_op jit(solution)/shard_map/all_to_all | solution.py:279
  77.7 3.5 %shard_map.233 = (f32[96,276]{1,0:T(8,128)S(1)}, bf16[96,276]{1,0:T(8,128)(2,1)S(1)}) custom-call(s32[2]{0:T(128)S(1)} %pad_add_fusion.info, f32[2304,144]{1,0:T(8,128)} %get-tuple-element.37.ds, bf16[12,276,144]{2,1,0:T(8,128)(2,1)S(1)} %copy-done), custom_call_target="tpu_custom_call" | custom-call | tf_op jit(solution)/shard_map/pallas_call | solution.py:69
  81.2 1.6 %collective-permute-start.13 = (bf16[96,276]{1,0:T(8,128)(2,1)S(1)}, bf16[96,276]{1,0:T(8,128)(2,1)S(1)}, u32[]{:S(2)}, u32[]{:S(2)}) collective-permute-start(bf16[96,276]{1,0:T(8,128)(2,1)S(1)} %get-tuple-element.39), channel_id=1, source_target_pairs={{0,16},{2,18},{4,20},{6,22},{8,24},{10,26},{12,28},{14,30},{16,0},... | collective-permute-start | bytes 158984 | tf_op jit(solution)/shard_map/ppermute | solution.py:231
  82.8 0.9 collective-permute-done.13
  83.8 1.4 %collective-permute-start.14 = (bf16[96,276]{1,0:T(8,128)(2,1)S(1)}, bf16[96,276]{1,0:T(8,128)(2,1)S(1)}, u32[]{:S(2)}, u32[]{:S(2)}) collective-permute-start(bf16[96,276]{1,0:T(8,128)(2,1)S(1)} %add_convert_fusion.3), channel_id=1, source_target_pairs={{0,32},{2,34},{4,36},{6,38},{8,40},{10,42},{12,44},{14,46},{16,48}... | collective-permute-start | bytes 158984 | tf_op jit(solution)/shard_map/ppermute | solution.py:231
  85.5 5.5 %collective-permute-done.14 = bf16[96,276]{1,0:T(8,128)(2,1)S(1)} collective-permute-done((bf16[96,276]{1,0:T(8,128)(2,1)S(1)}, bf16[96,276]{1,0:T(8,128)(2,1)S(1)}, u32[]{:S(2)}, u32[]{:S(2)}) %collective-permute-start.14) | collective-permute-done | bytes 53024 | tf_op jit(solution)/shard_map/ppermute | solution.py:231
  91.0 1.1 collective-permute-start.15
  92.4 1.1 collective-permute-start.6
  93.7 4.8 %collective-permute-start.11 = (bf16[1024,256]{1,0:T(8,128)(2,1)S(1)}, bf16[1024,256]{1,0:T(8,128)(2,1)S(1)}, u32[]{:S(2)}, u32[]{:S(2)}) collective-permute-start(bf16[1024,256]{1,0:T(8,128)(2,1)S(1)} %bitcast.9), channel_id=1, source_target_pairs={{0,16},{2,18},{4,20},{6,22},{8,24},{10,26},{12,28},{14,30},{16,0},... | collective-permute-start | bytes 1572872 | tf_op jit(solution)/shard_map/ppermute | solution.py:231
  98.5 0.9 add_convert_fusion.1
  99.4 2.7 %collective-permute-start.16 = (bf16[96,276]{1,0:T(8,128)(2,1)S(1)}, bf16[96,276]{1,0:T(8,128)(2,1)S(1)}, u32[]{:S(2)}, u32[]{:S(2)}) collective-permute-start(bf16[96,276]{1,0:T(8,128)(2,1)S(1)} %add_convert_fusion.1), channel_id=1, source_target_pairs={{0,128},{2,130},{4,132},{6,134},{8,136},{10,138},{12,140},{14,142}... | collective-permute-start | bytes 158984 | tf_op jit(solution)/shard_map/ppermute | solution.py:231
  102.5 2.3 %collective-permute-done.6.b3 = bf16[2,72,512]{2,1,0:T(8,128)(2,1)S(1)} collective-permute-done((bf16[2,72,512]{2,1,0:T(8,128)(2,1)S(1)}, bf16[2,72,512]{2,1,0:T(8,128)(2,1)S(1)}, u32[]{:S(2)}, u32[]{:S(2)}) %collective-permute-start.6) | collective-permute-done | bytes 147488 | tf_op jit(solution)/shard_map/ppermute | solution.py:240
  104.8 2.0 %shard_map.228 = (bf16[2,216,512]{2,1,0:T(8,128)(2,1)}, bf16[2,72,512]{2,1,0:T(8,128)(2,1)}, bf16[2,72,512]{2,1,0:T(8,128)(2,1)}) custom-call(bf16[2,216,512]{2,1,0:T(8,128)(2,1)S(1)} %get-tuple-element.24.a1, bf16[2,72,512]{2,1,0:T(8,128)(2,1)S(1)} %get-tuple-element.25.a2, bf16[2,72,512]{2,1,0:T(8,128)(2,1)S(1)} %get-tuple-element.26.a3, ...), custom_call_target="tpu_custom_call" | custom-call | tf_op jit(solution)/shard_map/pallas_call | solution.py:69
  106.8 1.3 collective-permute-start.7
  108.2 0.8 collective-permute-start.17
  109.0 2.9 %collective-permute-start.8 = (bf16[2,72,512]{2,1,0:T(8,128)(2,1)}, bf16[2,72,512]{2,1,0:T(8,128)(2,1)}, u32[]{:S(2)}, u32[]{:S(2)}) collective-permute-start(bf16[2,72,512]{2,1,0:T(8,128)(2,1)} %get-tuple-element.28), channel_id=1, source_target_pairs={{0,2},{2,4},{4,6},{6,8},{8,10},{10,12},{12,14},{14,0},{16,18},{18,... | collective-permute-start | bytes 442376 | tf_op jit(solution)/shard_map/ppermute | solution.py:225
  111.9 2.8 %collective-permute-start.9 = (bf16[2,72,512]{2,1,0:T(8,128)(2,1)}, bf16[2,72,512]{2,1,0:T(8,128)(2,1)}, u32[]{:S(2)}, u32[]{:S(2)}) collective-permute-start(bf16[2,72,512]{2,1,0:T(8,128)(2,1)} %get-tuple-element.29), channel_id=1, source_target_pairs={{0,18},{2,20},{4,22},{6,24},{8,26},{10,28},{12,30},{14,16},{16,34}... | collective-permute-start | bytes 442376 | tf_op jit(solution)/shard_map/ppermute | solution.py:225
  114.7 2.2 %reshape.55.latent = bf16[576,512]{1,0:T(8,128)(2,1)} reshape(bf16[12,12,4,512]{3,2,1,0:T(4,128)(2,1)} %param.19) | data formatting | bytes 1179648 | tf_op jit(solution)/shard_map/reshape | solution.py:310
  116.9 2.2 %reshape.56.cot = bf16[576,512]{1,0:T(8,128)(2,1)} reshape(bf16[12,12,4,512]{3,2,1,0:T(4,128)(2,1)} %param.20) | data formatting | bytes 1179648 | tf_op jit(solution)/shard_map/reshape | solution.py:310
  119.0 2.1 %shard_map.232 = (f32[3,512,256]{2,1,0:T(8,128)}, f32[256,512]{1,0:T(8,128)}, f32[512,1]{1,0:T(8,128)S(1)}) custom-call(s32[2]{0:T(128)S(1)} %pad_add_fusion.info, bf16[1024,256]{1,0:T(8,128)(2,1)S(1)} %bitcast.10, bf16[1024,256]{1,0:T(8,128)(2,1)S(1)} %collective-permute-done.11.other, bf16[3,512,256]{2,1,0:T(8,128)(2,1)S(1)} %copy-done.1), custom_call_target="tpu_custom_call" | custom-call | tf_op jit(solution)/shard_map/pallas_call | solution.py:69
  121.1 0.7 copy-done.10
  121.8 1.1 reduce
  123.0 0.9 collective-permute-start.12
  123.9 1.0 fusion
  125.3 1.0 reshape.69
  126.4 3.2 %shard_map.229 = (bf16[576,512]{1,0:T(8,128)(2,1)S(1)}, bf16[576,512]{1,0:T(8,128)(2,1)S(1)}) custom-call(bf16[576,512]{1,0:T(8,128)(2,1)} %reshape.55.latent, bf16[576,512]{1,0:T(8,128)(2,1)} %reshape.56.cot, f32[1,512]{1,0:T(1,128)S(1)} %bitcast.13, bf16[2,216,512]{2,1,0:T(8,128)(2,1)S(1)} %get-tuple-element.23.own_a, ...), custom_call_target="tpu_custom_call" | custom-call | tf_op jit(solution)/shard_map/pallas_call | solution.py:69
  129.6 1.0 reshape.60
  130.5 1.0 reshape.61
  131.5 0.6 add_divide_fusion
  (75 shorter events, 3.4 us)
Async XLA Ops:
  2.5 18.3 %copy-start.20 = (f32[2,2,4,3312]{3,2,1,0:T(4,128)S(1)}, f32[2,2,4,3312]{3,2,1,0:T(4,128)}, u32[]{:S(2)}) copy-start(f32[2,2,4,3312]{3,2,1,0:T(4,128)} %param.24) | copy-start | bytes 635908
  5.4 23.4 %collective-permute-start = (bf16[2,216,512]{2,1,0:T(8,128)(2,1)}, bf16[2,216,512]{2,1,0:T(8,128)(2,1)}, u32[]{:S(2)}, u32[]{:S(2)}) collective-permute-start(bf16[2,216,512]{2,1,0:T(8,128)(2,1)} %pad_maximum_fusion.1), channel_id=1, source_target_pairs={{0,240},{2,242},{4,244},{6,246},{8,248},{10,250},{12,252},{14,254}... | collective-permute-start | bytes 1327112 | tf_op jit(solution)/shard_map/ppermute | solution.py:225
  9.6 14.3 %copy-start = (bf16[12,276,144]{2,1,0:T(8,128)(2,1)S(1)}, bf16[12,276,144]{2,1,0:T(8,128)(2,1)}, u32[]{:S(2)}) copy-start(bf16[12,276,144]{2,1,0:T(8,128)(2,1)} %constant.65.clone.spread) | copy-start | bytes 2861572
  10.8 17.3 %collective-permute-start.1 = (bf16[2,72,512]{2,1,0:T(8,128)(2,1)S(1)}, bf16[2,72,512]{2,1,0:T(8,128)(2,1)S(1)}, u32[]{:S(2)}, u32[]{:S(2)}) collective-permute-start(bf16[2,72,512]{2,1,0:T(8,128)(2,1)S(1)} %pad_maximum_fusion.2), channel_id=1, source_target_pairs={{0,14},{2,0},{4,2},{6,4},{8,6},{10,8},{12,10},{14,12},{16,30},{18,... | collective-permute-start | bytes 442376 | tf_op jit(solution)/shard_map/ppermute | solution.py:225
  15.0 13.0 %collective-permute-start.2 = (bf16[2,72,512]{2,1,0:T(8,128)(2,1)}, bf16[2,72,512]{2,1,0:T(8,128)(2,1)S(1)}, u32[]{:S(2)}, u32[]{:S(2)}) collective-permute-start(bf16[2,72,512]{2,1,0:T(8,128)(2,1)} %pad_maximum_fusion.3), channel_id=1, source_target_pairs={{0,254},{2,240},{4,242},{6,244},{8,246},{10,248},{12,250},{14,252}... | collective-permute-start | bytes 442376 | tf_op jit(solution)/shard_map/ppermute | solution.py:225
  23.8 4.9 %copy-start.5 = (bf16[576,216]{1,0:T(8,128)(2,1)S(1)}, bf16[576,216]{1,0:T(8,128)(2,1)}, u32[]{:S(2)}) copy-start(bf16[576,216]{1,0:T(8,128)(2,1)} %constant.53.clone.t0) | copy-start | bytes 746500
  23.9 4.9 %copy-start.6 = (bf16[576,216]{1,0:T(8,128)(2,1)S(1)}, bf16[576,216]{1,0:T(8,128)(2,1)}, u32[]{:S(2)}) copy-start(bf16[576,216]{1,0:T(8,128)(2,1)} %constant.54.clone.t1) | copy-start | bytes 746500
  23.9 4.9 %copy-start.7 = (bf16[216,576]{1,0:T(8,128)(2,1)S(1)}, bf16[216,576]{1,0:T(8,128)(2,1)}, u32[]{:S(2)}) copy-start(bf16[216,576]{1,0:T(8,128)(2,1)} %constant.57.clone.b0) | copy-start | bytes 746500
  23.9 4.9 %copy-start.8 = (bf16[216,576]{1,0:T(8,128)(2,1)S(1)}, bf16[216,576]{1,0:T(8,128)(2,1)}, u32[]{:S(2)}) copy-start(bf16[216,576]{1,0:T(8,128)(2,1)} %constant.58.clone.b1) | copy-start | bytes 746500
  23.9 4.9 %copy-start.9 = (bf16[256,512]{1,0:T(8,128)(2,1)S(1)}, bf16[256,512]{1,0:T(8,128)(2,1)}, u32[]{:S(2)}) copy-start(bf16[256,512]{1,0:T(8,128)(2,1)} %w_out.1) | copy-start | bytes 786436
  23.9 4.9 %copy-start.13 = (bf16[576,72]{1,0:T(8,128)(2,1)S(1)}, bf16[576,72]{1,0:T(8,128)(2,1)}, u32[]{:S(2)}) copy-start(bf16[576,72]{1,0:T(8,128)(2,1)} %constant.55.clone.t2) | copy-start | bytes 248836
  23.9 4.9 %copy-start.14 = (bf16[576,72]{1,0:T(8,128)(2,1)S(1)}, bf16[576,72]{1,0:T(8,128)(2,1)}, u32[]{:S(2)}) copy-start(bf16[576,72]{1,0:T(8,128)(2,1)} %constant.56.clone.t3) | copy-start | bytes 248836
  23.9 4.9 %copy-start.17 = (bf16[72,576]{1,0:T(8,128)(2,1)S(1)}, bf16[72,576]{1,0:T(8,128)(2,1)}, u32[]{:S(2)}) copy-start(bf16[72,576]{1,0:T(8,128)(2,1)} %constant.59.clone.b2) | copy-start | bytes 248836
  23.9 4.9 %copy-start.18 = (bf16[72,576]{1,0:T(8,128)(2,1)S(1)}, bf16[72,576]{1,0:T(8,128)(2,1)}, u32[]{:S(2)}) copy-start(bf16[72,576]{1,0:T(8,128)(2,1)} %constant.60.clone.b3) | copy-start | bytes 248836
  24.0 4.9 %copy-start.19 = (f32[512]{0:T(512)S(1)}, f32[512]{0:T(512)}, u32[]{:S(2)}) copy-start(f32[512]{0:T(512)} %param.21) | copy-start | bytes 6148
  28.1 0.7 copy-start.15
  28.8 0.9 copy-start.16
  41.3 2.1 %collective-permute-start.10 = (bf16[1024,256]{1,0:T(8,128)(2,1)}, bf16[1024,256]{1,0:T(8,128)(2,1)S(1)}, u32[]{:S(2)}, u32[]{:S(2)}) collective-permute-start(bf16[1024,256]{1,0:T(8,128)(2,1)} %get-tuple-element.33), channel_id=1, source_target_pairs={{0,16},{2,18},{4,20},{6,22},{8,24},{10,26},{12,28},{14,30},{16,0},... | collective-permute-start | bytes 1572872 | tf_op jit(solution)/shard_map/ppermute | solution.py:231
  43.4 1.2 copy-start.2
  70.5 23.2 %all-to-all-start.1 = ((bf16[64,16,256]{2,1,0:T(8,128)(2,1)}), bf16[64,16,256]{2,1,0:T(8,128)(2,1)S(1)}, u32[]{:S(2)}, u32[]{:S(2)}) async-start(bf16[64,16,256]{2,1,0:T(8,128)(2,1)} %shard_map.231), calls=%async_computation.1 | async-start | bytes 1048576 | tf_op jit(solution)/shard_map/all_to_all | solution.py:279
  81.2 2.5 %collective-permute-start.13 = (bf16[96,276]{1,0:T(8,128)(2,1)S(1)}, bf16[96,276]{1,0:T(8,128)(2,1)S(1)}, u32[]{:S(2)}, u32[]{:S(2)}) collective-permute-start(bf16[96,276]{1,0:T(8,128)(2,1)S(1)} %get-tuple-element.39), channel_id=1, source_target_pairs={{0,16},{2,18},{4,20},{6,22},{8,24},{10,26},{12,28},{14,30},{16,0},... | collective-permute-start | bytes 158984 | tf_op jit(solution)/shard_map/ppermute | solution.py:231
  83.7 35.3 %copy-start.1 = (bf16[3,512,256]{2,1,0:T(8,128)(2,1)S(1)}, bf16[3,512,256]{2,1,0:T(8,128)(2,1)}, u32[]{:S(2)}) copy-start(bf16[3,512,256]{2,1,0:T(8,128)(2,1)} %w_qkv.3) | copy-start | bytes 2359300
  83.8 7.2 %collective-permute-start.14 = (bf16[96,276]{1,0:T(8,128)(2,1)S(1)}, bf16[96,276]{1,0:T(8,128)(2,1)S(1)}, u32[]{:S(2)}, u32[]{:S(2)}) collective-permute-start(bf16[96,276]{1,0:T(8,128)(2,1)S(1)} %add_convert_fusion.3), channel_id=1, source_target_pairs={{0,32},{2,34},{4,36},{6,38},{8,40},{10,42},{12,44},{14,46},{16,48}... | collective-permute-start | bytes 158984 | tf_op jit(solution)/shard_map/ppermute | solution.py:231
  85.2 19.7 %collective-permute-start.4 = (bf16[2,216,512]{2,1,0:T(8,128)(2,1)S(1)}, bf16[2,216,512]{2,1,0:T(8,128)(2,1)}, u32[]{:S(2)}, u32[]{:S(2)}) collective-permute-start(bf16[2,216,512]{2,1,0:T(8,128)(2,1)S(1)} %get-tuple-element.24.a1), channel_id=1, source_target_pairs={{0,1},{1,0},{2,3},{3,2},{4,5},{5,4},{6,7},{7,6},{8,9},{9,8},{10,11... | collective-permute-start | bytes 1327112 | tf_op jit(solution)/shard_map/ppermute | solution.py:240
  91.0 7.5 %collective-permute-start.15 = (bf16[96,276]{1,0:T(8,128)(2,1)S(1)}, bf16[96,276]{1,0:T(8,128)(2,1)}, u32[]{:S(2)}, u32[]{:S(2)}) collective-permute-start(bf16[96,276]{1,0:T(8,128)(2,1)S(1)} %add_convert_fusion.2), channel_id=1, source_target_pairs={{0,64},{2,66},{4,68},{6,70},{8,72},{10,74},{12,76},{14,78},{16,80}... | collective-permute-start | bytes 158984 | tf_op jit(solution)/shard_map/ppermute | solution.py:231
  92.1 10.0 %collective-permute-start.5 = (bf16[2,72,512]{2,1,0:T(8,128)(2,1)S(1)}, bf16[2,72,512]{2,1,0:T(8,128)(2,1)S(1)}, u32[]{:S(2)}, u32[]{:S(2)}) collective-permute-start(bf16[2,72,512]{2,1,0:T(8,128)(2,1)S(1)} %get-tuple-element.25.a2), channel_id=1, source_target_pairs={{0,1},{1,0},{2,3},{3,2},{4,5},{5,4},{6,7},{7,6},{8,9},{9,8},{10,11... | collective-permute-start | bytes 442376 | tf_op jit(solution)/shard_map/ppermute | solution.py:240
  92.4 12.4 %collective-permute-start.6 = (bf16[2,72,512]{2,1,0:T(8,128)(2,1)S(1)}, bf16[2,72,512]{2,1,0:T(8,128)(2,1)S(1)}, u32[]{:S(2)}, u32[]{:S(2)}) collective-permute-start(bf16[2,72,512]{2,1,0:T(8,128)(2,1)S(1)} %get-tuple-element.26.a3), channel_id=1, source_target_pairs={{0,1},{1,0},{2,3},{3,2},{4,5},{5,4},{6,7},{7,6},{8,9},{9,8},{10,11... | collective-permute-start | bytes 442376 | tf_op jit(solution)/shard_map/ppermute | solution.py:240
  93.7 18.2 %collective-permute-start.11 = (bf16[1024,256]{1,0:T(8,128)(2,1)S(1)}, bf16[1024,256]{1,0:T(8,128)(2,1)S(1)}, u32[]{:S(2)}, u32[]{:S(2)}) collective-permute-start(bf16[1024,256]{1,0:T(8,128)(2,1)S(1)} %bitcast.9), channel_id=1, source_target_pairs={{0,16},{2,18},{4,20},{6,22},{8,24},{10,26},{12,28},{14,30},{16,0},... | collective-permute-start | bytes 1572872 | tf_op jit(solution)/shard_map/ppermute | solution.py:231
  99.4 8.7 %collective-permute-start.16 = (bf16[96,276]{1,0:T(8,128)(2,1)S(1)}, bf16[96,276]{1,0:T(8,128)(2,1)S(1)}, u32[]{:S(2)}, u32[]{:S(2)}) collective-permute-start(bf16[96,276]{1,0:T(8,128)(2,1)S(1)} %add_convert_fusion.1), channel_id=1, source_target_pairs={{0,128},{2,130},{4,132},{6,134},{8,136},{10,138},{12,140},{14,142}... | collective-permute-start | bytes 158984 | tf_op jit(solution)/shard_map/ppermute | solution.py:231
  102.1 24.2 %collective-permute-start.3 = (bf16[2,216,512]{2,1,0:T(8,128)(2,1)S(1)}, bf16[2,216,512]{2,1,0:T(8,128)(2,1)}, u32[]{:S(2)}, u32[]{:S(2)}) collective-permute-start(bf16[2,216,512]{2,1,0:T(8,128)(2,1)S(1)} %get-tuple-element.23.own_a), channel_id=1, source_target_pairs={{0,1},{1,0},{2,3},{3,2},{4,5},{5,4},{6,7},{7,6},{8,9},{9,8},{10,11... | collective-permute-start | bytes 1327112 | tf_op jit(solution)/shard_map/ppermute | solution.py:240
  106.8 19.5 %collective-permute-start.7 = (bf16[2,216,512]{2,1,0:T(8,128)(2,1)}, bf16[2,216,512]{2,1,0:T(8,128)(2,1)S(1)}, u32[]{:S(2)}, u32[]{:S(2)}) collective-permute-start(bf16[2,216,512]{2,1,0:T(8,128)(2,1)} %get-tuple-element.27), channel_id=1, source_target_pairs={{0,16},{2,18},{4,20},{6,22},{8,24},{10,26},{12,28},{14,30},{16,32}... | collective-permute-start | bytes 1327112 | tf_op jit(solution)/shard_map/ppermute | solution.py:225
  108.2 14.8 %collective-permute-start.17 = (bf16[96,276]{1,0:T(8,128)(2,1)S(1)}, bf16[96,276]{1,0:T(8,128)(2,1)}, u32[]{:S(2)}, u32[]{:S(2)}) collective-permute-start(bf16[96,276]{1,0:T(8,128)(2,1)S(1)} %add_convert_fusion), channel_id=1, source_target_pairs={{0,16},{2,18},{4,20},{6,22},{8,24},{10,26},{12,28},{14,30},{16,0},... | collective-permute-start | bytes 158984 | tf_op jit(solution)/shard_map/ppermute | solution.py:231
  109.0 17.3 %collective-permute-start.8 = (bf16[2,72,512]{2,1,0:T(8,128)(2,1)}, bf16[2,72,512]{2,1,0:T(8,128)(2,1)}, u32[]{:S(2)}, u32[]{:S(2)}) collective-permute-start(bf16[2,72,512]{2,1,0:T(8,128)(2,1)} %get-tuple-element.28), channel_id=1, source_target_pairs={{0,2},{2,4},{4,6},{6,8},{8,10},{10,12},{12,14},{14,0},{16,18},{18,... | collective-permute-start | bytes 442376 | tf_op jit(solution)/shard_map/ppermute | solution.py:225
  111.9 14.4 %collective-permute-start.9 = (bf16[2,72,512]{2,1,0:T(8,128)(2,1)}, bf16[2,72,512]{2,1,0:T(8,128)(2,1)}, u32[]{:S(2)}, u32[]{:S(2)}) collective-permute-start(bf16[2,72,512]{2,1,0:T(8,128)(2,1)} %get-tuple-element.29), channel_id=1, source_target_pairs={{0,18},{2,20},{4,22},{6,24},{8,26},{10,28},{12,30},{14,16},{16,34}... | collective-permute-start | bytes 442376 | tf_op jit(solution)/shard_map/ppermute | solution.py:225
  119.0 7.3 %copy-start.3 = (bf16[576,216]{1,0:T(8,128)(2,1)S(1)}, bf16[576,216]{1,0:T(8,128)(2,1)}, u32[]{:S(2)}) copy-start(bf16[576,216]{1,0:T(8,128)(2,1)} %constant.61.clone.t0) | copy-start | bytes 746500
  119.0 7.3 %copy-start.4 = (bf16[576,216]{1,0:T(8,128)(2,1)S(1)}, bf16[576,216]{1,0:T(8,128)(2,1)}, u32[]{:S(2)}) copy-start(bf16[576,216]{1,0:T(8,128)(2,1)} %constant.62.clone.t1) | copy-start | bytes 746500
  121.1 0.7 copy-start.10
  121.8 4.5 %copy-start.11 = (bf16[576,72]{1,0:T(8,128)(2,1)S(1)}, bf16[576,72]{1,0:T(8,128)(2,1)}, u32[]{:S(2)}) copy-start(bf16[576,72]{1,0:T(8,128)(2,1)} %constant.63.clone.t2) | copy-start | bytes 248836
  121.8 4.5 %copy-start.12 = (bf16[576,72]{1,0:T(8,128)(2,1)S(1)}, bf16[576,72]{1,0:T(8,128)(2,1)}, u32[]{:S(2)}) copy-start(bf16[576,72]{1,0:T(8,128)(2,1)} %constant.64.clone.t3) | copy-start | bytes 248836
  123.0 8.5 %collective-permute-start.12 = (f32[512]{0:T(512)S(1)}, f32[512]{0:T(512)S(1)}, u32[]{:S(2)}, u32[]{:S(2)}) collective-permute-start(f32[512]{0:T(512)S(1)} %reduce), channel_id=1, source_target_pairs={{0,1},{1,0},{2,3},{3,2},{4,5},{5,4},{6,7},{7,6},{8,9},{9,8},{10,11... | collective-permute-start | bytes 6152 | tf_op jit(solution)/shard_map/ppermute | solution.py:240

commit v2 on v1

v2 whole, which is shorter than its diff:
```python
import jax
import jax.numpy as jnp
import numpy as np
from jax import lax
from jax.experimental import pallas as pl
from jax.experimental.pallas import tpu as pltpu
from jax.sharding import PartitionSpec as P

BF = jnp.bfloat16
F32 = jnp.float32
WTOK = 144
OFFS = 23
NT = (((1,), (1,)), ((), ()))
TN = (((0,), (0,)), ((), ()))
SECTIONS = (0, 216, 432, 504, 576)


def section_row(lon, lat, lev):
    lat_cells = 9 if lat < 9 else 3
    return (lon >= 6) + 2 * (lat >= 9), (lon % 6 * lat_cells + lat % 9) * 4 + lev


def placement():
    place = np.zeros((576, 576), np.float32)
    for a in range(2):
        for b in range(2):
            for p in range(12):
                for s in range(2):
                    for r in range(6):
                        row = (a * 2 + b) * WTOK + p * 12 + s * 6 + r
                        section, at = section_row(p, a * 6 + r, (b * 2 + s + 1) % 4)
                        place[row, SECTIONS[section] + at] = 1
    return place


def offset_order():
    order = np.zeros((276, 276), np.float32)
    for rs in range(12):
        for k in range(OFFS):
            order[rs * OFFS + k, k * 12 + rs] = 1
    return order


TO_WINDOW = placement()
ORDER = offset_order()


def dot(a, b, dims=(((1,), (0,)), ((), ()))):
    return lax.dot_general(a, b, dims, preferred_element_type=F32)


def call(body, outs, args, scratch=(), smem=1, after=(), us=1, mib=16, hbm=(), hbm_outs=()):
    vmem, far = pl.BlockSpec(memory_space=pltpu.VMEM), pl.BlockSpec(memory_space=pltpu.HBM)
    n = len(args)
    m = n + len(hbm)

    def kernel(*refs):
        body(*refs[:m], *refs[m + len(after) :])

    return pl.pallas_call(
        kernel,
        out_shape=[jax.ShapeDtypeStruct(s, t) for s, t in [*outs, *hbm_outs]],
        in_specs=[pl.BlockSpec(memory_space=pltpu.SMEM)] * smem
        + [vmem] * (n - smem)
        + [far] * len(hbm)
        + [pl.BlockSpec(memory_space=pl.ANY)] * len(after),
        out_specs=[vmem] * len(outs) + [far] * len(hbm_outs),
        scratch_shapes=list(scratch),
        compiler_params=pltpu.CompilerParams(vmem_limit_bytes=mib * 1024 * 1024),
        cost_estimate=pl.CostEstimate(flops=int(us * 1e9), bytes_accessed=0, transcendentals=0),
    )(*args, *hbm, *after)


TOKEN = ((8, 128), F32)


LOW_LON, LOW_LAT, HIGH_LON, HIGH_LAT = slice(0, 6), slice(0, 3), slice(6, 12), slice(3, 12)
PLACES = ((HIGH_LON, HIGH_LAT), (LOW_LON, HIGH_LAT), (HIGH_LON, LOW_LAT), (LOW_LON, LOW_LAT))


def halo_kernel(latent, cot, o_lon, o_lat, o_cor, tiles, sems):
    copies = []
    for j, grid in enumerate((latent, cot)):
        for k in range(4):
            rows = pl.ds(3 * k, 3)
            copies.append(pltpu.make_async_copy(grid.at[rows], tiles.at[j, rows], sems.at[4 * j + k]))
            copies[-1].start()
    for copy in copies:
        copy.wait()
    for (lon, lat), ref in zip(PLACES[1:], (o_lon, o_lat, o_cor)):
        for j in range(2):
            ref[j] = tiles[j, lon, lat].reshape(ref.shape[1:])


def bias_kernel(info, table, order, w_out, bias, w_copy, raw, entries, low_u, high_u):
    w_copy[...] = w_out[...]
    flat = table[...].reshape(16, 3312)
    for s_t in range(2):
        for s_u in range(2):
            for r_t in range(6):
                at = ((s_t * 2 + s_u) * 6 + r_t) * 138
                row = (s_t * 6 + r_t) * 16
                raw[row : row + 16, s_u * 138 : s_u * 138 + 138] = flat[:, at : at + 138]
    full = raw[...]
    high = full.astype(BF)
    rest = full - high.astype(F32)
    mid = rest.astype(BF)
    low = (rest - mid.astype(F32)).astype(BF)
    entries[...] = dot(low, order[...]) + dot(mid, order[...]) + dot(high, order[...])
    row = lax.broadcasted_iota(jnp.int32, (192, WTOK), 0)
    col = lax.broadcasted_iota(jnp.int32, (192, WTOK), 1)
    rs_t, rs_u, which = row // 16, col % 12, row % 16
    s_t, s_u = (rs_t >= 6).astype(jnp.int32), (rs_u >= 6).astype(jnp.int32)
    edge_t = (rs_t - s_t * 6 >= 3).astype(jnp.int32)
    edge_u = (rs_u - s_u * 6 >= 3).astype(jnp.int32)
    last_lat = (which >= 8).astype(jnp.int32) * info[0]
    last_lev = ((which % 8) >= 4).astype(jnp.int32)
    barred = (last_lat * (edge_t - edge_u) != 0) | (last_lev * (s_t - s_u) != 0)
    for p in range(12):
        at = entries[:, (11 - p) * 12 : (11 - p) * 12 + WTOK]
        at = jnp.where(barred, -jnp.inf, at)
        low_u[...] = at[:, 0:128]
        high_u[:, 0:16] = at[:, 128:144]
        for i in range(16):
            rows = slice(i * WTOK + p * 12, i * WTOK + p * 12 + 12)
            bias[rows, 0:128] = low_u[pl.ds(i, 12, stride=16), :]
            bias[rows, 128:WTOK] = high_u[pl.ds(i, 12, stride=16), :][:, 0:16]


def main_kernel(info, latent, cotangent, lon, lat, cor, place, gain, w_qkv, w_out, bias,
                keep, send, o_ds, att_s, gq_s, gk_s, gv_s, joined):
    def gathered(which):
        own = (latent, cotangent)[which][HIGH_LON, HIGH_LAT].reshape(216, 512)
        for j, rows in enumerate((own, lon[which], lat[which], cor[which])):
            joined[SECTIONS[j] : SECTIONS[j + 1], :] = rows.astype(F32)
        return dot(place[...], joined[...].astype(BF))

    values = gathered(0)
    cot = gathered(1).astype(BF)
    shifted = values - jnp.mean(values, -1, keepdims=True)
    normed = shifted * lax.rsqrt(jnp.mean(shifted * shifted, -1, keepdims=True) + 1e-05)
    hidden = (normed * gain[...]).astype(BF)
    q, k, v = [dot(hidden, w_qkv[j]).astype(BF) for j in range(3)]
    down = dot(cot, w_out[...], NT).astype(BF)
    head = lax.broadcasted_iota(jnp.int32, (WTOK, 256), 1) // 64

    def stacked(rows):
        return jnp.concatenate([jnp.where(head == h, rows, jnp.zeros_like(rows)) for h in range(4)], 0)

    def unstacked(rows):
        total = jnp.zeros((WTOK, 256), F32)
        for h in range(4):
            total = jnp.where(head == h, rows[h * WTOK : (h + 1) * WTOK], total)
        return total

    for w in range(4):
        rows = slice(w * WTOK, (w + 1) * WTOK)
        four = slice(w * 576, (w + 1) * 576)
        qs, ds_ = stacked(q[rows]), stacked(down[rows])
        scores = dot(qs, k[rows], NT) * 0.125 + bias[four, :]
        exps = jnp.exp(scores - jnp.max(scores, -1, keepdims=True))
        probs = exps / jnp.sum(exps, -1, keepdims=True)
        probs_low = probs.astype(BF)
        att_s[rows, :] = unstacked(dot(probs_low, v[rows])).astype(BF)
        dp = dot(ds_, v[rows], NT)
        gv_s[rows, :] = dot(probs_low, ds_, TN).astype(BF)
        grad = probs * (dp - jnp.sum(dp * probs, -1, keepdims=True))
        o_ds[four, :] = grad
        grad_low = grad.astype(BF)
        gq_s[rows, :] = unstacked(dot(grad_low, k[rows]) * 0.125).astype(BF)
        gk_s[rows, :] = (dot(grad_low, qs, TN) * 0.125).astype(BF)

    att, gq, gk, gv = att_s[...], gq_s[...], gk_s[...], gv_s[...]
    wo = dot(att, cot, TN)
    first = [dot(hidden, gq, TN), dot(hidden, gk, TN)]
    second = [dot(hidden, gv, TN), jnp.concatenate([wo[:, :256], wo[:, 256:]], 0)]
    core = info[1]
    for j in range(2):
        rows = slice(j * 512, (j + 1) * 512)
        keep[rows, :] = jnp.where(core == 0, first[j], second[j])
        send[rows, :] = jnp.where(core == 0, second[j], first[j]).astype(BF)

def terms_kernel(att, gq, gk, gv, w_qkv, back, terms):
    hid_part = dot(gq[...], w_qkv[0], NT) + dot(gk[...], w_qkv[1], NT) + dot(gv[...], w_qkv[2], NT)
    terms[:, 0:256] = dot(back[...], att[...]).astype(BF)
    terms[:, 256:768] = dot(back[...], hid_part.astype(BF)).astype(BF)


def core_sum_kernel(keep, recv, total):
    total[...] = (keep[...] + recv[...].astype(F32)).astype(BF)


def y_sum_kernel(parts, b_keep, b_recv, message):
    total = parts[0].astype(F32)
    for j in range(1, 4):
        total = total + parts[j].astype(F32)
    total = total.astype(BF)
    tail = jnp.zeros((16, 118), BF)
    for z in range(8):
        for x in range(2):
            j = z * 2 + x
            message[j, 0:16, :] = total[j * 16 : (j + 1) * 16]
            both = (b_keep[z, x].astype(F32) + b_recv[z, x].astype(F32)).astype(BF)
            message[j, 16:32, :] = jnp.concatenate([both, tail], 1)


def zx_sum_kernel(parts, copies):
    total = jnp.zeros((16, 256), F32)
    biases = []
    for x in range(2):
        bias = jnp.zeros((16, 256), F32)
        for z in range(8):
            total = total + parts[z * 2 + x, 0:16, :].astype(F32)
            bias = bias + parts[z * 2 + x, 16:32, :].astype(F32)
        biases.append(bias.astype(BF))
    total = total.astype(BF)
    for z in range(8):
        for x in range(2):
            copies[z * 2 + x, 0:16, :] = total
            copies[z * 2 + x, 16:32, :] = biases[x]


def pair_kernel(terms, others, w_out, w_other, o_own, o_lon, o_lat, o_cor, held, sems):
    copies = []
    for j, w in enumerate((w_out, w_other)):
        for k in range(2):
            rows = pl.ds(128 * k, 128)
            copies.append(pltpu.make_async_copy(w.at[rows], held.at[j, rows], sems.at[2 * j + k]))
            copies[-1].start()
    for copy in copies:
        copy.wait()
    out = dot(terms[:, 0:256], held[0]).astype(BF).astype(F32)
    out = out + dot(others[:, 0:256], held[1]).astype(BF).astype(F32)
    hid = terms[:, 256:768].astype(F32) + others[:, 256:768].astype(F32)
    for k, ref in enumerate((o_own, o_lon, o_lat, o_cor)):
        rows = slice(SECTIONS[k], SECTIONS[k + 1])
        ref[0] = out[rows].astype(BF)
        ref[1] = hid[rows].astype(BF)


def spread_kernel(parts, copies, b_half):
    for j in range(16):
        for k in range(4):
            copies[k, j * 16 : (j + 1) * 16, :] = parts[j, 0:16, :]
        b_half[j] = parts[j, 16:32, :]


def gain_kernel(info, mine, w_qkv, out):
    rows = mine[...].astype(F32)
    w0, w1, w2 = [w_qkv[j].astype(F32) for j in range(3)]
    total = jnp.where(info[1] == 0, rows[:512] * w0 + rows[512:] * w1, rows[:512] * w2)
    ones = jnp.ones((8, 256), F32)
    out[...] = lax.dot_general(ones, total, NT, precision=lax.Precision.HIGHEST, preferred_element_type=F32)


def gain_sum_kernel(mine, other, gain, out):
    out[...] = (mine[0:1, :] + other[0:1, :]) / gain[...]


def bias_out_kernel(info, mine, other, grad_bias, token, low, high, flat):
    token[...] = jnp.zeros_like(token)
    first = jnp.where(info[1] == 0, mine[...], other[...]).astype(F32)
    second = jnp.where(info[1] == 0, other[...], mine[...]).astype(F32)
    for j, half in enumerate((first, second)):
        half = half.reshape(256, 256)
        low[256 * j : 256 * j + 256, :] = half[:, 0:128]
        high[256 * j : 256 * j + 256, :] = half[:, 128:256]
    for s_t in range(2):
        for j in range(12):
            at = (s_t * 12 + j) * 138
            rows = pl.ds(s_t * 16 + j, 16, stride=32)
            flat[:, at : at + 128] = low[rows, :]
            flat[:, at + 128 : at + 138] = high[rows, :][:, 0:10]
    grad_bias[...] = flat[...].reshape(grad_bias.shape)


def weights_kernel(info, mine, other, token, wqkv, wout, held, held_out, sems):
    token[...] = jnp.zeros_like(token)
    first = jnp.where(info[1] == 0, mine[...], other[...]).astype(F32)
    second = jnp.where(info[1] == 0, other[...], mine[...]).astype(F32)
    copies = []
    for k in range(6):
        rows = pl.ds(k % 2 * 256, 256)
        half = first if k < 4 else second
        held[k] = half[k % 4 * 256 : (k % 4 + 1) * 256]
        copies.append(pltpu.make_async_copy(held.at[k], wqkv.at[k // 2, rows], sems.at[k]))
        copies[-1].start()
    held_out[:, 0:256] = second[512:768]
    held_out[:, 256:512] = second[768:]
    for k in range(2):
        rows = pl.ds(k * 128, 128)
        copies.append(pltpu.make_async_copy(held_out.at[rows], wout.at[rows], sems.at[6 + k]))
        copies[-1].start()
    for copy in copies:
        copy.wait()


def bias_grad_kernel(info, ds, order, keep, send, part, entries, tables):
    entries[...] = jnp.zeros_like(entries)
    for p in range(12):
        for i in range(16):
            part[i * 12 : i * 12 + 12, :] = ds[i * WTOK + p * 12 : i * WTOK + p * 12 + 12, :]
        at = slice((11 - p) * 12, (11 - p) * 12 + WTOK)
        entries[:, at] = entries[:, at] + part[...]
    total = entries[...].astype(BF)
    tables[...] = jnp.zeros_like(tables)
    for s_u in range(2):
        rows = dot(total, order[s_u], NT)
        for i in range(16):
            for s_t in range(2):
                tables[i, s_t, s_u * 6 : s_u * 6 + 6, :] = rows[i * 12 + s_t * 6 : i * 12 + s_t * 6 + 6]
    mine, other = tables[0:8], tables[8:16]
    keep[...] = jnp.where(info[1] == 0, mine, other).astype(BF)
    send[...] = jnp.where(info[1] == 0, other, mine).astype(BF)


def final_kernel(latent, cot, gain, own, lon, lat, cor, output, grad, token):
    token[...] = jnp.zeros_like(token)
    for (by_lon, by_lat), ref in zip(PLACES, (own, lon, lat, cor)):
        out_term, hid_term = ref[0].astype(F32), ref[1].astype(F32)
        tile = latent[by_lon, by_lat]
        values = tile.reshape(out_term.shape).astype(F32)
        output[by_lon, by_lat] = (values + out_term).astype(BF).reshape(tile.shape)
        shifted = values - jnp.mean(values, -1, keepdims=True)
        inv_std = lax.rsqrt(jnp.mean(shifted * shifted, -1, keepdims=True) + 1e-05)
        normed = shifted * inv_std
        scaled = hid_term * gain[...]
        inner = scaled - jnp.mean(scaled, -1, keepdims=True) - normed * jnp.mean(scaled * normed, -1, keepdims=True)
        above = cot[by_lon, by_lat].reshape(out_term.shape).astype(F32)
        grad[by_lon, by_lat] = (above + inv_std * inner).astype(BF).reshape(tile.shape)


def moved(value, by_lon, by_lat):
    n_lon, n_lat = lax.axis_size("lon"), lax.axis_size("lat")
    pairs = [
        (i * n_lat + j, (i + by_lon) % n_lon * n_lat + (j + by_lat) % n_lat)
        for i in range(n_lon)
        for j in range(n_lat)
    ]
    return lax.ppermute(value, ("lon", "lat"), pairs)


def swapped(value, lon_bits, lat_bits):
    n_lon, n_lat = lax.axis_size("lon"), lax.axis_size("lat")
    pairs = [(i * n_lat + j, (i ^ lon_bits) * n_lat + (j ^ lat_bits)) for i in range(n_lon) for j in range(n_lat)]
    return lax.ppermute(value, ("lon", "lat"), pairs)


def across_y(value):
    n_lat = lax.axis_size("lat")
    groups = [list(range(x, n_lat, 2)) for x in range(2)]
    return lax.all_to_all(value, "lat", 0, 0, axis_index_groups=groups)


def across_zx(value):
    n_lon, n_lat = lax.axis_size("lon"), lax.axis_size("lat")
    groups = [
        [i * n_lat + j + x for i in range(core, n_lon, 2) for x in range(2)]
        for core in range(2)
        for j in range(0, n_lat, 2)
    ]
    return lax.all_to_all(value, ("lon", "lat"), 0, 0, axis_index_groups=groups)


def other_group(value):
    return lax.ppermute(value, "tp", [(0, 1), (1, 0)])


def on_device(latent, cotangent, ln_gain, w_qkv, w_out, bias_table):
    place, back = jnp.asarray(TO_WINDOW, BF), jnp.asarray(TO_WINDOW.T, BF)
    order = jnp.asarray(ORDER, BF)
    order_halves = jnp.asarray(ORDER.reshape(2, 138, 276), BF)
    i_lon, i_lat = lax.axis_index("lon"), lax.axis_index("lat")
    last = (i_lat == lax.axis_size("lat") - 1).astype(jnp.int32)
    core = i_lon % 2
    info = jnp.stack([last, core]).astype(jnp.int32)
    gain = ln_gain.reshape(1, 512)

    part = lambda n: ((2, n, 512), BF)
    halos = [part(216), part(72), part(72)]
    s_lon, s_lat, s_cor = call(
        halo_kernel,
        halos,
        [],
        [pltpu.VMEM((2,) + latent.shape, BF), pltpu.SemaphoreType.DMA((8,))],
        smem=0,
        hbm=[latent, cotangent],
    )
    in_lon, in_lat, in_cor = moved(s_lon, -1, 0), moved(s_lat, 0, -1), moved(s_cor, -1, -1)

    bias, w_copy = call(
        bias_kernel,
        [((16 * WTOK, WTOK), F32), (w_out.shape, BF)],
        [info, bias_table, order, w_out],
        [pltpu.VMEM((192, 276), F32)] * 2 + [pltpu.VMEM((192, 128), F32)] * 2,
        us=2,
    )
    w_other = other_group(w_copy)

    keep, send, ds, att, gq, gk, gv = call(
        main_kernel,
        [((1024, 256), F32), ((1024, 256), BF), ((16 * WTOK, WTOK), F32)] + [((576, 256), BF)] * 4,
        [info, latent, cotangent, in_lon, in_lat, in_cor, place, gain, w_qkv, w_out, bias],
        [pltpu.VMEM((576, 512), F32)],
        us=9,
        mib=32,
    )
    recv = swapped(send, 1, 0)
    (terms,) = call(terms_kernel, [((576, 768), BF)], [att, gq, gk, gv, w_qkv, back], smem=0, after=[w_other], us=2)
    others = other_group(terms)
    own, s_lon, s_lat, s_cor = call(
        pair_kernel,
        [part(216)] + halos,
        [terms, others],
        [pltpu.VMEM((2, 256, 512), BF), pltpu.SemaphoreType.DMA((4,))],
        smem=0,
        us=2,
        hbm=[w_out, w_other],
    )

    (total,) = call(core_sum_kernel, [((1024, 256), BF)], [keep, recv], smem=0, after=[terms], us=0.5)
    parts = across_y(total.reshape(4, 256, 256))
    b_keep, b_send = call(
        bias_grad_kernel,
        [((8, 2, 16, 138), BF)] * 2,
        [info, ds, order_halves],
        [pltpu.VMEM((192, WTOK), F32), pltpu.VMEM((192, 276), F32), pltpu.VMEM((16, 2, 16, 138), F32)],
        us=2.5,
    )
    b_recv = swapped(b_send, 1, 0)
    (message,) = call(y_sum_kernel, [((16, 32, 256), BF)], [parts, b_keep, b_recv], smem=0, us=1)
    r_lon, r_lat, r_cor = moved(s_lon, 1, 0), moved(s_lat, 0, 1), moved(s_cor, 1, 1)
    (copies,) = call(zx_sum_kernel, [((16, 32, 256), BF)], [across_zx(message)], smem=0, us=1)

    output, grad_latent, done = call(
        final_kernel,
        [(latent.shape, BF), (latent.shape, BF), TOKEN],
        [latent, cotangent, gain, own, r_lon, r_lat, r_cor],
        smem=0,
        us=30,
    )

    copies, b_half = call(
        spread_kernel,
        [((4, 256, 256), BF), ((16, 16, 256), BF)],
        [across_zx(copies)],
        smem=0,
        after=[done],
        us=1,
    )
    mine = across_y(copies).reshape(1024, 256)
    b_other = swapped(b_half, 1, 0)
    grad_bias, done = call(
        bias_out_kernel,
        [(bias_table.shape, F32), TOKEN],
        [info, b_half, b_other],
        [pltpu.VMEM((512, 128), F32)] * 2 + [pltpu.VMEM((16, 3312), F32)],
        us=30,
    )

    (g_mine,) = call(
        gain_kernel, [((8, 512), F32)], [info, mine, w_qkv], after=[done], us=1
    )
    g_other = swapped(g_mine, 1, 0)
    g_pair = g_mine + g_other
    done, grad_wqkv, grad_wout = call(
        weights_kernel,
        [TOKEN],
        [info, mine, swapped(mine, 1, 0)],
        [pltpu.VMEM((6, 256, 256), F32), pltpu.VMEM((256, 512), F32), pltpu.SemaphoreType.DMA((8,))],
        hbm_outs=[((3, 512, 256), F32), ((256, 512), F32)],
        us=2,
    )
    (grad_gain,) = call(
        gain_sum_kernel, [((1, 512), F32)], [g_pair, other_group(g_pair), gain], smem=0, after=[done]
    )
    grad_gain = grad_gain.reshape(512)
    return output, grad_latent, grad_gain, grad_wqkv, grad_wout, grad_bias


def solution(mesh):
    specs = (
        P("lon", "lat", None, None),
        P("lon", "lat", None, None),
        P(),
        P(None, None, "tp"),
        P("tp", None),
        P("lat", None, "tp", None),
    )
    return jax.shard_map(on_device, mesh=mesh, in_specs=specs, out_specs=specs, check_vma=False)
```

time: 133 us -> 109 us (0.82)
  blocking collectives: 24.9 us -> 0 us
  local copies, waits for them, and re-layouts: 20.3 us -> 7.51 us
  starting transfers between devices: 42.3 us -> 52.7 us
  waiting for transfers between devices: 10.8 us -> 20.2 us
  other arithmetic: 5.32 us -> 0.08 us
    all_to_all x1 -> x0, blocking collectives: 24.9 us -> none  [on_device(): lax.all_to_all(total.reshape(64, 16, 256), ('lon', 'lat'), 0, 0, axis_ind...]
    all_to_all x1 -> x4, starting transfers between devices: 7.19 us -> 24.2 us  [the longest x2 16.8 us: across_zx(): return lax.all_to_all(value, ('lon', 'lat'), 0, 0, axis_index_groups=groups)]
    all_to_all x1 -> x4, waiting for transfers between devices: 0.14 us -> 16.3 us  [the longest x2 8.7 us: across_y(): return lax.all_to_all(value, 'lat', 0, 0, axis_index_groups=groups)]
    reshape x9 -> x0, local copies, waits for them, and re-layouts: 8.45 us -> none  [the longest x1 2.16 us: on_device(): latent.reshape(576, 512)]
    ppermute x7 -> x5, waiting for transfers between devices: 8.34 us -> 2.17 us  [swapped(): return lax.ppermute(value, ('lon', 'lat'), pairs)]
    slice x4 -> x0, local copies, waits for them, and re-layouts: 5.89 us -> none  [the longest x2 3.03 us: section(): cotangent[lon, lat].reshape(-1, 512)]
    ppermute x7 -> x5, starting transfers between devices: 12.6 us -> 8.21 us  [swapped(): return lax.ppermute(value, ('lon', 'lat'), pairs)]
    unnamed x42, local copies, waits for them, and re-layouts: 3.58 us -> 7.51 us
  transfers between devices with their start and end apart: 19 -> 18, of which waited for: 5 -> 8; matrix products, arithmetic and copies ran while one was open for 13% -> 0% of each run, Pallas kernels for 11% -> 22%
where the time goes in v2:
time: 109 us
  starting transfers between devices  52.7 us (48%)
  Pallas kernels  27.3 us (25%)
  waiting for transfers between devices  20.2 us (19%)
  local copies, waits for them, and re-layouts  7.51 us (7%)
    pallas_call x15, Pallas kernels, call(): pl.pallas_call(kernel, out_shape=[jax.ShapeDtypeStruct(s, t) for s, t in...  27.3 us
    ppermute x6, starting transfers between devices, moved(): return lax.ppermute(value, ('lon', 'lat'), pairs)  18.6 us
    all_to_all x2, starting transfers between devices, across_zx(): return lax.all_to_all(value, ('lon', 'lat'), 0, 0, axis_index_groups=groups)  16.8 us
    all_to_all x2, waiting for transfers between devices, across_y(): return lax.all_to_all(value, 'lat', 0, 0, axis_index_groups=groups)  8.7 us
    ppermute x5, starting transfers between devices, swapped(): return lax.ppermute(value, ('lon', 'lat'), pairs)  8.21 us
    all_to_all x2, waiting for transfers between devices, across_zx(): return lax.all_to_all(value, ('lon', 'lat'), 0, 0, axis_index_groups=groups)  7.6 us
    unnamed x42, local copies, waits for them, and re-layouts  7.51 us
    all_to_all x2, starting transfers between devices, across_y(): return lax.all_to_all(value, 'lat', 0, 0, axis_index_groups=groups)  7.33 us
  transfers between devices with their start and end apart: 18, of which 8 were waited for; matrix products, arithmetic and copies ran while one was open for 0% of the time, Pallas kernels for 22%

profile of v2, /device:TPU:1, one launch (start us, length us, event | category | flops | bytes accessed | tf_op | source)
XLA Modules:
  0.0 108.7 jit_solution(6314675971772199261)
XLA Ops:
  0.6 1.1 copy-done.1
  1.7 1.1 copy-done.4
  2.8 1.7 %shard_map.145 = (bf16[2,216,512]{2,1,0:T(8,128)(2,1)S(1)}, bf16[2,72,512]{2,1,0:T(8,128)(2,1)S(1)}, bf16[2,72,512]{2,1,0:T(8,128)(2,1)S(1)}) custom-call(bf16[12,12,4,512]{3,2,1,0:T(4,128)(2,1)S(1)} %copy-done.1, bf16[12,12,4,512]{3,2,1,0:T(4,128)(2,1)S(1)} %copy-done.4), custom_call_target="tpu_custom_call" | custom-call | flops 1000000000 | tf_op jit(solution)/shard_map/pallas_call | solution.py:60
  4.5 3.3 %collective-permute-start = (bf16[2,216,512]{2,1,0:T(8,128)(2,1)S(1)}, bf16[2,216,512]{2,1,0:T(8,128)(2,1)S(1)}, u32[]{:S(2)}, u32[]{:S(2)}) collective-permute-start(bf16[2,216,512]{2,1,0:T(8,128)(2,1)S(1)} %get-tuple-element.34), channel_id=1, source_target_pairs={{0,240},{2,242},{4,244},{6,246},{8,248},{10,250},{12,252},{14,254}... | collective-permute-start | bytes 1327112 | tf_op jit(solution)/shard_map/ppermute | solution.py:340
  7.7 3.5 %collective-permute-start.1 = (bf16[2,72,512]{2,1,0:T(8,128)(2,1)S(1)}, bf16[2,72,512]{2,1,0:T(8,128)(2,1)S(1)}, u32[]{:S(2)}, u32[]{:S(2)}) collective-permute-start(bf16[2,72,512]{2,1,0:T(8,128)(2,1)S(1)} %get-tuple-element.35), channel_id=1, source_target_pairs={{0,14},{2,0},{4,2},{6,4},{8,6},{10,8},{12,10},{14,12},{16,30},{18,... | collective-permute-start | bytes 442376 | tf_op jit(solution)/shard_map/ppermute | solution.py:340
  11.2 5.7 %collective-permute-start.2 = (bf16[2,72,512]{2,1,0:T(8,128)(2,1)S(1)}, bf16[2,72,512]{2,1,0:T(8,128)(2,1)S(1)}, u32[]{:S(2)}, u32[]{:S(2)}) collective-permute-start(bf16[2,72,512]{2,1,0:T(8,128)(2,1)S(1)} %get-tuple-element.36), channel_id=1, source_target_pairs={{0,254},{2,240},{4,242},{6,244},{8,246},{10,248},{12,250},{14,252}... | collective-permute-start | bytes 442376 | tf_op jit(solution)/shard_map/ppermute | solution.py:340
  16.9 0.1 pad_add_fusion.refs_0_
  17.0 2.7 %shard_map.146 = (f32[2304,144]{1,0:T(8,128)S(1)}, bf16[256,512]{1,0:T(8,128)(2,1)S(1)}) custom-call(s32[2]{0:T(128)S(1)} %pad_add_fusion.refs_0_, f32[2,2,4,3312]{3,2,1,0:T(4,128)S(1)} %copy-done.11, bf16[276,276]{1,0:T(8,128)(2,1)S(1)} %copy-done.16, bf16[256,512]{1,0:T(8,128)(2,1)S(1)} %copy-done.7), custom_call_target="tpu_custom_call" | custom-call | flops 2000000000 | tf_op jit(solution)/shard_map/pallas_call | solution.py:60
  19.7 1.3 %collective-permute-start.3 = (bf16[256,512]{1,0:T(8,128)(2,1)S(1)}, bf16[256,512]{1,0:T(8,128)(2,1)S(1)}, u32[]{:S(2)}, u32[]{:S(2)}) collective-permute-start(bf16[256,512]{1,0:T(8,128)(2,1)S(1)} %get-tuple-element.42), channel_id=1, source_target_pairs={{0,1},{1,0},{2,3},{3,2},{4,5},{5,4},{6,7},{7,6},{8,9},{9,8},{10,11... | collective-permute-start | bytes 786440 | tf_op jit(solution)/shard_map/ppermute | solution.py:366
  21.1 6.2 %shard_map.147 = (f32[1024,256]{1,0:T(8,128)S(1)}, bf16[1024,256]{1,0:T(8,128)(2,1)S(1)}, f32[2304,144]{1,0:T(8,128)S(1)}, bf16[576,256]{1,0:T(8,128)(2,1)S(1)},...) custom-call(s32[2]{0:T(128)S(1)} %pad_add_fusion.refs_0_, ...), custom_call_target="tpu_custom_call" | custom-call | flops 8999999488 | tf_op jit(solution)/shard_map/pallas_call | solution.py:60
  27.3 1.9 %collective-permute-start.8 = (bf16[1024,256]{1,0:T(8,128)(2,1)S(1)}, bf16[1024,256]{1,0:T(8,128)(2,1)S(1)}, u32[]{:S(2)}, u32[]{:S(2)}) collective-permute-start(bf16[1024,256]{1,0:T(8,128)(2,1)S(1)} %get-tuple-element.50), channel_id=1, source_target_pairs={{0,16},{2,18},{4,20},{6,22},{8,24},{10,26},{12,28},{14,30},{16,0},... | collective-permute-start | bytes 1572872 | tf_op jit(solution)/shard_map/ppermute | solution.py:346
  29.2 1.4 %shard_map.148.refs_0_.refs_2_ = bf16[576,768]{1,0:T(8,128)(2,1)S(1)} custom-call(bf16[576,256]{1,0:T(8,128)(2,1)S(1)} %get-tuple-element.38.refs_0_, bf16[576,256]{1,0:T(8,128)(2,1)S(1)} %get-tuple-element.39.refs_1_, bf16[576,256]{1,0:T(8,128)(2,1)S(1)} %get-tuple-element.40.refs_2_, bf16[576,256]{1,0:T(8,128)(2,1)S(1)} %get-tuple-element.41.refs_3_, ...), custom_call_target="tpu_custom_call" | custom-call | flops 2000000000 | tf_op jit(solution)/shard_map/pallas_call | solution.py:60
  30.6 0.4 collective-permute-start.4
  31.0 0.9 shard_map.151
  31.9 3.7 %all-to-all-start = ((bf16[4,256,256]{2,1,0:T(8,128)(2,1)}), bf16[4,256,256]{2,1,0:T(8,128)(2,1)S(1)}, u32[]{:S(2)}, u32[]{:S(2)}) async-start(bf16[4,256,256]{2,1,0:T(8,128)(2,1)} %bitcast.3), calls=%async_computation | async-start | bytes 1048576 | tf_op jit(solution)/shard_map/all_to_all | solution.py:352
  35.6 1.7 %copy-done.18 = f32[2304,144]{1,0:T(8,128)S(1)} copy-done((f32[2304,144]{1,0:T(8,128)S(1)}, f32[2304,144]{1,0:T(8,128)}, u32[]{:S(2)}) %copy-start.18) | copy-done | bytes 1327128
  37.3 1.6 %shard_map.152 = (bf16[8,2,16,138]{3,2,1,0:T(8,128)(2,1)S(1)}, bf16[8,2,16,138]{3,2,1,0:T(8,128)(2,1)S(1)}) custom-call(s32[2]{0:T(128)S(1)} %pad_add_fusion.refs_0_, f32[2304,144]{1,0:T(8,128)S(1)} %copy-done.18, bf16[2,138,276]{2,1,0:T(8,128)(2,1)S(1)} %copy-done.15), custom_call_target="tpu_custom_call" | custom-call | flops 2500000000 | tf_op jit(solution)/shard_map/pallas_call | solution.py:60
  38.8 0.6 collective-permute-start.9
  39.4 1.0 collective-permute-done.9.refs_2_
  40.4 4.0 %all-to-all-done.refs_0_ = bf16[4,256,256]{2,1,0:T(8,128)(2,1)S(1)} async-done(((bf16[4,256,256]{2,1,0:T(8,128)(2,1)}), bf16[4,256,256]{2,1,0:T(8,128)(2,1)S(1)}, u32[]{:S(2)}, u32[]{:S(2)}) %all-to-all-start) | async-done | bytes 524320 | tf_op jit(solution)/shard_map/all_to_all | solution.py:352
  44.4 0.8 shard_map.153
  45.2 9.1 %all-to-all-start.1 = ((bf16[16,32,256]{2,1,0:T(8,128)(2,1)}), bf16[16,32,256]{2,1,0:T(8,128)(2,1)S(1)}, u32[]{:S(2)}, u32[]{:S(2)}) async-start(bf16[16,32,256]{2,1,0:T(8,128)(2,1)} %shard_map.153), calls=%async_computation.1 | async-start | bytes 524288 | tf_op jit(solution)/shard_map/all_to_all | solution.py:362
  54.4 0.9 copy-done.8
  55.4 0.9 copy-done.10
  56.3 2.0 %shard_map.149 = (bf16[2,216,512]{2,1,0:T(8,128)(2,1)S(1)}, bf16[2,216,512]{2,1,0:T(8,128)(2,1)S(1)}, bf16[2,72,512]{2,1,0:T(8,128)(2,1)}, bf16[2,72,512]{2,1,0:T(8,128)(2,1)}) custom-call(bf16[576,768]{1,0:T(8,128)(2,1)S(1)} %shard_map.148.refs_0_.refs_2_, bf16[576,768]{1,0:T(8,128)(2,1)S(1)} %collective-permute-done.4.refs_1_, ...), custom_call_target="tpu_custom_call" | custom-call | flops 2000000000 | tf_op jit(solution)/shard_map/pallas_call | solution.py:60
  58.4 0.8 copy-done.19
  59.1 3.3 %collective-permute-start.5 = (bf16[2,216,512]{2,1,0:T(8,128)(2,1)S(1)}, bf16[2,216,512]{2,1,0:T(8,128)(2,1)S(1)}, u32[]{:S(2)}, u32[]{:S(2)}) collective-permute-start(bf16[2,216,512]{2,1,0:T(8,128)(2,1)S(1)} %get-tuple-element.44), channel_id=1, source_target_pairs={{0,16},{2,18},{4,20},{6,22},{8,24},{10,26},{12,28},{14,30},{16,32}... | collective-permute-start | bytes 1327112 | tf_op jit(solution)/shard_map/ppermute | solution.py:340
  62.4 2.7 %collective-permute-start.6 = (bf16[2,72,512]{2,1,0:T(8,128)(2,1)}, bf16[2,72,512]{2,1,0:T(8,128)(2,1)}, u32[]{:S(2)}, u32[]{:S(2)}) collective-permute-start(bf16[2,72,512]{2,1,0:T(8,128)(2,1)} %get-tuple-element.45), channel_id=1, source_target_pairs={{0,2},{2,4},{4,6},{6,8},{8,10},{10,12},{12,14},{14,0},{16,18},{18,... | collective-permute-start | bytes 442376 | tf_op jit(solution)/shard_map/ppermute | solution.py:340
  65.1 0.3 collective-permute-start.7
  65.4 0.3 all-to-all-done.1.refs_0_
  65.6 0.7 shard_map.154
  66.4 7.7 %all-to-all-start.2 = ((bf16[16,32,256]{2,1,0:T(8,128)(2,1)}), bf16[16,32,256]{2,1,0:T(8,128)(2,1)S(1)}, u32[]{:S(2)}, u32[]{:S(2)}) async-start(bf16[16,32,256]{2,1,0:T(8,128)(2,1)} %shard_map.154), calls=%async_computation.2 | async-start | bytes 524288 | tf_op jit(solution)/shard_map/all_to_all | solution.py:362
  74.1 1.0 collective-permute-done.7.refs_6_
  75.2 1.0 copy-done.20
  76.2 3.1 %shard_map.150 = (bf16[12,12,4,512]{3,2,1,0:T(4,128)(2,1)}, bf16[12,12,4,512]{3,2,1,0:T(4,128)(2,1)}, f32[8,128]{1,0:T(8,128)S(1)}) custom-call(bf16[12,12,4,512]{3,2,1,0:T(4,128)(2,1)S(1)} %copy-done.3, bf16[12,12,4,512]{3,2,1,0:T(4,128)(2,1)S(1)} %copy-done.6, f32[1,512]{1,0:T(1,128)S(1)} %bitcast.10, bf16[2,216,512]{2,1,0:T(8,128)(2,1)S(1)} %copy-done.20, ...), custom_call_target="tpu_custom_call" | custom-call | flops 30000001024 | tf_op jit(solution)/shard_map/pallas_call | solution.py:60
  79.2 7.3 %all-to-all-done.2.refs_0_ = bf16[16,32,256]{2,1,0:T(8,128)(2,1)S(1)} async-done(((bf16[16,32,256]{2,1,0:T(8,128)(2,1)}), bf16[16,32,256]{2,1,0:T(8,128)(2,1)S(1)}, u32[]{:S(2)}, u32[]{:S(2)}) %all-to-all-start.2) | async-done | bytes 262176 | tf_op jit(solution)/shard_map/all_to_all | solution.py:362
  86.5 0.8 shard_map.155
  87.4 3.7 %all-to-all-start.3 = ((bf16[4,256,256]{2,1,0:T(8,128)(2,1)}), bf16[4,256,256]{2,1,0:T(8,128)(2,1)S(1)}, u32[]{:S(2)}, u32[]{:S(2)}) async-start(bf16[4,256,256]{2,1,0:T(8,128)(2,1)} %get-tuple-element.55), calls=%async_computation.3 | async-start | bytes 1048576 | tf_op jit(solution)/shard_map/all_to_all | solution.py:352
  91.1 2.3 %collective-permute-start.10 = (bf16[16,16,256]{2,1,0:T(8,128)(2,1)S(1)}, bf16[16,16,256]{2,1,0:T(8,128)(2,1)S(1)}, u32[]{:S(2)}, u32[]{:S(2)}) collective-permute-start(bf16[16,16,256]{2,1,0:T(8,128)(2,1)S(1)} %get-tuple-element.56.refs_1_), channel_id=1, source_target_pairs={{0,16},{2,18},{4,20},{6,22},{8,24},{10,26},{12,28},{14,30},{16,0},... | collective-permute-start | bytes 393224 | tf_op jit(solution)/shard_map/ppermute | solution.py:346
  93.3 4.7 %all-to-all-done.3 = bf16[4,256,256]{2,1,0:T(8,128)(2,1)S(1)} async-done(((bf16[4,256,256]{2,1,0:T(8,128)(2,1)}), bf16[4,256,256]{2,1,0:T(8,128)(2,1)S(1)}, u32[]{:S(2)}, u32[]{:S(2)}) %all-to-all-start.3) | async-done | bytes 524320 | tf_op jit(solution)/shard_map/all_to_all | solution.py:352
  98.0 3.5 %collective-permute-start.13 = (bf16[1024,256]{1,0:T(8,128)(2,1)S(1)}, bf16[1024,256]{1,0:T(8,128)(2,1)S(1)}, u32[]{:S(2)}, u32[]{:S(2)}) collective-permute-start(bf16[1024,256]{1,0:T(8,128)(2,1)S(1)} %bitcast.6), channel_id=1, source_target_pairs={{0,16},{2,18},{4,20},{6,22},{8,24},{10,26},{12,28},{14,30},{16,0},... | collective-permute-start | bytes 1572872 | tf_op jit(solution)/shard_map/ppermute | solution.py:346
  101.5 1.6 %shard_map.156 = (f32[2,2,4,3312]{3,2,1,0:T(4,128)}, f32[8,128]{1,0:T(8,128)S(1)}) custom-call(s32[2]{0:T(128)S(1)} %pad_add_fusion.refs_0_, bf16[16,16,256]{2,1,0:T(8,128)(2,1)S(1)} %get-tuple-element.56.refs_1_, bf16[16,16,256]{2,1,0:T(8,128)(2,1)S(1)} %collective-permute-done.10.refs_2_), custom_call_target="tpu_custom_call" | custom-call | flops 30000001024 | tf_op jit(solution)/shard_map/pallas_call | solution.py:60
  103.1 1.2 %shard_map.157 = f32[8,512]{1,0:T(8,128)S(1)} custom-call(s32[2]{0:T(128)S(1)} %pad_add_fusion.refs_0_, bf16[1024,256]{1,0:T(8,128)(2,1)S(1)} %bitcast.7, bf16[3,512,256]{2,1,0:T(8,128)(2,1)S(1)} %copy-done, f32[8,128]{1,0:T(8,128)S(1)} %get-tuple-element.57.refs_3_), custom_call_target="tpu_custom_call" | custom-call | flops 1000000000 | tf_op jit(solution)/shard_map/pallas_call | solution.py:60
  104.3 0.0 collective-permute-start.11
  104.3 1.2 %collective-permute-done.11 = f32[8,512]{1,0:T(8,128)S(1)} collective-permute-done((f32[8,512]{1,0:T(8,128)S(1)}, f32[8,512]{1,0:T(8,128)S(1)}, u32[]{:S(2)}, u32[]{:S(2)}) %collective-permute-start.11) | collective-permute-done | bytes 16416 | tf_op jit(solution)/shard_map/ppermute | solution.py:346
  105.5 1.9 %shard_map.158 = (f32[8,128]{1,0:T(8,128)S(1)}, f32[3,512,256]{2,1,0:T(8,128)}, f32[256,512]{1,0:T(8,128)}) custom-call(s32[2]{0:T(128)S(1)} %pad_add_fusion.refs_0_, bf16[1024,256]{1,0:T(8,128)(2,1)S(1)} %bitcast.8, bf16[1024,256]{1,0:T(8,128)(2,1)S(1)} %collective-permute-done.13.refs_2_), custom_call_target="tpu_custom_call" | custom-call | flops 2000000000 | tf_op jit(solution)/shard_map/pallas_call | solution.py:60
  107.4 0.6 collective-permute-done.12.refs_1_
  108.1 0.6 shard_map.159
  (47 shorter events, 0.1 us)
Async XLA Ops:
  0.6 1.1 copy-start.1
  1.7 1.1 copy-start.4
  2.8 14.2 %copy-start.7 = (bf16[256,512]{1,0:T(8,128)(2,1)S(1)}, bf16[256,512]{1,0:T(8,128)(2,1)}, u32[]{:S(2)}) copy-start(bf16[256,512]{1,0:T(8,128)(2,1)} %refs_2_.6) | copy-start | bytes 786436
  2.8 14.2 %copy-start.11 = (f32[2,2,4,3312]{3,2,1,0:T(4,128)S(1)}, f32[2,2,4,3312]{3,2,1,0:T(4,128)}, u32[]{:S(2)}) copy-start(f32[2,2,4,3312]{3,2,1,0:T(4,128)} %refs_1_.5) | copy-start | bytes 635908
  2.8 14.2 %copy-start.16 = (bf16[276,276]{1,0:T(8,128)(2,1)S(1)}, bf16[276,276]{1,0:T(8,128)(2,1)}, u32[]{:S(2)}) copy-start(bf16[276,276]{1,0:T(8,128)(2,1)} %constant.36.clone.refs_2_) | copy-start | bytes 457060
  4.5 16.6 %collective-permute-start = (bf16[2,216,512]{2,1,0:T(8,128)(2,1)S(1)}, bf16[2,216,512]{2,1,0:T(8,128)(2,1)S(1)}, u32[]{:S(2)}, u32[]{:S(2)}) collective-permute-start(bf16[2,216,512]{2,1,0:T(8,128)(2,1)S(1)} %get-tuple-element.34), channel_id=1, source_target_pairs={{0,240},{2,242},{4,244},{6,246},{8,248},{10,250},{12,252},{14,254}... | collective-permute-start | bytes 1327112 | tf_op jit(solution)/shard_map/ppermute | solution.py:340
  7.7 13.3 %collective-permute-start.1 = (bf16[2,72,512]{2,1,0:T(8,128)(2,1)S(1)}, bf16[2,72,512]{2,1,0:T(8,128)(2,1)S(1)}, u32[]{:S(2)}, u32[]{:S(2)}) collective-permute-start(bf16[2,72,512]{2,1,0:T(8,128)(2,1)S(1)} %get-tuple-element.35), channel_id=1, source_target_pairs={{0,14},{2,0},{4,2},{6,4},{8,6},{10,8},{12,10},{14,12},{16,30},{18,... | collective-permute-start | bytes 442376 | tf_op jit(solution)/shard_map/ppermute | solution.py:340
  11.2 9.9 %collective-permute-start.2 = (bf16[2,72,512]{2,1,0:T(8,128)(2,1)S(1)}, bf16[2,72,512]{2,1,0:T(8,128)(2,1)S(1)}, u32[]{:S(2)}, u32[]{:S(2)}) collective-permute-start(bf16[2,72,512]{2,1,0:T(8,128)(2,1)S(1)} %get-tuple-element.36), channel_id=1, source_target_pairs={{0,254},{2,240},{4,242},{6,244},{8,246},{10,248},{12,250},{14,252}... | collective-permute-start | bytes 442376 | tf_op jit(solution)/shard_map/ppermute | solution.py:340
  16.9 4.1 %copy-start = (bf16[3,512,256]{2,1,0:T(8,128)(2,1)S(1)}, bf16[3,512,256]{2,1,0:T(8,128)(2,1)}, u32[]{:S(2)}) copy-start(bf16[3,512,256]{2,1,0:T(8,128)(2,1)} %refs_2_.7) | copy-start | bytes 2359300
  16.9 4.1 %copy-start.2 = (bf16[12,12,4,512]{3,2,1,0:T(4,128)(2,1)S(1)}, bf16[12,12,4,512]{3,2,1,0:T(4,128)(2,1)}, u32[]{:S(2)}) copy-start(bf16[12,12,4,512]{3,2,1,0:T(4,128)(2,1)} %refs_0_.3) | copy-start | bytes 1769476
  17.0 4.1 %copy-start.5 = (bf16[12,12,4,512]{3,2,1,0:T(4,128)(2,1)S(1)}, bf16[12,12,4,512]{3,2,1,0:T(4,128)(2,1)}, u32[]{:S(2)}) copy-start(bf16[12,12,4,512]{3,2,1,0:T(4,128)(2,1)} %refs_1_.7) | copy-start | bytes 1769476
  17.0 4.1 %copy-start.12 = (f32[512]{0:T(512)S(1)}, f32[512]{0:T(512)}, u32[]{:S(2)}) copy-start(f32[512]{0:T(512)} %param.12) | copy-start | bytes 6148
  17.0 4.1 %copy-start.14 = (bf16[576,576]{1,0:T(8,128)(2,1)S(1)}, bf16[576,576]{1,0:T(8,128)(2,1)}, u32[]{:S(2)}) copy-start(bf16[576,576]{1,0:T(8,128)(2,1)} %constant.34.clone.refs_6_) | copy-start | bytes 1990660
  19.7 9.5 %collective-permute-start.3 = (bf16[256,512]{1,0:T(8,128)(2,1)S(1)}, bf16[256,512]{1,0:T(8,128)(2,1)S(1)}, u32[]{:S(2)}, u32[]{:S(2)}) collective-permute-start(bf16[256,512]{1,0:T(8,128)(2,1)S(1)} %get-tuple-element.42), channel_id=1, source_target_pairs={{0,1},{1,0},{2,3},{3,2},{4,5},{5,4},{6,7},{7,6},{8,9},{9,8},{10,11... | collective-permute-start | bytes 786440 | tf_op jit(solution)/shard_map/ppermute | solution.py:366
  21.1 8.1 %copy-start.13 = (bf16[576,576]{1,0:T(8,128)(2,1)S(1)}, bf16[576,576]{1,0:T(8,128)(2,1)}, u32[]{:S(2)}) copy-start(bf16[576,576]{1,0:T(8,128)(2,1)} %constant.35.clone.refs_5_) | copy-start | bytes 1990660
  27.3 3.3 %copy-start.17 = (f32[2304,144]{1,0:T(8,128)}, f32[2304,144]{1,0:T(8,128)S(1)}, u32[]{:S(2)}) copy-start(f32[2304,144]{1,0:T(8,128)S(1)} %get-tuple-element.51.refs_1_) | copy-start | bytes 3981316
  27.3 3.7 %collective-permute-start.8 = (bf16[1024,256]{1,0:T(8,128)(2,1)S(1)}, bf16[1024,256]{1,0:T(8,128)(2,1)S(1)}, u32[]{:S(2)}, u32[]{:S(2)}) collective-permute-start(bf16[1024,256]{1,0:T(8,128)(2,1)S(1)} %get-tuple-element.50), channel_id=1, source_target_pairs={{0,16},{2,18},{4,20},{6,22},{8,24},{10,26},{12,28},{14,30},{16,0},... | collective-permute-start | bytes 1572872 | tf_op jit(solution)/shard_map/ppermute | solution.py:346
  29.2 1.4 %copy-start.9 = (bf16[256,512]{1,0:T(8,128)(2,1)}, bf16[256,512]{1,0:T(8,128)(2,1)S(1)}, u32[]{:S(2)}) copy-start(bf16[256,512]{1,0:T(8,128)(2,1)S(1)} %collective-permute-done.3.refs_6_.refs_3_) | copy-start | bytes 786436
  30.6 5.0 %copy-start.15 = (bf16[2,138,276]{2,1,0:T(8,128)(2,1)S(1)}, bf16[2,138,276]{2,1,0:T(8,128)(2,1)}, u32[]{:S(2)}) copy-start(bf16[2,138,276]{2,1,0:T(8,128)(2,1)} %constant.37.clone.refs_2_) | copy-start | bytes 457060
  30.6 23.8 %collective-permute-start.4 = (bf16[576,768]{1,0:T(8,128)(2,1)S(1)}, bf16[576,768]{1,0:T(8,128)(2,1)S(1)}, u32[]{:S(2)}, u32[]{:S(2)}) collective-permute-start(bf16[576,768]{1,0:T(8,128)(2,1)S(1)} %shard_map.148.refs_0_.refs_2_), channel_id=1, source_target_pairs={{0,1},{1,0},{2,3},{3,2},{4,5},{5,4},{6,7},{7,6},{8,9},{9,8},{10,11... | collective-permute-start | bytes 2654216 | tf_op jit(solution)/shard_map/ppermute | solution.py:366
  31.9 12.5 %all-to-all-start = ((bf16[4,256,256]{2,1,0:T(8,128)(2,1)}), bf16[4,256,256]{2,1,0:T(8,128)(2,1)S(1)}, u32[]{:S(2)}, u32[]{:S(2)}) async-start(bf16[4,256,256]{2,1,0:T(8,128)(2,1)} %bitcast.3), calls=%async_computation | async-start | bytes 1048576 | tf_op jit(solution)/shard_map/all_to_all | solution.py:352
  35.6 1.7 %copy-start.18 = (f32[2304,144]{1,0:T(8,128)S(1)}, f32[2304,144]{1,0:T(8,128)}, u32[]{:S(2)}) copy-start(f32[2304,144]{1,0:T(8,128)} %copy-done.17) | copy-start | bytes 3981316
  38.8 1.6 %collective-permute-start.9 = (bf16[8,2,16,138]{3,2,1,0:T(8,128)(2,1)S(1)}, bf16[8,2,16,138]{3,2,1,0:T(8,128)(2,1)S(1)}, u32[]{:S(2)}, u32[]{:S(2)}) collective-permute-start(bf16[8,2,16,138]{3,2,1,0:T(8,128)(2,1)S(1)} %get-tuple-element.53), channel_id=1, source_target_pairs={{0,16},{2,18},{4,20},{6,22},{8,24},{10,26},{12,28},{14,30},{16,0},... | collective-permute-start | bytes 211976 | tf_op jit(solution)/shard_map/ppermute | solution.py:346
  45.2 20.4 %all-to-all-start.1 = ((bf16[16,32,256]{2,1,0:T(8,128)(2,1)}), bf16[16,32,256]{2,1,0:T(8,128)(2,1)S(1)}, u32[]{:S(2)}, u32[]{:S(2)}) async-start(bf16[16,32,256]{2,1,0:T(8,128)(2,1)} %shard_map.153), calls=%async_computation.1 | async-start | bytes 524288 | tf_op jit(solution)/shard_map/all_to_all | solution.py:362
  54.4 1.0 copy-start.8
  55.3 0.9 copy-start.10
  58.3 0.8 copy-start.19
  59.1 16.0 %copy-start.3 = (bf16[12,12,4,512]{3,2,1,0:T(4,128)(2,1)S(1)}, bf16[12,12,4,512]{3,2,1,0:T(4,128)(2,1)}, u32[]{:S(2)}) copy-start(bf16[12,12,4,512]{3,2,1,0:T(4,128)(2,1)} %refs_0_.3) | copy-start | bytes 1769476
  59.1 16.0 %copy-start.6 = (bf16[12,12,4,512]{3,2,1,0:T(4,128)(2,1)S(1)}, bf16[12,12,4,512]{3,2,1,0:T(4,128)(2,1)}, u32[]{:S(2)}) copy-start(bf16[12,12,4,512]{3,2,1,0:T(4,128)(2,1)} %refs_1_.7) | copy-start | bytes 1769476
  59.1 16.0 %collective-permute-start.5 = (bf16[2,216,512]{2,1,0:T(8,128)(2,1)S(1)}, bf16[2,216,512]{2,1,0:T(8,128)(2,1)S(1)}, u32[]{:S(2)}, u32[]{:S(2)}) collective-permute-start(bf16[2,216,512]{2,1,0:T(8,128)(2,1)S(1)} %get-tuple-element.44), channel_id=1, source_target_pairs={{0,16},{2,18},{4,20},{6,22},{8,24},{10,26},{12,28},{14,30},{16,32}... | collective-permute-start | bytes 1327112 | tf_op jit(solution)/shard_map/ppermute | solution.py:340
  62.4 11.7 %collective-permute-start.6 = (bf16[2,72,512]{2,1,0:T(8,128)(2,1)}, bf16[2,72,512]{2,1,0:T(8,128)(2,1)}, u32[]{:S(2)}, u32[]{:S(2)}) collective-permute-start(bf16[2,72,512]{2,1,0:T(8,128)(2,1)} %get-tuple-element.45), channel_id=1, source_target_pairs={{0,2},{2,4},{4,6},{6,8},{8,10},{10,12},{12,14},{14,0},{16,18},{18,... | collective-permute-start | bytes 442376 | tf_op jit(solution)/shard_map/ppermute | solution.py:340
  65.1 10.1 %collective-permute-start.7 = (bf16[2,72,512]{2,1,0:T(8,128)(2,1)}, bf16[2,72,512]{2,1,0:T(8,128)(2,1)}, u32[]{:S(2)}, u32[]{:S(2)}) collective-permute-start(bf16[2,72,512]{2,1,0:T(8,128)(2,1)} %get-tuple-element.46), channel_id=1, source_target_pairs={{0,18},{2,20},{4,22},{6,24},{8,26},{10,28},{12,30},{14,16},{16,34}... | collective-permute-start | bytes 442376 | tf_op jit(solution)/shard_map/ppermute | solution.py:340
  66.4 20.2 %all-to-all-start.2 = ((bf16[16,32,256]{2,1,0:T(8,128)(2,1)}), bf16[16,32,256]{2,1,0:T(8,128)(2,1)S(1)}, u32[]{:S(2)}, u32[]{:S(2)}) async-start(bf16[16,32,256]{2,1,0:T(8,128)(2,1)} %shard_map.154), calls=%async_computation.2 | async-start | bytes 524288 | tf_op jit(solution)/shard_map/all_to_all | solution.py:362
  75.2 1.0 copy-start.20
  87.4 10.6 %all-to-all-start.3 = ((bf16[4,256,256]{2,1,0:T(8,128)(2,1)}), bf16[4,256,256]{2,1,0:T(8,128)(2,1)S(1)}, u32[]{:S(2)}, u32[]{:S(2)}) async-start(bf16[4,256,256]{2,1,0:T(8,128)(2,1)} %get-tuple-element.55), calls=%async_computation.3 | async-start | bytes 1048576 | tf_op jit(solution)/shard_map/all_to_all | solution.py:352
  91.1 10.4 %collective-permute-start.10 = (bf16[16,16,256]{2,1,0:T(8,128)(2,1)S(1)}, bf16[16,16,256]{2,1,0:T(8,128)(2,1)S(1)}, u32[]{:S(2)}, u32[]{:S(2)}) collective-permute-start(bf16[16,16,256]{2,1,0:T(8,128)(2,1)S(1)} %get-tuple-element.56.refs_1_), channel_id=1, source_target_pairs={{0,16},{2,18},{4,20},{6,22},{8,24},{10,26},{12,28},{14,30},{16,0},... | collective-permute-start | bytes 393224 | tf_op jit(solution)/shard_map/ppermute | solution.py:346
  98.0 7.5 %collective-permute-start.13 = (bf16[1024,256]{1,0:T(8,128)(2,1)S(1)}, bf16[1024,256]{1,0:T(8,128)(2,1)S(1)}, u32[]{:S(2)}, u32[]{:S(2)}) collective-permute-start(bf16[1024,256]{1,0:T(8,128)(2,1)S(1)} %bitcast.6), channel_id=1, source_target_pairs={{0,16},{2,18},{4,20},{6,22},{8,24},{10,26},{12,28},{14,30},{16,0},... | collective-permute-start | bytes 1572872 | tf_op jit(solution)/shard_map/ppermute | solution.py:346
  104.3 1.2 %collective-permute-start.11 = (f32[8,512]{1,0:T(8,128)S(1)}, f32[8,512]{1,0:T(8,128)S(1)}, u32[]{:S(2)}, u32[]{:S(2)}) collective-permute-start(f32[8,512]{1,0:T(8,128)S(1)} %shard_map.157), channel_id=1, source_target_pairs={{0,16},{2,18},{4,20},{6,22},{8,24},{10,26},{12,28},{14,30},{16,0},... | collective-permute-start | bytes 49160 | tf_op jit(solution)/shard_map/ppermute | solution.py:346
  105.5 2.6 %collective-permute-start.12 = (f32[8,512]{1,0:T(8,128)S(1)}, f32[8,512]{1,0:T(8,128)S(1)}, u32[]{:S(2)}, u32[]{:S(2)}) collective-permute-start(f32[8,512]{1,0:T(8,128)S(1)} %add.8.refs_0_), channel_id=1, source_target_pairs={{0,1},{1,0},{2,3},{3,2},{4,5},{5,4},{6,7},{7,6},{8,9},{9,8},{10,11... | collective-permute-start | bytes 49160 | tf_op jit(solution)/shard_map/ppermute | solution.py:366

commit v3 on v2

--- a/solution.py
+++ b/solution.py
@@ -78,18 +78,10 @@
 PLACES = ((HIGH_LON, HIGH_LAT), (LOW_LON, HIGH_LAT), (HIGH_LON, LOW_LAT), (LOW_LON, LOW_LAT))
 
 
-def halo_kernel(latent, cot, o_lon, o_lat, o_cor, tiles, sems):
-    copies = []
-    for j, grid in enumerate((latent, cot)):
-        for k in range(4):
-            rows = pl.ds(3 * k, 3)
-            copies.append(pltpu.make_async_copy(grid.at[rows], tiles.at[j, rows], sems.at[4 * j + k]))
-            copies[-1].start()
-    for copy in copies:
-        copy.wait()
-    for (lon, lat), ref in zip(PLACES[1:], (o_lon, o_lat, o_cor)):
-        for j in range(2):
-            ref[j] = tiles[j, lon, lat].reshape(ref.shape[1:])
+def halo_kernel(latent, cot, *outs):
+    for (lon, lat), ref in zip(PLACES[1:], outs):
+        for j, grid in enumerate((latent, cot)):
+            ref[j] = grid[lon, lat].reshape(ref.shape[1:])
 
 
 def bias_kernel(info, table, order, w_out, bias, w_copy, raw, entries, low_u, high_u):
@@ -220,17 +212,10 @@
             copies[z * 2 + x, 16:32, :] = biases[x]
 
 
-def pair_kernel(terms, others, w_out, w_other, o_own, o_lon, o_lat, o_cor, held, sems):
-    copies = []
-    for j, w in enumerate((w_out, w_other)):
-        for k in range(2):
-            rows = pl.ds(128 * k, 128)
-            copies.append(pltpu.make_async_copy(w.at[rows], held.at[j, rows], sems.at[2 * j + k]))
-            copies[-1].start()
-    for copy in copies:
-        copy.wait()
-    out = dot(terms[:, 0:256], held[0]).astype(BF).astype(F32)
-    out = out + dot(others[:, 0:256], held[1]).astype(BF).astype(F32)
+def pair_kernel(terms, others, w_out, w_other, o_own, o_lon, o_lat, o_cor, token):
+    token[...] = jnp.zeros_like(token)
+    out = dot(terms[:, 0:256], w_out[...]).astype(BF).astype(F32)
+    out = out + dot(others[:, 0:256], w_other[...]).astype(BF).astype(F32)
     hid = terms[:, 256:768].astype(F32) + others[:, 256:768].astype(F32)
     for k, ref in enumerate((o_own, o_lon, o_lat, o_cor)):
         rows = slice(SECTIONS[k], SECTIONS[k + 1])
@@ -378,14 +363,7 @@
 
     part = lambda n: ((2, n, 512), BF)
     halos = [part(216), part(72), part(72)]
-    s_lon, s_lat, s_cor = call(
-        halo_kernel,
-        halos,
-        [],
-        [pltpu.VMEM((2,) + latent.shape, BF), pltpu.SemaphoreType.DMA((8,))],
-        smem=0,
-        hbm=[latent, cotangent],
-    )
+    s_lon, s_lat, s_cor = call(halo_kernel, halos, [latent, cotangent], smem=0)
     in_lon, in_lat, in_cor = moved(s_lon, -1, 0), moved(s_lat, 0, -1), moved(s_cor, -1, -1)
 
     bias, w_copy = call(
@@ -408,14 +386,8 @@
     recv = swapped(send, 1, 0)
     (terms,) = call(terms_kernel, [((576, 768), BF)], [att, gq, gk, gv, w_qkv, back], smem=0, after=[w_other], us=2)
     others = other_group(terms)
-    own, s_lon, s_lat, s_cor = call(
-        pair_kernel,
-        [part(216)] + halos,
-        [terms, others],
-        [pltpu.VMEM((2, 256, 512), BF), pltpu.SemaphoreType.DMA((4,))],
-        smem=0,
-        us=2,
-        hbm=[w_out, w_other],
+    own, s_lon, s_lat, s_cor, paired = call(
+        pair_kernel, [part(216)] + halos + [TOKEN], [terms, others, w_out, w_other], smem=0, us=30
     )
 
     (total,) = call(core_sum_kernel, [((1024, 256), BF)], [keep, recv], smem=0, after=[terms], us=0.5)
@@ -430,9 +402,9 @@
     b_recv = swapped(b_send, 1, 0)
     (message,) = call(y_sum_kernel, [((16, 32, 256), BF)], [parts, b_keep, b_recv], smem=0, us=1)
     r_lon, r_lat, r_cor = moved(s_lon, 1, 0), moved(s_lat, 0, 1), moved(s_cor, 1, 1)
-    (copies,) = call(zx_sum_kernel, [((16, 32, 256), BF)], [across_zx(message)], smem=0, us=1)
-
-    output, grad_latent, done = call(
+    (copies,) = call(zx_sum_kernel, [((16, 32, 256), BF)], [across_zx(message)], smem=0, after=[paired], us=1)
+
+    output, grad_latent, placed = call(
         final_kernel,
         [(latent.shape, BF), (latent.shape, BF), TOKEN],
         [latent, cotangent, gain, own, r_lon, r_lat, r_cor],
@@ -445,7 +417,6 @@
         [((4, 256, 256), BF), ((16, 16, 256), BF)],
         [across_zx(copies)],
         smem=0,
-        after=[done],
         us=1,
     )
     mine = across_y(copies).reshape(1024, 256)
@@ -455,11 +426,11 @@
         [(bias_table.shape, F32), TOKEN],
         [info, b_half, b_other],
         [pltpu.VMEM((512, 128), F32)] * 2 + [pltpu.VMEM((16, 3312), F32)],
-        us=30,
+        after=[placed],
     )
 
     (g_mine,) = call(
-        gain_kernel, [((8, 512), F32)], [info, mine, w_qkv], after=[done], us=1
+        gain_kernel, [((8, 512), F32)], [info, mine, w_qkv], after=[done], us=30
     )
     g_other = swapped(g_mine, 1, 0)
     g_pair = g_mine + g_other

time: 109 us -> 105 us (0.963)
  waiting for transfers between devices: 20.2 us -> 15.9 us
  local copies, waits for them, and re-layouts: 7.51 us -> 10.4 us
  Pallas kernels: 27.3 us -> 24.9 us
    all_to_all x2, waiting for transfers between devices: 8.7 us -> 3.13 us  [across_y(): return lax.all_to_all(value, 'lat', 0, 0, axis_index_groups=groups)]
    all_to_all x2, starting transfers between devices: 16.8 us -> 13 us  [across_zx(): return lax.all_to_all(value, ('lon', 'lat'), 0, 0, axis_index_groups=groups)]
    unnamed x42 -> x54, local copies, waits for them, and re-layouts: 7.51 us -> 10.4 us
    ppermute x5, starting transfers between devices: 8.21 us -> 10.7 us  [swapped(): return lax.ppermute(value, ('lon', 'lat'), pairs)]
    all_to_all x2, waiting for transfers between devices: 7.6 us -> 9.99 us  [across_zx(): return lax.all_to_all(value, ('lon', 'lat'), 0, 0, axis_index_groups=groups)]
    pallas_call x15, Pallas kernels: 27.3 us -> 24.9 us  [call(): pl.pallas_call(kernel, out_shape=[jax.ShapeDtypeStruct(s, t) for s, t in...]
    ppermute x6, starting transfers between devices: 18.6 us -> 20 us  [moved(): return lax.ppermute(value, ('lon', 'lat'), pairs)]
  transfers between devices with their start and end apart: 18 -> 18, of which waited for: 8 -> 6; matrix products, arithmetic and copies ran while one was open for 0% -> 0% of each run, Pallas kernels for 22% -> 22%
where the time goes in v3:
time: 105 us
  starting transfers between devices  52.5 us (50%)
  Pallas kernels  24.9 us (24%)
  waiting for transfers between devices  15.9 us (15%)
  local copies, waits for them, and re-layouts  10.4 us (10%)
    pallas_call x15, Pallas kernels, call(): pl.pallas_call(kernel, out_shape=[jax.ShapeDtypeStruct(s, t) for s, t in...  24.9 us
    ppermute x6, starting transfers between devices, moved(): return lax.ppermute(value, ('lon', 'lat'), pairs)  20 us
    all_to_all x2, starting transfers between devices, across_zx(): return lax.all_to_all(value, ('lon', 'lat'), 0, 0, axis_index_groups=groups)  13 us
    ppermute x5, starting transfers between devices, swapped(): return lax.ppermute(value, ('lon', 'lat'), pairs)  10.7 us
    unnamed x54, local copies, waits for them, and re-layouts  10.4 us
    all_to_all x2, waiting for transfers between devices, across_zx(): return lax.all_to_all(value, ('lon', 'lat'), 0, 0, axis_index_groups=groups)  9.99 us
    all_to_all x2, starting transfers between devices, across_y(): return lax.all_to_all(value, 'lat', 0, 0, axis_index_groups=groups)  7.12 us
    all_to_all x2, waiting for transfers between devices, across_y(): return lax.all_to_all(value, 'lat', 0, 0, axis_index_groups=groups)  3.13 us
  transfers between devices with their start and end apart: 18, of which 6 were waited for; matrix products, arithmetic and copies ran while one was open for 0% of the time, Pallas kernels for 22%

profile of v3, /device:TPU:1, one launch (start us, length us, event | category | flops | bytes accessed | tf_op | source)
XLA Modules:
  0.0 104.8 jit_solution(2586008894200306028)
XLA Ops:
  0.6 1.1 %copy-done.1 = bf16[12,12,4,512]{3,2,1,0:T(4,128)(2,1)S(1)} copy-done((bf16[12,12,4,512]{3,2,1,0:T(4,128)(2,1)S(1)}, bf16[12,12,4,512]{3,2,1,0:T(4,128)(2,1)}, u32[]{:S(2)}) %copy-start.1) | copy-done | bytes 589848
  1.7 1.1 %copy-done.4 = bf16[12,12,4,512]{3,2,1,0:T(4,128)(2,1)S(1)} copy-done((bf16[12,12,4,512]{3,2,1,0:T(4,128)(2,1)S(1)}, bf16[12,12,4,512]{3,2,1,0:T(4,128)(2,1)}, u32[]{:S(2)}) %copy-start.4) | copy-done | bytes 589848
  2.8 0.1 shard_map.145
  2.9 3.3 %collective-permute-start = (bf16[2,216,512]{2,1,0:T(8,128)(2,1)S(1)}, bf16[2,216,512]{2,1,0:T(8,128)(2,1)S(1)}, u32[]{:S(2)}, u32[]{:S(2)}) collective-permute-start(bf16[2,216,512]{2,1,0:T(8,128)(2,1)S(1)} %get-tuple-element.35), channel_id=1, source_target_pairs={{0,240},{2,242},{4,244},{6,246},{8,248},{10,250},{12,252},{14,254}... | collective-permute-start | bytes 1327112 | tf_op jit(solution)/shard_map/ppermute | solution.py:325
  6.1 3.5 %collective-permute-start.1 = (bf16[2,72,512]{2,1,0:T(8,128)(2,1)S(1)}, bf16[2,72,512]{2,1,0:T(8,128)(2,1)S(1)}, u32[]{:S(2)}, u32[]{:S(2)}) collective-permute-start(bf16[2,72,512]{2,1,0:T(8,128)(2,1)S(1)} %get-tuple-element.36), channel_id=1, source_target_pairs={{0,14},{2,0},{4,2},{6,4},{8,6},{10,8},{12,10},{14,12},{16,30},{18,... | collective-permute-start | bytes 442376 | tf_op jit(solution)/shard_map/ppermute | solution.py:325
  9.6 5.7 %collective-permute-start.2 = (bf16[2,72,512]{2,1,0:T(8,128)(2,1)S(1)}, bf16[2,72,512]{2,1,0:T(8,128)(2,1)S(1)}, u32[]{:S(2)}, u32[]{:S(2)}) collective-permute-start(bf16[2,72,512]{2,1,0:T(8,128)(2,1)S(1)} %get-tuple-element.37), channel_id=1, source_target_pairs={{0,254},{2,240},{4,242},{6,244},{8,246},{10,248},{12,250},{14,252}... | collective-permute-start | bytes 442376 | tf_op jit(solution)/shard_map/ppermute | solution.py:325
  15.4 2.7 %shard_map.146 = (f32[2304,144]{1,0:T(8,128)S(1)}, bf16[256,512]{1,0:T(8,128)(2,1)S(1)}) custom-call(s32[2]{0:T(128)S(1)} %pad_add_fusion.refs_0_, f32[2,2,4,3312]{3,2,1,0:T(4,128)S(1)} %copy-done.11, bf16[276,276]{1,0:T(8,128)(2,1)S(1)} %copy-done.22, bf16[256,512]{1,0:T(8,128)(2,1)S(1)} %copy-done.7), custom_call_target="tpu_custom_call" | custom-call | flops 2000000000 | tf_op jit(solution)/shard_map/pallas_call | solution.py:60
  18.1 1.3 %collective-permute-start.3 = (bf16[256,512]{1,0:T(8,128)(2,1)S(1)}, bf16[256,512]{1,0:T(8,128)(2,1)S(1)}, u32[]{:S(2)}, u32[]{:S(2)}) collective-permute-start(bf16[256,512]{1,0:T(8,128)(2,1)S(1)} %get-tuple-element.43), channel_id=1, source_target_pairs={{0,1},{1,0},{2,3},{3,2},{4,5},{5,4},{6,7},{7,6},{8,9},{9,8},{10,11... | collective-permute-start | bytes 786440 | tf_op jit(solution)/shard_map/ppermute | solution.py:351
  19.5 6.1 %shard_map.147 = (f32[1024,256]{1,0:T(8,128)S(1)}, bf16[1024,256]{1,0:T(8,128)(2,1)S(1)}, f32[2304,144]{1,0:T(8,128)S(1)}, bf16[576,256]{1,0:T(8,128)(2,1)S(1)},...) custom-call(s32[2]{0:T(128)S(1)} %pad_add_fusion.refs_0_, ...), custom_call_target="tpu_custom_call" | custom-call | flops 8999999488 | tf_op jit(solution)/shard_map/pallas_call | solution.py:60
  25.6 1.9 %collective-permute-start.8 = (bf16[1024,256]{1,0:T(8,128)(2,1)S(1)}, bf16[1024,256]{1,0:T(8,128)(2,1)S(1)}, u32[]{:S(2)}, u32[]{:S(2)}) collective-permute-start(bf16[1024,256]{1,0:T(8,128)(2,1)S(1)} %get-tuple-element.51), channel_id=1, source_target_pairs={{0,16},{2,18},{4,20},{6,22},{8,24},{10,26},{12,28},{14,30},{16,0},... | collective-permute-start | bytes 1572872 | tf_op jit(solution)/shard_map/ppermute | solution.py:331
  27.5 1.4 %shard_map.148.refs_0_.refs_2_ = bf16[576,768]{1,0:T(8,128)(2,1)S(1)} custom-call(bf16[576,256]{1,0:T(8,128)(2,1)S(1)} %get-tuple-element.39.refs_0_, bf16[576,256]{1,0:T(8,128)(2,1)S(1)} %get-tuple-element.40.refs_1_, bf16[576,256]{1,0:T(8,128)(2,1)S(1)} %get-tuple-element.41.refs_2_, bf16[576,256]{1,0:T(8,128)(2,1)S(1)} %get-tuple-element.42.refs_3_, ...), custom_call_target="tpu_custom_call" | custom-call | flops 2000000000 | tf_op jit(solution)/shard_map/pallas_call | solution.py:60
  28.9 0.4 collective-permute-start.4
  29.3 0.9 shard_map.151
  30.2 3.7 %all-to-all-start = ((bf16[4,256,256]{2,1,0:T(8,128)(2,1)}), bf16[4,256,256]{2,1,0:T(8,128)(2,1)S(1)}, u32[]{:S(2)}, u32[]{:S(2)}) async-start(bf16[4,256,256]{2,1,0:T(8,128)(2,1)} %bitcast.3), calls=%async_computation | async-start | bytes 1048576 | tf_op jit(solution)/shard_map/all_to_all | solution.py:337
  33.9 1.7 %copy-done.24 = f32[2304,144]{1,0:T(8,128)S(1)} copy-done((f32[2304,144]{1,0:T(8,128)S(1)}, f32[2304,144]{1,0:T(8,128)}, u32[]{:S(2)}) %copy-start.24) | copy-done | bytes 1327128
  35.5 1.6 %shard_map.152 = (bf16[8,2,16,138]{3,2,1,0:T(8,128)(2,1)S(1)}, bf16[8,2,16,138]{3,2,1,0:T(8,128)(2,1)S(1)}) custom-call(s32[2]{0:T(128)S(1)} %pad_add_fusion.refs_0_, f32[2304,144]{1,0:T(8,128)S(1)} %copy-done.24, bf16[2,138,276]{2,1,0:T(8,128)(2,1)S(1)} %copy-done.21), custom_call_target="tpu_custom_call" | custom-call | flops 2500000000 | tf_op jit(solution)/shard_map/pallas_call | solution.py:60
  37.1 0.7 collective-permute-start.9
  37.8 1.0 collective-permute-done.9.refs_2_
  38.8 0.7 copy-done.16
  39.5 3.1 %all-to-all-done.refs_0_ = bf16[4,256,256]{2,1,0:T(8,128)(2,1)S(1)} async-done(((bf16[4,256,256]{2,1,0:T(8,128)(2,1)}), bf16[4,256,256]{2,1,0:T(8,128)(2,1)S(1)}, u32[]{:S(2)}, u32[]{:S(2)}) %all-to-all-start) | async-done | bytes 524320 | tf_op jit(solution)/shard_map/all_to_all | solution.py:337
  42.6 0.9 copy-done.17
  43.5 0.8 shard_map.153
  44.3 9.3 %all-to-all-start.1 = ((bf16[16,32,256]{2,1,0:T(8,128)(2,1)}), bf16[16,32,256]{2,1,0:T(8,128)(2,1)S(1)}, u32[]{:S(2)}, u32[]{:S(2)}) async-start(bf16[16,32,256]{2,1,0:T(8,128)(2,1)} %shard_map.153), calls=%async_computation.1 | async-start | bytes 524288 | tf_op jit(solution)/shard_map/all_to_all | solution.py:347
  53.6 0.9 copy-done.8
  54.5 0.9 copy-done.10
  55.5 1.4 %shard_map.149 = (bf16[2,216,512]{2,1,0:T(8,128)(2,1)S(1)}, bf16[2,216,512]{2,1,0:T(8,128)(2,1)S(1)}, bf16[2,72,512]{2,1,0:T(8,128)(2,1)}, bf16[2,72,512]{2,1,0:T(8,128)(2,1)S(1)}, f32[8,128]{1,0:T(8,128)S(1)}) custom-call(bf16[576,768]{1,0:T(8,128)(2,1)S(1)} %shard_map.148.refs_0_.refs_2_, bf16[576,768]{1,0:T(8,128)(2,1)S(1)} %collective-permute-done.4.refs_1_, ...), custom_call_target="tpu_custom_call" | custom-call | flops 30000001024 | tf_op jit(solution)/shard_map/pallas_call | solution.py:60
  56.9 0.7 copy-done.12
  57.5 0.8 copy-done.25
  58.3 6.5 %all-to-all-done.1.refs_0_ = bf16[16,32,256]{2,1,0:T(8,128)(2,1)S(1)} async-done(((bf16[16,32,256]{2,1,0:T(8,128)(2,1)}), bf16[16,32,256]{2,1,0:T(8,128)(2,1)S(1)}, u32[]{:S(2)}, u32[]{:S(2)}) %all-to-all-start.1) | async-done | bytes 262176 | tf_op jit(solution)/shard_map/all_to_all | solution.py:347
  64.8 0.7 shard_map.154
  65.6 3.7 %all-to-all-start.2 = ((bf16[16,32,256]{2,1,0:T(8,128)(2,1)}), bf16[16,32,256]{2,1,0:T(8,128)(2,1)S(1)}, u32[]{:S(2)}, u32[]{:S(2)}) async-start(bf16[16,32,256]{2,1,0:T(8,128)(2,1)} %shard_map.154), calls=%async_computation.2 | async-start | bytes 524288 | tf_op jit(solution)/shard_map/all_to_all | solution.py:347
  69.3 4.6 %collective-permute-start.5 = (bf16[2,216,512]{2,1,0:T(8,128)(2,1)S(1)}, bf16[2,216,512]{2,1,0:T(8,128)(2,1)S(1)}, u32[]{:S(2)}, u32[]{:S(2)}) collective-permute-start(bf16[2,216,512]{2,1,0:T(8,128)(2,1)S(1)} %get-tuple-element.45), channel_id=1, source_target_pairs={{0,16},{2,18},{4,20},{6,22},{8,24},{10,26},{12,28},{14,30},{16,32}... | collective-permute-start | bytes 1327112 | tf_op jit(solution)/shard_map/ppermute | solution.py:325
  73.9 2.7 %collective-permute-start.6 = (bf16[2,72,512]{2,1,0:T(8,128)(2,1)}, bf16[2,72,512]{2,1,0:T(8,128)(2,1)}, u32[]{:S(2)}, u32[]{:S(2)}) collective-permute-start(bf16[2,72,512]{2,1,0:T(8,128)(2,1)} %get-tuple-element.46), channel_id=1, source_target_pairs={{0,2},{2,4},{4,6},{6,8},{8,10},{10,12},{12,14},{14,0},{16,18},{18,... | collective-permute-start | bytes 442376 | tf_op jit(solution)/shard_map/ppermute | solution.py:325
  76.6 0.4 collective-permute-start.7
  76.9 3.5 %all-to-all-done.2.refs_0_ = bf16[16,32,256]{2,1,0:T(8,128)(2,1)S(1)} async-done(((bf16[16,32,256]{2,1,0:T(8,128)(2,1)}), bf16[16,32,256]{2,1,0:T(8,128)(2,1)S(1)}, u32[]{:S(2)}, u32[]{:S(2)}) %all-to-all-start.2) | async-done | bytes 262176 | tf_op jit(solution)/shard_map/all_to_all | solution.py:347
  80.4 0.8 shard_map.155
  81.3 0.7 copy-done.14
  81.9 3.5 %all-to-all-start.3 = ((bf16[4,256,256]{2,1,0:T(8,128)(2,1)}), bf16[4,256,256]{2,1,0:T(8,128)(2,1)S(1)}, u32[]{:S(2)}, u32[]{:S(2)}) async-start(bf16[4,256,256]{2,1,0:T(8,128)(2,1)} %get-tuple-element.56), calls=%async_computation.3 | async-start | bytes 1048576 | tf_op jit(solution)/shard_map/all_to_all | solution.py:337
  85.4 5.9 %collective-permute-start.10 = (bf16[16,16,256]{2,1,0:T(8,128)(2,1)}, bf16[16,16,256]{2,1,0:T(8,128)(2,1)S(1)}, u32[]{:S(2)}, u32[]{:S(2)}) collective-permute-start(bf16[16,16,256]{2,1,0:T(8,128)(2,1)} %copy-done.14), channel_id=1, source_target_pairs={{0,16},{2,18},{4,20},{6,22},{8,24},{10,26},{12,28},{14,30},{16,0},... | collective-permute-start | bytes 393224 | tf_op jit(solution)/shard_map/ppermute | solution.py:331
  91.3 1.0 copy-done.26
  92.4 3.1 %shard_map.150 = (bf16[12,12,4,512]{3,2,1,0:T(4,128)(2,1)}, bf16[12,12,4,512]{3,2,1,0:T(4,128)(2,1)}, f32[8,128]{1,0:T(8,128)S(1)}) custom-call(bf16[12,12,4,512]{3,2,1,0:T(4,128)(2,1)S(1)} %copy-done.3, bf16[12,12,4,512]{3,2,1,0:T(4,128)(2,1)S(1)} %copy-done.6, f32[1,512]{1,0:T(1,128)S(1)} %bitcast.10, bf16[2,216,512]{2,1,0:T(8,128)(2,1)S(1)} %copy-done.26, ...), custom_call_target="tpu_custom_call" | custom-call | flops 30000001024 | tf_op jit(solution)/shard_map/pallas_call | solution.py:60
  95.5 1.6 %shard_map.156 = (f32[2,2,4,3312]{3,2,1,0:T(4,128)}, f32[8,128]{1,0:T(8,128)S(1)}) custom-call(s32[2]{0:T(128)S(1)} %pad_add_fusion.refs_0_, bf16[16,16,256]{2,1,0:T(8,128)(2,1)S(1)} %copy-done.15, bf16[16,16,256]{2,1,0:T(8,128)(2,1)S(1)} %collective-permute-done.10.refs_2_, f32[8,128]{1,0:T(8,128)S(1)} %get-tuple-element.58.refs_3_), custom_call_target="tpu_custom_call" | custom-call | flops 1000000000 | tf_op jit(solution)/shard_map/pallas_call | solution.py:60
  97.1 2.2 %collective-permute-start.13 = (bf16[1024,256]{1,0:T(8,128)(2,1)S(1)}, bf16[1024,256]{1,0:T(8,128)(2,1)S(1)}, u32[]{:S(2)}, u32[]{:S(2)}) collective-permute-start(bf16[1024,256]{1,0:T(8,128)(2,1)S(1)} %bitcast.6), channel_id=1, source_target_pairs={{0,16},{2,18},{4,20},{6,22},{8,24},{10,26},{12,28},{14,30},{16,0},... | collective-permute-start | bytes 1572872 | tf_op jit(solution)/shard_map/ppermute | solution.py:331
  99.3 1.2 %shard_map.157 = f32[8,512]{1,0:T(8,128)S(1)} custom-call(s32[2]{0:T(128)S(1)} %pad_add_fusion.refs_0_, bf16[1024,256]{1,0:T(8,128)(2,1)S(1)} %bitcast.7, bf16[3,512,256]{2,1,0:T(8,128)(2,1)S(1)} %copy-done, f32[8,128]{1,0:T(8,128)S(1)} %get-tuple-element.59.refs_3_), custom_call_target="tpu_custom_call" | custom-call | flops 30000001024 | tf_op jit(solution)/shard_map/pallas_call | solution.py:60
  100.5 1.2 %collective-permute-done.11 = f32[8,512]{1,0:T(8,128)S(1)} collective-permute-done((f32[8,512]{1,0:T(8,128)S(1)}, f32[8,512]{1,0:T(8,128)S(1)}, u32[]{:S(2)}, u32[]{:S(2)}) %collective-permute-start.11) | collective-permute-done | bytes 16416 | tf_op jit(solution)/shard_map/ppermute | solution.py:331
  101.7 1.9 %shard_map.158 = (f32[8,128]{1,0:T(8,128)S(1)}, f32[3,512,256]{2,1,0:T(8,128)}, f32[256,512]{1,0:T(8,128)}) custom-call(s32[2]{0:T(128)S(1)} %pad_add_fusion.refs_0_, bf16[1024,256]{1,0:T(8,128)(2,1)S(1)} %bitcast.8, bf16[1024,256]{1,0:T(8,128)(2,1)S(1)} %collective-permute-done.13.refs_2_), custom_call_target="tpu_custom_call" | custom-call | flops 2000000000 | tf_op jit(solution)/shard_map/pallas_call | solution.py:60
  103.6 0.6 collective-permute-done.12.refs_1_
  104.3 0.6 shard_map.159
  (59 shorter events, 0.2 us)
Async XLA Ops:
  0.6 1.1 %copy-start.1 = (bf16[12,12,4,512]{3,2,1,0:T(4,128)(2,1)S(1)}, bf16[12,12,4,512]{3,2,1,0:T(4,128)(2,1)}, u32[]{:S(2)}) copy-start(bf16[12,12,4,512]{3,2,1,0:T(4,128)(2,1)} %refs_0_.3) | copy-start | bytes 1769476
  1.7 1.1 %copy-start.4 = (bf16[12,12,4,512]{3,2,1,0:T(4,128)(2,1)S(1)}, bf16[12,12,4,512]{3,2,1,0:T(4,128)(2,1)}, u32[]{:S(2)}) copy-start(bf16[12,12,4,512]{3,2,1,0:T(4,128)(2,1)} %refs_1_.7) | copy-start | bytes 1769476
  2.8 12.6 %copy-start.7 = (bf16[256,512]{1,0:T(8,128)(2,1)S(1)}, bf16[256,512]{1,0:T(8,128)(2,1)}, u32[]{:S(2)}) copy-start(bf16[256,512]{1,0:T(8,128)(2,1)} %refs_2_.6) | copy-start | bytes 786436
  2.8 12.6 %copy-start.11 = (f32[2,2,4,3312]{3,2,1,0:T(4,128)S(1)}, f32[2,2,4,3312]{3,2,1,0:T(4,128)}, u32[]{:S(2)}) copy-start(f32[2,2,4,3312]{3,2,1,0:T(4,128)} %refs_1_.5) | copy-start | bytes 635908
  2.8 12.6 %copy-start.22 = (bf16[276,276]{1,0:T(8,128)(2,1)S(1)}, bf16[276,276]{1,0:T(8,128)(2,1)}, u32[]{:S(2)}) copy-start(bf16[276,276]{1,0:T(8,128)(2,1)} %constant.36.clone.refs_2_) | copy-start | bytes 457060
  2.9 16.6 %collective-permute-start = (bf16[2,216,512]{2,1,0:T(8,128)(2,1)S(1)}, bf16[2,216,512]{2,1,0:T(8,128)(2,1)S(1)}, u32[]{:S(2)}, u32[]{:S(2)}) collective-permute-start(bf16[2,216,512]{2,1,0:T(8,128)(2,1)S(1)} %get-tuple-element.35), channel_id=1, source_target_pairs={{0,240},{2,242},{4,244},{6,246},{8,248},{10,250},{12,252},{14,254}... | collective-permute-start | bytes 1327112 | tf_op jit(solution)/shard_map/ppermute | solution.py:325
  6.1 13.3 %collective-permute-start.1 = (bf16[2,72,512]{2,1,0:T(8,128)(2,1)S(1)}, bf16[2,72,512]{2,1,0:T(8,128)(2,1)S(1)}, u32[]{:S(2)}, u32[]{:S(2)}) collective-permute-start(bf16[2,72,512]{2,1,0:T(8,128)(2,1)S(1)} %get-tuple-element.36), channel_id=1, source_target_pairs={{0,14},{2,0},{4,2},{6,4},{8,6},{10,8},{12,10},{14,12},{16,30},{18,... | collective-permute-start | bytes 442376 | tf_op jit(solution)/shard_map/ppermute | solution.py:325
  9.6 9.9 %collective-permute-start.2 = (bf16[2,72,512]{2,1,0:T(8,128)(2,1)S(1)}, bf16[2,72,512]{2,1,0:T(8,128)(2,1)S(1)}, u32[]{:S(2)}, u32[]{:S(2)}) collective-permute-start(bf16[2,72,512]{2,1,0:T(8,128)(2,1)S(1)} %get-tuple-element.37), channel_id=1, source_target_pairs={{0,254},{2,240},{4,242},{6,244},{8,246},{10,248},{12,250},{14,252}... | collective-permute-start | bytes 442376 | tf_op jit(solution)/shard_map/ppermute | solution.py:325
  15.3 4.1 %copy-start = (bf16[3,512,256]{2,1,0:T(8,128)(2,1)S(1)}, bf16[3,512,256]{2,1,0:T(8,128)(2,1)}, u32[]{:S(2)}) copy-start(bf16[3,512,256]{2,1,0:T(8,128)(2,1)} %refs_2_.7) | copy-start | bytes 2359300
  15.3 4.1 %copy-start.2 = (bf16[12,12,4,512]{3,2,1,0:T(4,128)(2,1)S(1)}, bf16[12,12,4,512]{3,2,1,0:T(4,128)(2,1)}, u32[]{:S(2)}) copy-start(bf16[12,12,4,512]{3,2,1,0:T(4,128)(2,1)} %refs_0_.3) | copy-start | bytes 1769476
  15.4 4.1 %copy-start.5 = (bf16[12,12,4,512]{3,2,1,0:T(4,128)(2,1)S(1)}, bf16[12,12,4,512]{3,2,1,0:T(4,128)(2,1)}, u32[]{:S(2)}) copy-start(bf16[12,12,4,512]{3,2,1,0:T(4,128)(2,1)} %refs_1_.7) | copy-start | bytes 1769476
  15.4 4.1 %copy-start.18 = (f32[512]{0:T(512)S(1)}, f32[512]{0:T(512)}, u32[]{:S(2)}) copy-start(f32[512]{0:T(512)} %param.12) | copy-start | bytes 6148
  15.4 4.1 %copy-start.20 = (bf16[576,576]{1,0:T(8,128)(2,1)S(1)}, bf16[576,576]{1,0:T(8,128)(2,1)}, u32[]{:S(2)}) copy-start(bf16[576,576]{1,0:T(8,128)(2,1)} %constant.34.clone.refs_6_) | copy-start | bytes 1990660
  18.1 9.4 %collective-permute-start.3 = (bf16[256,512]{1,0:T(8,128)(2,1)S(1)}, bf16[256,512]{1,0:T(8,128)(2,1)S(1)}, u32[]{:S(2)}, u32[]{:S(2)}) collective-permute-start(bf16[256,512]{1,0:T(8,128)(2,1)S(1)} %get-tuple-element.43), channel_id=1, source_target_pairs={{0,1},{1,0},{2,3},{3,2},{4,5},{5,4},{6,7},{7,6},{8,9},{9,8},{10,11... | collective-permute-start | bytes 786440 | tf_op jit(solution)/shard_map/ppermute | solution.py:351
  19.5 8.0 %copy-start.19 = (bf16[576,576]{1,0:T(8,128)(2,1)S(1)}, bf16[576,576]{1,0:T(8,128)(2,1)}, u32[]{:S(2)}) copy-start(bf16[576,576]{1,0:T(8,128)(2,1)} %constant.35.clone.refs_5_) | copy-start | bytes 1990660
  25.6 3.3 %copy-start.23 = (f32[2304,144]{1,0:T(8,128)}, f32[2304,144]{1,0:T(8,128)S(1)}, u32[]{:S(2)}) copy-start(f32[2304,144]{1,0:T(8,128)S(1)} %get-tuple-element.52.refs_1_) | copy-start | bytes 3981316
  25.6 3.7 %collective-permute-start.8 = (bf16[1024,256]{1,0:T(8,128)(2,1)S(1)}, bf16[1024,256]{1,0:T(8,128)(2,1)S(1)}, u32[]{:S(2)}, u32[]{:S(2)}) collective-permute-start(bf16[1024,256]{1,0:T(8,128)(2,1)S(1)} %get-tuple-element.51), channel_id=1, source_target_pairs={{0,16},{2,18},{4,20},{6,22},{8,24},{10,26},{12,28},{14,30},{16,0},... | collective-permute-start | bytes 1572872 | tf_op jit(solution)/shard_map/ppermute | solution.py:331
  27.5 1.4 %copy-start.9 = (bf16[256,512]{1,0:T(8,128)(2,1)}, bf16[256,512]{1,0:T(8,128)(2,1)S(1)}, u32[]{:S(2)}) copy-start(bf16[256,512]{1,0:T(8,128)(2,1)S(1)} %collective-permute-done.3.refs_6_.refs_3_) | copy-start | bytes 786436
  28.9 5.0 %copy-start.21 = (bf16[2,138,276]{2,1,0:T(8,128)(2,1)S(1)}, bf16[2,138,276]{2,1,0:T(8,128)(2,1)}, u32[]{:S(2)}) copy-start(bf16[2,138,276]{2,1,0:T(8,128)(2,1)} %constant.37.clone.refs_2_) | copy-start | bytes 457060
  28.9 24.7 %collective-permute-start.4 = (bf16[576,768]{1,0:T(8,128)(2,1)S(1)}, bf16[576,768]{1,0:T(8,128)(2,1)S(1)}, u32[]{:S(2)}, u32[]{:S(2)}) collective-permute-start(bf16[576,768]{1,0:T(8,128)(2,1)S(1)} %shard_map.148.refs_0_.refs_2_), channel_id=1, source_target_pairs={{0,1},{1,0},{2,3},{3,2},{4,5},{5,4},{6,7},{7,6},{8,9},{9,8},{10,11... | collective-permute-start | bytes 2654216 | tf_op jit(solution)/shard_map/ppermute | solution.py:351
  30.2 12.4 %all-to-all-start = ((bf16[4,256,256]{2,1,0:T(8,128)(2,1)}), bf16[4,256,256]{2,1,0:T(8,128)(2,1)S(1)}, u32[]{:S(2)}, u32[]{:S(2)}) async-start(bf16[4,256,256]{2,1,0:T(8,128)(2,1)} %bitcast.3), calls=%async_computation | async-start | bytes 1048576 | tf_op jit(solution)/shard_map/all_to_all | solution.py:337
  33.9 1.7 %copy-start.24 = (f32[2304,144]{1,0:T(8,128)S(1)}, f32[2304,144]{1,0:T(8,128)}, u32[]{:S(2)}) copy-start(f32[2304,144]{1,0:T(8,128)} %copy-done.23) | copy-start | bytes 3981316
  37.1 1.7 %collective-permute-start.9 = (bf16[8,2,16,138]{3,2,1,0:T(8,128)(2,1)S(1)}, bf16[8,2,16,138]{3,2,1,0:T(8,128)(2,1)S(1)}, u32[]{:S(2)}, u32[]{:S(2)}) collective-permute-start(bf16[8,2,16,138]{3,2,1,0:T(8,128)(2,1)S(1)} %get-tuple-element.54), channel_id=1, source_target_pairs={{0,16},{2,18},{4,20},{6,22},{8,24},{10,26},{12,28},{14,30},{16,0},... | collective-permute-start | bytes 211976 | tf_op jit(solution)/shard_map/ppermute | solution.py:331
  38.8 0.7 copy-start.16
  42.6 0.9 copy-start.17
  44.3 20.5 %all-to-all-start.1 = ((bf16[16,32,256]{2,1,0:T(8,128)(2,1)}), bf16[16,32,256]{2,1,0:T(8,128)(2,1)S(1)}, u32[]{:S(2)}, u32[]{:S(2)}) async-start(bf16[16,32,256]{2,1,0:T(8,128)(2,1)} %shard_map.153), calls=%async_computation.1 | async-start | bytes 524288 | tf_op jit(solution)/shard_map/all_to_all | solution.py:347
  53.6 1.0 copy-start.8
  54.5 0.9 copy-start.10
  56.9 0.7 copy-start.12
  57.5 0.8 copy-start.25
  64.8 11.8 %copy-start.13 = (bf16[2,72,512]{2,1,0:T(8,128)(2,1)S(1)}, bf16[2,72,512]{2,1,0:T(8,128)(2,1)}, u32[]{:S(2)}) copy-start(bf16[2,72,512]{2,1,0:T(8,128)(2,1)} %copy-done.12) | copy-start | bytes 442372
  65.6 14.9 %all-to-all-start.2 = ((bf16[16,32,256]{2,1,0:T(8,128)(2,1)}), bf16[16,32,256]{2,1,0:T(8,128)(2,1)S(1)}, u32[]{:S(2)}, u32[]{:S(2)}) async-start(bf16[16,32,256]{2,1,0:T(8,128)(2,1)} %shard_map.154), calls=%async_computation.2 | async-start | bytes 524288 | tf_op jit(solution)/shard_map/all_to_all | solution.py:347
  69.3 22.0 %collective-permute-start.5 = (bf16[2,216,512]{2,1,0:T(8,128)(2,1)S(1)}, bf16[2,216,512]{2,1,0:T(8,128)(2,1)S(1)}, u32[]{:S(2)}, u32[]{:S(2)}) collective-permute-start(bf16[2,216,512]{2,1,0:T(8,128)(2,1)S(1)} %get-tuple-element.45), channel_id=1, source_target_pairs={{0,16},{2,18},{4,20},{6,22},{8,24},{10,26},{12,28},{14,30},{16,32}... | collective-permute-start | bytes 1327112 | tf_op jit(solution)/shard_map/ppermute | solution.py:325
  73.9 17.4 %collective-permute-start.6 = (bf16[2,72,512]{2,1,0:T(8,128)(2,1)}, bf16[2,72,512]{2,1,0:T(8,128)(2,1)}, u32[]{:S(2)}, u32[]{:S(2)}) collective-permute-start(bf16[2,72,512]{2,1,0:T(8,128)(2,1)} %get-tuple-element.46), channel_id=1, source_target_pairs={{0,2},{2,4},{4,6},{6,8},{8,10},{10,12},{12,14},{14,0},{16,18},{18,... | collective-permute-start | bytes 442376 | tf_op jit(solution)/shard_map/ppermute | solution.py:325
  76.6 14.7 %copy-start.3 = (bf16[12,12,4,512]{3,2,1,0:T(4,128)(2,1)S(1)}, bf16[12,12,4,512]{3,2,1,0:T(4,128)(2,1)}, u32[]{:S(2)}) copy-start(bf16[12,12,4,512]{3,2,1,0:T(4,128)(2,1)} %refs_0_.3) | copy-start | bytes 1769476
  76.6 14.7 %copy-start.6 = (bf16[12,12,4,512]{3,2,1,0:T(4,128)(2,1)S(1)}, bf16[12,12,4,512]{3,2,1,0:T(4,128)(2,1)}, u32[]{:S(2)}) copy-start(bf16[12,12,4,512]{3,2,1,0:T(4,128)(2,1)} %refs_1_.7) | copy-start | bytes 1769476
  76.6 14.7 %collective-permute-start.7 = (bf16[2,72,512]{2,1,0:T(8,128)(2,1)S(1)}, bf16[2,72,512]{2,1,0:T(8,128)(2,1)}, u32[]{:S(2)}, u32[]{:S(2)}) collective-permute-start(bf16[2,72,512]{2,1,0:T(8,128)(2,1)S(1)} %copy-done.13), channel_id=1, source_target_pairs={{0,18},{2,20},{4,22},{6,24},{8,26},{10,28},{12,30},{14,16},{16,34}... | collective-permute-start | bytes 442376 | tf_op jit(solution)/shard_map/ppermute | solution.py:325
  81.3 0.7 copy-start.14
  81.9 15.1 %all-to-all-start.3 = ((bf16[4,256,256]{2,1,0:T(8,128)(2,1)}), bf16[4,256,256]{2,1,0:T(8,128)(2,1)S(1)}, u32[]{:S(2)}, u32[]{:S(2)}) async-start(bf16[4,256,256]{2,1,0:T(8,128)(2,1)} %get-tuple-element.56), calls=%async_computation.3 | async-start | bytes 1048576 | tf_op jit(solution)/shard_map/all_to_all | solution.py:337
  85.4 10.1 %collective-permute-start.10 = (bf16[16,16,256]{2,1,0:T(8,128)(2,1)}, bf16[16,16,256]{2,1,0:T(8,128)(2,1)S(1)}, u32[]{:S(2)}, u32[]{:S(2)}) collective-permute-start(bf16[16,16,256]{2,1,0:T(8,128)(2,1)} %copy-done.14), channel_id=1, source_target_pairs={{0,16},{2,18},{4,20},{6,22},{8,24},{10,26},{12,28},{14,30},{16,0},... | collective-permute-start | bytes 393224 | tf_op jit(solution)/shard_map/ppermute | solution.py:331
  91.3 1.0 copy-start.26
  92.4 3.1 %copy-start.15 = (bf16[16,16,256]{2,1,0:T(8,128)(2,1)S(1)}, bf16[16,16,256]{2,1,0:T(8,128)(2,1)}, u32[]{:S(2)}) copy-start(bf16[16,16,256]{2,1,0:T(8,128)(2,1)} %copy-done.14) | copy-start | bytes 393220
  97.1 4.6 %collective-permute-start.13 = (bf16[1024,256]{1,0:T(8,128)(2,1)S(1)}, bf16[1024,256]{1,0:T(8,128)(2,1)S(1)}, u32[]{:S(2)}, u32[]{:S(2)}) collective-permute-start(bf16[1024,256]{1,0:T(8,128)(2,1)S(1)} %bitcast.6), channel_id=1, source_target_pairs={{0,16},{2,18},{4,20},{6,22},{8,24},{10,26},{12,28},{14,30},{16,0},... | collective-permute-start | bytes 1572872 | tf_op jit(solution)/shard_map/ppermute | solution.py:331
  100.5 1.2 %collective-permute-start.11 = (f32[8,512]{1,0:T(8,128)S(1)}, f32[8,512]{1,0:T(8,128)S(1)}, u32[]{:S(2)}, u32[]{:S(2)}) collective-permute-start(f32[8,512]{1,0:T(8,128)S(1)} %shard_map.157), channel_id=1, source_target_pairs={{0,16},{2,18},{4,20},{6,22},{8,24},{10,26},{12,28},{14,30},{16,0},... | collective-permute-start | bytes 49160 | tf_op jit(solution)/shard_map/ppermute | solution.py:331
  101.7 2.6 %collective-permute-start.12 = (f32[8,512]{1,0:T(8,128)S(1)}, f32[8,512]{1,0:T(8,128)S(1)}, u32[]{:S(2)}, u32[]{:S(2)}) collective-permute-start(f32[8,512]{1,0:T(8,128)S(1)} %add.8.refs_0_), channel_id=1, source_target_pairs={{0,1},{1,0},{2,3},{3,2},{4,5},{5,4},{6,7},{7,6},{8,9},{9,8},{10,11... | collective-permute-start | bytes 49160 | tf_op jit(solution)/shard_map/ppermute | solution.py:351

commit v4 on v3

--- a/solution.py
+++ b/solution.py
@@ -187,29 +187,27 @@
     for j in range(1, 4):
         total = total + parts[j].astype(F32)
     total = total.astype(BF)
-    tail = jnp.zeros((16, 118), BF)
-    for z in range(8):
-        for x in range(2):
-            j = z * 2 + x
-            message[j, 0:16, :] = total[j * 16 : (j + 1) * 16]
-            both = (b_keep[z, x].astype(F32) + b_recv[z, x].astype(F32)).astype(BF)
-            message[j, 16:32, :] = jnp.concatenate([both, tail], 1)
+    both = (b_keep[...].astype(F32) + b_recv[...].astype(F32)).astype(BF)
+    for j in range(16):
+        rows = slice(j * 16, (j + 1) * 16)
+        message[j, :, 0:256] = total[rows]
+        message[j, :, 256:384] = both[rows]
 
 
 def zx_sum_kernel(parts, copies):
     total = jnp.zeros((16, 256), F32)
     biases = []
     for x in range(2):
-        bias = jnp.zeros((16, 256), F32)
+        bias = jnp.zeros((16, 128), F32)
         for z in range(8):
-            total = total + parts[z * 2 + x, 0:16, :].astype(F32)
-            bias = bias + parts[z * 2 + x, 16:32, :].astype(F32)
+            total = total + parts[z * 2 + x, :, 0:256].astype(F32)
+            bias = bias + parts[z * 2 + x, :, 256:384].astype(F32)
         biases.append(bias.astype(BF))
     total = total.astype(BF)
     for z in range(8):
         for x in range(2):
-            copies[z * 2 + x, 0:16, :] = total
-            copies[z * 2 + x, 16:32, :] = biases[x]
+            copies[z * 2 + x, :, 0:256] = total
+            copies[z * 2 + x, :, 256:384] = biases[x]
 
 
 def pair_kernel(terms, others, w_out, w_other, o_own, o_lon, o_lat, o_cor, token):
@@ -225,9 +223,10 @@
 
 def spread_kernel(parts, copies, b_half):
     for j in range(16):
+        rows = slice(j * 16, (j + 1) * 16)
         for k in range(4):
-            copies[k, j * 16 : (j + 1) * 16, :] = parts[j, 0:16, :]
-        b_half[j] = parts[j, 16:32, :]
+            copies[k, rows, :] = parts[j, :, 0:256]
+        b_half[rows, :] = parts[j, :, 256:384]
 
 
 def gain_kernel(info, mine, w_qkv, out):
@@ -242,20 +241,16 @@
     out[...] = (mine[0:1, :] + other[0:1, :]) / gain[...]
 
 
-def bias_out_kernel(info, mine, other, grad_bias, token, low, high, flat):
+def bias_out_kernel(info, mine, other, grad_bias, token, rows, flat):
     token[...] = jnp.zeros_like(token)
-    first = jnp.where(info[1] == 0, mine[...], other[...]).astype(F32)
-    second = jnp.where(info[1] == 0, other[...], mine[...]).astype(F32)
-    for j, half in enumerate((first, second)):
-        half = half.reshape(256, 256)
-        low[256 * j : 256 * j + 256, :] = half[:, 0:128]
-        high[256 * j : 256 * j + 256, :] = half[:, 128:256]
+    rows[0:256, :] = jnp.where(info[1] == 0, mine[...], other[...]).astype(F32)
+    rows[256:512, :] = jnp.where(info[1] == 0, other[...], mine[...]).astype(F32)
     for s_t in range(2):
         for j in range(12):
             at = (s_t * 12 + j) * 138
-            rows = pl.ds(s_t * 16 + j, 16, stride=32)
-            flat[:, at : at + 128] = low[rows, :]
-            flat[:, at + 128 : at + 138] = high[rows, :][:, 0:10]
+            flat[:, at : at + 115] = rows[pl.ds(s_t * 16 + j, 16, stride=32), :][:, 0:115]
+            last = rows[pl.ds(s_t * 16 + 12 + j // 3, 16, stride=32), :]
+            flat[:, at + 115 : at + 138] = last[:, j % 3 * 23 : j % 3 * 23 + 23]
     grad_bias[...] = flat[...].reshape(grad_bias.shape)
 
 
@@ -280,7 +275,7 @@
         copy.wait()
 
 
-def bias_grad_kernel(info, ds, order, keep, send, part, entries, tables):
+def bias_grad_kernel(info, ds, order, keep, send, part, entries, packed, *ends):
     entries[...] = jnp.zeros_like(entries)
     for p in range(12):
         for i in range(16):
@@ -288,13 +283,23 @@
         at = slice((11 - p) * 12, (11 - p) * 12 + WTOK)
         entries[:, at] = entries[:, at] + part[...]
     total = entries[...].astype(BF)
-    tables[...] = jnp.zeros_like(tables)
+    packed[...] = jnp.zeros_like(packed)
     for s_u in range(2):
         rows = dot(total, order[s_u], NT)
-        for i in range(16):
-            for s_t in range(2):
-                tables[i, s_t, s_u * 6 : s_u * 6 + 6, :] = rows[i * 12 + s_t * 6 : i * 12 + s_t * 6 + 6]
-    mine, other = tables[0:8], tables[8:16]
+        for half in range(32):
+            at = half * 16 + s_u * 6
+            packed[at : at + 6, 0:115] = rows[half * 6 : half * 6 + 6, 0:115]
+        for q in range(3):
+            last = ends[s_u * 3 + q]
+            last[...] = jnp.zeros_like(last)
+            last[:, q * 23 : q * 23 + 23] = rows[:, 115:138]
+    for k in range(4):
+        row = jnp.zeros((32, 128), F32)
+        for q in range(3):
+            s_u, r_t = (k * 3 + q) // 6, (k * 3 + q) % 6
+            row = row + ends[s_u * 3 + q][pl.ds(r_t, 32, stride=6), :]
+        packed[pl.ds(12 + k, 32, stride=16), :] = row
+    mine, other = packed[0:256, :], packed[256:512, :]
     keep[...] = jnp.where(info[1] == 0, mine, other).astype(BF)
     send[...] = jnp.where(info[1] == 0, other, mine).astype(BF)
 
@@ -394,15 +399,16 @@
     parts = across_y(total.reshape(4, 256, 256))
     b_keep, b_send = call(
         bias_grad_kernel,
-        [((8, 2, 16, 138), BF)] * 2,
+        [((256, 128), BF)] * 2,
         [info, ds, order_halves],
-        [pltpu.VMEM((192, WTOK), F32), pltpu.VMEM((192, 276), F32), pltpu.VMEM((16, 2, 16, 138), F32)],
+        [pltpu.VMEM((192, WTOK), F32), pltpu.VMEM((192, 276), F32), pltpu.VMEM((512, 128), F32)]
+        + [pltpu.VMEM((192, 128), F32)] * 6,
         us=2.5,
     )
     b_recv = swapped(b_send, 1, 0)
-    (message,) = call(y_sum_kernel, [((16, 32, 256), BF)], [parts, b_keep, b_recv], smem=0, us=1)
+    (message,) = call(y_sum_kernel, [((16, 16, 384), BF)], [parts, b_keep, b_recv], smem=0, us=1)
     r_lon, r_lat, r_cor = moved(s_lon, 1, 0), moved(s_lat, 0, 1), moved(s_cor, 1, 1)
-    (copies,) = call(zx_sum_kernel, [((16, 32, 256), BF)], [across_zx(message)], smem=0, after=[paired], us=1)
+    (copies,) = call(zx_sum_kernel, [((16, 16, 384), BF)], [across_zx(message)], smem=0, after=[paired], us=1)
 
     output, grad_latent, placed = call(
         final_kernel,
@@ -414,7 +420,7 @@
 
     copies, b_half = call(
         spread_kernel,
-        [((4, 256, 256), BF), ((16, 16, 256), BF)],
+        [((4, 256, 256), BF), ((256, 128), BF)],
         [across_zx(copies)],
         smem=0,
         us=1,
@@ -425,7 +431,7 @@
         bias_out_kernel,
         [(bias_table.shape, F32), TOKEN],
         [info, b_half, b_other],
-        [pltpu.VMEM((512, 128), F32)] * 2 + [pltpu.VMEM((16, 3312), F32)],
+        [pltpu.VMEM((512, 128), F32), pltpu.VMEM((16, 3312), F32)],
         after=[placed],
     )
 

time: 105 us -> 103 us (0.981)
  local copies, waits for them, and re-layouts: 10.4 us -> 8.81 us
    unnamed x54 -> x50, local copies, waits for them, and re-layouts: 10.4 us -> 8.81 us
  transfers between devices with their start and end apart: 18 -> 18, of which waited for: 6 -> 6; matrix products, arithmetic and copies ran while one was open for 0% -> 0% of each run, Pallas kernels for 22% -> 23%
where the time goes in v4:
time: 103 us; the launch traced here: 102 us
  starting transfers between devices  51.7 us (50%)
  Pallas kernels  25.1 us (24%)
  waiting for transfers between devices  15.3 us (15%)
  local copies, waits for them, and re-layouts  8.81 us (9%)
    pallas_call x15, Pallas kernels, call(): pl.pallas_call(kernel, out_shape=[jax.ShapeDtypeStruct(s, t) for s, t in...  25.1 us
    ppermute x6, starting transfers between devices, moved(): return lax.ppermute(value, ('lon', 'lat'), pairs)  19.9 us
    all_to_all x2, starting transfers between devices, across_zx(): return lax.all_to_all(value, ('lon', 'lat'), 0, 0, axis_index_groups=groups)  12.8 us
    ppermute x5, starting transfers between devices, swapped(): return lax.ppermute(value, ('lon', 'lat'), pairs)  10.2 us
    all_to_all x2, waiting for transfers between devices, across_zx(): return lax.all_to_all(value, ('lon', 'lat'), 0, 0, axis_index_groups=groups)  8.99 us
    unnamed x50, local copies, waits for them, and re-layouts  8.81 us
    all_to_all x2, starting transfers between devices, across_y(): return lax.all_to_all(value, 'lat', 0, 0, axis_index_groups=groups)  7.12 us
    all_to_all x2, waiting for transfers between devices, across_y(): return lax.all_to_all(value, 'lat', 0, 0, axis_index_groups=groups)  3.54 us
  transfers between devices with their start and end apart: 18, of which 6 were waited for; matrix products, arithmetic and copies ran while one was open for 0% of the time, Pallas kernels for 23%

profile of v4, /device:TPU:1, one launch (start us, length us, event | category | flops | bytes accessed | tf_op | source)
XLA Modules:
  0.0 101.9 jit_solution(5480530885519283735)
XLA Ops:
  0.6 1.1 %copy-done.1 = bf16[12,12,4,512]{3,2,1,0:T(4,128)(2,1)S(1)} copy-done((bf16[12,12,4,512]{3,2,1,0:T(4,128)(2,1)S(1)}, bf16[12,12,4,512]{3,2,1,0:T(4,128)(2,1)}, u32[]{:S(2)}) %copy-start.1) | copy-done | bytes 589848
  1.7 1.1 %copy-done.4 = bf16[12,12,4,512]{3,2,1,0:T(4,128)(2,1)S(1)} copy-done((bf16[12,12,4,512]{3,2,1,0:T(4,128)(2,1)S(1)}, bf16[12,12,4,512]{3,2,1,0:T(4,128)(2,1)}, u32[]{:S(2)}) %copy-start.4) | copy-done | bytes 589848
  2.8 0.1 shard_map.145
  2.9 3.3 %collective-permute-start = (bf16[2,216,512]{2,1,0:T(8,128)(2,1)S(1)}, bf16[2,216,512]{2,1,0:T(8,128)(2,1)S(1)}, u32[]{:S(2)}, u32[]{:S(2)}) collective-permute-start(bf16[2,216,512]{2,1,0:T(8,128)(2,1)S(1)} %get-tuple-element.35), channel_id=1, source_target_pairs={{0,240},{2,242},{4,244},{6,246},{8,248},{10,250},{12,252},{14,254}... | collective-permute-start | bytes 1327112 | tf_op jit(solution)/shard_map/ppermute | solution.py:330
  6.1 3.5 %collective-permute-start.1 = (bf16[2,72,512]{2,1,0:T(8,128)(2,1)S(1)}, bf16[2,72,512]{2,1,0:T(8,128)(2,1)S(1)}, u32[]{:S(2)}, u32[]{:S(2)}) collective-permute-start(bf16[2,72,512]{2,1,0:T(8,128)(2,1)S(1)} %get-tuple-element.36), channel_id=1, source_target_pairs={{0,14},{2,0},{4,2},{6,4},{8,6},{10,8},{12,10},{14,12},{16,30},{18,... | collective-permute-start | bytes 442376 | tf_op jit(solution)/shard_map/ppermute | solution.py:330
  9.6 5.7 %collective-permute-start.2 = (bf16[2,72,512]{2,1,0:T(8,128)(2,1)S(1)}, bf16[2,72,512]{2,1,0:T(8,128)(2,1)S(1)}, u32[]{:S(2)}, u32[]{:S(2)}) collective-permute-start(bf16[2,72,512]{2,1,0:T(8,128)(2,1)S(1)} %get-tuple-element.37), channel_id=1, source_target_pairs={{0,254},{2,240},{4,242},{6,244},{8,246},{10,248},{12,250},{14,252}... | collective-permute-start | bytes 442376 | tf_op jit(solution)/shard_map/ppermute | solution.py:330
  15.3 0.1 pad_add_fusion.refs_0_
  15.4 2.7 %shard_map.146 = (f32[2304,144]{1,0:T(8,128)S(1)}, bf16[256,512]{1,0:T(8,128)(2,1)S(1)}) custom-call(s32[2]{0:T(128)S(1)} %pad_add_fusion.refs_0_, f32[2,2,4,3312]{3,2,1,0:T(4,128)S(1)} %copy-done.11, bf16[276,276]{1,0:T(8,128)(2,1)S(1)} %copy-done.20, bf16[256,512]{1,0:T(8,128)(2,1)S(1)} %copy-done.7), custom_call_target="tpu_custom_call" | custom-call | flops 2000000000 | tf_op jit(solution)/shard_map/pallas_call | solution.py:60
  18.1 1.3 %collective-permute-start.3 = (bf16[256,512]{1,0:T(8,128)(2,1)S(1)}, bf16[256,512]{1,0:T(8,128)(2,1)S(1)}, u32[]{:S(2)}, u32[]{:S(2)}) collective-permute-start(bf16[256,512]{1,0:T(8,128)(2,1)S(1)} %get-tuple-element.43), channel_id=1, source_target_pairs={{0,1},{1,0},{2,3},{3,2},{4,5},{5,4},{6,7},{7,6},{8,9},{9,8},{10,11... | collective-permute-start | bytes 786440 | tf_op jit(solution)/shard_map/ppermute | solution.py:356
  19.5 6.1 %shard_map.147 = (f32[1024,256]{1,0:T(8,128)S(1)}, bf16[1024,256]{1,0:T(8,128)(2,1)S(1)}, f32[2304,144]{1,0:T(8,128)S(1)}, bf16[576,256]{1,0:T(8,128)(2,1)S(1)},...) custom-call(s32[2]{0:T(128)S(1)} %pad_add_fusion.refs_0_, ...), custom_call_target="tpu_custom_call" | custom-call | flops 8999999488 | tf_op jit(solution)/shard_map/pallas_call | solution.py:60
  25.6 1.9 %collective-permute-start.8 = (bf16[1024,256]{1,0:T(8,128)(2,1)S(1)}, bf16[1024,256]{1,0:T(8,128)(2,1)S(1)}, u32[]{:S(2)}, u32[]{:S(2)}) collective-permute-start(bf16[1024,256]{1,0:T(8,128)(2,1)S(1)} %get-tuple-element.51), channel_id=1, source_target_pairs={{0,16},{2,18},{4,20},{6,22},{8,24},{10,26},{12,28},{14,30},{16,0},... | collective-permute-start | bytes 1572872 | tf_op jit(solution)/shard_map/ppermute | solution.py:336
  27.5 1.4 %shard_map.148.refs_0_.refs_2_ = bf16[576,768]{1,0:T(8,128)(2,1)S(1)} custom-call(bf16[576,256]{1,0:T(8,128)(2,1)S(1)} %get-tuple-element.39.refs_0_, bf16[576,256]{1,0:T(8,128)(2,1)S(1)} %get-tuple-element.40.refs_1_, bf16[576,256]{1,0:T(8,128)(2,1)S(1)} %get-tuple-element.41.refs_2_, bf16[576,256]{1,0:T(8,128)(2,1)S(1)} %get-tuple-element.42.refs_3_, ...), custom_call_target="tpu_custom_call" | custom-call | flops 2000000000 | tf_op jit(solution)/shard_map/pallas_call | solution.py:60
  28.9 0.4 collective-permute-start.4
  29.3 0.9 shard_map.151
  30.2 3.7 %all-to-all-start = ((bf16[4,256,256]{2,1,0:T(8,128)(2,1)}), bf16[4,256,256]{2,1,0:T(8,128)(2,1)S(1)}, u32[]{:S(2)}, u32[]{:S(2)}) async-start(bf16[4,256,256]{2,1,0:T(8,128)(2,1)} %bitcast.3), calls=%async_computation | async-start | bytes 1048576 | tf_op jit(solution)/shard_map/all_to_all | solution.py:342
  33.9 1.7 %copy-done.22 = f32[2304,144]{1,0:T(8,128)S(1)} copy-done((f32[2304,144]{1,0:T(8,128)S(1)}, f32[2304,144]{1,0:T(8,128)}, u32[]{:S(2)}) %copy-start.22) | copy-done | bytes 1327128
  35.5 1.9 %shard_map.152 = (bf16[256,128]{1,0:T(8,128)(2,1)S(1)}, bf16[256,128]{1,0:T(8,128)(2,1)S(1)}) custom-call(s32[2]{0:T(128)S(1)} %pad_add_fusion.refs_0_, f32[2304,144]{1,0:T(8,128)S(1)} %copy-done.22, bf16[2,138,276]{2,1,0:T(8,128)(2,1)S(1)} %copy-done.19), custom_call_target="tpu_custom_call" | custom-call | flops 2500000000 | tf_op jit(solution)/shard_map/pallas_call | solution.py:60
  37.4 0.7 collective-permute-start.9
  38.1 0.9 collective-permute-done.9.refs_2_
  39.0 3.5 %all-to-all-done.refs_0_ = bf16[4,256,256]{2,1,0:T(8,128)(2,1)S(1)} async-done(((bf16[4,256,256]{2,1,0:T(8,128)(2,1)}), bf16[4,256,256]{2,1,0:T(8,128)(2,1)S(1)}, u32[]{:S(2)}, u32[]{:S(2)}) %all-to-all-start) | async-done | bytes 524320 | tf_op jit(solution)/shard_map/all_to_all | solution.py:342
  42.6 0.8 shard_map.153
  43.3 9.3 %all-to-all-start.1 = ((bf16[16,16,384]{2,1,0:T(8,128)(2,1)}), bf16[16,16,384]{2,1,0:T(8,128)(2,1)S(1)}, u32[]{:S(2)}, u32[]{:S(2)}) async-start(bf16[16,16,384]{2,1,0:T(8,128)(2,1)} %shard_map.153), calls=%async_computation.1 | async-start | bytes 393216 | tf_op jit(solution)/shard_map/all_to_all | solution.py:352
  52.6 0.9 copy-done.8
  53.6 0.9 copy-done.10
  54.5 1.4 %shard_map.149 = (bf16[2,216,512]{2,1,0:T(8,128)(2,1)S(1)}, bf16[2,216,512]{2,1,0:T(8,128)(2,1)S(1)}, bf16[2,72,512]{2,1,0:T(8,128)(2,1)}, bf16[2,72,512]{2,1,0:T(8,128)(2,1)S(1)}, f32[8,128]{1,0:T(8,128)S(1)}) custom-call(bf16[576,768]{1,0:T(8,128)(2,1)S(1)} %shard_map.148.refs_0_.refs_2_, bf16[576,768]{1,0:T(8,128)(2,1)S(1)} %collective-permute-done.4.refs_1_, ...), custom_call_target="tpu_custom_call" | custom-call | flops 30000001024 | tf_op jit(solution)/shard_map/pallas_call | solution.py:60
  55.9 0.7 copy-done.12
  56.6 0.8 copy-done.23
  57.4 5.9 %all-to-all-done.1.refs_0_ = bf16[16,16,384]{2,1,0:T(8,128)(2,1)S(1)} async-done(((bf16[16,16,384]{2,1,0:T(8,128)(2,1)}), bf16[16,16,384]{2,1,0:T(8,128)(2,1)S(1)}, u32[]{:S(2)}, u32[]{:S(2)}) %all-to-all-start.1) | async-done | bytes 196640 | tf_op jit(solution)/shard_map/all_to_all | solution.py:352
  63.3 0.7 shard_map.154
  64.0 3.5 %all-to-all-start.2 = ((bf16[16,16,384]{2,1,0:T(8,128)(2,1)}), bf16[16,16,384]{2,1,0:T(8,128)(2,1)S(1)}, u32[]{:S(2)}, u32[]{:S(2)}) async-start(bf16[16,16,384]{2,1,0:T(8,128)(2,1)} %shard_map.154), calls=%async_computation.2 | async-start | bytes 393216 | tf_op jit(solution)/shard_map/all_to_all | solution.py:352
  67.5 4.4 %collective-permute-start.5 = (bf16[2,216,512]{2,1,0:T(8,128)(2,1)S(1)}, bf16[2,216,512]{2,1,0:T(8,128)(2,1)S(1)}, u32[]{:S(2)}, u32[]{:S(2)}) collective-permute-start(bf16[2,216,512]{2,1,0:T(8,128)(2,1)S(1)} %get-tuple-element.45), channel_id=1, source_target_pairs={{0,16},{2,18},{4,20},{6,22},{8,24},{10,26},{12,28},{14,30},{16,32}... | collective-permute-start | bytes 1327112 | tf_op jit(solution)/shard_map/ppermute | solution.py:330
  72.0 2.7 %collective-permute-start.6 = (bf16[2,72,512]{2,1,0:T(8,128)(2,1)}, bf16[2,72,512]{2,1,0:T(8,128)(2,1)}, u32[]{:S(2)}, u32[]{:S(2)}) collective-permute-start(bf16[2,72,512]{2,1,0:T(8,128)(2,1)} %get-tuple-element.46), channel_id=1, source_target_pairs={{0,2},{2,4},{4,6},{6,8},{8,10},{10,12},{12,14},{14,0},{16,18},{18,... | collective-permute-start | bytes 442376 | tf_op jit(solution)/shard_map/ppermute | solution.py:330
  74.7 0.4 collective-permute-start.7
  75.0 3.1 %all-to-all-done.2.refs_0_ = bf16[16,16,384]{2,1,0:T(8,128)(2,1)S(1)} async-done(((bf16[16,16,384]{2,1,0:T(8,128)(2,1)}), bf16[16,16,384]{2,1,0:T(8,128)(2,1)S(1)}, u32[]{:S(2)}, u32[]{:S(2)}) %all-to-all-start.2) | async-done | bytes 196640 | tf_op jit(solution)/shard_map/all_to_all | solution.py:352
  78.1 0.8 shard_map.155
  78.9 0.6 copy-done.14
  79.6 3.5 %all-to-all-start.3 = ((bf16[4,256,256]{2,1,0:T(8,128)(2,1)}), bf16[4,256,256]{2,1,0:T(8,128)(2,1)S(1)}, u32[]{:S(2)}, u32[]{:S(2)}) async-start(bf16[4,256,256]{2,1,0:T(8,128)(2,1)} %get-tuple-element.56), calls=%async_computation.3 | async-start | bytes 1048576 | tf_op jit(solution)/shard_map/all_to_all | solution.py:342
  83.1 5.4 %collective-permute-start.10 = (bf16[256,128]{1,0:T(8,128)(2,1)}, bf16[256,128]{1,0:T(8,128)(2,1)S(1)}, u32[]{:S(2)}, u32[]{:S(2)}) collective-permute-start(bf16[256,128]{1,0:T(8,128)(2,1)} %copy-done.14), channel_id=1, source_target_pairs={{0,16},{2,18},{4,20},{6,22},{8,24},{10,26},{12,28},{14,30},{16,0},... | collective-permute-start | bytes 196616 | tf_op jit(solution)/shard_map/ppermute | solution.py:336
  88.4 1.0 copy-done.24
  89.5 3.1 %shard_map.150 = (bf16[12,12,4,512]{3,2,1,0:T(4,128)(2,1)}, bf16[12,12,4,512]{3,2,1,0:T(4,128)(2,1)}, f32[8,128]{1,0:T(8,128)S(1)}) custom-call(bf16[12,12,4,512]{3,2,1,0:T(4,128)(2,1)S(1)} %copy-done.3, bf16[12,12,4,512]{3,2,1,0:T(4,128)(2,1)S(1)} %copy-done.6, f32[1,512]{1,0:T(1,128)S(1)} %bitcast.10, bf16[2,216,512]{2,1,0:T(8,128)(2,1)S(1)} %copy-done.24, ...), custom_call_target="tpu_custom_call" | custom-call | flops 30000001024 | tf_op jit(solution)/shard_map/pallas_call | solution.py:60
  92.6 1.5 %shard_map.156 = (f32[2,2,4,3312]{3,2,1,0:T(4,128)}, f32[8,128]{1,0:T(8,128)S(1)}) custom-call(s32[2]{0:T(128)S(1)} %pad_add_fusion.refs_0_, bf16[256,128]{1,0:T(8,128)(2,1)S(1)} %copy-done.15, bf16[256,128]{1,0:T(8,128)(2,1)S(1)} %collective-permute-done.10.refs_2_, f32[8,128]{1,0:T(8,128)S(1)} %get-tuple-element.58.refs_3_), custom_call_target="tpu_custom_call" | custom-call | flops 1000000000 | tf_op jit(solution)/shard_map/pallas_call | solution.py:60
  94.1 2.3 %collective-permute-start.13 = (bf16[1024,256]{1,0:T(8,128)(2,1)S(1)}, bf16[1024,256]{1,0:T(8,128)(2,1)S(1)}, u32[]{:S(2)}, u32[]{:S(2)}) collective-permute-start(bf16[1024,256]{1,0:T(8,128)(2,1)S(1)} %bitcast.6), channel_id=1, source_target_pairs={{0,16},{2,18},{4,20},{6,22},{8,24},{10,26},{12,28},{14,30},{16,0},... | collective-permute-start | bytes 1572872 | tf_op jit(solution)/shard_map/ppermute | solution.py:336
  96.4 1.2 %shard_map.157 = f32[8,512]{1,0:T(8,128)S(1)} custom-call(s32[2]{0:T(128)S(1)} %pad_add_fusion.refs_0_, bf16[1024,256]{1,0:T(8,128)(2,1)S(1)} %bitcast.7, bf16[3,512,256]{2,1,0:T(8,128)(2,1)S(1)} %copy-done, f32[8,128]{1,0:T(8,128)S(1)} %get-tuple-element.59.refs_3_), custom_call_target="tpu_custom_call" | custom-call | flops 30000001024 | tf_op jit(solution)/shard_map/pallas_call | solution.py:60
  97.6 0.0 collective-permute-start.11
  97.6 1.2 %collective-permute-done.11 = f32[8,512]{1,0:T(8,128)S(1)} collective-permute-done((f32[8,512]{1,0:T(8,128)S(1)}, f32[8,512]{1,0:T(8,128)S(1)}, u32[]{:S(2)}, u32[]{:S(2)}) %collective-permute-start.11) | collective-permute-done | bytes 16416 | tf_op jit(solution)/shard_map/ppermute | solution.py:336
  98.8 1.9 %shard_map.158 = (f32[8,128]{1,0:T(8,128)S(1)}, f32[3,512,256]{2,1,0:T(8,128)}, f32[256,512]{1,0:T(8,128)}) custom-call(s32[2]{0:T(128)S(1)} %pad_add_fusion.refs_0_, bf16[1024,256]{1,0:T(8,128)(2,1)S(1)} %bitcast.8, bf16[1024,256]{1,0:T(8,128)(2,1)S(1)} %collective-permute-done.13.refs_2_), custom_call_target="tpu_custom_call" | custom-call | flops 2000000000 | tf_op jit(solution)/shard_map/pallas_call | solution.py:60
  100.7 0.6 collective-permute-done.12.refs_1_
  101.4 0.6 shard_map.159
  (55 shorter events, 0.1 us)
Async XLA Ops:
  0.6 1.1 %copy-start.1 = (bf16[12,12,4,512]{3,2,1,0:T(4,128)(2,1)S(1)}, bf16[12,12,4,512]{3,2,1,0:T(4,128)(2,1)}, u32[]{:S(2)}) copy-start(bf16[12,12,4,512]{3,2,1,0:T(4,128)(2,1)} %refs_0_.3) | copy-start | bytes 1769476
  1.7 1.1 %copy-start.4 = (bf16[12,12,4,512]{3,2,1,0:T(4,128)(2,1)S(1)}, bf16[12,12,4,512]{3,2,1,0:T(4,128)(2,1)}, u32[]{:S(2)}) copy-start(bf16[12,12,4,512]{3,2,1,0:T(4,128)(2,1)} %refs_1_.7) | copy-start | bytes 1769476
  2.8 12.6 %copy-start.7 = (bf16[256,512]{1,0:T(8,128)(2,1)S(1)}, bf16[256,512]{1,0:T(8,128)(2,1)}, u32[]{:S(2)}) copy-start(bf16[256,512]{1,0:T(8,128)(2,1)} %refs_2_.6) | copy-start | bytes 786436
  2.8 12.6 %copy-start.11 = (f32[2,2,4,3312]{3,2,1,0:T(4,128)S(1)}, f32[2,2,4,3312]{3,2,1,0:T(4,128)}, u32[]{:S(2)}) copy-start(f32[2,2,4,3312]{3,2,1,0:T(4,128)} %refs_1_.5) | copy-start | bytes 635908
  2.8 12.6 %copy-start.20 = (bf16[276,276]{1,0:T(8,128)(2,1)S(1)}, bf16[276,276]{1,0:T(8,128)(2,1)}, u32[]{:S(2)}) copy-start(bf16[276,276]{1,0:T(8,128)(2,1)} %constant.36.clone.refs_2_) | copy-start | bytes 457060
  2.9 16.6 %collective-permute-start = (bf16[2,216,512]{2,1,0:T(8,128)(2,1)S(1)}, bf16[2,216,512]{2,1,0:T(8,128)(2,1)S(1)}, u32[]{:S(2)}, u32[]{:S(2)}) collective-permute-start(bf16[2,216,512]{2,1,0:T(8,128)(2,1)S(1)} %get-tuple-element.35), channel_id=1, source_target_pairs={{0,240},{2,242},{4,244},{6,246},{8,248},{10,250},{12,252},{14,254}... | collective-permute-start | bytes 1327112 | tf_op jit(solution)/shard_map/ppermute | solution.py:330
  6.1 13.3 %collective-permute-start.1 = (bf16[2,72,512]{2,1,0:T(8,128)(2,1)S(1)}, bf16[2,72,512]{2,1,0:T(8,128)(2,1)S(1)}, u32[]{:S(2)}, u32[]{:S(2)}) collective-permute-start(bf16[2,72,512]{2,1,0:T(8,128)(2,1)S(1)} %get-tuple-element.36), channel_id=1, source_target_pairs={{0,14},{2,0},{4,2},{6,4},{8,6},{10,8},{12,10},{14,12},{16,30},{18,... | collective-permute-start | bytes 442376 | tf_op jit(solution)/shard_map/ppermute | solution.py:330
  9.6 9.9 %collective-permute-start.2 = (bf16[2,72,512]{2,1,0:T(8,128)(2,1)S(1)}, bf16[2,72,512]{2,1,0:T(8,128)(2,1)S(1)}, u32[]{:S(2)}, u32[]{:S(2)}) collective-permute-start(bf16[2,72,512]{2,1,0:T(8,128)(2,1)S(1)} %get-tuple-element.37), channel_id=1, source_target_pairs={{0,254},{2,240},{4,242},{6,244},{8,246},{10,248},{12,250},{14,252}... | collective-permute-start | bytes 442376 | tf_op jit(solution)/shard_map/ppermute | solution.py:330
  15.3 4.1 %copy-start = (bf16[3,512,256]{2,1,0:T(8,128)(2,1)S(1)}, bf16[3,512,256]{2,1,0:T(8,128)(2,1)}, u32[]{:S(2)}) copy-start(bf16[3,512,256]{2,1,0:T(8,128)(2,1)} %refs_2_.7) | copy-start | bytes 2359300
  15.3 4.1 %copy-start.2 = (bf16[12,12,4,512]{3,2,1,0:T(4,128)(2,1)S(1)}, bf16[12,12,4,512]{3,2,1,0:T(4,128)(2,1)}, u32[]{:S(2)}) copy-start(bf16[12,12,4,512]{3,2,1,0:T(4,128)(2,1)} %refs_0_.3) | copy-start | bytes 1769476
  15.4 4.1 %copy-start.5 = (bf16[12,12,4,512]{3,2,1,0:T(4,128)(2,1)S(1)}, bf16[12,12,4,512]{3,2,1,0:T(4,128)(2,1)}, u32[]{:S(2)}) copy-start(bf16[12,12,4,512]{3,2,1,0:T(4,128)(2,1)} %refs_1_.7) | copy-start | bytes 1769476
  15.4 4.1 %copy-start.16 = (f32[512]{0:T(512)S(1)}, f32[512]{0:T(512)}, u32[]{:S(2)}) copy-start(f32[512]{0:T(512)} %param.12) | copy-start | bytes 6148
  15.4 4.1 %copy-start.18 = (bf16[576,576]{1,0:T(8,128)(2,1)S(1)}, bf16[576,576]{1,0:T(8,128)(2,1)}, u32[]{:S(2)}) copy-start(bf16[576,576]{1,0:T(8,128)(2,1)} %constant.34.clone.refs_6_) | copy-start | bytes 1990660
  18.1 9.4 %collective-permute-start.3 = (bf16[256,512]{1,0:T(8,128)(2,1)S(1)}, bf16[256,512]{1,0:T(8,128)(2,1)S(1)}, u32[]{:S(2)}, u32[]{:S(2)}) collective-permute-start(bf16[256,512]{1,0:T(8,128)(2,1)S(1)} %get-tuple-element.43), channel_id=1, source_target_pairs={{0,1},{1,0},{2,3},{3,2},{4,5},{5,4},{6,7},{7,6},{8,9},{9,8},{10,11... | collective-permute-start | bytes 786440 | tf_op jit(solution)/shard_map/ppermute | solution.py:356
  19.5 8.0 %copy-start.17 = (bf16[576,576]{1,0:T(8,128)(2,1)S(1)}, bf16[576,576]{1,0:T(8,128)(2,1)}, u32[]{:S(2)}) copy-start(bf16[576,576]{1,0:T(8,128)(2,1)} %constant.35.clone.refs_5_) | copy-start | bytes 1990660
  25.6 3.3 %copy-start.21 = (f32[2304,144]{1,0:T(8,128)}, f32[2304,144]{1,0:T(8,128)S(1)}, u32[]{:S(2)}) copy-start(f32[2304,144]{1,0:T(8,128)S(1)} %get-tuple-element.52.refs_1_) | copy-start | bytes 3981316
  25.6 3.7 %collective-permute-start.8 = (bf16[1024,256]{1,0:T(8,128)(2,1)S(1)}, bf16[1024,256]{1,0:T(8,128)(2,1)S(1)}, u32[]{:S(2)}, u32[]{:S(2)}) collective-permute-start(bf16[1024,256]{1,0:T(8,128)(2,1)S(1)} %get-tuple-element.51), channel_id=1, source_target_pairs={{0,16},{2,18},{4,20},{6,22},{8,24},{10,26},{12,28},{14,30},{16,0},... | collective-permute-start | bytes 1572872 | tf_op jit(solution)/shard_map/ppermute | solution.py:336
  27.5 1.4 %copy-start.9 = (bf16[256,512]{1,0:T(8,128)(2,1)}, bf16[256,512]{1,0:T(8,128)(2,1)S(1)}, u32[]{:S(2)}) copy-start(bf16[256,512]{1,0:T(8,128)(2,1)S(1)} %collective-permute-done.3.refs_6_.refs_3_) | copy-start | bytes 786436
  28.9 5.0 %copy-start.19 = (bf16[2,138,276]{2,1,0:T(8,128)(2,1)S(1)}, bf16[2,138,276]{2,1,0:T(8,128)(2,1)}, u32[]{:S(2)}) copy-start(bf16[2,138,276]{2,1,0:T(8,128)(2,1)} %constant.37.clone.refs_2_) | copy-start | bytes 457060
  28.9 23.7 %collective-permute-start.4 = (bf16[576,768]{1,0:T(8,128)(2,1)S(1)}, bf16[576,768]{1,0:T(8,128)(2,1)S(1)}, u32[]{:S(2)}, u32[]{:S(2)}) collective-permute-start(bf16[576,768]{1,0:T(8,128)(2,1)S(1)} %shard_map.148.refs_0_.refs_2_), channel_id=1, source_target_pairs={{0,1},{1,0},{2,3},{3,2},{4,5},{5,4},{6,7},{7,6},{8,9},{9,8},{10,11... | collective-permute-start | bytes 2654216 | tf_op jit(solution)/shard_map/ppermute | solution.py:356
  30.2 12.4 %all-to-all-start = ((bf16[4,256,256]{2,1,0:T(8,128)(2,1)}), bf16[4,256,256]{2,1,0:T(8,128)(2,1)S(1)}, u32[]{:S(2)}, u32[]{:S(2)}) async-start(bf16[4,256,256]{2,1,0:T(8,128)(2,1)} %bitcast.3), calls=%async_computation | async-start | bytes 1048576 | tf_op jit(solution)/shard_map/all_to_all | solution.py:342
  33.9 1.7 %copy-start.22 = (f32[2304,144]{1,0:T(8,128)S(1)}, f32[2304,144]{1,0:T(8,128)}, u32[]{:S(2)}) copy-start(f32[2304,144]{1,0:T(8,128)} %copy-done.21) | copy-start | bytes 3981316
  37.4 1.6 %collective-permute-start.9 = (bf16[256,128]{1,0:T(8,128)(2,1)S(1)}, bf16[256,128]{1,0:T(8,128)(2,1)S(1)}, u32[]{:S(2)}, u32[]{:S(2)}) collective-permute-start(bf16[256,128]{1,0:T(8,128)(2,1)S(1)} %get-tuple-element.54), channel_id=1, source_target_pairs={{0,16},{2,18},{4,20},{6,22},{8,24},{10,26},{12,28},{14,30},{16,0},... | collective-permute-start | bytes 196616 | tf_op jit(solution)/shard_map/ppermute | solution.py:336
  43.3 19.9 %all-to-all-start.1 = ((bf16[16,16,384]{2,1,0:T(8,128)(2,1)}), bf16[16,16,384]{2,1,0:T(8,128)(2,1)S(1)}, u32[]{:S(2)}, u32[]{:S(2)}) async-start(bf16[16,16,384]{2,1,0:T(8,128)(2,1)} %shard_map.153), calls=%async_computation.1 | async-start | bytes 393216 | tf_op jit(solution)/shard_map/all_to_all | solution.py:352
  52.6 1.0 copy-start.8
  53.6 0.9 copy-start.10
  55.9 0.7 copy-start.12
  56.6 0.8 copy-start.23
  63.3 11.4 %copy-start.13 = (bf16[2,72,512]{2,1,0:T(8,128)(2,1)S(1)}, bf16[2,72,512]{2,1,0:T(8,128)(2,1)}, u32[]{:S(2)}) copy-start(bf16[2,72,512]{2,1,0:T(8,128)(2,1)} %copy-done.12) | copy-start | bytes 442372
  64.0 14.1 %all-to-all-start.2 = ((bf16[16,16,384]{2,1,0:T(8,128)(2,1)}), bf16[16,16,384]{2,1,0:T(8,128)(2,1)S(1)}, u32[]{:S(2)}, u32[]{:S(2)}) async-start(bf16[16,16,384]{2,1,0:T(8,128)(2,1)} %shard_map.154), calls=%async_computation.2 | async-start | bytes 393216 | tf_op jit(solution)/shard_map/all_to_all | solution.py:352
  67.5 20.9 %collective-permute-start.5 = (bf16[2,216,512]{2,1,0:T(8,128)(2,1)S(1)}, bf16[2,216,512]{2,1,0:T(8,128)(2,1)S(1)}, u32[]{:S(2)}, u32[]{:S(2)}) collective-permute-start(bf16[2,216,512]{2,1,0:T(8,128)(2,1)S(1)} %get-tuple-element.45), channel_id=1, source_target_pairs={{0,16},{2,18},{4,20},{6,22},{8,24},{10,26},{12,28},{14,30},{16,32}... | collective-permute-start | bytes 1327112 | tf_op jit(solution)/shard_map/ppermute | solution.py:330
  72.0 16.4 %collective-permute-start.6 = (bf16[2,72,512]{2,1,0:T(8,128)(2,1)}, bf16[2,72,512]{2,1,0:T(8,128)(2,1)}, u32[]{:S(2)}, u32[]{:S(2)}) collective-permute-start(bf16[2,72,512]{2,1,0:T(8,128)(2,1)} %get-tuple-element.46), channel_id=1, source_target_pairs={{0,2},{2,4},{4,6},{6,8},{8,10},{10,12},{12,14},{14,0},{16,18},{18,... | collective-permute-start | bytes 442376 | tf_op jit(solution)/shard_map/ppermute | solution.py:330
  74.7 13.7 %copy-start.3 = (bf16[12,12,4,512]{3,2,1,0:T(4,128)(2,1)S(1)}, bf16[12,12,4,512]{3,2,1,0:T(4,128)(2,1)}, u32[]{:S(2)}) copy-start(bf16[12,12,4,512]{3,2,1,0:T(4,128)(2,1)} %refs_0_.3) | copy-start | bytes 1769476
  74.7 13.8 %copy-start.6 = (bf16[12,12,4,512]{3,2,1,0:T(4,128)(2,1)S(1)}, bf16[12,12,4,512]{3,2,1,0:T(4,128)(2,1)}, u32[]{:S(2)}) copy-start(bf16[12,12,4,512]{3,2,1,0:T(4,128)(2,1)} %refs_1_.7) | copy-start | bytes 1769476
  74.7 13.7 %collective-permute-start.7 = (bf16[2,72,512]{2,1,0:T(8,128)(2,1)S(1)}, bf16[2,72,512]{2,1,0:T(8,128)(2,1)}, u32[]{:S(2)}, u32[]{:S(2)}) collective-permute-start(bf16[2,72,512]{2,1,0:T(8,128)(2,1)S(1)} %copy-done.13), channel_id=1, source_target_pairs={{0,18},{2,20},{4,22},{6,24},{8,26},{10,28},{12,30},{14,16},{16,34}... | collective-permute-start | bytes 442376 | tf_op jit(solution)/shard_map/ppermute | solution.py:330
  78.9 0.6 copy-start.14
  79.6 14.5 %all-to-all-start.3 = ((bf16[4,256,256]{2,1,0:T(8,128)(2,1)}), bf16[4,256,256]{2,1,0:T(8,128)(2,1)S(1)}, u32[]{:S(2)}, u32[]{:S(2)}) async-start(bf16[4,256,256]{2,1,0:T(8,128)(2,1)} %get-tuple-element.56), calls=%async_computation.3 | async-start | bytes 1048576 | tf_op jit(solution)/shard_map/all_to_all | solution.py:342
  83.1 9.5 %collective-permute-start.10 = (bf16[256,128]{1,0:T(8,128)(2,1)}, bf16[256,128]{1,0:T(8,128)(2,1)S(1)}, u32[]{:S(2)}, u32[]{:S(2)}) collective-permute-start(bf16[256,128]{1,0:T(8,128)(2,1)} %copy-done.14), channel_id=1, source_target_pairs={{0,16},{2,18},{4,20},{6,22},{8,24},{10,26},{12,28},{14,30},{16,0},... | collective-permute-start | bytes 196616 | tf_op jit(solution)/shard_map/ppermute | solution.py:336
  88.4 1.0 copy-start.24
  89.5 3.1 %copy-start.15 = (bf16[256,128]{1,0:T(8,128)(2,1)S(1)}, bf16[256,128]{1,0:T(8,128)(2,1)}, u32[]{:S(2)}) copy-start(bf16[256,128]{1,0:T(8,128)(2,1)} %copy-done.14) | copy-start | bytes 196612
  94.1 4.7 %collective-permute-start.13 = (bf16[1024,256]{1,0:T(8,128)(2,1)S(1)}, bf16[1024,256]{1,0:T(8,128)(2,1)S(1)}, u32[]{:S(2)}, u32[]{:S(2)}) collective-permute-start(bf16[1024,256]{1,0:T(8,128)(2,1)S(1)} %bitcast.6), channel_id=1, source_target_pairs={{0,16},{2,18},{4,20},{6,22},{8,24},{10,26},{12,28},{14,30},{16,0},... | collective-permute-start | bytes 1572872 | tf_op jit(solution)/shard_map/ppermute | solution.py:336
  97.6 1.2 %collective-permute-start.11 = (f32[8,512]{1,0:T(8,128)S(1)}, f32[8,512]{1,0:T(8,128)S(1)}, u32[]{:S(2)}, u32[]{:S(2)}) collective-permute-start(f32[8,512]{1,0:T(8,128)S(1)} %shard_map.157), channel_id=1, source_target_pairs={{0,16},{2,18},{4,20},{6,22},{8,24},{10,26},{12,28},{14,30},{16,0},... | collective-permute-start | bytes 49160 | tf_op jit(solution)/shard_map/ppermute | solution.py:336
  98.8 2.6 %collective-permute-start.12 = (f32[8,512]{1,0:T(8,128)S(1)}, f32[8,512]{1,0:T(8,128)S(1)}, u32[]{:S(2)}, u32[]{:S(2)}) collective-permute-start(f32[8,512]{1,0:T(8,128)S(1)} %add.8.refs_0_), channel_id=1, source_target_pairs={{0,1},{1,0},{2,3},{3,2},{4,5},{5,4},{6,7},{7,6},{8,9},{9,8},{10,11... | collective-permute-start | bytes 49160 | tf_op jit(solution)/shard_map/ppermute | solution.py:356

commit v5 on v4

--- a/solution.py
+++ b/solution.py
@@ -84,8 +84,7 @@
             ref[j] = grid[lon, lat].reshape(ref.shape[1:])
 
 
-def bias_kernel(info, table, order, w_out, bias, w_copy, raw, entries, low_u, high_u):
-    w_copy[...] = w_out[...]
+def bias_kernel(info, table, order, bias, raw, entries, low_u, high_u):
     flat = table[...].reshape(16, 3312)
     for s_t in range(2):
         for s_u in range(2):
@@ -188,26 +187,25 @@
         total = total + parts[j].astype(F32)
     total = total.astype(BF)
     both = (b_keep[...].astype(F32) + b_recv[...].astype(F32)).astype(BF)
-    for j in range(16):
-        rows = slice(j * 16, (j + 1) * 16)
+    for j in range(8):
+        rows = slice(j * 32, (j + 1) * 32)
         message[j, :, 0:256] = total[rows]
         message[j, :, 256:384] = both[rows]
 
 
-def zx_sum_kernel(parts, copies):
-    total = jnp.zeros((16, 256), F32)
-    biases = []
-    for x in range(2):
-        bias = jnp.zeros((16, 128), F32)
-        for z in range(8):
-            total = total + parts[z * 2 + x, :, 0:256].astype(F32)
-            bias = bias + parts[z * 2 + x, :, 256:384].astype(F32)
-        biases.append(bias.astype(BF))
-    total = total.astype(BF)
-    for z in range(8):
-        for x in range(2):
-            copies[z * 2 + x, :, 0:256] = total
-            copies[z * 2 + x, :, 256:384] = biases[x]
+def z_sum_kernel(parts, mine, bias):
+    total = parts[0].astype(F32)
+    for j in range(1, 8):
+        total = total + parts[j].astype(F32)
+    mine[...] = total[:, 0:256].astype(BF)
+    bias[...] = total[:, 256:384].astype(BF)
+
+
+def x_sum_kernel(mine, recv, bias, copies):
+    total = (mine[...].astype(F32) + recv[...].astype(F32)).astype(BF)
+    for j in range(8):
+        copies[j, :, 0:256] = total
+        copies[j, :, 256:384] = bias[...]
 
 
 def pair_kernel(terms, others, w_out, w_other, o_own, o_lon, o_lat, o_cor, token):
@@ -222,8 +220,8 @@
 
 
 def spread_kernel(parts, copies, b_half):
-    for j in range(16):
-        rows = slice(j * 16, (j + 1) * 16)
+    for j in range(8):
+        rows = slice(j * 32, (j + 1) * 32)
         for k in range(4):
             copies[k, rows, :] = parts[j, :, 0:256]
         b_half[rows, :] = parts[j, :, 256:384]
@@ -237,8 +235,9 @@
     out[...] = lax.dot_general(ones, total, NT, precision=lax.Precision.HIGHEST, preferred_element_type=F32)
 
 
-def gain_sum_kernel(mine, other, gain, out):
-    out[...] = (mine[0:1, :] + other[0:1, :]) / gain[...]
+def gain_sum_kernel(mine, other, mine_tp, other_tp, gain, out):
+    total = (mine[0:1, :] + other[0:1, :]) + (mine_tp[0:1, :] + other_tp[0:1, :])
+    out[...] = total / gain[...]
 
 
 def bias_out_kernel(info, mine, other, grad_bias, token, rows, flat):
@@ -342,18 +341,19 @@
     return lax.all_to_all(value, "lat", 0, 0, axis_index_groups=groups)
 
 
-def across_zx(value):
-    n_lon, n_lat = lax.axis_size("lon"), lax.axis_size("lat")
-    groups = [
-        [i * n_lat + j + x for i in range(core, n_lon, 2) for x in range(2)]
-        for core in range(2)
-        for j in range(0, n_lat, 2)
-    ]
-    return lax.all_to_all(value, ("lon", "lat"), 0, 0, axis_index_groups=groups)
+def across_z(value):
+    n_lon = lax.axis_size("lon")
+    groups = [list(range(core, n_lon, 2)) for core in range(2)]
+    return lax.all_to_all(value, "lon", 0, 0, axis_index_groups=groups)
 
 
 def other_group(value):
     return lax.ppermute(value, "tp", [(0, 1), (1, 0)])
+
+
+def other_group_and_core(value):
+    n_lon = lax.axis_size("lon")
+    return lax.ppermute(value, ("lon", "tp"), [(i * 2 + j, (i ^ 1) * 2 + (j ^ 1)) for i in range(n_lon) for j in range(2)])
 
 
 def on_device(latent, cotangent, ln_gain, w_qkv, w_out, bias_table):
@@ -371,14 +371,14 @@
     s_lon, s_lat, s_cor = call(halo_kernel, halos, [latent, cotangent], smem=0)
     in_lon, in_lat, in_cor = moved(s_lon, -1, 0), moved(s_lat, 0, -1), moved(s_cor, -1, -1)
 
-    bias, w_copy = call(
+    (bias,) = call(
         bias_kernel,
-        [((16 * WTOK, WTOK), F32), (w_out.shape, BF)],
-        [info, bias_table, order, w_out],
+        [((16 * WTOK, WTOK), F32)],
+        [info, bias_table, order],
         [pltpu.VMEM((192, 276), F32)] * 2 + [pltpu.VMEM((192, 128), F32)] * 2,
         us=2,
     )
-    w_other = other_group(w_copy)
+    w_other = other_group(w_out)
 
     keep, send, ds, att, gq, gk, gv = call(
         main_kernel,
@@ -389,7 +389,7 @@
         mib=32,
     )
     recv = swapped(send, 1, 0)
-    (terms,) = call(terms_kernel, [((576, 768), BF)], [att, gq, gk, gv, w_qkv, back], smem=0, after=[w_other], us=2)
+    (terms,) = call(terms_kernel, [((576, 768), BF)], [att, gq, gk, gv, w_qkv, back], smem=0, us=2)
     others = other_group(terms)
     own, s_lon, s_lat, s_cor, paired = call(
         pair_kernel, [part(216)] + halos + [TOKEN], [terms, others, w_out, w_other], smem=0, us=30
@@ -406,9 +406,12 @@
         us=2.5,
     )
     b_recv = swapped(b_send, 1, 0)
-    (message,) = call(y_sum_kernel, [((16, 16, 384), BF)], [parts, b_keep, b_recv], smem=0, us=1)
+    (message,) = call(y_sum_kernel, [((8, 32, 384), BF)], [parts, b_keep, b_recv], smem=0, us=1)
+    x_mine, b_sum = call(
+        z_sum_kernel, [((32, 256), BF), ((32, 128), BF)], [across_z(message)], smem=0, after=[paired], us=1
+    )
+    (copies,) = call(x_sum_kernel, [((8, 32, 384), BF)], [x_mine, swapped(x_mine, 0, 1), b_sum], smem=0, us=1)
     r_lon, r_lat, r_cor = moved(s_lon, 1, 0), moved(s_lat, 0, 1), moved(s_cor, 1, 1)
-    (copies,) = call(zx_sum_kernel, [((16, 16, 384), BF)], [across_zx(message)], smem=0, after=[paired], us=1)
 
     output, grad_latent, placed = call(
         final_kernel,
@@ -421,7 +424,7 @@
     copies, b_half = call(
         spread_kernel,
         [((4, 256, 256), BF), ((256, 128), BF)],
-        [across_zx(copies)],
+        [across_z(copies)],
         smem=0,
         us=1,
     )
@@ -438,8 +441,7 @@
     (g_mine,) = call(
         gain_kernel, [((8, 512), F32)], [info, mine, w_qkv], after=[done], us=30
     )
-    g_other = swapped(g_mine, 1, 0)
-    g_pair = g_mine + g_other
+    g_parts = [g_mine, swapped(g_mine, 1, 0), other_group(g_mine), other_group_and_core(g_mine)]
     done, grad_wqkv, grad_wout = call(
         weights_kernel,
         [TOKEN],
@@ -449,7 +451,7 @@
         us=2,
     )
     (grad_gain,) = call(
-        gain_sum_kernel, [((1, 512), F32)], [g_pair, other_group(g_pair), gain], smem=0, after=[done]
+        gain_sum_kernel, [((1, 512), F32)], [*g_parts, gain], smem=0, after=[done]
     )
     grad_gain = grad_gain.reshape(512)
     return output, grad_latent, grad_gain, grad_wqkv, grad_wout, grad_bias

time: 103 us -> 103 us (level)
    ppermute x3, waiting for transfers between devices: 0.63 us -> 7.7 us  [other_group(): return lax.ppermute(value, 'tp', [(0, 1), (1, 0)])]
    all_to_all x2, waiting for transfers between devices: 8.99 us -> 2.79 us  [across_z(): return lax.all_to_all(value, 'lon', 0, 0, axis_index_groups=groups)]
    all_to_all x2, starting transfers between devices: 12.8 us -> 9.12 us  [across_z(): return lax.all_to_all(value, 'lon', 0, 0, axis_index_groups=groups)]
    all_to_all x2, waiting for transfers between devices: 3.54 us -> 1.75 us  [across_y(): return lax.all_to_all(value, 'lat', 0, 0, axis_index_groups=groups)]
    ppermute x0 -> x1, starting transfers between devices: none -> 1.78 us  [other_group_and_core(): lax.ppermute(value, ('lon', 'tp'), [(i * 2 + j, (i ^ 1) * 2 + (j ^ 1)) fo...]
    ppermute x6, starting transfers between devices: 19.9 us -> 21.1 us  [moved(): return lax.ppermute(value, ('lon', 'lat'), pairs)]
    pallas_call x15 -> x16, Pallas kernels: 25.1 us -> 26.1 us  [call(): pl.pallas_call(kernel, out_shape=[jax.ShapeDtypeStruct(s, t) for s, t in...]
    ppermute x5 -> x6, starting transfers between devices: 10.2 us -> 9.38 us  [swapped(): return lax.ppermute(value, ('lon', 'lat'), pairs)]
  transfers between devices with their start and end apart: 18 -> 20, of which waited for: 6 -> 6; matrix products, arithmetic and copies ran while one was open for 0% -> 0% of each run, Pallas kernels for 23% -> 19%
where the time goes in v5:
time: 103 us; the launch traced here: 102 us
  starting transfers between devices  50.9 us (49%)
  Pallas kernels  26.1 us (25%)
  waiting for transfers between devices  14.9 us (14%)
  local copies, waits for them, and re-layouts  8.8 us (9%)
    pallas_call x16, Pallas kernels, call(): pl.pallas_call(kernel, out_shape=[jax.ShapeDtypeStruct(s, t) for s, t in...  26.1 us
    ppermute x6, starting transfers between devices, moved(): return lax.ppermute(value, ('lon', 'lat'), pairs)  21.1 us
    ppermute x6, starting transfers between devices, swapped(): return lax.ppermute(value, ('lon', 'lat'), pairs)  9.38 us
    all_to_all x2, starting transfers between devices, across_z(): return lax.all_to_all(value, 'lon', 0, 0, axis_index_groups=groups)  9.12 us
    unnamed x46, local copies, waits for them, and re-layouts  8.8 us
    ppermute x3, waiting for transfers between devices, other_group(): return lax.ppermute(value, 'tp', [(0, 1), (1, 0)])  7.7 us
    all_to_all x2, starting transfers between devices, across_y(): return lax.all_to_all(value, 'lat', 0, 0, axis_index_groups=groups)  7.26 us
    all_to_all x2, waiting for transfers between devices, across_z(): return lax.all_to_all(value, 'lon', 0, 0, axis_index_groups=groups)  2.79 us
  transfers between devices with their start and end apart: 20, of which 6 were waited for; matrix products, arithmetic and copies ran while one was open for 0% of the time, Pallas kernels for 19%

profile of v5, /device:TPU:1, one launch (start us, length us, event | category | flops | bytes accessed | tf_op | source)
XLA Modules:
  0.0 101.7 jit_solution(13575330868776317747)
XLA Ops:
  0.6 1.1 %copy-done.1 = bf16[12,12,4,512]{3,2,1,0:T(4,128)(2,1)S(1)} copy-done((bf16[12,12,4,512]{3,2,1,0:T(4,128)(2,1)S(1)}, bf16[12,12,4,512]{3,2,1,0:T(4,128)(2,1)}, u32[]{:S(2)}) %copy-start.1) | copy-done | bytes 589848
  1.7 1.1 %copy-done.4 = bf16[12,12,4,512]{3,2,1,0:T(4,128)(2,1)S(1)} copy-done((bf16[12,12,4,512]{3,2,1,0:T(4,128)(2,1)S(1)}, bf16[12,12,4,512]{3,2,1,0:T(4,128)(2,1)}, u32[]{:S(2)}) %copy-start.4) | copy-done | bytes 589848
  2.9 3.3 %collective-permute-start = (bf16[2,216,512]{2,1,0:T(8,128)(2,1)S(1)}, bf16[2,216,512]{2,1,0:T(8,128)(2,1)S(1)}, u32[]{:S(2)}, u32[]{:S(2)}) collective-permute-start(bf16[2,216,512]{2,1,0:T(8,128)(2,1)S(1)} %get-tuple-element.35), channel_id=1, source_target_pairs={{0,240},{2,242},{4,244},{6,246},{8,248},{10,250},{12,252},{14,254}... | collective-permute-start | bytes 1327112 | tf_op jit(solution)/shard_map/ppermute | solution.py:329
  6.1 3.5 %collective-permute-start.1 = (bf16[2,72,512]{2,1,0:T(8,128)(2,1)S(1)}, bf16[2,72,512]{2,1,0:T(8,128)(2,1)S(1)}, u32[]{:S(2)}, u32[]{:S(2)}) collective-permute-start(bf16[2,72,512]{2,1,0:T(8,128)(2,1)S(1)} %get-tuple-element.36), channel_id=1, source_target_pairs={{0,14},{2,0},{4,2},{6,4},{8,6},{10,8},{12,10},{14,12},{16,30},{18,... | collective-permute-start | bytes 442376 | tf_op jit(solution)/shard_map/ppermute | solution.py:329
  9.6 5.7 %collective-permute-start.2 = (bf16[2,72,512]{2,1,0:T(8,128)(2,1)S(1)}, bf16[2,72,512]{2,1,0:T(8,128)(2,1)S(1)}, u32[]{:S(2)}, u32[]{:S(2)}) collective-permute-start(bf16[2,72,512]{2,1,0:T(8,128)(2,1)S(1)} %get-tuple-element.37), channel_id=1, source_target_pairs={{0,254},{2,240},{4,242},{6,244},{8,246},{10,248},{12,250},{14,252}... | collective-permute-start | bytes 442376 | tf_op jit(solution)/shard_map/ppermute | solution.py:329
  15.4 2.7 %shard_map.146.refs_10_ = f32[2304,144]{1,0:T(8,128)S(1)} custom-call(s32[2]{0:T(128)S(1)} %pad_add_fusion.refs_0_, f32[2,2,4,3312]{3,2,1,0:T(4,128)S(1)} %copy-done.9, bf16[276,276]{1,0:T(8,128)(2,1)S(1)} %copy-done.18), custom_call_target="tpu_custom_call" | custom-call | flops 2000000000 | tf_op jit(solution)/shard_map/pallas_call | solution.py:60
  18.1 0.7 collective-permute-done.2.refs_5_
  18.9 6.2 %shard_map.147 = (f32[1024,256]{1,0:T(8,128)S(1)}, bf16[1024,256]{1,0:T(8,128)(2,1)S(1)}, f32[2304,144]{1,0:T(8,128)S(1)}, bf16[576,256]{1,0:T(8,128)(2,1)S(1)},...) custom-call(s32[2]{0:T(128)S(1)} %pad_add_fusion.refs_0_, ...), custom_call_target="tpu_custom_call" | custom-call | flops 8999999488 | tf_op jit(solution)/shard_map/pallas_call | solution.py:60
  25.1 2.5 %collective-permute-start.8 = (bf16[1024,256]{1,0:T(8,128)(2,1)S(1)}, bf16[1024,256]{1,0:T(8,128)(2,1)S(1)}, u32[]{:S(2)}, u32[]{:S(2)}) collective-permute-start(bf16[1024,256]{1,0:T(8,128)(2,1)S(1)} %get-tuple-element.49), channel_id=1, source_target_pairs={{0,16},{2,18},{4,20},{6,22},{8,24},{10,26},{12,28},{14,30},{16,0},... | collective-permute-start | bytes 1572872 | tf_op jit(solution)/shard_map/ppermute | solution.py:335
  27.6 1.4 %shard_map.148.refs_0_.refs_2_ = bf16[576,768]{1,0:T(8,128)(2,1)S(1)} custom-call(bf16[576,256]{1,0:T(8,128)(2,1)S(1)} %get-tuple-element.38.refs_0_, bf16[576,256]{1,0:T(8,128)(2,1)S(1)} %get-tuple-element.39.refs_1_, bf16[576,256]{1,0:T(8,128)(2,1)S(1)} %get-tuple-element.40.refs_2_, bf16[576,256]{1,0:T(8,128)(2,1)S(1)} %get-tuple-element.41.refs_3_, ...), custom_call_target="tpu_custom_call" | custom-call | flops 2000000000 | tf_op jit(solution)/shard_map/pallas_call | solution.py:60
  29.0 0.4 collective-permute-start.3
  29.4 0.9 shard_map.151
  30.3 3.5 %all-to-all-start = ((bf16[4,256,256]{2,1,0:T(8,128)(2,1)}), bf16[4,256,256]{2,1,0:T(8,128)(2,1)S(1)}, u32[]{:S(2)}, u32[]{:S(2)}) async-start(bf16[4,256,256]{2,1,0:T(8,128)(2,1)} %bitcast.3), calls=%async_computation | async-start | bytes 1048576 | tf_op jit(solution)/shard_map/all_to_all | solution.py:341
  33.8 1.4 %collective-permute-start.4 = (bf16[256,512]{1,0:T(8,128)(2,1)S(1)}, bf16[256,512]{1,0:T(8,128)(2,1)}, u32[]{:S(2)}, u32[]{:S(2)}) collective-permute-start(bf16[256,512]{1,0:T(8,128)(2,1)S(1)} %copy-done.7), channel_id=1, source_target_pairs={{0,1},{1,0},{2,3},{3,2},{4,5},{5,4},{6,7},{7,6},{8,9},{9,8},{10,11... | collective-permute-start | bytes 786440 | tf_op jit(solution)/shard_map/ppermute | solution.py:351
  35.2 0.9 copy-done.17
  36.1 1.7 %copy-done.20 = f32[2304,144]{1,0:T(8,128)S(1)} copy-done((f32[2304,144]{1,0:T(8,128)S(1)}, f32[2304,144]{1,0:T(8,128)}, u32[]{:S(2)}) %copy-start.20) | copy-done | bytes 1327128
  37.8 1.9 %shard_map.152 = (bf16[256,128]{1,0:T(8,128)(2,1)S(1)}, bf16[256,128]{1,0:T(8,128)(2,1)S(1)}) custom-call(s32[2]{0:T(128)S(1)} %pad_add_fusion.refs_0_, f32[2304,144]{1,0:T(8,128)S(1)} %copy-done.20, bf16[2,138,276]{2,1,0:T(8,128)(2,1)S(1)} %copy-done.17), custom_call_target="tpu_custom_call" | custom-call | flops 2500000000 | tf_op jit(solution)/shard_map/pallas_call | solution.py:60
  39.7 0.7 collective-permute-start.9
  40.4 0.9 collective-permute-done.9.refs_2_
  41.3 1.7 %all-to-all-done.refs_0_ = bf16[4,256,256]{2,1,0:T(8,128)(2,1)S(1)} async-done(((bf16[4,256,256]{2,1,0:T(8,128)(2,1)}), bf16[4,256,256]{2,1,0:T(8,128)(2,1)S(1)}, u32[]{:S(2)}, u32[]{:S(2)}) %all-to-all-start) | async-done | bytes 524320 | tf_op jit(solution)/shard_map/all_to_all | solution.py:341
  43.0 0.8 shard_map.153
  43.8 4.6 %all-to-all-start.1 = ((bf16[8,32,384]{2,1,0:T(8,128)(2,1)}), bf16[8,32,384]{2,1,0:T(8,128)(2,1)S(1)}, u32[]{:S(2)}, u32[]{:S(2)}) async-start(bf16[8,32,384]{2,1,0:T(8,128)(2,1)} %shard_map.153), calls=%async_computation.1 | async-start | bytes 393216 | tf_op jit(solution)/shard_map/all_to_all | solution.py:347
  48.4 7.7 %collective-permute-done.4.refs_3_ = bf16[256,512]{1,0:T(8,128)(2,1)} collective-permute-done((bf16[256,512]{1,0:T(8,128)(2,1)S(1)}, bf16[256,512]{1,0:T(8,128)(2,1)}, u32[]{:S(2)}, u32[]{:S(2)}) %collective-permute-start.4) | collective-permute-done | bytes 262176 | tf_op jit(solution)/shard_map/ppermute | solution.py:351
  56.0 0.9 copy-done.8
  57.0 2.3 %shard_map.149 = (bf16[2,216,512]{2,1,0:T(8,128)(2,1)S(1)}, bf16[2,216,512]{2,1,0:T(8,128)(2,1)S(1)}, bf16[2,72,512]{2,1,0:T(8,128)(2,1)}, bf16[2,72,512]{2,1,0:T(8,128)(2,1)S(1)}, f32[8,128]{1,0:T(8,128)S(1)}) custom-call(bf16[576,768]{1,0:T(8,128)(2,1)S(1)} %shard_map.148.refs_0_.refs_2_, bf16[576,768]{1,0:T(8,128)(2,1)S(1)} %collective-permute-done.3.refs_1_, ...), custom_call_target="tpu_custom_call" | custom-call | flops 30000001024 | tf_op jit(solution)/shard_map/pallas_call | solution.py:60
  59.3 0.7 copy-done.10
  59.9 0.8 copy-done.21
  60.7 0.4 collective-permute-start.10
  61.1 2.8 %collective-permute-start.5 = (bf16[2,216,512]{2,1,0:T(8,128)(2,1)S(1)}, bf16[2,216,512]{2,1,0:T(8,128)(2,1)S(1)}, u32[]{:S(2)}, u32[]{:S(2)}) collective-permute-start(bf16[2,216,512]{2,1,0:T(8,128)(2,1)S(1)} %get-tuple-element.43), channel_id=1, source_target_pairs={{0,16},{2,18},{4,20},{6,22},{8,24},{10,26},{12,28},{14,30},{16,32}... | collective-permute-start | bytes 1327112 | tf_op jit(solution)/shard_map/ppermute | solution.py:329
  63.9 1.0 %collective-permute-done.10.refs_1_ = bf16[32,256]{1,0:T(8,128)(2,1)S(1)} collective-permute-done((bf16[32,256]{1,0:T(8,128)(2,1)S(1)}, bf16[32,256]{1,0:T(8,128)(2,1)S(1)}, u32[]{:S(2)}, u32[]{:S(2)}) %collective-permute-start.10) | collective-permute-done | bytes 16416 | tf_op jit(solution)/shard_map/ppermute | solution.py:335
  64.9 0.7 shard_map.155
  65.6 4.6 %all-to-all-start.2 = ((bf16[8,32,384]{2,1,0:T(8,128)(2,1)}), bf16[8,32,384]{2,1,0:T(8,128)(2,1)S(1)}, u32[]{:S(2)}, u32[]{:S(2)}) async-start(bf16[8,32,384]{2,1,0:T(8,128)(2,1)} %shard_map.155), calls=%async_computation.2 | async-start | bytes 393216 | tf_op jit(solution)/shard_map/all_to_all | solution.py:347
  70.2 1.4 %collective-permute-start.6 = (bf16[2,72,512]{2,1,0:T(8,128)(2,1)}, bf16[2,72,512]{2,1,0:T(8,128)(2,1)}, u32[]{:S(2)}, u32[]{:S(2)}) collective-permute-start(bf16[2,72,512]{2,1,0:T(8,128)(2,1)} %get-tuple-element.44), channel_id=1, source_target_pairs={{0,2},{2,4},{4,6},{6,8},{8,10},{10,12},{12,14},{14,0},{16,18},{18,... | collective-permute-start | bytes 442376 | tf_op jit(solution)/shard_map/ppermute | solution.py:329
  71.5 4.6 %collective-permute-start.7 = (bf16[2,72,512]{2,1,0:T(8,128)(2,1)S(1)}, bf16[2,72,512]{2,1,0:T(8,128)(2,1)}, u32[]{:S(2)}, u32[]{:S(2)}) collective-permute-start(bf16[2,72,512]{2,1,0:T(8,128)(2,1)S(1)} %copy-done.11), channel_id=1, source_target_pairs={{0,18},{2,20},{4,22},{6,24},{8,26},{10,28},{12,30},{14,16},{16,34}... | collective-permute-start | bytes 442376 | tf_op jit(solution)/shard_map/ppermute | solution.py:329
  76.2 2.8 %all-to-all-done.2.refs_0_ = bf16[8,32,384]{2,1,0:T(8,128)(2,1)S(1)} async-done(((bf16[8,32,384]{2,1,0:T(8,128)(2,1)}), bf16[8,32,384]{2,1,0:T(8,128)(2,1)S(1)}, u32[]{:S(2)}, u32[]{:S(2)}) %all-to-all-start.2) | async-done | bytes 196640 | tf_op jit(solution)/shard_map/all_to_all | solution.py:347
  78.9 0.8 shard_map.156
  79.8 0.6 copy-done.12
  80.4 3.8 %all-to-all-start.3 = ((bf16[4,256,256]{2,1,0:T(8,128)(2,1)}), bf16[4,256,256]{2,1,0:T(8,128)(2,1)S(1)}, u32[]{:S(2)}, u32[]{:S(2)}) async-start(bf16[4,256,256]{2,1,0:T(8,128)(2,1)} %get-tuple-element.56), calls=%async_computation.3 | async-start | bytes 1048576 | tf_op jit(solution)/shard_map/all_to_all | solution.py:341
  84.2 3.4 %collective-permute-start.11 = (bf16[256,128]{1,0:T(8,128)(2,1)}, bf16[256,128]{1,0:T(8,128)(2,1)S(1)}, u32[]{:S(2)}, u32[]{:S(2)}) collective-permute-start(bf16[256,128]{1,0:T(8,128)(2,1)} %copy-done.12), channel_id=1, source_target_pairs={{0,16},{2,18},{4,20},{6,22},{8,24},{10,26},{12,28},{14,30},{16,0},... | collective-permute-start | bytes 196616 | tf_op jit(solution)/shard_map/ppermute | solution.py:335
  87.7 1.0 copy-done.22
  88.7 3.1 %shard_map.150 = (bf16[12,12,4,512]{3,2,1,0:T(4,128)(2,1)}, bf16[12,12,4,512]{3,2,1,0:T(4,128)(2,1)}, f32[8,128]{1,0:T(8,128)S(1)}) custom-call(bf16[12,12,4,512]{3,2,1,0:T(4,128)(2,1)S(1)} %copy-done.3, bf16[12,12,4,512]{3,2,1,0:T(4,128)(2,1)S(1)} %copy-done.6, f32[1,512]{1,0:T(1,128)S(1)} %bitcast.10, bf16[2,216,512]{2,1,0:T(8,128)(2,1)S(1)} %copy-done.22, ...), custom_call_target="tpu_custom_call" | custom-call | flops 30000001024 | tf_op jit(solution)/shard_map/pallas_call | solution.py:60
  91.8 1.5 %shard_map.157 = (f32[2,2,4,3312]{3,2,1,0:T(4,128)}, f32[8,128]{1,0:T(8,128)S(1)}) custom-call(s32[2]{0:T(128)S(1)} %pad_add_fusion.refs_0_, bf16[256,128]{1,0:T(8,128)(2,1)S(1)} %copy-done.13, bf16[256,128]{1,0:T(8,128)(2,1)S(1)} %collective-permute-done.11.refs_2_, f32[8,128]{1,0:T(8,128)S(1)} %get-tuple-element.58.refs_3_), custom_call_target="tpu_custom_call" | custom-call | flops 1000000000 | tf_op jit(solution)/shard_map/pallas_call | solution.py:60
  93.3 2.4 %collective-permute-start.15 = (bf16[1024,256]{1,0:T(8,128)(2,1)S(1)}, bf16[1024,256]{1,0:T(8,128)(2,1)S(1)}, u32[]{:S(2)}, u32[]{:S(2)}) collective-permute-start(bf16[1024,256]{1,0:T(8,128)(2,1)S(1)} %bitcast.6), channel_id=1, source_target_pairs={{0,16},{2,18},{4,20},{6,22},{8,24},{10,26},{12,28},{14,30},{16,0},... | collective-permute-start | bytes 1572872 | tf_op jit(solution)/shard_map/ppermute | solution.py:335
  95.7 1.2 %shard_map.158.refs_0_ = f32[8,512]{1,0:T(8,128)S(1)} custom-call(s32[2]{0:T(128)S(1)} %pad_add_fusion.refs_0_, bf16[1024,256]{1,0:T(8,128)(2,1)S(1)} %bitcast.7, bf16[3,512,256]{2,1,0:T(8,128)(2,1)S(1)} %copy-done, f32[8,128]{1,0:T(8,128)S(1)} %get-tuple-element.59.refs_3_), custom_call_target="tpu_custom_call" | custom-call | flops 30000001024 | tf_op jit(solution)/shard_map/pallas_call | solution.py:60
  96.9 0.4 collective-permute-start.13
  97.3 1.8 %collective-permute-start.14 = (f32[8,512]{1,0:T(8,128)S(1)}, f32[8,512]{1,0:T(8,128)S(1)}, u32[]{:S(2)}, u32[]{:S(2)}) collective-permute-start(f32[8,512]{1,0:T(8,128)S(1)} %shard_map.158.refs_0_), channel_id=1, source_target_pairs={{0,17},{1,16},{16,1},{17,0},{32,49},{33,48},{48,33},{49,32},{64,81... | collective-permute-start | bytes 49160 | tf_op jit(solution)/shard_map/ppermute | solution.py:356
  99.1 1.9 %shard_map.159 = (f32[8,128]{1,0:T(8,128)S(1)}, f32[3,512,256]{2,1,0:T(8,128)}, f32[256,512]{1,0:T(8,128)}) custom-call(s32[2]{0:T(128)S(1)} %pad_add_fusion.refs_0_, bf16[1024,256]{1,0:T(8,128)(2,1)S(1)} %bitcast.8, bf16[1024,256]{1,0:T(8,128)(2,1)S(1)} %collective-permute-done.15.refs_2_), custom_call_target="tpu_custom_call" | custom-call | flops 2000000000 | tf_op jit(solution)/shard_map/pallas_call | solution.py:60
  101.1 0.6 shard_map.160
  (55 shorter events, 0.3 us)
Async XLA Ops:
  0.6 1.1 %copy-start.1 = (bf16[12,12,4,512]{3,2,1,0:T(4,128)(2,1)S(1)}, bf16[12,12,4,512]{3,2,1,0:T(4,128)(2,1)}, u32[]{:S(2)}) copy-start(bf16[12,12,4,512]{3,2,1,0:T(4,128)(2,1)} %refs_0_.3) | copy-start | bytes 1769476
  1.7 1.1 %copy-start.4 = (bf16[12,12,4,512]{3,2,1,0:T(4,128)(2,1)S(1)}, bf16[12,12,4,512]{3,2,1,0:T(4,128)(2,1)}, u32[]{:S(2)}) copy-start(bf16[12,12,4,512]{3,2,1,0:T(4,128)(2,1)} %refs_1_.7) | copy-start | bytes 1769476
  2.8 12.6 %copy-start.9 = (f32[2,2,4,3312]{3,2,1,0:T(4,128)S(1)}, f32[2,2,4,3312]{3,2,1,0:T(4,128)}, u32[]{:S(2)}) copy-start(f32[2,2,4,3312]{3,2,1,0:T(4,128)} %refs_1_.5) | copy-start | bytes 635908
  2.8 12.6 %copy-start.18 = (bf16[276,276]{1,0:T(8,128)(2,1)S(1)}, bf16[276,276]{1,0:T(8,128)(2,1)}, u32[]{:S(2)}) copy-start(bf16[276,276]{1,0:T(8,128)(2,1)} %constant.36.clone.refs_2_) | copy-start | bytes 457060
  2.9 16.0 %collective-permute-start = (bf16[2,216,512]{2,1,0:T(8,128)(2,1)S(1)}, bf16[2,216,512]{2,1,0:T(8,128)(2,1)S(1)}, u32[]{:S(2)}, u32[]{:S(2)}) collective-permute-start(bf16[2,216,512]{2,1,0:T(8,128)(2,1)S(1)} %get-tuple-element.35), channel_id=1, source_target_pairs={{0,240},{2,242},{4,244},{6,246},{8,248},{10,250},{12,252},{14,254}... | collective-permute-start | bytes 1327112 | tf_op jit(solution)/shard_map/ppermute | solution.py:329
  6.1 12.0 %collective-permute-start.1 = (bf16[2,72,512]{2,1,0:T(8,128)(2,1)S(1)}, bf16[2,72,512]{2,1,0:T(8,128)(2,1)S(1)}, u32[]{:S(2)}, u32[]{:S(2)}) collective-permute-start(bf16[2,72,512]{2,1,0:T(8,128)(2,1)S(1)} %get-tuple-element.36), channel_id=1, source_target_pairs={{0,14},{2,0},{4,2},{6,4},{8,6},{10,8},{12,10},{14,12},{16,30},{18,... | collective-permute-start | bytes 442376 | tf_op jit(solution)/shard_map/ppermute | solution.py:329
  9.6 9.3 %collective-permute-start.2 = (bf16[2,72,512]{2,1,0:T(8,128)(2,1)S(1)}, bf16[2,72,512]{2,1,0:T(8,128)(2,1)S(1)}, u32[]{:S(2)}, u32[]{:S(2)}) collective-permute-start(bf16[2,72,512]{2,1,0:T(8,128)(2,1)S(1)} %get-tuple-element.37), channel_id=1, source_target_pairs={{0,254},{2,240},{4,242},{6,244},{8,246},{10,248},{12,250},{14,252}... | collective-permute-start | bytes 442376 | tf_op jit(solution)/shard_map/ppermute | solution.py:329
  15.3 3.5 %copy-start = (bf16[3,512,256]{2,1,0:T(8,128)(2,1)S(1)}, bf16[3,512,256]{2,1,0:T(8,128)(2,1)}, u32[]{:S(2)}) copy-start(bf16[3,512,256]{2,1,0:T(8,128)(2,1)} %refs_2_.7) | copy-start | bytes 2359300
  15.3 3.5 %copy-start.2 = (bf16[12,12,4,512]{3,2,1,0:T(4,128)(2,1)S(1)}, bf16[12,12,4,512]{3,2,1,0:T(4,128)(2,1)}, u32[]{:S(2)}) copy-start(bf16[12,12,4,512]{3,2,1,0:T(4,128)(2,1)} %refs_0_.3) | copy-start | bytes 1769476
  15.3 3.5 %copy-start.5 = (bf16[12,12,4,512]{3,2,1,0:T(4,128)(2,1)S(1)}, bf16[12,12,4,512]{3,2,1,0:T(4,128)(2,1)}, u32[]{:S(2)}) copy-start(bf16[12,12,4,512]{3,2,1,0:T(4,128)(2,1)} %refs_1_.7) | copy-start | bytes 1769476
  15.4 3.5 %copy-start.7 = (bf16[256,512]{1,0:T(8,128)(2,1)S(1)}, bf16[256,512]{1,0:T(8,128)(2,1)}, u32[]{:S(2)}) copy-start(bf16[256,512]{1,0:T(8,128)(2,1)} %refs_2_.6) | copy-start | bytes 786436
  15.4 3.5 %copy-start.14 = (f32[512]{0:T(512)S(1)}, f32[512]{0:T(512)}, u32[]{:S(2)}) copy-start(f32[512]{0:T(512)} %param.12) | copy-start | bytes 6148
  15.4 3.5 %copy-start.16 = (bf16[576,576]{1,0:T(8,128)(2,1)S(1)}, bf16[576,576]{1,0:T(8,128)(2,1)}, u32[]{:S(2)}) copy-start(bf16[576,576]{1,0:T(8,128)(2,1)} %constant.34.clone.refs_6_) | copy-start | bytes 1990660
  18.9 8.7 %copy-start.15 = (bf16[576,576]{1,0:T(8,128)(2,1)S(1)}, bf16[576,576]{1,0:T(8,128)(2,1)}, u32[]{:S(2)}) copy-start(bf16[576,576]{1,0:T(8,128)(2,1)} %constant.35.clone.refs_5_) | copy-start | bytes 1990660
  25.1 3.9 %copy-start.19 = (f32[2304,144]{1,0:T(8,128)}, f32[2304,144]{1,0:T(8,128)S(1)}, u32[]{:S(2)}) copy-start(f32[2304,144]{1,0:T(8,128)S(1)} %get-tuple-element.50.refs_1_) | copy-start | bytes 3981316
  25.1 4.3 %collective-permute-start.8 = (bf16[1024,256]{1,0:T(8,128)(2,1)S(1)}, bf16[1024,256]{1,0:T(8,128)(2,1)S(1)}, u32[]{:S(2)}, u32[]{:S(2)}) collective-permute-start(bf16[1024,256]{1,0:T(8,128)(2,1)S(1)} %get-tuple-element.49), channel_id=1, source_target_pairs={{0,16},{2,18},{4,20},{6,22},{8,24},{10,26},{12,28},{14,30},{16,0},... | collective-permute-start | bytes 1572872 | tf_op jit(solution)/shard_map/ppermute | solution.py:335
  29.0 27.1 %collective-permute-start.3 = (bf16[576,768]{1,0:T(8,128)(2,1)S(1)}, bf16[576,768]{1,0:T(8,128)(2,1)S(1)}, u32[]{:S(2)}, u32[]{:S(2)}) collective-permute-start(bf16[576,768]{1,0:T(8,128)(2,1)S(1)} %shard_map.148.refs_0_.refs_2_), channel_id=1, source_target_pairs={{0,1},{1,0},{2,3},{3,2},{4,5},{5,4},{6,7},{7,6},{8,9},{9,8},{10,11... | collective-permute-start | bytes 2654216 | tf_op jit(solution)/shard_map/ppermute | solution.py:351
  30.3 12.7 %all-to-all-start = ((bf16[4,256,256]{2,1,0:T(8,128)(2,1)}), bf16[4,256,256]{2,1,0:T(8,128)(2,1)S(1)}, u32[]{:S(2)}, u32[]{:S(2)}) async-start(bf16[4,256,256]{2,1,0:T(8,128)(2,1)} %bitcast.3), calls=%async_computation | async-start | bytes 1048576 | tf_op jit(solution)/shard_map/all_to_all | solution.py:341
  33.8 22.3 %collective-permute-start.4 = (bf16[256,512]{1,0:T(8,128)(2,1)S(1)}, bf16[256,512]{1,0:T(8,128)(2,1)}, u32[]{:S(2)}, u32[]{:S(2)}) collective-permute-start(bf16[256,512]{1,0:T(8,128)(2,1)S(1)} %copy-done.7), channel_id=1, source_target_pairs={{0,1},{1,0},{2,3},{3,2},{4,5},{5,4},{6,7},{7,6},{8,9},{9,8},{10,11... | collective-permute-start | bytes 786440 | tf_op jit(solution)/shard_map/ppermute | solution.py:351
  35.2 0.9 copy-start.17
  36.1 1.7 %copy-start.20 = (f32[2304,144]{1,0:T(8,128)S(1)}, f32[2304,144]{1,0:T(8,128)}, u32[]{:S(2)}) copy-start(f32[2304,144]{1,0:T(8,128)} %copy-done.19) | copy-start | bytes 3981316
  39.7 1.6 %collective-permute-start.9 = (bf16[256,128]{1,0:T(8,128)(2,1)S(1)}, bf16[256,128]{1,0:T(8,128)(2,1)S(1)}, u32[]{:S(2)}, u32[]{:S(2)}) collective-permute-start(bf16[256,128]{1,0:T(8,128)(2,1)S(1)} %get-tuple-element.52), channel_id=1, source_target_pairs={{0,16},{2,18},{4,20},{6,22},{8,24},{10,26},{12,28},{14,30},{16,0},... | collective-permute-start | bytes 196616 | tf_op jit(solution)/shard_map/ppermute | solution.py:335
  43.8 16.9 %all-to-all-start.1 = ((bf16[8,32,384]{2,1,0:T(8,128)(2,1)}), bf16[8,32,384]{2,1,0:T(8,128)(2,1)S(1)}, u32[]{:S(2)}, u32[]{:S(2)}) async-start(bf16[8,32,384]{2,1,0:T(8,128)(2,1)} %shard_map.153), calls=%async_computation.1 | async-start | bytes 393216 | tf_op jit(solution)/shard_map/all_to_all | solution.py:347
  56.0 1.0 copy-start.8
  59.3 0.7 copy-start.10
  59.9 0.8 copy-start.21
  60.7 10.8 %copy-start.11 = (bf16[2,72,512]{2,1,0:T(8,128)(2,1)S(1)}, bf16[2,72,512]{2,1,0:T(8,128)(2,1)}, u32[]{:S(2)}) copy-start(bf16[2,72,512]{2,1,0:T(8,128)(2,1)} %copy-done.10) | copy-start | bytes 442372
  60.7 4.2 %collective-permute-start.10 = (bf16[32,256]{1,0:T(8,128)(2,1)S(1)}, bf16[32,256]{1,0:T(8,128)(2,1)S(1)}, u32[]{:S(2)}, u32[]{:S(2)}) collective-permute-start(bf16[32,256]{1,0:T(8,128)(2,1)S(1)} %get-tuple-element.54.refs_0_), channel_id=1, source_target_pairs={{0,2},{2,0},{4,6},{6,4},{8,10},{10,8},{12,14},{14,12},{16,18},{18,... | collective-permute-start | bytes 49160 | tf_op jit(solution)/shard_map/ppermute | solution.py:335
  61.1 26.6 %collective-permute-start.5 = (bf16[2,216,512]{2,1,0:T(8,128)(2,1)S(1)}, bf16[2,216,512]{2,1,0:T(8,128)(2,1)S(1)}, u32[]{:S(2)}, u32[]{:S(2)}) collective-permute-start(bf16[2,216,512]{2,1,0:T(8,128)(2,1)S(1)} %get-tuple-element.43), channel_id=1, source_target_pairs={{0,16},{2,18},{4,20},{6,22},{8,24},{10,26},{12,28},{14,30},{16,32}... | collective-permute-start | bytes 1327112 | tf_op jit(solution)/shard_map/ppermute | solution.py:329
  65.6 13.3 %all-to-all-start.2 = ((bf16[8,32,384]{2,1,0:T(8,128)(2,1)}), bf16[8,32,384]{2,1,0:T(8,128)(2,1)S(1)}, u32[]{:S(2)}, u32[]{:S(2)}) async-start(bf16[8,32,384]{2,1,0:T(8,128)(2,1)} %shard_map.155), calls=%async_computation.2 | async-start | bytes 393216 | tf_op jit(solution)/shard_map/all_to_all | solution.py:347
  70.2 17.5 %collective-permute-start.6 = (bf16[2,72,512]{2,1,0:T(8,128)(2,1)}, bf16[2,72,512]{2,1,0:T(8,128)(2,1)}, u32[]{:S(2)}, u32[]{:S(2)}) collective-permute-start(bf16[2,72,512]{2,1,0:T(8,128)(2,1)} %get-tuple-element.44), channel_id=1, source_target_pairs={{0,2},{2,4},{4,6},{6,8},{8,10},{10,12},{12,14},{14,0},{16,18},{18,... | collective-permute-start | bytes 442376 | tf_op jit(solution)/shard_map/ppermute | solution.py:329
  71.5 16.1 %copy-start.3 = (bf16[12,12,4,512]{3,2,1,0:T(4,128)(2,1)S(1)}, bf16[12,12,4,512]{3,2,1,0:T(4,128)(2,1)}, u32[]{:S(2)}) copy-start(bf16[12,12,4,512]{3,2,1,0:T(4,128)(2,1)} %refs_0_.3) | copy-start | bytes 1769476
  71.5 16.1 %copy-start.6 = (bf16[12,12,4,512]{3,2,1,0:T(4,128)(2,1)S(1)}, bf16[12,12,4,512]{3,2,1,0:T(4,128)(2,1)}, u32[]{:S(2)}) copy-start(bf16[12,12,4,512]{3,2,1,0:T(4,128)(2,1)} %refs_1_.7) | copy-start | bytes 1769476
  71.5 16.1 %collective-permute-start.7 = (bf16[2,72,512]{2,1,0:T(8,128)(2,1)S(1)}, bf16[2,72,512]{2,1,0:T(8,128)(2,1)}, u32[]{:S(2)}, u32[]{:S(2)}) collective-permute-start(bf16[2,72,512]{2,1,0:T(8,128)(2,1)S(1)} %copy-done.11), channel_id=1, source_target_pairs={{0,18},{2,20},{4,22},{6,24},{8,26},{10,28},{12,30},{14,16},{16,34}... | collective-permute-start | bytes 442376 | tf_op jit(solution)/shard_map/ppermute | solution.py:329
  79.8 0.6 copy-start.12
  80.4 12.9 %all-to-all-start.3 = ((bf16[4,256,256]{2,1,0:T(8,128)(2,1)}), bf16[4,256,256]{2,1,0:T(8,128)(2,1)S(1)}, u32[]{:S(2)}, u32[]{:S(2)}) async-start(bf16[4,256,256]{2,1,0:T(8,128)(2,1)} %get-tuple-element.56), calls=%async_computation.3 | async-start | bytes 1048576 | tf_op jit(solution)/shard_map/all_to_all | solution.py:341
  84.2 7.6 %collective-permute-start.11 = (bf16[256,128]{1,0:T(8,128)(2,1)}, bf16[256,128]{1,0:T(8,128)(2,1)S(1)}, u32[]{:S(2)}, u32[]{:S(2)}) collective-permute-start(bf16[256,128]{1,0:T(8,128)(2,1)} %copy-done.12), channel_id=1, source_target_pairs={{0,16},{2,18},{4,20},{6,22},{8,24},{10,26},{12,28},{14,30},{16,0},... | collective-permute-start | bytes 196616 | tf_op jit(solution)/shard_map/ppermute | solution.py:335
  87.7 1.0 copy-start.22
  88.7 3.1 %copy-start.13 = (bf16[256,128]{1,0:T(8,128)(2,1)S(1)}, bf16[256,128]{1,0:T(8,128)(2,1)}, u32[]{:S(2)}) copy-start(bf16[256,128]{1,0:T(8,128)(2,1)} %copy-done.12) | copy-start | bytes 196612
  93.3 5.8 %collective-permute-start.15 = (bf16[1024,256]{1,0:T(8,128)(2,1)S(1)}, bf16[1024,256]{1,0:T(8,128)(2,1)S(1)}, u32[]{:S(2)}, u32[]{:S(2)}) collective-permute-start(bf16[1024,256]{1,0:T(8,128)(2,1)S(1)} %bitcast.6), channel_id=1, source_target_pairs={{0,16},{2,18},{4,20},{6,22},{8,24},{10,26},{12,28},{14,30},{16,0},... | collective-permute-start | bytes 1572872 | tf_op jit(solution)/shard_map/ppermute | solution.py:335
  96.9 4.1 %collective-permute-start.12 = (f32[8,512]{1,0:T(8,128)S(1)}, f32[8,512]{1,0:T(8,128)S(1)}, u32[]{:S(2)}, u32[]{:S(2)}) collective-permute-start(f32[8,512]{1,0:T(8,128)S(1)} %shard_map.158.refs_0_), channel_id=1, source_target_pairs={{0,16},{2,18},{4,20},{6,22},{8,24},{10,26},{12,28},{14,30},{16,0},... | collective-permute-start | bytes 49160 | tf_op jit(solution)/shard_map/ppermute | solution.py:335
  96.9 4.1 %collective-permute-start.13 = (f32[8,512]{1,0:T(8,128)S(1)}, f32[8,512]{1,0:T(8,128)S(1)}, u32[]{:S(2)}, u32[]{:S(2)}) collective-permute-start(f32[8,512]{1,0:T(8,128)S(1)} %shard_map.158.refs_0_), channel_id=1, source_target_pairs={{0,1},{1,0},{2,3},{3,2},{4,5},{5,4},{6,7},{7,6},{8,9},{9,8},{10,11... | collective-permute-start | bytes 49160 | tf_op jit(solution)/shard_map/ppermute | solution.py:351
  97.3 3.8 %collective-permute-start.14 = (f32[8,512]{1,0:T(8,128)S(1)}, f32[8,512]{1,0:T(8,128)S(1)}, u32[]{:S(2)}, u32[]{:S(2)}) collective-permute-start(f32[8,512]{1,0:T(8,128)S(1)} %shard_map.158.refs_0_), channel_id=1, source_target_pairs={{0,17},{1,16},{16,1},{17,0},{32,49},{33,48},{48,33},{49,32},{64,81... | collective-permute-start | bytes 49160 | tf_op jit(solution)/shard_map/ppermute | solution.py:356

commit v6 on v5

--- a/solution.py
+++ b/solution.py
@@ -84,7 +84,8 @@
             ref[j] = grid[lon, lat].reshape(ref.shape[1:])
 
 
-def bias_kernel(info, table, order, bias, raw, entries, low_u, high_u):
+def bias_kernel(info, table, order, w_out, bias, w_copy, raw, entries, low_u, high_u):
+    w_copy[...] = w_out[...]
     flat = table[...].reshape(16, 3312)
     for s_t in range(2):
         for s_u in range(2):
@@ -321,12 +322,14 @@
 
 def moved(value, by_lon, by_lat):
     n_lon, n_lat = lax.axis_size("lon"), lax.axis_size("lat")
+    flip = 1 if by_lat else 0
     pairs = [
-        (i * n_lat + j, (i + by_lon) % n_lon * n_lat + (j + by_lat) % n_lat)
+        ((i * n_lat + j) * 2 + k, ((i + by_lon) % n_lon * n_lat + (j + by_lat) % n_lat) * 2 + (k ^ flip))
         for i in range(n_lon)
         for j in range(n_lat)
+        for k in range(2)
     ]
-    return lax.ppermute(value, ("lon", "lat"), pairs)
+    return lax.ppermute(value, ("lon", "lat", "tp"), pairs)
 
 
 def swapped(value, lon_bits, lat_bits):
@@ -371,14 +374,14 @@
     s_lon, s_lat, s_cor = call(halo_kernel, halos, [latent, cotangent], smem=0)
     in_lon, in_lat, in_cor = moved(s_lon, -1, 0), moved(s_lat, 0, -1), moved(s_cor, -1, -1)
 
-    (bias,) = call(
+    bias, w_copy = call(
         bias_kernel,
-        [((16 * WTOK, WTOK), F32)],
-        [info, bias_table, order],
+        [((16 * WTOK, WTOK), F32), (w_out.shape, BF)],
+        [info, bias_table, order, w_out],
         [pltpu.VMEM((192, 276), F32)] * 2 + [pltpu.VMEM((192, 128), F32)] * 2,
         us=2,
     )
-    w_other = other_group(w_out)
+    w_other = other_group(w_copy)
 
     keep, send, ds, att, gq, gk, gv = call(
         main_kernel,
@@ -389,7 +392,7 @@
         mib=32,
     )
     recv = swapped(send, 1, 0)
-    (terms,) = call(terms_kernel, [((576, 768), BF)], [att, gq, gk, gv, w_qkv, back], smem=0, us=2)
+    (terms,) = call(terms_kernel, [((576, 768), BF)], [att, gq, gk, gv, w_qkv, back], smem=0, after=[w_other], us=2)
     others = other_group(terms)
     own, s_lon, s_lat, s_cor, paired = call(
         pair_kernel, [part(216)] + halos + [TOKEN], [terms, others, w_out, w_other], smem=0, us=30

time: 103 us -> 98.9 us (0.960)
  waiting for transfers between devices: 14.9 us -> 12.5 us
    ppermute x3, waiting for transfers between devices: 7.7 us -> 2.33 us  [other_group(): return lax.ppermute(value, 'tp', [(0, 1), (1, 0)])]
    ppermute x6, starting transfers between devices: 9.38 us -> 12.9 us  [swapped(): return lax.ppermute(value, ('lon', 'lat'), pairs)]
    all_to_all x2, waiting for transfers between devices: 1.75 us -> 4.07 us  [across_y(): return lax.all_to_all(value, 'lat', 0, 0, axis_index_groups=groups)]
    all_to_all x2, waiting for transfers between devices: 2.79 us -> 4.58 us  [across_z(): return lax.all_to_all(value, 'lon', 0, 0, axis_index_groups=groups)]
    ppermute x1, starting transfers between devices: 1.78 us -> 0.14 us  [other_group_and_core(): lax.ppermute(value, ('lon', 'tp'), [(i * 2 + j, (i ^ 1) * 2 + (j ^ 1)) fo...]
    unnamed x46 -> x50, local copies, waits for them, and re-layouts: 8.8 us -> 8.82 us
  transfers between devices with their start and end apart: 20 -> 20, of which waited for: 6 -> 6; matrix products, arithmetic and copies ran while one was open for 0% -> 0% of each run, Pallas kernels for 19% -> 25%
where the time goes in v6:
time: 98.9 us; the launch traced here: 98.2 us
  starting transfers between devices  50.7 us (51%)
  Pallas kernels  25.1 us (25%)
  waiting for transfers between devices  12.5 us (13%)
  local copies, waits for them, and re-layouts  8.82 us (9%)
    pallas_call x16, Pallas kernels, call(): pl.pallas_call(kernel, out_shape=[jax.ShapeDtypeStruct(s, t) for s, t in...  25.1 us
    ppermute x6, starting transfers between devices, moved(): return lax.ppermute(value, ('lon', 'lat', 'tp'), pairs)  20.9 us
    ppermute x6, starting transfers between devices, swapped(): return lax.ppermute(value, ('lon', 'lat'), pairs)  12.9 us
    unnamed x50, local copies, waits for them, and re-layouts  8.82 us
    all_to_all x2, starting transfers between devices, across_z(): return lax.all_to_all(value, 'lon', 0, 0, axis_index_groups=groups)  8.23 us
    all_to_all x2, starting transfers between devices, across_y(): return lax.all_to_all(value, 'lat', 0, 0, axis_index_groups=groups)  7.12 us
    all_to_all x2, waiting for transfers between devices, across_z(): return lax.all_to_all(value, 'lon', 0, 0, axis_index_groups=groups)  4.58 us
    all_to_all x2, waiting for transfers between devices, across_y(): return lax.all_to_all(value, 'lat', 0, 0, axis_index_groups=groups)  4.07 us
  transfers between devices with their start and end apart: 20, of which 6 were waited for; matrix products, arithmetic and copies ran while one was open for 0% of the time, Pallas kernels for 25%

profile of v6, /device:TPU:1, one launch (start us, length us, event | category | flops | bytes accessed | tf_op | source)
XLA Modules:
  0.0 98.2 jit_solution(15742705493206487759)
XLA Ops:
  0.6 1.1 %copy-done.1 = bf16[12,12,4,512]{3,2,1,0:T(4,128)(2,1)S(1)} copy-done((bf16[12,12,4,512]{3,2,1,0:T(4,128)(2,1)S(1)}, bf16[12,12,4,512]{3,2,1,0:T(4,128)(2,1)}, u32[]{:S(2)}) %copy-start.1) | copy-done | bytes 589848
  1.7 1.1 %copy-done.4 = bf16[12,12,4,512]{3,2,1,0:T(4,128)(2,1)S(1)} copy-done((bf16[12,12,4,512]{3,2,1,0:T(4,128)(2,1)S(1)}, bf16[12,12,4,512]{3,2,1,0:T(4,128)(2,1)}, u32[]{:S(2)}) %copy-start.4) | copy-done | bytes 589848
  2.9 3.3 %collective-permute-start = (bf16[2,216,512]{2,1,0:T(8,128)(2,1)S(1)}, bf16[2,216,512]{2,1,0:T(8,128)(2,1)S(1)}, u32[]{:S(2)}, u32[]{:S(2)}) collective-permute-start(bf16[2,216,512]{2,1,0:T(8,128)(2,1)S(1)} %get-tuple-element.37), channel_id=1, source_target_pairs={{0,240},{1,241},{2,242},{3,243},{4,244},{5,245},{6,246},{7,247},{8... | collective-permute-start | bytes 1327112 | tf_op jit(solution)/shard_map/ppermute | solution.py:332
  6.1 3.2 %collective-permute-start.1 = (bf16[2,72,512]{2,1,0:T(8,128)(2,1)S(1)}, bf16[2,72,512]{2,1,0:T(8,128)(2,1)S(1)}, u32[]{:S(2)}, u32[]{:S(2)}) collective-permute-start(bf16[2,72,512]{2,1,0:T(8,128)(2,1)S(1)} %get-tuple-element.38), channel_id=1, source_target_pairs={{0,15},{1,14},{2,1},{3,0},{4,3},{5,2},{6,5},{7,4},{8,7},{9,6},{10,... | collective-permute-start | bytes 442376 | tf_op jit(solution)/shard_map/ppermute | solution.py:332
  9.3 5.7 %collective-permute-start.2 = (bf16[2,72,512]{2,1,0:T(8,128)(2,1)S(1)}, bf16[2,72,512]{2,1,0:T(8,128)(2,1)S(1)}, u32[]{:S(2)}, u32[]{:S(2)}) collective-permute-start(bf16[2,72,512]{2,1,0:T(8,128)(2,1)S(1)} %get-tuple-element.39), channel_id=1, source_target_pairs={{0,255},{1,254},{2,241},{3,240},{4,243},{5,242},{6,245},{7,244},{8... | collective-permute-start | bytes 442376 | tf_op jit(solution)/shard_map/ppermute | solution.py:332
  15.1 2.7 %shard_map.146 = (f32[2304,144]{1,0:T(8,128)S(1)}, bf16[256,512]{1,0:T(8,128)(2,1)S(1)}) custom-call(s32[2]{0:T(128)S(1)} %pad_add_fusion.refs_0_, f32[2,2,4,3312]{3,2,1,0:T(4,128)S(1)} %copy-done.11, bf16[276,276]{1,0:T(8,128)(2,1)S(1)} %copy-done.20, bf16[256,512]{1,0:T(8,128)(2,1)S(1)} %copy-done.7), custom_call_target="tpu_custom_call" | custom-call | flops 2000000000 | tf_op jit(solution)/shard_map/pallas_call | solution.py:60
  17.8 0.1 collective-permute-start.3
  17.9 0.6 collective-permute-done.2.refs_5_
  18.6 6.1 %shard_map.147 = (f32[1024,256]{1,0:T(8,128)S(1)}, bf16[1024,256]{1,0:T(8,128)(2,1)S(1)}, f32[2304,144]{1,0:T(8,128)S(1)}, bf16[576,256]{1,0:T(8,128)(2,1)S(1)},...) custom-call(s32[2]{0:T(128)S(1)} %pad_add_fusion.refs_0_, ...), custom_call_target="tpu_custom_call" | custom-call | flops 8999999488 | tf_op jit(solution)/shard_map/pallas_call | solution.py:60
  24.7 2.2 %collective-permute-start.8 = (bf16[1024,256]{1,0:T(8,128)(2,1)S(1)}, bf16[1024,256]{1,0:T(8,128)(2,1)S(1)}, u32[]{:S(2)}, u32[]{:S(2)}) collective-permute-start(bf16[1024,256]{1,0:T(8,128)(2,1)S(1)} %get-tuple-element.53), channel_id=1, source_target_pairs={{0,16},{2,18},{4,20},{6,22},{8,24},{10,26},{12,28},{14,30},{16,0},... | collective-permute-start | bytes 1572872 | tf_op jit(solution)/shard_map/ppermute | solution.py:338
  26.9 1.4 %shard_map.148.refs_0_.refs_2_ = bf16[576,768]{1,0:T(8,128)(2,1)S(1)} custom-call(bf16[576,256]{1,0:T(8,128)(2,1)S(1)} %get-tuple-element.41.refs_0_, bf16[576,256]{1,0:T(8,128)(2,1)S(1)} %get-tuple-element.42.refs_1_, bf16[576,256]{1,0:T(8,128)(2,1)S(1)} %get-tuple-element.43.refs_2_, bf16[576,256]{1,0:T(8,128)(2,1)S(1)} %get-tuple-element.44.refs_3_, ...), custom_call_target="tpu_custom_call" | custom-call | flops 2000000000 | tf_op jit(solution)/shard_map/pallas_call | solution.py:60
  28.3 0.1 collective-permute-start.4
  28.5 0.9 shard_map.151
  29.4 3.7 %all-to-all-start = ((bf16[4,256,256]{2,1,0:T(8,128)(2,1)}), bf16[4,256,256]{2,1,0:T(8,128)(2,1)S(1)}, u32[]{:S(2)}, u32[]{:S(2)}) async-start(bf16[4,256,256]{2,1,0:T(8,128)(2,1)} %bitcast.3), calls=%async_computation | async-start | bytes 1048576 | tf_op jit(solution)/shard_map/all_to_all | solution.py:344
  33.0 1.7 %copy-done.22 = f32[2304,144]{1,0:T(8,128)S(1)} copy-done((f32[2304,144]{1,0:T(8,128)S(1)}, f32[2304,144]{1,0:T(8,128)}, u32[]{:S(2)}) %copy-start.22) | copy-done | bytes 1327128
  34.7 1.9 %shard_map.152 = (bf16[256,128]{1,0:T(8,128)(2,1)S(1)}, bf16[256,128]{1,0:T(8,128)(2,1)S(1)}) custom-call(s32[2]{0:T(128)S(1)} %pad_add_fusion.refs_0_, f32[2304,144]{1,0:T(8,128)S(1)} %copy-done.22, bf16[2,138,276]{2,1,0:T(8,128)(2,1)S(1)} %copy-done.19), custom_call_target="tpu_custom_call" | custom-call | flops 2500000000 | tf_op jit(solution)/shard_map/pallas_call | solution.py:60
  36.6 0.5 collective-permute-start.9
  37.1 0.9 collective-permute-done.9.refs_2_
  38.0 4.1 %all-to-all-done.refs_0_ = bf16[4,256,256]{2,1,0:T(8,128)(2,1)S(1)} async-done(((bf16[4,256,256]{2,1,0:T(8,128)(2,1)}), bf16[4,256,256]{2,1,0:T(8,128)(2,1)S(1)}, u32[]{:S(2)}, u32[]{:S(2)}) %all-to-all-start) | async-done | bytes 524320 | tf_op jit(solution)/shard_map/all_to_all | solution.py:344
  42.0 0.8 shard_map.153
  42.8 4.6 %all-to-all-start.1 = ((bf16[8,32,384]{2,1,0:T(8,128)(2,1)}), bf16[8,32,384]{2,1,0:T(8,128)(2,1)S(1)}, u32[]{:S(2)}, u32[]{:S(2)}) async-start(bf16[8,32,384]{2,1,0:T(8,128)(2,1)} %shard_map.153), calls=%async_computation.1 | async-start | bytes 393216 | tf_op jit(solution)/shard_map/all_to_all | solution.py:350
  47.3 2.3 %collective-permute-done.4.refs_1_ = bf16[576,768]{1,0:T(8,128)(2,1)S(1)} collective-permute-done((bf16[576,768]{1,0:T(8,128)(2,1)S(1)}, bf16[576,768]{1,0:T(8,128)(2,1)S(1)}, u32[]{:S(2)}, u32[]{:S(2)}) %collective-permute-start.4) | collective-permute-done | bytes 884768 | tf_op jit(solution)/shard_map/ppermute | solution.py:354
  49.7 0.9 copy-done.8
  50.6 0.9 copy-done.10
  51.6 1.4 %shard_map.149 = (bf16[2,216,512]{2,1,0:T(8,128)(2,1)S(1)}, bf16[2,216,512]{2,1,0:T(8,128)(2,1)S(1)}, bf16[2,72,512]{2,1,0:T(8,128)(2,1)}, bf16[2,72,512]{2,1,0:T(8,128)(2,1)S(1)}, f32[8,128]{1,0:T(8,128)S(1)}) custom-call(bf16[576,768]{1,0:T(8,128)(2,1)S(1)} %shard_map.148.refs_0_.refs_2_, bf16[576,768]{1,0:T(8,128)(2,1)S(1)} %collective-permute-done.4.refs_1_, ...), custom_call_target="tpu_custom_call" | custom-call | flops 30000001024 | tf_op jit(solution)/shard_map/pallas_call | solution.py:60
  53.0 0.7 copy-done.12
  53.6 0.8 copy-done.23
  54.4 1.4 %all-to-all-done.1.refs_0_ = bf16[8,32,384]{2,1,0:T(8,128)(2,1)S(1)} async-done(((bf16[8,32,384]{2,1,0:T(8,128)(2,1)}), bf16[8,32,384]{2,1,0:T(8,128)(2,1)S(1)}, u32[]{:S(2)}, u32[]{:S(2)}) %all-to-all-start.1) | async-done | bytes 196640 | tf_op jit(solution)/shard_map/all_to_all | solution.py:350
  55.9 4.3 %collective-permute-start.10 = (bf16[32,256]{1,0:T(8,128)(2,1)S(1)}, bf16[32,256]{1,0:T(8,128)(2,1)S(1)}, u32[]{:S(2)}, u32[]{:S(2)}) collective-permute-start(bf16[32,256]{1,0:T(8,128)(2,1)S(1)} %get-tuple-element.58.refs_0_), channel_id=1, source_target_pairs={{0,2},{2,0},{4,6},{6,4},{8,10},{10,8},{12,14},{14,12},{16,18},{18,... | collective-permute-start | bytes 49160 | tf_op jit(solution)/shard_map/ppermute | solution.py:338
  60.1 3.3 %collective-permute-start.5 = (bf16[2,216,512]{2,1,0:T(8,128)(2,1)S(1)}, bf16[2,216,512]{2,1,0:T(8,128)(2,1)S(1)}, u32[]{:S(2)}, u32[]{:S(2)}) collective-permute-start(bf16[2,216,512]{2,1,0:T(8,128)(2,1)S(1)} %get-tuple-element.47), channel_id=1, source_target_pairs={{0,16},{1,17},{2,18},{3,19},{4,20},{5,21},{6,22},{7,23},{8,24},{9,... | collective-permute-start | bytes 1327112 | tf_op jit(solution)/shard_map/ppermute | solution.py:332
  63.5 0.7 shard_map.155
  64.2 3.7 %all-to-all-start.2 = ((bf16[8,32,384]{2,1,0:T(8,128)(2,1)}), bf16[8,32,384]{2,1,0:T(8,128)(2,1)S(1)}, u32[]{:S(2)}, u32[]{:S(2)}) async-start(bf16[8,32,384]{2,1,0:T(8,128)(2,1)} %shard_map.155), calls=%async_computation.2 | async-start | bytes 393216 | tf_op jit(solution)/shard_map/all_to_all | solution.py:350
  67.9 5.4 %collective-permute-start.7 = (bf16[2,72,512]{2,1,0:T(8,128)(2,1)S(1)}, bf16[2,72,512]{2,1,0:T(8,128)(2,1)}, u32[]{:S(2)}, u32[]{:S(2)}) collective-permute-start(bf16[2,72,512]{2,1,0:T(8,128)(2,1)S(1)} %copy-done.13), channel_id=1, source_target_pairs={{0,19},{1,18},{2,21},{3,20},{4,23},{5,22},{6,25},{7,24},{8,27},{9,... | collective-permute-start | bytes 442376 | tf_op jit(solution)/shard_map/ppermute | solution.py:332
  73.3 3.2 %all-to-all-done.2.refs_0_ = bf16[8,32,384]{2,1,0:T(8,128)(2,1)S(1)} async-done(((bf16[8,32,384]{2,1,0:T(8,128)(2,1)}), bf16[8,32,384]{2,1,0:T(8,128)(2,1)S(1)}, u32[]{:S(2)}, u32[]{:S(2)}) %all-to-all-start.2) | async-done | bytes 196640 | tf_op jit(solution)/shard_map/all_to_all | solution.py:350
  76.5 0.8 shard_map.156
  77.3 0.6 copy-done.14
  78.0 3.5 %all-to-all-start.3 = ((bf16[4,256,256]{2,1,0:T(8,128)(2,1)}), bf16[4,256,256]{2,1,0:T(8,128)(2,1)S(1)}, u32[]{:S(2)}, u32[]{:S(2)}) async-start(bf16[4,256,256]{2,1,0:T(8,128)(2,1)} %get-tuple-element.60), calls=%async_computation.3 | async-start | bytes 1048576 | tf_op jit(solution)/shard_map/all_to_all | solution.py:344
  81.5 2.9 %collective-permute-start.11 = (bf16[256,128]{1,0:T(8,128)(2,1)}, bf16[256,128]{1,0:T(8,128)(2,1)S(1)}, u32[]{:S(2)}, u32[]{:S(2)}) collective-permute-start(bf16[256,128]{1,0:T(8,128)(2,1)} %copy-done.14), channel_id=1, source_target_pairs={{0,16},{2,18},{4,20},{6,22},{8,24},{10,26},{12,28},{14,30},{16,0},... | collective-permute-start | bytes 196616 | tf_op jit(solution)/shard_map/ppermute | solution.py:338
  84.4 1.0 %copy-done.24 = bf16[2,216,512]{2,1,0:T(8,128)(2,1)S(1)} copy-done((bf16[2,216,512]{2,1,0:T(8,128)(2,1)S(1)}, bf16[2,216,512]{2,1,0:T(8,128)(2,1)}, u32[]{:S(2)}) %copy-start.24) | copy-done | bytes 442392
  85.4 3.1 %shard_map.150 = (bf16[12,12,4,512]{3,2,1,0:T(4,128)(2,1)}, bf16[12,12,4,512]{3,2,1,0:T(4,128)(2,1)}, f32[8,128]{1,0:T(8,128)S(1)}) custom-call(bf16[12,12,4,512]{3,2,1,0:T(4,128)(2,1)S(1)} %copy-done.3, bf16[12,12,4,512]{3,2,1,0:T(4,128)(2,1)S(1)} %copy-done.6, f32[1,512]{1,0:T(1,128)S(1)} %bitcast.10, bf16[2,216,512]{2,1,0:T(8,128)(2,1)S(1)} %copy-done.24, ...), custom_call_target="tpu_custom_call" | custom-call | flops 30000001024 | tf_op jit(solution)/shard_map/pallas_call | solution.py:60
  88.5 1.5 %shard_map.157 = (f32[2,2,4,3312]{3,2,1,0:T(4,128)}, f32[8,128]{1,0:T(8,128)S(1)}) custom-call(s32[2]{0:T(128)S(1)} %pad_add_fusion.refs_0_, bf16[256,128]{1,0:T(8,128)(2,1)S(1)} %copy-done.15, bf16[256,128]{1,0:T(8,128)(2,1)S(1)} %collective-permute-done.11.refs_2_, f32[8,128]{1,0:T(8,128)S(1)} %get-tuple-element.62.refs_3_), custom_call_target="tpu_custom_call" | custom-call | flops 1000000000 | tf_op jit(solution)/shard_map/pallas_call | solution.py:60
  90.0 2.3 %collective-permute-start.15 = (bf16[1024,256]{1,0:T(8,128)(2,1)S(1)}, bf16[1024,256]{1,0:T(8,128)(2,1)S(1)}, u32[]{:S(2)}, u32[]{:S(2)}) collective-permute-start(bf16[1024,256]{1,0:T(8,128)(2,1)S(1)} %bitcast.6), channel_id=1, source_target_pairs={{0,16},{2,18},{4,20},{6,22},{8,24},{10,26},{12,28},{14,30},{16,0},... | collective-permute-start | bytes 1572872 | tf_op jit(solution)/shard_map/ppermute | solution.py:338
  92.3 1.2 %shard_map.158.refs_0_ = f32[8,512]{1,0:T(8,128)S(1)} custom-call(s32[2]{0:T(128)S(1)} %pad_add_fusion.refs_0_, bf16[1024,256]{1,0:T(8,128)(2,1)S(1)} %bitcast.7, bf16[3,512,256]{2,1,0:T(8,128)(2,1)S(1)} %copy-done, f32[8,128]{1,0:T(8,128)S(1)} %get-tuple-element.63.refs_3_), custom_call_target="tpu_custom_call" | custom-call | flops 30000001024 | tf_op jit(solution)/shard_map/pallas_call | solution.py:60
  93.5 0.1 collective-permute-start.14
  93.6 1.2 %collective-permute-start.13 = (f32[8,512]{1,0:T(8,128)S(1)}, f32[8,512]{1,0:T(8,128)S(1)}, u32[]{:S(2)}, u32[]{:S(2)}) collective-permute-start(f32[8,512]{1,0:T(8,128)S(1)} %shard_map.158.refs_0_), channel_id=1, source_target_pairs={{0,1},{1,0},{2,3},{3,2},{4,5},{5,4},{6,7},{7,6},{8,9},{9,8},{10,11... | collective-permute-start | bytes 49160 | tf_op jit(solution)/shard_map/ppermute | solution.py:354
  94.9 0.8 collective-permute-start.12
  95.7 1.9 %shard_map.159 = (f32[8,128]{1,0:T(8,128)S(1)}, f32[3,512,256]{2,1,0:T(8,128)}, f32[256,512]{1,0:T(8,128)}) custom-call(s32[2]{0:T(128)S(1)} %pad_add_fusion.refs_0_, bf16[1024,256]{1,0:T(8,128)(2,1)S(1)} %bitcast.8, bf16[1024,256]{1,0:T(8,128)(2,1)S(1)} %collective-permute-done.15.refs_2_), custom_call_target="tpu_custom_call" | custom-call | flops 2000000000 | tf_op jit(solution)/shard_map/pallas_call | solution.py:60
  97.6 0.6 shard_map.160
  (59 shorter events, 0.3 us)
Async XLA Ops:
  0.6 1.1 %copy-start.1 = (bf16[12,12,4,512]{3,2,1,0:T(4,128)(2,1)S(1)}, bf16[12,12,4,512]{3,2,1,0:T(4,128)(2,1)}, u32[]{:S(2)}) copy-start(bf16[12,12,4,512]{3,2,1,0:T(4,128)(2,1)} %refs_0_.3) | copy-start | bytes 1769476
  1.7 1.1 %copy-start.4 = (bf16[12,12,4,512]{3,2,1,0:T(4,128)(2,1)S(1)}, bf16[12,12,4,512]{3,2,1,0:T(4,128)(2,1)}, u32[]{:S(2)}) copy-start(bf16[12,12,4,512]{3,2,1,0:T(4,128)(2,1)} %refs_1_.7) | copy-start | bytes 1769476
  2.8 12.3 %copy-start.7 = (bf16[256,512]{1,0:T(8,128)(2,1)S(1)}, bf16[256,512]{1,0:T(8,128)(2,1)}, u32[]{:S(2)}) copy-start(bf16[256,512]{1,0:T(8,128)(2,1)} %refs_2_.6) | copy-start | bytes 786436
  2.8 12.3 %copy-start.11 = (f32[2,2,4,3312]{3,2,1,0:T(4,128)S(1)}, f32[2,2,4,3312]{3,2,1,0:T(4,128)}, u32[]{:S(2)}) copy-start(f32[2,2,4,3312]{3,2,1,0:T(4,128)} %refs_1_.5) | copy-start | bytes 635908
  2.8 12.3 %copy-start.20 = (bf16[276,276]{1,0:T(8,128)(2,1)S(1)}, bf16[276,276]{1,0:T(8,128)(2,1)}, u32[]{:S(2)}) copy-start(bf16[276,276]{1,0:T(8,128)(2,1)} %constant.36.clone.refs_2_) | copy-start | bytes 457060
  2.9 15.7 %collective-permute-start = (bf16[2,216,512]{2,1,0:T(8,128)(2,1)S(1)}, bf16[2,216,512]{2,1,0:T(8,128)(2,1)S(1)}, u32[]{:S(2)}, u32[]{:S(2)}) collective-permute-start(bf16[2,216,512]{2,1,0:T(8,128)(2,1)S(1)} %get-tuple-element.37), channel_id=1, source_target_pairs={{0,240},{1,241},{2,242},{3,243},{4,244},{5,245},{6,246},{7,247},{8... | collective-permute-start | bytes 1327112 | tf_op jit(solution)/shard_map/ppermute | solution.py:332
  6.1 11.8 %collective-permute-start.1 = (bf16[2,72,512]{2,1,0:T(8,128)(2,1)S(1)}, bf16[2,72,512]{2,1,0:T(8,128)(2,1)S(1)}, u32[]{:S(2)}, u32[]{:S(2)}) collective-permute-start(bf16[2,72,512]{2,1,0:T(8,128)(2,1)S(1)} %get-tuple-element.38), channel_id=1, source_target_pairs={{0,15},{1,14},{2,1},{3,0},{4,3},{5,2},{6,5},{7,4},{8,7},{9,6},{10,... | collective-permute-start | bytes 442376 | tf_op jit(solution)/shard_map/ppermute | solution.py:332
  9.3 9.2 %collective-permute-start.2 = (bf16[2,72,512]{2,1,0:T(8,128)(2,1)S(1)}, bf16[2,72,512]{2,1,0:T(8,128)(2,1)S(1)}, u32[]{:S(2)}, u32[]{:S(2)}) collective-permute-start(bf16[2,72,512]{2,1,0:T(8,128)(2,1)S(1)} %get-tuple-element.39), channel_id=1, source_target_pairs={{0,255},{1,254},{2,241},{3,240},{4,243},{5,242},{6,245},{7,244},{8... | collective-permute-start | bytes 442376 | tf_op jit(solution)/shard_map/ppermute | solution.py:332
  15.0 3.5 %copy-start = (bf16[3,512,256]{2,1,0:T(8,128)(2,1)S(1)}, bf16[3,512,256]{2,1,0:T(8,128)(2,1)}, u32[]{:S(2)}) copy-start(bf16[3,512,256]{2,1,0:T(8,128)(2,1)} %refs_2_.7) | copy-start | bytes 2359300
  15.1 3.5 %copy-start.2 = (bf16[12,12,4,512]{3,2,1,0:T(4,128)(2,1)S(1)}, bf16[12,12,4,512]{3,2,1,0:T(4,128)(2,1)}, u32[]{:S(2)}) copy-start(bf16[12,12,4,512]{3,2,1,0:T(4,128)(2,1)} %refs_0_.3) | copy-start | bytes 1769476
  15.1 3.5 %copy-start.5 = (bf16[12,12,4,512]{3,2,1,0:T(4,128)(2,1)S(1)}, bf16[12,12,4,512]{3,2,1,0:T(4,128)(2,1)}, u32[]{:S(2)}) copy-start(bf16[12,12,4,512]{3,2,1,0:T(4,128)(2,1)} %refs_1_.7) | copy-start | bytes 1769476
  15.1 3.5 %copy-start.16 = (f32[512]{0:T(512)S(1)}, f32[512]{0:T(512)}, u32[]{:S(2)}) copy-start(f32[512]{0:T(512)} %param.12) | copy-start | bytes 6148
  15.1 3.5 %copy-start.18 = (bf16[576,576]{1,0:T(8,128)(2,1)S(1)}, bf16[576,576]{1,0:T(8,128)(2,1)}, u32[]{:S(2)}) copy-start(bf16[576,576]{1,0:T(8,128)(2,1)} %constant.34.clone.refs_6_) | copy-start | bytes 1990660
  17.8 9.1 %collective-permute-start.3 = (bf16[256,512]{1,0:T(8,128)(2,1)S(1)}, bf16[256,512]{1,0:T(8,128)(2,1)S(1)}, u32[]{:S(2)}, u32[]{:S(2)}) collective-permute-start(bf16[256,512]{1,0:T(8,128)(2,1)S(1)} %get-tuple-element.45), channel_id=1, source_target_pairs={{0,1},{1,0},{2,3},{3,2},{4,5},{5,4},{6,7},{7,6},{8,9},{9,8},{10,11... | collective-permute-start | bytes 786440 | tf_op jit(solution)/shard_map/ppermute | solution.py:354
  18.6 8.4 %copy-start.17 = (bf16[576,576]{1,0:T(8,128)(2,1)S(1)}, bf16[576,576]{1,0:T(8,128)(2,1)}, u32[]{:S(2)}) copy-start(bf16[576,576]{1,0:T(8,128)(2,1)} %constant.35.clone.refs_5_) | copy-start | bytes 1990660
  24.7 3.6 %copy-start.21 = (f32[2304,144]{1,0:T(8,128)}, f32[2304,144]{1,0:T(8,128)S(1)}, u32[]{:S(2)}) copy-start(f32[2304,144]{1,0:T(8,128)S(1)} %get-tuple-element.54.refs_1_) | copy-start | bytes 3981316
  24.7 3.8 %collective-permute-start.8 = (bf16[1024,256]{1,0:T(8,128)(2,1)S(1)}, bf16[1024,256]{1,0:T(8,128)(2,1)S(1)}, u32[]{:S(2)}, u32[]{:S(2)}) collective-permute-start(bf16[1024,256]{1,0:T(8,128)(2,1)S(1)} %get-tuple-element.53), channel_id=1, source_target_pairs={{0,16},{2,18},{4,20},{6,22},{8,24},{10,26},{12,28},{14,30},{16,0},... | collective-permute-start | bytes 1572872 | tf_op jit(solution)/shard_map/ppermute | solution.py:338
  26.9 1.4 %copy-start.9 = (bf16[256,512]{1,0:T(8,128)(2,1)}, bf16[256,512]{1,0:T(8,128)(2,1)S(1)}, u32[]{:S(2)}) copy-start(bf16[256,512]{1,0:T(8,128)(2,1)S(1)} %collective-permute-done.3.refs_6_.refs_3_) | copy-start | bytes 786436
  28.3 4.7 %copy-start.19 = (bf16[2,138,276]{2,1,0:T(8,128)(2,1)S(1)}, bf16[2,138,276]{2,1,0:T(8,128)(2,1)}, u32[]{:S(2)}) copy-start(bf16[2,138,276]{2,1,0:T(8,128)(2,1)} %constant.37.clone.refs_2_) | copy-start | bytes 457060
  28.3 21.3 %collective-permute-start.4 = (bf16[576,768]{1,0:T(8,128)(2,1)S(1)}, bf16[576,768]{1,0:T(8,128)(2,1)S(1)}, u32[]{:S(2)}, u32[]{:S(2)}) collective-permute-start(bf16[576,768]{1,0:T(8,128)(2,1)S(1)} %shard_map.148.refs_0_.refs_2_), channel_id=1, source_target_pairs={{0,1},{1,0},{2,3},{3,2},{4,5},{5,4},{6,7},{7,6},{8,9},{9,8},{10,11... | collective-permute-start | bytes 2654216 | tf_op jit(solution)/shard_map/ppermute | solution.py:354
  29.4 12.7 %all-to-all-start = ((bf16[4,256,256]{2,1,0:T(8,128)(2,1)}), bf16[4,256,256]{2,1,0:T(8,128)(2,1)S(1)}, u32[]{:S(2)}, u32[]{:S(2)}) async-start(bf16[4,256,256]{2,1,0:T(8,128)(2,1)} %bitcast.3), calls=%async_computation | async-start | bytes 1048576 | tf_op jit(solution)/shard_map/all_to_all | solution.py:344
  33.0 1.7 %copy-start.22 = (f32[2304,144]{1,0:T(8,128)S(1)}, f32[2304,144]{1,0:T(8,128)}, u32[]{:S(2)}) copy-start(f32[2304,144]{1,0:T(8,128)} %copy-done.21) | copy-start | bytes 3981316
  36.6 1.4 %collective-permute-start.9 = (bf16[256,128]{1,0:T(8,128)(2,1)S(1)}, bf16[256,128]{1,0:T(8,128)(2,1)S(1)}, u32[]{:S(2)}, u32[]{:S(2)}) collective-permute-start(bf16[256,128]{1,0:T(8,128)(2,1)S(1)} %get-tuple-element.56), channel_id=1, source_target_pairs={{0,16},{2,18},{4,20},{6,22},{8,24},{10,26},{12,28},{14,30},{16,0},... | collective-permute-start | bytes 196616 | tf_op jit(solution)/shard_map/ppermute | solution.py:338
  42.8 13.0 %all-to-all-start.1 = ((bf16[8,32,384]{2,1,0:T(8,128)(2,1)}), bf16[8,32,384]{2,1,0:T(8,128)(2,1)S(1)}, u32[]{:S(2)}, u32[]{:S(2)}) async-start(bf16[8,32,384]{2,1,0:T(8,128)(2,1)} %shard_map.153), calls=%async_computation.1 | async-start | bytes 393216 | tf_op jit(solution)/shard_map/all_to_all | solution.py:350
  49.7 1.0 copy-start.8
  50.6 0.9 copy-start.10
  53.0 0.7 copy-start.12
  53.6 0.8 copy-start.23
  55.9 12.0 %copy-start.13 = (bf16[2,72,512]{2,1,0:T(8,128)(2,1)S(1)}, bf16[2,72,512]{2,1,0:T(8,128)(2,1)}, u32[]{:S(2)}) copy-start(bf16[2,72,512]{2,1,0:T(8,128)(2,1)} %copy-done.12) | copy-start | bytes 442372
  55.9 7.6 %collective-permute-start.10 = (bf16[32,256]{1,0:T(8,128)(2,1)S(1)}, bf16[32,256]{1,0:T(8,128)(2,1)S(1)}, u32[]{:S(2)}, u32[]{:S(2)}) collective-permute-start(bf16[32,256]{1,0:T(8,128)(2,1)S(1)} %get-tuple-element.58.refs_0_), channel_id=1, source_target_pairs={{0,2},{2,0},{4,6},{6,4},{8,10},{10,8},{12,14},{14,12},{16,18},{18,... | collective-permute-start | bytes 49160 | tf_op jit(solution)/shard_map/ppermute | solution.py:338
  60.1 24.2 %collective-permute-start.5 = (bf16[2,216,512]{2,1,0:T(8,128)(2,1)S(1)}, bf16[2,216,512]{2,1,0:T(8,128)(2,1)S(1)}, u32[]{:S(2)}, u32[]{:S(2)}) collective-permute-start(bf16[2,216,512]{2,1,0:T(8,128)(2,1)S(1)} %get-tuple-element.47), channel_id=1, source_target_pairs={{0,16},{1,17},{2,18},{3,19},{4,20},{5,21},{6,22},{7,23},{8,24},{9,... | collective-permute-start | bytes 1327112 | tf_op jit(solution)/shard_map/ppermute | solution.py:332
  64.2 12.3 %all-to-all-start.2 = ((bf16[8,32,384]{2,1,0:T(8,128)(2,1)}), bf16[8,32,384]{2,1,0:T(8,128)(2,1)S(1)}, u32[]{:S(2)}, u32[]{:S(2)}) async-start(bf16[8,32,384]{2,1,0:T(8,128)(2,1)} %shard_map.155), calls=%async_computation.2 | async-start | bytes 393216 | tf_op jit(solution)/shard_map/all_to_all | solution.py:350
  67.9 16.5 %collective-permute-start.6 = (bf16[2,72,512]{2,1,0:T(8,128)(2,1)}, bf16[2,72,512]{2,1,0:T(8,128)(2,1)}, u32[]{:S(2)}, u32[]{:S(2)}) collective-permute-start(bf16[2,72,512]{2,1,0:T(8,128)(2,1)} %get-tuple-element.48), channel_id=1, source_target_pairs={{0,3},{1,2},{2,5},{3,4},{4,7},{5,6},{6,9},{7,8},{8,11},{9,10},{10,... | collective-permute-start | bytes 442376 | tf_op jit(solution)/shard_map/ppermute | solution.py:332
  67.9 16.5 %copy-start.3 = (bf16[12,12,4,512]{3,2,1,0:T(4,128)(2,1)S(1)}, bf16[12,12,4,512]{3,2,1,0:T(4,128)(2,1)}, u32[]{:S(2)}) copy-start(bf16[12,12,4,512]{3,2,1,0:T(4,128)(2,1)} %refs_0_.3) | copy-start | bytes 1769476
  67.9 16.5 %copy-start.6 = (bf16[12,12,4,512]{3,2,1,0:T(4,128)(2,1)S(1)}, bf16[12,12,4,512]{3,2,1,0:T(4,128)(2,1)}, u32[]{:S(2)}) copy-start(bf16[12,12,4,512]{3,2,1,0:T(4,128)(2,1)} %refs_1_.7) | copy-start | bytes 1769476
  67.9 16.4 %collective-permute-start.7 = (bf16[2,72,512]{2,1,0:T(8,128)(2,1)S(1)}, bf16[2,72,512]{2,1,0:T(8,128)(2,1)}, u32[]{:S(2)}, u32[]{:S(2)}) collective-permute-start(bf16[2,72,512]{2,1,0:T(8,128)(2,1)S(1)} %copy-done.13), channel_id=1, source_target_pairs={{0,19},{1,18},{2,21},{3,20},{4,23},{5,22},{6,25},{7,24},{8,27},{9,... | collective-permute-start | bytes 442376 | tf_op jit(solution)/shard_map/ppermute | solution.py:332
  77.3 0.6 copy-start.14
  78.0 12.0 %all-to-all-start.3 = ((bf16[4,256,256]{2,1,0:T(8,128)(2,1)}), bf16[4,256,256]{2,1,0:T(8,128)(2,1)S(1)}, u32[]{:S(2)}, u32[]{:S(2)}) async-start(bf16[4,256,256]{2,1,0:T(8,128)(2,1)} %get-tuple-element.60), calls=%async_computation.3 | async-start | bytes 1048576 | tf_op jit(solution)/shard_map/all_to_all | solution.py:344
  81.5 7.0 %collective-permute-start.11 = (bf16[256,128]{1,0:T(8,128)(2,1)}, bf16[256,128]{1,0:T(8,128)(2,1)S(1)}, u32[]{:S(2)}, u32[]{:S(2)}) collective-permute-start(bf16[256,128]{1,0:T(8,128)(2,1)} %copy-done.14), channel_id=1, source_target_pairs={{0,16},{2,18},{4,20},{6,22},{8,24},{10,26},{12,28},{14,30},{16,0},... | collective-permute-start | bytes 196616 | tf_op jit(solution)/shard_map/ppermute | solution.py:338
  84.4 1.0 %copy-start.24 = (bf16[2,216,512]{2,1,0:T(8,128)(2,1)S(1)}, bf16[2,216,512]{2,1,0:T(8,128)(2,1)}, u32[]{:S(2)}) copy-start(bf16[2,216,512]{2,1,0:T(8,128)(2,1)} %copy-done.23) | copy-start | bytes 1327108
  85.4 3.1 %copy-start.15 = (bf16[256,128]{1,0:T(8,128)(2,1)S(1)}, bf16[256,128]{1,0:T(8,128)(2,1)}, u32[]{:S(2)}) copy-start(bf16[256,128]{1,0:T(8,128)(2,1)} %copy-done.14) | copy-start | bytes 196612
  90.0 5.7 %collective-permute-start.15 = (bf16[1024,256]{1,0:T(8,128)(2,1)S(1)}, bf16[1024,256]{1,0:T(8,128)(2,1)S(1)}, u32[]{:S(2)}, u32[]{:S(2)}) collective-permute-start(bf16[1024,256]{1,0:T(8,128)(2,1)S(1)} %bitcast.6), channel_id=1, source_target_pairs={{0,16},{2,18},{4,20},{6,22},{8,24},{10,26},{12,28},{14,30},{16,0},... | collective-permute-start | bytes 1572872 | tf_op jit(solution)/shard_map/ppermute | solution.py:338
  93.5 4.1 %collective-permute-start.14 = (f32[8,512]{1,0:T(8,128)S(1)}, f32[8,512]{1,0:T(8,128)S(1)}, u32[]{:S(2)}, u32[]{:S(2)}) collective-permute-start(f32[8,512]{1,0:T(8,128)S(1)} %shard_map.158.refs_0_), channel_id=1, source_target_pairs={{0,17},{1,16},{16,1},{17,0},{32,49},{33,48},{48,33},{49,32},{64,81... | collective-permute-start | bytes 49160 | tf_op jit(solution)/shard_map/ppermute | solution.py:359
  93.6 4.0 %collective-permute-start.13 = (f32[8,512]{1,0:T(8,128)S(1)}, f32[8,512]{1,0:T(8,128)S(1)}, u32[]{:S(2)}, u32[]{:S(2)}) collective-permute-start(f32[8,512]{1,0:T(8,128)S(1)} %shard_map.158.refs_0_), channel_id=1, source_target_pairs={{0,1},{1,0},{2,3},{3,2},{4,5},{5,4},{6,7},{7,6},{8,9},{9,8},{10,11... | collective-permute-start | bytes 49160 | tf_op jit(solution)/shard_map/ppermute | solution.py:354
  94.9 2.8 %collective-permute-start.12 = (f32[8,512]{1,0:T(8,128)S(1)}, f32[8,512]{1,0:T(8,128)S(1)}, u32[]{:S(2)}, u32[]{:S(2)}) collective-permute-start(f32[8,512]{1,0:T(8,128)S(1)} %shard_map.158.refs_0_), channel_id=1, source_target_pairs={{0,16},{2,18},{4,20},{6,22},{8,24},{10,26},{12,28},{14,30},{16,0},... | collective-permute-start | bytes 49160 | tf_op jit(solution)/shard_map/ppermute | solution.py:338

commit v7 on v6

--- a/solution.py
+++ b/solution.py
@@ -12,24 +12,23 @@
 OFFS = 23
 NT = (((1,), (1,)), ((), ()))
 TN = (((0,), (0,)), ((), ()))
-SECTIONS = (0, 216, 432, 504, 576)
 
 
 def section_row(lon, lat, lev):
-    lat_cells = 9 if lat < 9 else 3
-    return (lon >= 6) + 2 * (lat >= 9), (lon % 6 * lat_cells + lat % 9) * 4 + lev
+    if lat < 6:
+        return (lon >= 6) * 144 + (lon % 6 * 6 + lat) * 4 + lev
+    return (lat >= 9) * 144 + (lon >= 6) * 72 + (lon % 6 * 3 + lat % 3) * 4 + lev
 
 
 def placement():
-    place = np.zeros((576, 576), np.float32)
+    place = np.zeros((2, 288, 288), np.float32)
     for a in range(2):
         for b in range(2):
             for p in range(12):
                 for s in range(2):
                     for r in range(6):
-                        row = (a * 2 + b) * WTOK + p * 12 + s * 6 + r
-                        section, at = section_row(p, a * 6 + r, (b * 2 + s + 1) % 4)
-                        place[row, SECTIONS[section] + at] = 1
+                        row = b * WTOK + p * 12 + s * 6 + r
+                        place[a, row, section_row(p, a * 6 + r, (b * 2 + s + 1) % 4)] = 1
     return place
 
 
@@ -74,14 +73,23 @@
 TOKEN = ((8, 128), F32)
 
 
-LOW_LON, LOW_LAT, HIGH_LON, HIGH_LAT = slice(0, 6), slice(0, 3), slice(6, 12), slice(3, 12)
-PLACES = ((HIGH_LON, HIGH_LAT), (LOW_LON, HIGH_LAT), (HIGH_LON, LOW_LAT), (LOW_LON, LOW_LAT))
+LOW_LON, LOW_LAT, HIGH_LON, MID_LAT, HIGH_LAT = slice(0, 6), slice(0, 3), slice(6, 12), slice(3, 9), slice(9, 12)
+PLACES = (
+    ((HIGH_LON, MID_LAT), (HIGH_LON, HIGH_LAT)),
+    ((LOW_LON, MID_LAT), (LOW_LON, HIGH_LAT)),
+    ((HIGH_LON, LOW_LAT),),
+    ((LOW_LON, LOW_LAT),),
+)
+
+
+def flat(tile):
+    return tile.reshape(-1, tile.shape[-1])
 
 
 def halo_kernel(latent, cot, *outs):
-    for (lon, lat), ref in zip(PLACES[1:], outs):
+    for places, ref in zip(PLACES[1:], outs):
         for j, grid in enumerate((latent, cot)):
-            ref[j] = grid[lon, lat].reshape(ref.shape[1:])
+            ref[j] = jnp.concatenate([flat(grid[lon, lat]) for lon, lat in places], 0)
 
 
 def bias_kernel(info, table, order, w_out, bias, w_copy, raw, entries, low_u, high_u):
@@ -122,10 +130,15 @@
 def main_kernel(info, latent, cotangent, lon, lat, cor, place, gain, w_qkv, w_out, bias,
                 keep, send, o_ds, att_s, gq_s, gk_s, gv_s, joined):
     def gathered(which):
-        own = (latent, cotangent)[which][HIGH_LON, HIGH_LAT].reshape(216, 512)
-        for j, rows in enumerate((own, lon[which], lat[which], cor[which])):
-            joined[SECTIONS[j] : SECTIONS[j + 1], :] = rows.astype(F32)
-        return dot(place[...], joined[...].astype(BF))
+        grid = (latent, cotangent)[which]
+        beside = lon[which].astype(F32)
+        parts = (flat(grid[HIGH_LON, MID_LAT]), beside[0:144], flat(grid[HIGH_LON, HIGH_LAT]), beside[144:216])
+        start = 0
+        for rows in (*parts, lat[which], cor[which]):
+            joined[start : start + rows.shape[0], :] = rows.astype(F32)
+            start += rows.shape[0]
+        rows = joined[...].astype(BF)
+        return jnp.concatenate([dot(place[a], rows[a * 288 : (a + 1) * 288]) for a in range(2)], 0)
 
     values = gathered(0)
     cot = gathered(1).astype(BF)
@@ -174,24 +187,43 @@
 
 def terms_kernel(att, gq, gk, gv, w_qkv, back, terms):
     hid_part = dot(gq[...], w_qkv[0], NT) + dot(gk[...], w_qkv[1], NT) + dot(gv[...], w_qkv[2], NT)
-    terms[:, 0:256] = dot(back[...], att[...]).astype(BF)
-    terms[:, 256:768] = dot(back[...], hid_part.astype(BF)).astype(BF)
-
-
-def core_sum_kernel(keep, recv, total):
-    total[...] = (keep[...] + recv[...].astype(F32)).astype(BF)
-
-
-def y_sum_kernel(parts, b_keep, b_recv, message):
-    total = parts[0].astype(F32)
-    for j in range(1, 4):
-        total = total + parts[j].astype(F32)
-    total = total.astype(BF)
-    both = (b_keep[...].astype(F32) + b_recv[...].astype(F32)).astype(BF)
+    hid_part = hid_part.astype(BF)
+    for a in range(2):
+        rows = slice(a * 288, (a + 1) * 288)
+        terms[rows, 0:256] = dot(back[a], att[rows, :]).astype(BF)
+        terms[rows, 256:768] = dot(back[a], hid_part[rows]).astype(BF)
+
+
+def sent(copies, source, target, sem):
+    copies.append(pltpu.make_async_copy(source, target, sem))
+    copies[-1].start()
+
+
+def finish(copies):
+    for copy in copies:
+        copy.wait()
+
+
+def core_sum_kernel(keep, recv, total, held, sems):
+    copies = []
+    for k in range(4):
+        rows = slice(k * 256, (k + 1) * 256)
+        held[k] = (keep[rows, :] + recv[rows, :].astype(F32)).astype(BF)
+        sent(copies, held.at[k], total.at[k], sems.at[k])
+    finish(copies)
+
+
+def y_sum_kernel(parts, b_keep, b_recv, message, held, sems):
+    copies = []
     for j in range(8):
         rows = slice(j * 32, (j + 1) * 32)
-        message[j, :, 0:256] = total[rows]
-        message[j, :, 256:384] = both[rows]
+        total = parts[0, rows, :].astype(F32)
+        for k in range(1, 4):
+            total = total + parts[k, rows, :].astype(F32)
+        held[j, :, 0:256] = total.astype(BF)
+        held[j, :, 256:384] = (b_keep[rows, :].astype(F32) + b_recv[rows, :].astype(F32)).astype(BF)
+        sent(copies, held.at[j], message.at[j], sems.at[j])
+    finish(copies)
 
 
 def z_sum_kernel(parts, mine, bias):
@@ -202,11 +234,13 @@
     bias[...] = total[:, 256:384].astype(BF)
 
 
-def x_sum_kernel(mine, recv, bias, copies):
-    total = (mine[...].astype(F32) + recv[...].astype(F32)).astype(BF)
+def x_sum_kernel(mine, recv, bias, out, held, sems):
+    held[:, 0:256] = (mine[...].astype(F32) + recv[...].astype(F32)).astype(BF)
+    held[:, 256:384] = bias[...]
+    copies = []
     for j in range(8):
-        copies[j, :, 0:256] = total
-        copies[j, :, 256:384] = bias[...]
+        sent(copies, held, out.at[j], sems.at[j])
+    finish(copies)
 
 
 def pair_kernel(terms, others, w_out, w_other, o_own, o_lon, o_lat, o_cor, token):
@@ -214,26 +248,33 @@
     out = dot(terms[:, 0:256], w_out[...]).astype(BF).astype(F32)
     out = out + dot(others[:, 0:256], w_other[...]).astype(BF).astype(F32)
     hid = terms[:, 256:768].astype(F32) + others[:, 256:768].astype(F32)
-    for k, ref in enumerate((o_own, o_lon, o_lat, o_cor)):
-        rows = slice(SECTIONS[k], SECTIONS[k + 1])
-        ref[0] = out[rows].astype(BF)
-        ref[1] = hid[rows].astype(BF)
-
-
-def spread_kernel(parts, copies, b_half):
+    for j, rows in enumerate((out, hid)):
+        o_own[j] = jnp.concatenate([rows[0:144], rows[288:360]], 0).astype(BF)
+        o_lon[j] = jnp.concatenate([rows[144:288], rows[360:432]], 0).astype(BF)
+        o_lat[j] = rows[432:504].astype(BF)
+        o_cor[j] = rows[504:576].astype(BF)
+
+
+def spread_kernel(parts, b_half, out, held, sems):
     for j in range(8):
         rows = slice(j * 32, (j + 1) * 32)
-        for k in range(4):
-            copies[k, rows, :] = parts[j, :, 0:256]
+        held[rows, :] = parts[j, :, 0:256]
         b_half[rows, :] = parts[j, :, 256:384]
+    copies = []
+    for k in range(4):
+        sent(copies, held, out.at[k], sems.at[k])
+    finish(copies)
 
 
 def gain_kernel(info, mine, w_qkv, out):
     rows = mine[...].astype(F32)
     w0, w1, w2 = [w_qkv[j].astype(F32) for j in range(3)]
     total = jnp.where(info[1] == 0, rows[:512] * w0 + rows[512:] * w1, rows[:512] * w2)
-    ones = jnp.ones((8, 256), F32)
-    out[...] = lax.dot_general(ones, total, NT, precision=lax.Precision.HIGHEST, preferred_element_type=F32)
+    total = total[:, 0:128] + total[:, 128:256]
+    high = total.astype(BF)
+    low = (total - high.astype(F32)).astype(BF)
+    ones = jnp.ones((8, 128), BF)
+    out[...] = dot(ones, high, NT) + dot(ones, low, NT)
 
 
 def gain_sum_kernel(mine, other, mine_tp, other_tp, gain, out):
@@ -304,20 +345,32 @@
     send[...] = jnp.where(info[1] == 0, other, mine).astype(BF)
 
 
-def final_kernel(latent, cot, gain, own, lon, lat, cor, output, grad, token):
+def final_kernel(latent, cot, gain, own, lon, lat, cor, token, output, grad, held, sems):
     token[...] = jnp.zeros_like(token)
-    for (by_lon, by_lat), ref in zip(PLACES, (own, lon, lat, cor)):
-        out_term, hid_term = ref[0].astype(F32), ref[1].astype(F32)
-        tile = latent[by_lon, by_lat]
-        values = tile.reshape(out_term.shape).astype(F32)
-        output[by_lon, by_lat] = (values + out_term).astype(BF).reshape(tile.shape)
-        shifted = values - jnp.mean(values, -1, keepdims=True)
-        inv_std = lax.rsqrt(jnp.mean(shifted * shifted, -1, keepdims=True) + 1e-05)
-        normed = shifted * inv_std
-        scaled = hid_term * gain[...]
-        inner = scaled - jnp.mean(scaled, -1, keepdims=True) - normed * jnp.mean(scaled * normed, -1, keepdims=True)
-        above = cot[by_lon, by_lat].reshape(out_term.shape).astype(F32)
-        grad[by_lon, by_lat] = (above + inv_std * inner).astype(BF).reshape(tile.shape)
+    copies = []
+    for k in (1, 3, 0, 2):
+        ref = (own, lon, lat, cor)[k]
+        out_terms, hid_terms = ref[0].astype(F32), ref[1].astype(F32)
+        start = 0
+        for by_lon, by_lat in PLACES[k]:
+            tile = latent[by_lon, by_lat]
+            values = flat(tile).astype(F32)
+            rows = slice(start, start + values.shape[0])
+            start += values.shape[0]
+            held[0, by_lon, by_lat] = (values + out_terms[rows]).astype(BF).reshape(tile.shape)
+            shifted = values - jnp.mean(values, -1, keepdims=True)
+            inv_std = lax.rsqrt(jnp.mean(shifted * shifted, -1, keepdims=True) + 1e-05)
+            normed = shifted * inv_std
+            scaled = hid_terms[rows] * gain[...]
+            inner = scaled - jnp.mean(scaled, -1, keepdims=True) - normed * jnp.mean(scaled * normed, -1, keepdims=True)
+            above = flat(cot[by_lon, by_lat]).astype(F32)
+            held[1, by_lon, by_lat] = (above + inv_std * inner).astype(BF).reshape(tile.shape)
+        if k >= 2:
+            for j, ref in enumerate((output, grad)):
+                for first in (0, 3):
+                    rows = pl.ds(first + (6 if k == 2 else 0), 3)
+                    sent(copies, held.at[j, rows], ref.at[rows], sems.at[len(copies)])
+    finish(copies)
 
 
 def moved(value, by_lon, by_lat):
@@ -360,7 +413,7 @@
 
 
 def on_device(latent, cotangent, ln_gain, w_qkv, w_out, bias_table):
-    place, back = jnp.asarray(TO_WINDOW, BF), jnp.asarray(TO_WINDOW.T, BF)
+    place, back = jnp.asarray(TO_WINDOW, BF), jnp.asarray(TO_WINDOW.transpose(0, 2, 1), BF)
     order = jnp.asarray(ORDER, BF)
     order_halves = jnp.asarray(ORDER.reshape(2, 138, 276), BF)
     i_lon, i_lat = lax.axis_index("lon"), lax.axis_index("lat")
@@ -398,8 +451,17 @@
         pair_kernel, [part(216)] + halos + [TOKEN], [terms, others, w_out, w_other], smem=0, us=30
     )
 
-    (total,) = call(core_sum_kernel, [((1024, 256), BF)], [keep, recv], smem=0, after=[terms], us=0.5)
-    parts = across_y(total.reshape(4, 256, 256))
+    (total,) = call(
+        core_sum_kernel,
+        [],
+        [keep, recv],
+        [pltpu.VMEM((4, 256, 256), BF), pltpu.SemaphoreType.DMA((4,))],
+        smem=0,
+        after=[terms],
+        us=0.5,
+        hbm_outs=[((4, 256, 256), BF)],
+    )
+    parts = across_y(total)
     b_keep, b_send = call(
         bias_grad_kernel,
         [((256, 128), BF)] * 2,
@@ -409,27 +471,44 @@
         us=2.5,
     )
     b_recv = swapped(b_send, 1, 0)
-    (message,) = call(y_sum_kernel, [((8, 32, 384), BF)], [parts, b_keep, b_recv], smem=0, us=1)
+    (message,) = call(
+        y_sum_kernel,
+        [],
+        [parts, b_keep, b_recv],
+        [pltpu.VMEM((8, 32, 384), BF), pltpu.SemaphoreType.DMA((8,))],
+        smem=0,
+        hbm_outs=[((8, 32, 384), BF)],
+    )
     x_mine, b_sum = call(
         z_sum_kernel, [((32, 256), BF), ((32, 128), BF)], [across_z(message)], smem=0, after=[paired], us=1
     )
-    (copies,) = call(x_sum_kernel, [((8, 32, 384), BF)], [x_mine, swapped(x_mine, 0, 1), b_sum], smem=0, us=1)
+    (copies,) = call(
+        x_sum_kernel,
+        [],
+        [x_mine, swapped(x_mine, 0, 1), b_sum],
+        [pltpu.VMEM((32, 384), BF), pltpu.SemaphoreType.DMA((8,))],
+        smem=0,
+        hbm_outs=[((8, 32, 384), BF)],
+    )
     r_lon, r_lat, r_cor = moved(s_lon, 1, 0), moved(s_lat, 0, 1), moved(s_cor, 1, 1)
 
-    output, grad_latent, placed = call(
+    placed, output, grad_latent = call(
         final_kernel,
-        [(latent.shape, BF), (latent.shape, BF), TOKEN],
+        [TOKEN],
         [latent, cotangent, gain, own, r_lon, r_lat, r_cor],
+        [pltpu.VMEM((2,) + latent.shape, BF), pltpu.SemaphoreType.DMA((8,))],
+        hbm_outs=[(latent.shape, BF)] * 2,
         smem=0,
         us=30,
     )
 
-    copies, b_half = call(
+    b_half, copies = call(
         spread_kernel,
-        [((4, 256, 256), BF), ((256, 128), BF)],
+        [((256, 128), BF)],
         [across_z(copies)],
+        [pltpu.VMEM((256, 256), BF), pltpu.SemaphoreType.DMA((4,))],
         smem=0,
-        us=1,
+        hbm_outs=[((4, 256, 256), BF)],
     )
     mine = across_y(copies).reshape(1024, 256)
     b_other = swapped(b_half, 1, 0)

time: 98.9 us -> 98.1 us (level)
  transfers between devices with their start and end apart: 20 -> 20, of which waited for: 6 -> 7; matrix products, arithmetic and copies ran while one was open for 0% -> 0% of each run, Pallas kernels for 25% -> 24%
where the time goes in v7:
time: 98.1 us; the launch traced here: 97.4 us
  starting transfers between devices  50.4 us (51%)
  Pallas kernels  24.3 us (25%)
  waiting for transfers between devices  12.8 us (13%)
  local copies, waits for them, and re-layouts  8.82 us (9%)
  between operations  1.01 us (1%)
    pallas_call x16, Pallas kernels, call(): pl.pallas_call(kernel, out_shape=[jax.ShapeDtypeStruct(s, t) for s, t in...  24.3 us
    ppermute x6, starting transfers between devices, moved(): return lax.ppermute(value, ('lon', 'lat', 'tp'), pairs)  20.9 us
    ppermute x6, starting transfers between devices, swapped(): return lax.ppermute(value, ('lon', 'lat'), pairs)  12.6 us
    unnamed x50, local copies, waits for them, and re-layouts  8.82 us
    all_to_all x2, starting transfers between devices, across_z(): return lax.all_to_all(value, 'lon', 0, 0, axis_index_groups=groups)  8.25 us
    all_to_all x2, starting transfers between devices, across_y(): return lax.all_to_all(value, 'lat', 0, 0, axis_index_groups=groups)  7.14 us
    all_to_all x2, waiting for transfers between devices, across_z(): return lax.all_to_all(value, 'lon', 0, 0, axis_index_groups=groups)  4.86 us
    all_to_all x2, waiting for transfers between devices, across_y(): return lax.all_to_all(value, 'lat', 0, 0, axis_index_groups=groups)  4.07 us
  transfers between devices with their start and end apart: 20, of which 7 were waited for; matrix products, arithmetic and copies ran while one was open for 0% of the time, Pallas kernels for 24%

profile of v7, /device:TPU:1, one launch (start us, length us, event | category | flops | bytes accessed | tf_op | source)
XLA Modules:
  0.0 97.4 jit_solution(7777080453778604687)
XLA Ops:
  0.6 1.1 %copy-done.1 = bf16[12,12,4,512]{3,2,1,0:T(4,128)(2,1)S(1)} copy-done((bf16[12,12,4,512]{3,2,1,0:T(4,128)(2,1)S(1)}, bf16[12,12,4,512]{3,2,1,0:T(4,128)(2,1)}, u32[]{:S(2)}) %copy-start.1) | copy-done | bytes 589848
  1.7 1.1 %copy-done.4 = bf16[12,12,4,512]{3,2,1,0:T(4,128)(2,1)S(1)} copy-done((bf16[12,12,4,512]{3,2,1,0:T(4,128)(2,1)S(1)}, bf16[12,12,4,512]{3,2,1,0:T(4,128)(2,1)}, u32[]{:S(2)}) %copy-start.4) | copy-done | bytes 589848
  2.9 3.3 %collective-permute-start = (bf16[2,216,512]{2,1,0:T(8,128)(2,1)S(1)}, bf16[2,216,512]{2,1,0:T(8,128)(2,1)S(1)}, u32[]{:S(2)}, u32[]{:S(2)}) collective-permute-start(bf16[2,216,512]{2,1,0:T(8,128)(2,1)S(1)} %get-tuple-element.37), channel_id=1, source_target_pairs={{0,240},{1,241},{2,242},{3,243},{4,244},{5,245},{6,246},{7,247},{8... | collective-permute-start | bytes 1327112 | tf_op jit(solution)/shard_map/ppermute | solution.py:385
  6.1 3.2 %collective-permute-start.1 = (bf16[2,72,512]{2,1,0:T(8,128)(2,1)S(1)}, bf16[2,72,512]{2,1,0:T(8,128)(2,1)S(1)}, u32[]{:S(2)}, u32[]{:S(2)}) collective-permute-start(bf16[2,72,512]{2,1,0:T(8,128)(2,1)S(1)} %get-tuple-element.38), channel_id=1, source_target_pairs={{0,15},{1,14},{2,1},{3,0},{4,3},{5,2},{6,5},{7,4},{8,7},{9,6},{10,... | collective-permute-start | bytes 442376 | tf_op jit(solution)/shard_map/ppermute | solution.py:385
  9.3 5.7 %collective-permute-start.2 = (bf16[2,72,512]{2,1,0:T(8,128)(2,1)S(1)}, bf16[2,72,512]{2,1,0:T(8,128)(2,1)S(1)}, u32[]{:S(2)}, u32[]{:S(2)}) collective-permute-start(bf16[2,72,512]{2,1,0:T(8,128)(2,1)S(1)} %get-tuple-element.39), channel_id=1, source_target_pairs={{0,255},{1,254},{2,241},{3,240},{4,243},{5,242},{6,245},{7,244},{8... | collective-permute-start | bytes 442376 | tf_op jit(solution)/shard_map/ppermute | solution.py:385
  15.1 2.7 %shard_map.146 = (f32[2304,144]{1,0:T(8,128)S(1)}, bf16[256,512]{1,0:T(8,128)(2,1)S(1)}) custom-call(s32[2]{0:T(128)S(1)} %pad_add_fusion.refs_0_, f32[2,2,4,3312]{3,2,1,0:T(4,128)S(1)} %copy-done.11, bf16[276,276]{1,0:T(8,128)(2,1)S(1)} %copy-done.20, bf16[256,512]{1,0:T(8,128)(2,1)S(1)} %copy-done.7), custom_call_target="tpu_custom_call" | custom-call | flops 2000000000 | tf_op jit(solution)/shard_map/pallas_call | solution.py:59
  17.8 0.1 collective-permute-start.3
  17.9 0.6 collective-permute-done.2.refs_5_
  18.6 5.8 %shard_map.147 = (f32[1024,256]{1,0:T(8,128)S(1)}, bf16[1024,256]{1,0:T(8,128)(2,1)S(1)}, f32[2304,144]{1,0:T(8,128)S(1)}, bf16[576,256]{1,0:T(8,128)(2,1)S(1)},...) custom-call(s32[2]{0:T(128)S(1)} %pad_add_fusion.refs_0_, ...), custom_call_target="tpu_custom_call" | custom-call | flops 8999999488 | tf_op jit(solution)/shard_map/pallas_call | solution.py:59
  24.4 2.2 %collective-permute-start.8 = (bf16[1024,256]{1,0:T(8,128)(2,1)S(1)}, bf16[1024,256]{1,0:T(8,128)(2,1)S(1)}, u32[]{:S(2)}, u32[]{:S(2)}) collective-permute-start(bf16[1024,256]{1,0:T(8,128)(2,1)S(1)} %get-tuple-element.53), channel_id=1, source_target_pairs={{0,16},{2,18},{4,20},{6,22},{8,24},{10,26},{12,28},{14,30},{16,0},... | collective-permute-start | bytes 1572872 | tf_op jit(solution)/shard_map/ppermute | solution.py:391
  26.6 1.1 %shard_map.148.refs_0_.refs_2_ = bf16[576,768]{1,0:T(8,128)(2,1)S(1)} custom-call(bf16[576,256]{1,0:T(8,128)(2,1)S(1)} %get-tuple-element.41.refs_0_, bf16[576,256]{1,0:T(8,128)(2,1)S(1)} %get-tuple-element.42.refs_1_, bf16[576,256]{1,0:T(8,128)(2,1)S(1)} %get-tuple-element.43.refs_2_, bf16[576,256]{1,0:T(8,128)(2,1)S(1)} %get-tuple-element.44.refs_3_, ...), custom_call_target="tpu_custom_call" | custom-call | flops 2000000000 | tf_op jit(solution)/shard_map/pallas_call | solution.py:59
  27.8 0.1 collective-permute-start.4
  27.9 0.3 collective-permute-done.8.refs_1_
  28.1 0.8 shard_map.151
  29.0 3.7 %all-to-all-start = ((bf16[4,256,256]{2,1,0:T(8,128)(2,1)}), bf16[4,256,256]{2,1,0:T(8,128)(2,1)S(1)}, u32[]{:S(2)}, u32[]{:S(2)}) async-start(bf16[4,256,256]{2,1,0:T(8,128)(2,1)} %shard_map.151), calls=%async_computation | async-start | bytes 1048576 | tf_op jit(solution)/shard_map/all_to_all | solution.py:397
  32.7 1.7 %copy-done.22 = f32[2304,144]{1,0:T(8,128)S(1)} copy-done((f32[2304,144]{1,0:T(8,128)S(1)}, f32[2304,144]{1,0:T(8,128)}, u32[]{:S(2)}) %copy-start.22) | copy-done | bytes 1327128
  34.3 1.9 %shard_map.152 = (bf16[256,128]{1,0:T(8,128)(2,1)S(1)}, bf16[256,128]{1,0:T(8,128)(2,1)S(1)}) custom-call(s32[2]{0:T(128)S(1)} %pad_add_fusion.refs_0_, f32[2304,144]{1,0:T(8,128)S(1)} %copy-done.22, bf16[2,138,276]{2,1,0:T(8,128)(2,1)S(1)} %copy-done.19), custom_call_target="tpu_custom_call" | custom-call | flops 2500000000 | tf_op jit(solution)/shard_map/pallas_call | solution.py:59
  36.2 0.5 collective-permute-start.9
  36.7 0.9 collective-permute-done.9.refs_2_
  37.6 4.1 %all-to-all-done.refs_0_ = bf16[4,256,256]{2,1,0:T(8,128)(2,1)S(1)} async-done(((bf16[4,256,256]{2,1,0:T(8,128)(2,1)}), bf16[4,256,256]{2,1,0:T(8,128)(2,1)S(1)}, u32[]{:S(2)}, u32[]{:S(2)}) %all-to-all-start) | async-done | bytes 524320 | tf_op jit(solution)/shard_map/all_to_all | solution.py:397
  41.7 0.8 shard_map.153
  42.4 4.6 %all-to-all-start.1 = ((bf16[8,32,384]{2,1,0:T(8,128)(2,1)}), bf16[8,32,384]{2,1,0:T(8,128)(2,1)S(1)}, u32[]{:S(2)}, u32[]{:S(2)}) async-start(bf16[8,32,384]{2,1,0:T(8,128)(2,1)} %shard_map.153), calls=%async_computation.1 | async-start | bytes 393216 | tf_op jit(solution)/shard_map/all_to_all | solution.py:403
  47.0 2.1 %collective-permute-done.4.refs_1_ = bf16[576,768]{1,0:T(8,128)(2,1)S(1)} collective-permute-done((bf16[576,768]{1,0:T(8,128)(2,1)S(1)}, bf16[576,768]{1,0:T(8,128)(2,1)S(1)}, u32[]{:S(2)}, u32[]{:S(2)}) %collective-permute-start.4) | collective-permute-done | bytes 884768 | tf_op jit(solution)/shard_map/ppermute | solution.py:407
  49.1 0.9 copy-done.8
  50.0 0.9 copy-done.10
  51.0 1.4 %shard_map.149 = (bf16[2,216,512]{2,1,0:T(8,128)(2,1)S(1)}, bf16[2,216,512]{2,1,0:T(8,128)(2,1)S(1)}, bf16[2,72,512]{2,1,0:T(8,128)(2,1)}, bf16[2,72,512]{2,1,0:T(8,128)(2,1)S(1)}, f32[8,128]{1,0:T(8,128)S(1)}) custom-call(bf16[576,768]{1,0:T(8,128)(2,1)S(1)} %shard_map.148.refs_0_.refs_2_, bf16[576,768]{1,0:T(8,128)(2,1)S(1)} %collective-permute-done.4.refs_1_, ...), custom_call_target="tpu_custom_call" | custom-call | flops 30000001024 | tf_op jit(solution)/shard_map/pallas_call | solution.py:59
  52.4 0.7 copy-done.12
  53.1 0.8 copy-done.23
  53.8 1.7 %all-to-all-done.1.refs_0_ = bf16[8,32,384]{2,1,0:T(8,128)(2,1)S(1)} async-done(((bf16[8,32,384]{2,1,0:T(8,128)(2,1)}), bf16[8,32,384]{2,1,0:T(8,128)(2,1)S(1)}, u32[]{:S(2)}, u32[]{:S(2)}) %all-to-all-start.1) | async-done | bytes 196640 | tf_op jit(solution)/shard_map/all_to_all | solution.py:403
  55.5 4.1 %collective-permute-start.10 = (bf16[32,256]{1,0:T(8,128)(2,1)S(1)}, bf16[32,256]{1,0:T(8,128)(2,1)S(1)}, u32[]{:S(2)}, u32[]{:S(2)}) collective-permute-start(bf16[32,256]{1,0:T(8,128)(2,1)S(1)} %get-tuple-element.58.refs_0_), channel_id=1, source_target_pairs={{0,2},{2,0},{4,6},{6,4},{8,10},{10,8},{12,14},{14,12},{16,18},{18,... | collective-permute-start | bytes 49160 | tf_op jit(solution)/shard_map/ppermute | solution.py:391
  59.6 3.3 %collective-permute-start.5 = (bf16[2,216,512]{2,1,0:T(8,128)(2,1)S(1)}, bf16[2,216,512]{2,1,0:T(8,128)(2,1)S(1)}, u32[]{:S(2)}, u32[]{:S(2)}) collective-permute-start(bf16[2,216,512]{2,1,0:T(8,128)(2,1)S(1)} %get-tuple-element.47), channel_id=1, source_target_pairs={{0,16},{1,17},{2,18},{3,19},{4,20},{5,21},{6,22},{7,23},{8,24},{9,... | collective-permute-start | bytes 1327112 | tf_op jit(solution)/shard_map/ppermute | solution.py:385
  62.9 0.7 shard_map.155
  63.7 3.7 %all-to-all-start.2 = ((bf16[8,32,384]{2,1,0:T(8,128)(2,1)}), bf16[8,32,384]{2,1,0:T(8,128)(2,1)S(1)}, u32[]{:S(2)}, u32[]{:S(2)}) async-start(bf16[8,32,384]{2,1,0:T(8,128)(2,1)} %shard_map.155), calls=%async_computation.2 | async-start | bytes 393216 | tf_op jit(solution)/shard_map/all_to_all | solution.py:403
  67.4 5.4 %collective-permute-start.7 = (bf16[2,72,512]{2,1,0:T(8,128)(2,1)S(1)}, bf16[2,72,512]{2,1,0:T(8,128)(2,1)}, u32[]{:S(2)}, u32[]{:S(2)}) collective-permute-start(bf16[2,72,512]{2,1,0:T(8,128)(2,1)S(1)} %copy-done.13), channel_id=1, source_target_pairs={{0,19},{1,18},{2,21},{3,20},{4,23},{5,22},{6,25},{7,24},{8,27},{9,... | collective-permute-start | bytes 442376 | tf_op jit(solution)/shard_map/ppermute | solution.py:385
  72.9 3.2 %all-to-all-done.2.refs_0_ = bf16[8,32,384]{2,1,0:T(8,128)(2,1)S(1)} async-done(((bf16[8,32,384]{2,1,0:T(8,128)(2,1)}), bf16[8,32,384]{2,1,0:T(8,128)(2,1)S(1)}, u32[]{:S(2)}, u32[]{:S(2)}) %all-to-all-start.2) | async-done | bytes 196640 | tf_op jit(solution)/shard_map/all_to_all | solution.py:403
  76.1 0.8 shard_map.156
  76.9 0.6 copy-done.14
  77.5 3.5 %all-to-all-start.3 = ((bf16[4,256,256]{2,1,0:T(8,128)(2,1)}), bf16[4,256,256]{2,1,0:T(8,128)(2,1)S(1)}, u32[]{:S(2)}, u32[]{:S(2)}) async-start(bf16[4,256,256]{2,1,0:T(8,128)(2,1)} %get-tuple-element.60), calls=%async_computation.3 | async-start | bytes 1048576 | tf_op jit(solution)/shard_map/all_to_all | solution.py:397
  81.0 2.9 %collective-permute-start.11 = (bf16[256,128]{1,0:T(8,128)(2,1)}, bf16[256,128]{1,0:T(8,128)(2,1)S(1)}, u32[]{:S(2)}, u32[]{:S(2)}) collective-permute-start(bf16[256,128]{1,0:T(8,128)(2,1)} %copy-done.14), channel_id=1, source_target_pairs={{0,16},{2,18},{4,20},{6,22},{8,24},{10,26},{12,28},{14,30},{16,0},... | collective-permute-start | bytes 196616 | tf_op jit(solution)/shard_map/ppermute | solution.py:391
  83.9 1.0 %copy-done.24 = bf16[2,216,512]{2,1,0:T(8,128)(2,1)S(1)} copy-done((bf16[2,216,512]{2,1,0:T(8,128)(2,1)S(1)}, bf16[2,216,512]{2,1,0:T(8,128)(2,1)}, u32[]{:S(2)}) %copy-start.24) | copy-done | bytes 442392
  84.9 3.2 %shard_map.150 = (f32[8,128]{1,0:T(8,128)S(1)}, bf16[12,12,4,512]{3,2,1,0:T(4,128)(2,1)}, bf16[12,12,4,512]{3,2,1,0:T(4,128)(2,1)}) custom-call(bf16[12,12,4,512]{3,2,1,0:T(4,128)(2,1)S(1)} %copy-done.3, bf16[12,12,4,512]{3,2,1,0:T(4,128)(2,1)S(1)} %copy-done.6, f32[1,512]{1,0:T(1,128)S(1)} %bitcast.9, bf16[2,216,512]{2,1,0:T(8,128)(2,1)S(1)} %copy-done.24, ...), custom_call_target="tpu_custom_call" | custom-call | flops 30000001024 | tf_op jit(solution)/shard_map/pallas_call | solution.py:59
  88.1 1.5 %shard_map.157 = (f32[2,2,4,3312]{3,2,1,0:T(4,128)}, f32[8,128]{1,0:T(8,128)S(1)}) custom-call(s32[2]{0:T(128)S(1)} %pad_add_fusion.refs_0_, bf16[256,128]{1,0:T(8,128)(2,1)S(1)} %copy-done.15, bf16[256,128]{1,0:T(8,128)(2,1)S(1)} %collective-permute-done.11.refs_2_, f32[8,128]{1,0:T(8,128)S(1)} %get-tuple-element.62.refs_3_), custom_call_target="tpu_custom_call" | custom-call | flops 1000000000 | tf_op jit(solution)/shard_map/pallas_call | solution.py:59
  89.6 2.2 %collective-permute-start.15 = (bf16[1024,256]{1,0:T(8,128)(2,1)S(1)}, bf16[1024,256]{1,0:T(8,128)(2,1)S(1)}, u32[]{:S(2)}, u32[]{:S(2)}) collective-permute-start(bf16[1024,256]{1,0:T(8,128)(2,1)S(1)} %bitcast.5), channel_id=1, source_target_pairs={{0,16},{2,18},{4,20},{6,22},{8,24},{10,26},{12,28},{14,30},{16,0},... | collective-permute-start | bytes 1572872 | tf_op jit(solution)/shard_map/ppermute | solution.py:391
  91.8 0.9 shard_map.158.refs_0_
  92.8 1.3 %collective-permute-start.13 = (f32[8,512]{1,0:T(8,128)S(1)}, f32[8,512]{1,0:T(8,128)S(1)}, u32[]{:S(2)}, u32[]{:S(2)}) collective-permute-start(f32[8,512]{1,0:T(8,128)S(1)} %shard_map.158.refs_0_), channel_id=1, source_target_pairs={{0,1},{1,0},{2,3},{3,2},{4,5},{5,4},{6,7},{7,6},{8,9},{9,8},{10,11... | collective-permute-start | bytes 49160 | tf_op jit(solution)/shard_map/ppermute | solution.py:407
  94.1 0.8 collective-permute-start.12
  94.9 1.9 %shard_map.159 = (f32[8,128]{1,0:T(8,128)S(1)}, f32[3,512,256]{2,1,0:T(8,128)}, f32[256,512]{1,0:T(8,128)}) custom-call(s32[2]{0:T(128)S(1)} %pad_add_fusion.refs_0_, bf16[1024,256]{1,0:T(8,128)(2,1)S(1)} %bitcast.7, bf16[1024,256]{1,0:T(8,128)(2,1)S(1)} %collective-permute-done.15.refs_2_), custom_call_target="tpu_custom_call" | custom-call | flops 2000000000 | tf_op jit(solution)/shard_map/pallas_call | solution.py:59
  96.8 0.6 shard_map.160
  (59 shorter events, 0.4 us)
Async XLA Ops:
  0.6 1.1 %copy-start.1 = (bf16[12,12,4,512]{3,2,1,0:T(4,128)(2,1)S(1)}, bf16[12,12,4,512]{3,2,1,0:T(4,128)(2,1)}, u32[]{:S(2)}) copy-start(bf16[12,12,4,512]{3,2,1,0:T(4,128)(2,1)} %refs_0_.3) | copy-start | bytes 1769476
  1.7 1.1 %copy-start.4 = (bf16[12,12,4,512]{3,2,1,0:T(4,128)(2,1)S(1)}, bf16[12,12,4,512]{3,2,1,0:T(4,128)(2,1)}, u32[]{:S(2)}) copy-start(bf16[12,12,4,512]{3,2,1,0:T(4,128)(2,1)} %refs_1_.7) | copy-start | bytes 1769476
  2.8 12.3 %copy-start.7 = (bf16[256,512]{1,0:T(8,128)(2,1)S(1)}, bf16[256,512]{1,0:T(8,128)(2,1)}, u32[]{:S(2)}) copy-start(bf16[256,512]{1,0:T(8,128)(2,1)} %refs_2_.6) | copy-start | bytes 786436
  2.8 12.3 %copy-start.11 = (f32[2,2,4,3312]{3,2,1,0:T(4,128)S(1)}, f32[2,2,4,3312]{3,2,1,0:T(4,128)}, u32[]{:S(2)}) copy-start(f32[2,2,4,3312]{3,2,1,0:T(4,128)} %refs_1_.5) | copy-start | bytes 635908
  2.8 12.3 %copy-start.20 = (bf16[276,276]{1,0:T(8,128)(2,1)S(1)}, bf16[276,276]{1,0:T(8,128)(2,1)}, u32[]{:S(2)}) copy-start(bf16[276,276]{1,0:T(8,128)(2,1)} %constant.36.clone.refs_2_) | copy-start | bytes 457060
  2.9 15.7 %collective-permute-start = (bf16[2,216,512]{2,1,0:T(8,128)(2,1)S(1)}, bf16[2,216,512]{2,1,0:T(8,128)(2,1)S(1)}, u32[]{:S(2)}, u32[]{:S(2)}) collective-permute-start(bf16[2,216,512]{2,1,0:T(8,128)(2,1)S(1)} %get-tuple-element.37), channel_id=1, source_target_pairs={{0,240},{1,241},{2,242},{3,243},{4,244},{5,245},{6,246},{7,247},{8... | collective-permute-start | bytes 1327112 | tf_op jit(solution)/shard_map/ppermute | solution.py:385
  6.1 11.8 %collective-permute-start.1 = (bf16[2,72,512]{2,1,0:T(8,128)(2,1)S(1)}, bf16[2,72,512]{2,1,0:T(8,128)(2,1)S(1)}, u32[]{:S(2)}, u32[]{:S(2)}) collective-permute-start(bf16[2,72,512]{2,1,0:T(8,128)(2,1)S(1)} %get-tuple-element.38), channel_id=1, source_target_pairs={{0,15},{1,14},{2,1},{3,0},{4,3},{5,2},{6,5},{7,4},{8,7},{9,6},{10,... | collective-permute-start | bytes 442376 | tf_op jit(solution)/shard_map/ppermute | solution.py:385
  9.3 9.2 %collective-permute-start.2 = (bf16[2,72,512]{2,1,0:T(8,128)(2,1)S(1)}, bf16[2,72,512]{2,1,0:T(8,128)(2,1)S(1)}, u32[]{:S(2)}, u32[]{:S(2)}) collective-permute-start(bf16[2,72,512]{2,1,0:T(8,128)(2,1)S(1)} %get-tuple-element.39), channel_id=1, source_target_pairs={{0,255},{1,254},{2,241},{3,240},{4,243},{5,242},{6,245},{7,244},{8... | collective-permute-start | bytes 442376 | tf_op jit(solution)/shard_map/ppermute | solution.py:385
  15.0 3.5 %copy-start = (bf16[3,512,256]{2,1,0:T(8,128)(2,1)S(1)}, bf16[3,512,256]{2,1,0:T(8,128)(2,1)}, u32[]{:S(2)}) copy-start(bf16[3,512,256]{2,1,0:T(8,128)(2,1)} %refs_2_.7) | copy-start | bytes 2359300
  15.1 3.5 %copy-start.2 = (bf16[12,12,4,512]{3,2,1,0:T(4,128)(2,1)S(1)}, bf16[12,12,4,512]{3,2,1,0:T(4,128)(2,1)}, u32[]{:S(2)}) copy-start(bf16[12,12,4,512]{3,2,1,0:T(4,128)(2,1)} %refs_0_.3) | copy-start | bytes 1769476
  15.1 3.5 %copy-start.5 = (bf16[12,12,4,512]{3,2,1,0:T(4,128)(2,1)S(1)}, bf16[12,12,4,512]{3,2,1,0:T(4,128)(2,1)}, u32[]{:S(2)}) copy-start(bf16[12,12,4,512]{3,2,1,0:T(4,128)(2,1)} %refs_1_.7) | copy-start | bytes 1769476
  15.1 3.5 %copy-start.16 = (f32[512]{0:T(512)S(1)}, f32[512]{0:T(512)}, u32[]{:S(2)}) copy-start(f32[512]{0:T(512)} %param.12) | copy-start | bytes 6148
  15.1 3.5 %copy-start.18 = (bf16[2,288,288]{2,1,0:T(8,128)(2,1)S(1)}, bf16[2,288,288]{2,1,0:T(8,128)(2,1)}, u32[]{:S(2)}) copy-start(bf16[2,288,288]{2,1,0:T(8,128)(2,1)} %constant.34.clone.refs_6_) | copy-start | bytes 995332
  17.8 8.8 %collective-permute-start.3 = (bf16[256,512]{1,0:T(8,128)(2,1)S(1)}, bf16[256,512]{1,0:T(8,128)(2,1)S(1)}, u32[]{:S(2)}, u32[]{:S(2)}) collective-permute-start(bf16[256,512]{1,0:T(8,128)(2,1)S(1)} %get-tuple-element.45), channel_id=1, source_target_pairs={{0,1},{1,0},{2,3},{3,2},{4,5},{5,4},{6,7},{7,6},{8,9},{9,8},{10,11... | collective-permute-start | bytes 786440 | tf_op jit(solution)/shard_map/ppermute | solution.py:407
  18.6 8.0 %copy-start.17 = (bf16[2,288,288]{2,1,0:T(8,128)(2,1)S(1)}, bf16[2,288,288]{2,1,0:T(8,128)(2,1)}, u32[]{:S(2)}) copy-start(bf16[2,288,288]{2,1,0:T(8,128)(2,1)} %constant.35.clone.refs_5_) | copy-start | bytes 995332
  24.4 3.4 %copy-start.21 = (f32[2304,144]{1,0:T(8,128)}, f32[2304,144]{1,0:T(8,128)S(1)}, u32[]{:S(2)}) copy-start(f32[2304,144]{1,0:T(8,128)S(1)} %get-tuple-element.54.refs_1_) | copy-start | bytes 3981316
  24.4 3.8 %collective-permute-start.8 = (bf16[1024,256]{1,0:T(8,128)(2,1)S(1)}, bf16[1024,256]{1,0:T(8,128)(2,1)S(1)}, u32[]{:S(2)}, u32[]{:S(2)}) collective-permute-start(bf16[1024,256]{1,0:T(8,128)(2,1)S(1)} %get-tuple-element.53), channel_id=1, source_target_pairs={{0,16},{2,18},{4,20},{6,22},{8,24},{10,26},{12,28},{14,30},{16,0},... | collective-permute-start | bytes 1572872 | tf_op jit(solution)/shard_map/ppermute | solution.py:391
  26.6 1.2 %copy-start.9 = (bf16[256,512]{1,0:T(8,128)(2,1)}, bf16[256,512]{1,0:T(8,128)(2,1)S(1)}, u32[]{:S(2)}) copy-start(bf16[256,512]{1,0:T(8,128)(2,1)S(1)} %collective-permute-done.3.refs_6_.refs_3_) | copy-start | bytes 786436
  27.8 4.9 %copy-start.19 = (bf16[2,138,276]{2,1,0:T(8,128)(2,1)S(1)}, bf16[2,138,276]{2,1,0:T(8,128)(2,1)}, u32[]{:S(2)}) copy-start(bf16[2,138,276]{2,1,0:T(8,128)(2,1)} %constant.37.clone.refs_2_) | copy-start | bytes 457060
  27.8 21.3 %collective-permute-start.4 = (bf16[576,768]{1,0:T(8,128)(2,1)S(1)}, bf16[576,768]{1,0:T(8,128)(2,1)S(1)}, u32[]{:S(2)}, u32[]{:S(2)}) collective-permute-start(bf16[576,768]{1,0:T(8,128)(2,1)S(1)} %shard_map.148.refs_0_.refs_2_), channel_id=1, source_target_pairs={{0,1},{1,0},{2,3},{3,2},{4,5},{5,4},{6,7},{7,6},{8,9},{9,8},{10,11... | collective-permute-start | bytes 2654216 | tf_op jit(solution)/shard_map/ppermute | solution.py:407
  29.0 12.7 %all-to-all-start = ((bf16[4,256,256]{2,1,0:T(8,128)(2,1)}), bf16[4,256,256]{2,1,0:T(8,128)(2,1)S(1)}, u32[]{:S(2)}, u32[]{:S(2)}) async-start(bf16[4,256,256]{2,1,0:T(8,128)(2,1)} %shard_map.151), calls=%async_computation | async-start | bytes 1048576 | tf_op jit(solution)/shard_map/all_to_all | solution.py:397
  32.7 1.7 %copy-start.22 = (f32[2304,144]{1,0:T(8,128)S(1)}, f32[2304,144]{1,0:T(8,128)}, u32[]{:S(2)}) copy-start(f32[2304,144]{1,0:T(8,128)} %copy-done.21) | copy-start | bytes 3981316
  36.2 1.4 %collective-permute-start.9 = (bf16[256,128]{1,0:T(8,128)(2,1)S(1)}, bf16[256,128]{1,0:T(8,128)(2,1)S(1)}, u32[]{:S(2)}, u32[]{:S(2)}) collective-permute-start(bf16[256,128]{1,0:T(8,128)(2,1)S(1)} %get-tuple-element.56), channel_id=1, source_target_pairs={{0,16},{2,18},{4,20},{6,22},{8,24},{10,26},{12,28},{14,30},{16,0},... | collective-permute-start | bytes 196616 | tf_op jit(solution)/shard_map/ppermute | solution.py:391
  42.4 13.0 %all-to-all-start.1 = ((bf16[8,32,384]{2,1,0:T(8,128)(2,1)}), bf16[8,32,384]{2,1,0:T(8,128)(2,1)S(1)}, u32[]{:S(2)}, u32[]{:S(2)}) async-start(bf16[8,32,384]{2,1,0:T(8,128)(2,1)} %shard_map.153), calls=%async_computation.1 | async-start | bytes 393216 | tf_op jit(solution)/shard_map/all_to_all | solution.py:403
  49.1 1.0 copy-start.8
  50.0 0.9 copy-start.10
  52.4 0.7 copy-start.12
  53.1 0.8 copy-start.23
  55.5 11.9 %copy-start.13 = (bf16[2,72,512]{2,1,0:T(8,128)(2,1)S(1)}, bf16[2,72,512]{2,1,0:T(8,128)(2,1)}, u32[]{:S(2)}) copy-start(bf16[2,72,512]{2,1,0:T(8,128)(2,1)} %copy-done.12) | copy-start | bytes 442372
  55.5 7.4 %collective-permute-start.10 = (bf16[32,256]{1,0:T(8,128)(2,1)S(1)}, bf16[32,256]{1,0:T(8,128)(2,1)S(1)}, u32[]{:S(2)}, u32[]{:S(2)}) collective-permute-start(bf16[32,256]{1,0:T(8,128)(2,1)S(1)} %get-tuple-element.58.refs_0_), channel_id=1, source_target_pairs={{0,2},{2,0},{4,6},{6,4},{8,10},{10,8},{12,14},{14,12},{16,18},{18,... | collective-permute-start | bytes 49160 | tf_op jit(solution)/shard_map/ppermute | solution.py:391
  59.6 24.3 %collective-permute-start.5 = (bf16[2,216,512]{2,1,0:T(8,128)(2,1)S(1)}, bf16[2,216,512]{2,1,0:T(8,128)(2,1)S(1)}, u32[]{:S(2)}, u32[]{:S(2)}) collective-permute-start(bf16[2,216,512]{2,1,0:T(8,128)(2,1)S(1)} %get-tuple-element.47), channel_id=1, source_target_pairs={{0,16},{1,17},{2,18},{3,19},{4,20},{5,21},{6,22},{7,23},{8,24},{9,... | collective-permute-start | bytes 1327112 | tf_op jit(solution)/shard_map/ppermute | solution.py:385
  63.7 12.4 %all-to-all-start.2 = ((bf16[8,32,384]{2,1,0:T(8,128)(2,1)}), bf16[8,32,384]{2,1,0:T(8,128)(2,1)S(1)}, u32[]{:S(2)}, u32[]{:S(2)}) async-start(bf16[8,32,384]{2,1,0:T(8,128)(2,1)} %shard_map.155), calls=%async_computation.2 | async-start | bytes 393216 | tf_op jit(solution)/shard_map/all_to_all | solution.py:403
  67.4 16.5 %collective-permute-start.6 = (bf16[2,72,512]{2,1,0:T(8,128)(2,1)}, bf16[2,72,512]{2,1,0:T(8,128)(2,1)}, u32[]{:S(2)}, u32[]{:S(2)}) collective-permute-start(bf16[2,72,512]{2,1,0:T(8,128)(2,1)} %get-tuple-element.48), channel_id=1, source_target_pairs={{0,3},{1,2},{2,5},{3,4},{4,7},{5,6},{6,9},{7,8},{8,11},{9,10},{10,... | collective-permute-start | bytes 442376 | tf_op jit(solution)/shard_map/ppermute | solution.py:385
  67.4 16.5 %copy-start.3 = (bf16[12,12,4,512]{3,2,1,0:T(4,128)(2,1)S(1)}, bf16[12,12,4,512]{3,2,1,0:T(4,128)(2,1)}, u32[]{:S(2)}) copy-start(bf16[12,12,4,512]{3,2,1,0:T(4,128)(2,1)} %refs_0_.3) | copy-start | bytes 1769476
  67.4 16.5 %copy-start.6 = (bf16[12,12,4,512]{3,2,1,0:T(4,128)(2,1)S(1)}, bf16[12,12,4,512]{3,2,1,0:T(4,128)(2,1)}, u32[]{:S(2)}) copy-start(bf16[12,12,4,512]{3,2,1,0:T(4,128)(2,1)} %refs_1_.7) | copy-start | bytes 1769476
  67.4 16.4 %collective-permute-start.7 = (bf16[2,72,512]{2,1,0:T(8,128)(2,1)S(1)}, bf16[2,72,512]{2,1,0:T(8,128)(2,1)}, u32[]{:S(2)}, u32[]{:S(2)}) collective-permute-start(bf16[2,72,512]{2,1,0:T(8,128)(2,1)S(1)} %copy-done.13), channel_id=1, source_target_pairs={{0,19},{1,18},{2,21},{3,20},{4,23},{5,22},{6,25},{7,24},{8,27},{9,... | collective-permute-start | bytes 442376 | tf_op jit(solution)/shard_map/ppermute | solution.py:385
  76.9 0.6 copy-start.14
  77.5 12.1 %all-to-all-start.3 = ((bf16[4,256,256]{2,1,0:T(8,128)(2,1)}), bf16[4,256,256]{2,1,0:T(8,128)(2,1)S(1)}, u32[]{:S(2)}, u32[]{:S(2)}) async-start(bf16[4,256,256]{2,1,0:T(8,128)(2,1)} %get-tuple-element.60), calls=%async_computation.3 | async-start | bytes 1048576 | tf_op jit(solution)/shard_map/all_to_all | solution.py:397
  81.0 7.1 %collective-permute-start.11 = (bf16[256,128]{1,0:T(8,128)(2,1)}, bf16[256,128]{1,0:T(8,128)(2,1)S(1)}, u32[]{:S(2)}, u32[]{:S(2)}) collective-permute-start(bf16[256,128]{1,0:T(8,128)(2,1)} %copy-done.14), channel_id=1, source_target_pairs={{0,16},{2,18},{4,20},{6,22},{8,24},{10,26},{12,28},{14,30},{16,0},... | collective-permute-start | bytes 196616 | tf_op jit(solution)/shard_map/ppermute | solution.py:391
  83.9 1.0 %copy-start.24 = (bf16[2,216,512]{2,1,0:T(8,128)(2,1)S(1)}, bf16[2,216,512]{2,1,0:T(8,128)(2,1)}, u32[]{:S(2)}) copy-start(bf16[2,216,512]{2,1,0:T(8,128)(2,1)} %copy-done.23) | copy-start | bytes 1327108
  84.9 3.2 %copy-start.15 = (bf16[256,128]{1,0:T(8,128)(2,1)S(1)}, bf16[256,128]{1,0:T(8,128)(2,1)}, u32[]{:S(2)}) copy-start(bf16[256,128]{1,0:T(8,128)(2,1)} %copy-done.14) | copy-start | bytes 196612
  89.6 5.3 %collective-permute-start.15 = (bf16[1024,256]{1,0:T(8,128)(2,1)S(1)}, bf16[1024,256]{1,0:T(8,128)(2,1)S(1)}, u32[]{:S(2)}, u32[]{:S(2)}) collective-permute-start(bf16[1024,256]{1,0:T(8,128)(2,1)S(1)} %bitcast.5), channel_id=1, source_target_pairs={{0,16},{2,18},{4,20},{6,22},{8,24},{10,26},{12,28},{14,30},{16,0},... | collective-permute-start | bytes 1572872 | tf_op jit(solution)/shard_map/ppermute | solution.py:391
  92.7 4.1 %collective-permute-start.14 = (f32[8,512]{1,0:T(8,128)S(1)}, f32[8,512]{1,0:T(8,128)S(1)}, u32[]{:S(2)}, u32[]{:S(2)}) collective-permute-start(f32[8,512]{1,0:T(8,128)S(1)} %shard_map.158.refs_0_), channel_id=1, source_target_pairs={{0,17},{1,16},{16,1},{17,0},{32,49},{33,48},{48,33},{49,32},{64,81... | collective-permute-start | bytes 49160 | tf_op jit(solution)/shard_map/ppermute | solution.py:412
  92.8 4.1 %collective-permute-start.13 = (f32[8,512]{1,0:T(8,128)S(1)}, f32[8,512]{1,0:T(8,128)S(1)}, u32[]{:S(2)}, u32[]{:S(2)}) collective-permute-start(f32[8,512]{1,0:T(8,128)S(1)} %shard_map.158.refs_0_), channel_id=1, source_target_pairs={{0,1},{1,0},{2,3},{3,2},{4,5},{5,4},{6,7},{7,6},{8,9},{9,8},{10,11... | collective-permute-start | bytes 49160 | tf_op jit(solution)/shard_map/ppermute | solution.py:407
  94.1 2.8 %collective-permute-start.12 = (f32[8,512]{1,0:T(8,128)S(1)}, f32[8,512]{1,0:T(8,128)S(1)}, u32[]{:S(2)}, u32[]{:S(2)}) collective-permute-start(f32[8,512]{1,0:T(8,128)S(1)} %shard_map.158.refs_0_), channel_id=1, source_target_pairs={{0,16},{2,18},{4,20},{6,22},{8,24},{10,26},{12,28},{14,30},{16,0},... | collective-permute-start | bytes 49160 | tf_op jit(solution)/shard_map/ppermute | solution.py:391

commit v8 on v7

--- a/solution.py
+++ b/solution.py
@@ -86,13 +86,33 @@
     return tile.reshape(-1, tile.shape[-1])
 
 
-def halo_kernel(latent, cot, *outs):
-    for places, ref in zip(PLACES[1:], outs):
+def sent(copies, source, target, sem):
+    copies.append(pltpu.make_async_copy(source, target, sem))
+    copies[-1].start()
+
+
+def finish(copies):
+    for copy in copies:
+        copy.wait()
+
+
+def halo_kernel(latent, cot, o_lon, o_lat, o_cor, tiles, h_lon, h_lat, h_cor, in_sems, out_sems):
+    arrived, copies = [], []
+    for first in (0, 3, 6, 9):
         for j, grid in enumerate((latent, cot)):
-            ref[j] = jnp.concatenate([flat(grid[lon, lat]) for lon, lat in places], 0)
-
-
-def bias_kernel(info, table, order, w_out, bias, w_copy, raw, entries, low_u, high_u):
+            rows = pl.ds(first, 3)
+            sent(arrived, grid.at[rows], tiles.at[j, rows], in_sems.at[len(arrived)])
+    finish(arrived[:4])
+    for places, held, ref in ((PLACES[1], h_lon, o_lon), (PLACES[3], h_cor, o_cor), (PLACES[2], h_lat, o_lat)):
+        if held is h_lat:
+            finish(arrived[4:])
+        for j in range(2):
+            held[j] = jnp.concatenate([flat(tiles[j, lon, lat]) for lon, lat in places], 0)
+            sent(copies, held.at[j], ref.at[j], out_sems.at[len(copies)])
+    finish(copies)
+
+
+def bias_kernel(info, table, order, w_out, bias, w_copy, raw, entries, t0, t1, t2):
     w_copy[...] = w_out[...]
     flat = table[...].reshape(16, 3312)
     for s_t in range(2):
@@ -106,10 +126,18 @@
     rest = full - high.astype(F32)
     mid = rest.astype(BF)
     low = (rest - mid.astype(F32)).astype(BF)
-    entries[...] = dot(low, order[...]) + dot(mid, order[...]) + dot(high, order[...])
+    wide = dot(low, order[...]) + dot(mid, order[...]) + dot(high, order[...])
+    t0[...] = wide[:, 0:128]
+    t1[...] = wide[:, 128:256]
+    t2[:, 0:20] = wide[:, 256:276]
+    for i in range(16):
+        at, rows = pl.ds(i, 12, stride=16), slice(i * 12, i * 12 + 12)
+        entries[rows, 0:128] = t0[at, :]
+        entries[rows, 128:256] = t1[at, :]
+        entries[rows, 256:276] = t2[at, :][:, 0:20]
     row = lax.broadcasted_iota(jnp.int32, (192, WTOK), 0)
     col = lax.broadcasted_iota(jnp.int32, (192, WTOK), 1)
-    rs_t, rs_u, which = row // 16, col % 12, row % 16
+    rs_t, rs_u, which = row % 12, col % 12, row // 12
     s_t, s_u = (rs_t >= 6).astype(jnp.int32), (rs_u >= 6).astype(jnp.int32)
     edge_t = (rs_t - s_t * 6 >= 3).astype(jnp.int32)
     edge_u = (rs_u - s_u * 6 >= 3).astype(jnp.int32)
@@ -117,14 +145,9 @@
     last_lev = ((which % 8) >= 4).astype(jnp.int32)
     barred = (last_lat * (edge_t - edge_u) != 0) | (last_lev * (s_t - s_u) != 0)
     for p in range(12):
-        at = entries[:, (11 - p) * 12 : (11 - p) * 12 + WTOK]
-        at = jnp.where(barred, -jnp.inf, at)
-        low_u[...] = at[:, 0:128]
-        high_u[:, 0:16] = at[:, 128:144]
+        at = jnp.where(barred, -jnp.inf, entries[:, (11 - p) * 12 : (11 - p) * 12 + WTOK])
         for i in range(16):
-            rows = slice(i * WTOK + p * 12, i * WTOK + p * 12 + 12)
-            bias[rows, 0:128] = low_u[pl.ds(i, 12, stride=16), :]
-            bias[rows, 128:WTOK] = high_u[pl.ds(i, 12, stride=16), :][:, 0:16]
+            bias[i * WTOK + p * 12 : i * WTOK + p * 12 + 12, :] = at[i * 12 : i * 12 + 12]
 
 
 def main_kernel(info, latent, cotangent, lon, lat, cor, place, gain, w_qkv, w_out, bias,
@@ -192,16 +215,6 @@
         rows = slice(a * 288, (a + 1) * 288)
         terms[rows, 0:256] = dot(back[a], att[rows, :]).astype(BF)
         terms[rows, 256:768] = dot(back[a], hid_part[rows]).astype(BF)
-
-
-def sent(copies, source, target, sem):
-    copies.append(pltpu.make_async_copy(source, target, sem))
-    copies[-1].start()
-
-
-def finish(copies):
-    for copy in copies:
-        copy.wait()
 
 
 def core_sum_kernel(keep, recv, total, held, sems):
@@ -424,14 +437,25 @@
 
     part = lambda n: ((2, n, 512), BF)
     halos = [part(216), part(72), part(72)]
-    s_lon, s_lat, s_cor = call(halo_kernel, halos, [latent, cotangent], smem=0)
+    s_lon, s_lat, s_cor = call(
+        halo_kernel,
+        [],
+        [],
+        [pltpu.VMEM((2,) + latent.shape, BF)]
+        + [pltpu.VMEM(shape, BF) for shape, _ in halos]
+        + [pltpu.SemaphoreType.DMA((8,)), pltpu.SemaphoreType.DMA((6,))],
+        smem=0,
+        mib=60,
+        hbm=[latent, cotangent],
+        hbm_outs=halos,
+    )
     in_lon, in_lat, in_cor = moved(s_lon, -1, 0), moved(s_lat, 0, -1), moved(s_cor, -1, -1)
 
     bias, w_copy = call(
         bias_kernel,
         [((16 * WTOK, WTOK), F32), (w_out.shape, BF)],
         [info, bias_table, order, w_out],
-        [pltpu.VMEM((192, 276), F32)] * 2 + [pltpu.VMEM((192, 128), F32)] * 2,
+        [pltpu.VMEM((192, 276), F32)] * 2 + [pltpu.VMEM((192, 128), F32)] * 3,
         us=2,
     )
     w_other = other_group(w_copy)

time: 98.1 us -> 98.2 us (level)
  local copies, waits for them, and re-layouts: 8.82 us -> 6.7 us
  Pallas kernels: 24.3 us -> 25.5 us
  waiting for transfers between devices: 12.8 us -> 14 us
    unnamed x50 -> x46, local copies, waits for them, and re-layouts: 8.82 us -> 6.7 us
    ppermute x6, waiting for transfers between devices: 0.6 us -> 1.84 us  [moved(): return lax.ppermute(value, ('lon', 'lat', 'tp'), pairs)]
    pallas_call x16, Pallas kernels: 24.3 us -> 25.5 us  [call(): pl.pallas_call(kernel, out_shape=[jax.ShapeDtypeStruct(s, t) for s, t in...]
  transfers between devices with their start and end apart: 20 -> 20, of which waited for: 7 -> 7; matrix products, arithmetic and copies ran while one was open for 0% -> 0% of each run, Pallas kernels for 24% -> 23%
where the time goes in v8:
time: 98.2 us; the launch traced here: 97.7 us
  starting transfers between devices  50.3 us (51%)
  Pallas kernels  25.5 us (26%)
  waiting for transfers between devices  14 us (14%)
  local copies, waits for them, and re-layouts  6.7 us (7%)
  between operations  1.03 us (1%)
    pallas_call x16, Pallas kernels, call(): pl.pallas_call(kernel, out_shape=[jax.ShapeDtypeStruct(s, t) for s, t in...  25.5 us
    ppermute x6, starting transfers between devices, moved(): return lax.ppermute(value, ('lon', 'lat', 'tp'), pairs)  20.9 us
    ppermute x6, starting transfers between devices, swapped(): return lax.ppermute(value, ('lon', 'lat'), pairs)  12.7 us
    all_to_all x2, starting transfers between devices, across_z(): return lax.all_to_all(value, 'lon', 0, 0, axis_index_groups=groups)  8.25 us
    all_to_all x2, starting transfers between devices, across_y(): return lax.all_to_all(value, 'lat', 0, 0, axis_index_groups=groups)  6.96 us
    unnamed x46, local copies, waits for them, and re-layouts  6.7 us
    all_to_all x2, waiting for transfers between devices, across_z(): return lax.all_to_all(value, 'lon', 0, 0, axis_index_groups=groups)  4.86 us
    all_to_all x2, waiting for transfers between devices, across_y(): return lax.all_to_all(value, 'lat', 0, 0, axis_index_groups=groups)  4.07 us
  transfers between devices with their start and end apart: 20, of which 7 were waited for; matrix products, arithmetic and copies ran while one was open for 0% of the time, Pallas kernels for 23%

profile of v8, /device:TPU:1, one launch (start us, length us, event | category | flops | bytes accessed | tf_op | source)
XLA Modules:
  0.0 97.7 jit_solution(11624993694403705501)
XLA Ops:
  0.7 2.2 %shard_map.145 = (bf16[2,216,512]{2,1,0:T(8,128)(2,1)}, bf16[2,72,512]{2,1,0:T(8,128)(2,1)}, bf16[2,72,512]{2,1,0:T(8,128)(2,1)}) custom-call(bf16[12,12,4,512]{3,2,1,0:T(4,128)(2,1)} %refs_0_.3, bf16[12,12,4,512]{3,2,1,0:T(4,128)(2,1)} %refs_1_.7), custom_call_target="tpu_custom_call" | custom-call | flops 1000000000 | tf_op jit(solution)/shard_map/pallas_call | solution.py:59
  2.9 3.3 %collective-permute-start = (bf16[2,216,512]{2,1,0:T(8,128)(2,1)}, bf16[2,216,512]{2,1,0:T(8,128)(2,1)S(1)}, u32[]{:S(2)}, u32[]{:S(2)}) collective-permute-start(bf16[2,216,512]{2,1,0:T(8,128)(2,1)} %get-tuple-element.37), channel_id=1, source_target_pairs={{0,240},{1,241},{2,242},{3,243},{4,244},{5,245},{6,246},{7,247},{8... | collective-permute-start | bytes 1327112 | tf_op jit(solution)/shard_map/ppermute | solution.py:398
  6.1 3.2 %collective-permute-start.1 = (bf16[2,72,512]{2,1,0:T(8,128)(2,1)}, bf16[2,72,512]{2,1,0:T(8,128)(2,1)S(1)}, u32[]{:S(2)}, u32[]{:S(2)}) collective-permute-start(bf16[2,72,512]{2,1,0:T(8,128)(2,1)} %get-tuple-element.38), channel_id=1, source_target_pairs={{0,15},{1,14},{2,1},{3,0},{4,3},{5,2},{6,5},{7,4},{8,7},{9,6},{10,... | collective-permute-start | bytes 442376 | tf_op jit(solution)/shard_map/ppermute | solution.py:398
  9.3 5.7 %collective-permute-start.2 = (bf16[2,72,512]{2,1,0:T(8,128)(2,1)}, bf16[2,72,512]{2,1,0:T(8,128)(2,1)S(1)}, u32[]{:S(2)}, u32[]{:S(2)}) collective-permute-start(bf16[2,72,512]{2,1,0:T(8,128)(2,1)} %get-tuple-element.39), channel_id=1, source_target_pairs={{0,255},{1,254},{2,241},{3,240},{4,243},{5,242},{6,245},{7,244},{8... | collective-permute-start | bytes 442376 | tf_op jit(solution)/shard_map/ppermute | solution.py:398
  15.0 0.1 pad_add_fusion.refs_0_
  15.1 1.8 %shard_map.146 = (f32[2304,144]{1,0:T(8,128)S(1)}, bf16[256,512]{1,0:T(8,128)(2,1)S(1)}) custom-call(s32[2]{0:T(128)S(1)} %pad_add_fusion.refs_0_, f32[2,2,4,3312]{3,2,1,0:T(4,128)S(1)} %copy-done.9, bf16[276,276]{1,0:T(8,128)(2,1)S(1)} %copy-done.18, bf16[256,512]{1,0:T(8,128)(2,1)S(1)} %copy-done.5), custom_call_target="tpu_custom_call" | custom-call | flops 2000000000 | tf_op jit(solution)/shard_map/pallas_call | solution.py:59
  16.9 0.1 collective-permute-start.3
  17.0 1.8 %collective-permute-done.2.refs_5_ = bf16[2,72,512]{2,1,0:T(8,128)(2,1)S(1)} collective-permute-done((bf16[2,72,512]{2,1,0:T(8,128)(2,1)}, bf16[2,72,512]{2,1,0:T(8,128)(2,1)S(1)}, u32[]{:S(2)}, u32[]{:S(2)}) %collective-permute-start.2) | collective-permute-done | bytes 147488 | tf_op jit(solution)/shard_map/ppermute | solution.py:398
  18.9 5.8 %shard_map.147 = (f32[1024,256]{1,0:T(8,128)S(1)}, bf16[1024,256]{1,0:T(8,128)(2,1)S(1)}, f32[2304,144]{1,0:T(8,128)S(1)}, bf16[576,256]{1,0:T(8,128)(2,1)S(1)},...) custom-call(s32[2]{0:T(128)S(1)} %pad_add_fusion.refs_0_, ...), custom_call_target="tpu_custom_call" | custom-call | flops 8999999488 | tf_op jit(solution)/shard_map/pallas_call | solution.py:59
  24.7 2.1 %collective-permute-start.8 = (bf16[1024,256]{1,0:T(8,128)(2,1)S(1)}, bf16[1024,256]{1,0:T(8,128)(2,1)S(1)}, u32[]{:S(2)}, u32[]{:S(2)}) collective-permute-start(bf16[1024,256]{1,0:T(8,128)(2,1)S(1)} %get-tuple-element.53), channel_id=1, source_target_pairs={{0,16},{2,18},{4,20},{6,22},{8,24},{10,26},{12,28},{14,30},{16,0},... | collective-permute-start | bytes 1572872 | tf_op jit(solution)/shard_map/ppermute | solution.py:404
  26.8 1.1 %shard_map.148.refs_0_.refs_2_ = bf16[576,768]{1,0:T(8,128)(2,1)S(1)} custom-call(bf16[576,256]{1,0:T(8,128)(2,1)S(1)} %get-tuple-element.41.refs_0_, bf16[576,256]{1,0:T(8,128)(2,1)S(1)} %get-tuple-element.42.refs_1_, bf16[576,256]{1,0:T(8,128)(2,1)S(1)} %get-tuple-element.43.refs_2_, bf16[576,256]{1,0:T(8,128)(2,1)S(1)} %get-tuple-element.44.refs_3_, ...), custom_call_target="tpu_custom_call" | custom-call | flops 2000000000 | tf_op jit(solution)/shard_map/pallas_call | solution.py:59
  28.0 0.1 collective-permute-start.4
  28.1 0.3 collective-permute-done.8.refs_1_
  28.4 0.8 shard_map.151
  29.2 3.5 %all-to-all-start = ((bf16[4,256,256]{2,1,0:T(8,128)(2,1)}), bf16[4,256,256]{2,1,0:T(8,128)(2,1)S(1)}, u32[]{:S(2)}, u32[]{:S(2)}) async-start(bf16[4,256,256]{2,1,0:T(8,128)(2,1)} %shard_map.151), calls=%async_computation | async-start | bytes 1048576 | tf_op jit(solution)/shard_map/all_to_all | solution.py:410
  32.7 1.7 %copy-done.20 = f32[2304,144]{1,0:T(8,128)S(1)} copy-done((f32[2304,144]{1,0:T(8,128)S(1)}, f32[2304,144]{1,0:T(8,128)}, u32[]{:S(2)}) %copy-start.20) | copy-done | bytes 1327128
  34.4 1.9 %shard_map.152 = (bf16[256,128]{1,0:T(8,128)(2,1)S(1)}, bf16[256,128]{1,0:T(8,128)(2,1)S(1)}) custom-call(s32[2]{0:T(128)S(1)} %pad_add_fusion.refs_0_, f32[2304,144]{1,0:T(8,128)S(1)} %copy-done.20, bf16[2,138,276]{2,1,0:T(8,128)(2,1)S(1)} %copy-done.17), custom_call_target="tpu_custom_call" | custom-call | flops 2500000000 | tf_op jit(solution)/shard_map/pallas_call | solution.py:59
  36.3 0.6 collective-permute-start.9
  36.9 0.9 collective-permute-done.9.refs_2_
  37.8 4.1 %all-to-all-done.refs_0_ = bf16[4,256,256]{2,1,0:T(8,128)(2,1)S(1)} async-done(((bf16[4,256,256]{2,1,0:T(8,128)(2,1)}), bf16[4,256,256]{2,1,0:T(8,128)(2,1)S(1)}, u32[]{:S(2)}, u32[]{:S(2)}) %all-to-all-start) | async-done | bytes 524320 | tf_op jit(solution)/shard_map/all_to_all | solution.py:410
  41.9 0.8 shard_map.153
  42.7 4.6 %all-to-all-start.1 = ((bf16[8,32,384]{2,1,0:T(8,128)(2,1)}), bf16[8,32,384]{2,1,0:T(8,128)(2,1)S(1)}, u32[]{:S(2)}, u32[]{:S(2)}) async-start(bf16[8,32,384]{2,1,0:T(8,128)(2,1)} %shard_map.153), calls=%async_computation.1 | async-start | bytes 393216 | tf_op jit(solution)/shard_map/all_to_all | solution.py:416
  47.2 2.1 %collective-permute-done.4.refs_1_ = bf16[576,768]{1,0:T(8,128)(2,1)S(1)} collective-permute-done((bf16[576,768]{1,0:T(8,128)(2,1)S(1)}, bf16[576,768]{1,0:T(8,128)(2,1)S(1)}, u32[]{:S(2)}, u32[]{:S(2)}) %collective-permute-start.4) | collective-permute-done | bytes 884768 | tf_op jit(solution)/shard_map/ppermute | solution.py:420
  49.3 0.9 copy-done.6
  50.3 0.9 copy-done.8
  51.2 1.4 %shard_map.149 = (bf16[2,216,512]{2,1,0:T(8,128)(2,1)S(1)}, bf16[2,216,512]{2,1,0:T(8,128)(2,1)S(1)}, bf16[2,72,512]{2,1,0:T(8,128)(2,1)}, bf16[2,72,512]{2,1,0:T(8,128)(2,1)S(1)}, f32[8,128]{1,0:T(8,128)S(1)}) custom-call(bf16[576,768]{1,0:T(8,128)(2,1)S(1)} %shard_map.148.refs_0_.refs_2_, bf16[576,768]{1,0:T(8,128)(2,1)S(1)} %collective-permute-done.4.refs_1_, ...), custom_call_target="tpu_custom_call" | custom-call | flops 30000001024 | tf_op jit(solution)/shard_map/pallas_call | solution.py:59
  52.6 0.7 copy-done.10
  53.3 0.8 copy-done.21
  54.0 1.7 %all-to-all-done.1.refs_0_ = bf16[8,32,384]{2,1,0:T(8,128)(2,1)S(1)} async-done(((bf16[8,32,384]{2,1,0:T(8,128)(2,1)}), bf16[8,32,384]{2,1,0:T(8,128)(2,1)S(1)}, u32[]{:S(2)}, u32[]{:S(2)}) %all-to-all-start.1) | async-done | bytes 196640 | tf_op jit(solution)/shard_map/all_to_all | solution.py:416
  55.7 4.1 %collective-permute-start.10 = (bf16[32,256]{1,0:T(8,128)(2,1)S(1)}, bf16[32,256]{1,0:T(8,128)(2,1)S(1)}, u32[]{:S(2)}, u32[]{:S(2)}) collective-permute-start(bf16[32,256]{1,0:T(8,128)(2,1)S(1)} %get-tuple-element.58.refs_0_), channel_id=1, source_target_pairs={{0,2},{2,0},{4,6},{6,4},{8,10},{10,8},{12,14},{14,12},{16,18},{18,... | collective-permute-start | bytes 49160 | tf_op jit(solution)/shard_map/ppermute | solution.py:404
  59.8 3.3 %collective-permute-start.5 = (bf16[2,216,512]{2,1,0:T(8,128)(2,1)S(1)}, bf16[2,216,512]{2,1,0:T(8,128)(2,1)S(1)}, u32[]{:S(2)}, u32[]{:S(2)}) collective-permute-start(bf16[2,216,512]{2,1,0:T(8,128)(2,1)S(1)} %get-tuple-element.47), channel_id=1, source_target_pairs={{0,16},{1,17},{2,18},{3,19},{4,20},{5,21},{6,22},{7,23},{8,24},{9,... | collective-permute-start | bytes 1327112 | tf_op jit(solution)/shard_map/ppermute | solution.py:398
  63.2 0.7 shard_map.155
  63.9 3.7 %all-to-all-start.2 = ((bf16[8,32,384]{2,1,0:T(8,128)(2,1)}), bf16[8,32,384]{2,1,0:T(8,128)(2,1)S(1)}, u32[]{:S(2)}, u32[]{:S(2)}) async-start(bf16[8,32,384]{2,1,0:T(8,128)(2,1)} %shard_map.155), calls=%async_computation.2 | async-start | bytes 393216 | tf_op jit(solution)/shard_map/all_to_all | solution.py:416
  67.6 5.4 %collective-permute-start.7 = (bf16[2,72,512]{2,1,0:T(8,128)(2,1)S(1)}, bf16[2,72,512]{2,1,0:T(8,128)(2,1)}, u32[]{:S(2)}, u32[]{:S(2)}) collective-permute-start(bf16[2,72,512]{2,1,0:T(8,128)(2,1)S(1)} %copy-done.11), channel_id=1, source_target_pairs={{0,19},{1,18},{2,21},{3,20},{4,23},{5,22},{6,25},{7,24},{8,27},{9,... | collective-permute-start | bytes 442376 | tf_op jit(solution)/shard_map/ppermute | solution.py:398
  73.1 3.2 %all-to-all-done.2.refs_0_ = bf16[8,32,384]{2,1,0:T(8,128)(2,1)S(1)} async-done(((bf16[8,32,384]{2,1,0:T(8,128)(2,1)}), bf16[8,32,384]{2,1,0:T(8,128)(2,1)S(1)}, u32[]{:S(2)}, u32[]{:S(2)}) %all-to-all-start.2) | async-done | bytes 196640 | tf_op jit(solution)/shard_map/all_to_all | solution.py:416
  76.3 0.8 shard_map.156
  77.1 0.6 copy-done.12
  77.7 3.5 %all-to-all-start.3 = ((bf16[4,256,256]{2,1,0:T(8,128)(2,1)}), bf16[4,256,256]{2,1,0:T(8,128)(2,1)S(1)}, u32[]{:S(2)}, u32[]{:S(2)}) async-start(bf16[4,256,256]{2,1,0:T(8,128)(2,1)} %get-tuple-element.60), calls=%async_computation.3 | async-start | bytes 1048576 | tf_op jit(solution)/shard_map/all_to_all | solution.py:410
  81.2 2.9 %collective-permute-start.11 = (bf16[256,128]{1,0:T(8,128)(2,1)}, bf16[256,128]{1,0:T(8,128)(2,1)S(1)}, u32[]{:S(2)}, u32[]{:S(2)}) collective-permute-start(bf16[256,128]{1,0:T(8,128)(2,1)} %copy-done.12), channel_id=1, source_target_pairs={{0,16},{2,18},{4,20},{6,22},{8,24},{10,26},{12,28},{14,30},{16,0},... | collective-permute-start | bytes 196616 | tf_op jit(solution)/shard_map/ppermute | solution.py:404
  84.1 1.0 %copy-done.22 = bf16[2,216,512]{2,1,0:T(8,128)(2,1)S(1)} copy-done((bf16[2,216,512]{2,1,0:T(8,128)(2,1)S(1)}, bf16[2,216,512]{2,1,0:T(8,128)(2,1)}, u32[]{:S(2)}) %copy-start.22) | copy-done | bytes 442392
  85.1 3.2 %shard_map.150 = (f32[8,128]{1,0:T(8,128)S(1)}, bf16[12,12,4,512]{3,2,1,0:T(4,128)(2,1)}, bf16[12,12,4,512]{3,2,1,0:T(4,128)(2,1)}) custom-call(bf16[12,12,4,512]{3,2,1,0:T(4,128)(2,1)S(1)} %copy-done.2, bf16[12,12,4,512]{3,2,1,0:T(4,128)(2,1)S(1)} %copy-done.4, f32[1,512]{1,0:T(1,128)S(1)} %bitcast.9, bf16[2,216,512]{2,1,0:T(8,128)(2,1)S(1)} %copy-done.22, ...), custom_call_target="tpu_custom_call" | custom-call | flops 30000001024 | tf_op jit(solution)/shard_map/pallas_call | solution.py:59
  88.3 1.5 %shard_map.157 = (f32[2,2,4,3312]{3,2,1,0:T(4,128)}, f32[8,128]{1,0:T(8,128)S(1)}) custom-call(s32[2]{0:T(128)S(1)} %pad_add_fusion.refs_0_, bf16[256,128]{1,0:T(8,128)(2,1)S(1)} %copy-done.13, bf16[256,128]{1,0:T(8,128)(2,1)S(1)} %collective-permute-done.11.refs_2_, f32[8,128]{1,0:T(8,128)S(1)} %get-tuple-element.62.refs_3_), custom_call_target="tpu_custom_call" | custom-call | flops 1000000000 | tf_op jit(solution)/shard_map/pallas_call | solution.py:59
  89.8 2.2 %collective-permute-start.15 = (bf16[1024,256]{1,0:T(8,128)(2,1)S(1)}, bf16[1024,256]{1,0:T(8,128)(2,1)S(1)}, u32[]{:S(2)}, u32[]{:S(2)}) collective-permute-start(bf16[1024,256]{1,0:T(8,128)(2,1)S(1)} %bitcast.5), channel_id=1, source_target_pairs={{0,16},{2,18},{4,20},{6,22},{8,24},{10,26},{12,28},{14,30},{16,0},... | collective-permute-start | bytes 1572872 | tf_op jit(solution)/shard_map/ppermute | solution.py:404
  92.0 0.9 shard_map.158.refs_0_
  93.0 1.3 %collective-permute-start.13 = (f32[8,512]{1,0:T(8,128)S(1)}, f32[8,512]{1,0:T(8,128)S(1)}, u32[]{:S(2)}, u32[]{:S(2)}) collective-permute-start(f32[8,512]{1,0:T(8,128)S(1)} %shard_map.158.refs_0_), channel_id=1, source_target_pairs={{0,1},{1,0},{2,3},{3,2},{4,5},{5,4},{6,7},{7,6},{8,9},{9,8},{10,11... | collective-permute-start | bytes 49160 | tf_op jit(solution)/shard_map/ppermute | solution.py:420
  94.3 0.8 collective-permute-start.12
  95.1 1.9 %shard_map.159 = (f32[8,128]{1,0:T(8,128)S(1)}, f32[3,512,256]{2,1,0:T(8,128)}, f32[256,512]{1,0:T(8,128)}) custom-call(s32[2]{0:T(128)S(1)} %pad_add_fusion.refs_0_, bf16[1024,256]{1,0:T(8,128)(2,1)S(1)} %bitcast.7, bf16[1024,256]{1,0:T(8,128)(2,1)S(1)} %collective-permute-done.15.refs_2_), custom_call_target="tpu_custom_call" | custom-call | flops 2000000000 | tf_op jit(solution)/shard_map/pallas_call | solution.py:59
  97.1 0.6 shard_map.160
  (55 shorter events, 0.2 us)
Async XLA Ops:
  0.6 14.4 %copy-start.18 = (bf16[276,276]{1,0:T(8,128)(2,1)S(1)}, bf16[276,276]{1,0:T(8,128)(2,1)}, u32[]{:S(2)}) copy-start(bf16[276,276]{1,0:T(8,128)(2,1)} %constant.36.clone.refs_2_) | copy-start | bytes 457060
  0.6 14.4 %copy-start.5 = (bf16[256,512]{1,0:T(8,128)(2,1)S(1)}, bf16[256,512]{1,0:T(8,128)(2,1)}, u32[]{:S(2)}) copy-start(bf16[256,512]{1,0:T(8,128)(2,1)} %refs_2_.6) | copy-start | bytes 786436
  0.7 14.4 %copy-start.9 = (f32[2,2,4,3312]{3,2,1,0:T(4,128)S(1)}, f32[2,2,4,3312]{3,2,1,0:T(4,128)}, u32[]{:S(2)}) copy-start(f32[2,2,4,3312]{3,2,1,0:T(4,128)} %refs_1_.5) | copy-start | bytes 635908
  2.9 16.0 %collective-permute-start = (bf16[2,216,512]{2,1,0:T(8,128)(2,1)}, bf16[2,216,512]{2,1,0:T(8,128)(2,1)S(1)}, u32[]{:S(2)}, u32[]{:S(2)}) collective-permute-start(bf16[2,216,512]{2,1,0:T(8,128)(2,1)} %get-tuple-element.37), channel_id=1, source_target_pairs={{0,240},{1,241},{2,242},{3,243},{4,244},{5,245},{6,246},{7,247},{8... | collective-permute-start | bytes 1327112 | tf_op jit(solution)/shard_map/ppermute | solution.py:398
  6.1 10.9 %collective-permute-start.1 = (bf16[2,72,512]{2,1,0:T(8,128)(2,1)}, bf16[2,72,512]{2,1,0:T(8,128)(2,1)S(1)}, u32[]{:S(2)}, u32[]{:S(2)}) collective-permute-start(bf16[2,72,512]{2,1,0:T(8,128)(2,1)} %get-tuple-element.38), channel_id=1, source_target_pairs={{0,15},{1,14},{2,1},{3,0},{4,3},{5,2},{6,5},{7,4},{8,7},{9,6},{10,... | collective-permute-start | bytes 442376 | tf_op jit(solution)/shard_map/ppermute | solution.py:398
  9.3 9.5 %collective-permute-start.2 = (bf16[2,72,512]{2,1,0:T(8,128)(2,1)}, bf16[2,72,512]{2,1,0:T(8,128)(2,1)S(1)}, u32[]{:S(2)}, u32[]{:S(2)}) collective-permute-start(bf16[2,72,512]{2,1,0:T(8,128)(2,1)} %get-tuple-element.39), channel_id=1, source_target_pairs={{0,255},{1,254},{2,241},{3,240},{4,243},{5,242},{6,245},{7,244},{8... | collective-permute-start | bytes 442376 | tf_op jit(solution)/shard_map/ppermute | solution.py:398
  15.1 3.8 %copy-start = (bf16[3,512,256]{2,1,0:T(8,128)(2,1)S(1)}, bf16[3,512,256]{2,1,0:T(8,128)(2,1)}, u32[]{:S(2)}) copy-start(bf16[3,512,256]{2,1,0:T(8,128)(2,1)} %refs_2_.7) | copy-start | bytes 2359300
  15.1 3.8 %copy-start.1 = (bf16[12,12,4,512]{3,2,1,0:T(4,128)(2,1)S(1)}, bf16[12,12,4,512]{3,2,1,0:T(4,128)(2,1)}, u32[]{:S(2)}) copy-start(bf16[12,12,4,512]{3,2,1,0:T(4,128)(2,1)} %refs_0_.3) | copy-start | bytes 1769476
  15.1 3.8 %copy-start.3 = (bf16[12,12,4,512]{3,2,1,0:T(4,128)(2,1)S(1)}, bf16[12,12,4,512]{3,2,1,0:T(4,128)(2,1)}, u32[]{:S(2)}) copy-start(bf16[12,12,4,512]{3,2,1,0:T(4,128)(2,1)} %refs_1_.7) | copy-start | bytes 1769476
  15.1 3.8 %copy-start.14 = (f32[512]{0:T(512)S(1)}, f32[512]{0:T(512)}, u32[]{:S(2)}) copy-start(f32[512]{0:T(512)} %param.12) | copy-start | bytes 6148
  15.1 3.8 %copy-start.16 = (bf16[2,288,288]{2,1,0:T(8,128)(2,1)S(1)}, bf16[2,288,288]{2,1,0:T(8,128)(2,1)}, u32[]{:S(2)}) copy-start(bf16[2,288,288]{2,1,0:T(8,128)(2,1)} %constant.34.clone.refs_6_) | copy-start | bytes 995332
  16.9 9.9 %collective-permute-start.3 = (bf16[256,512]{1,0:T(8,128)(2,1)S(1)}, bf16[256,512]{1,0:T(8,128)(2,1)S(1)}, u32[]{:S(2)}, u32[]{:S(2)}) collective-permute-start(bf16[256,512]{1,0:T(8,128)(2,1)S(1)} %get-tuple-element.45), channel_id=1, source_target_pairs={{0,1},{1,0},{2,3},{3,2},{4,5},{5,4},{6,7},{7,6},{8,9},{9,8},{10,11... | collective-permute-start | bytes 786440 | tf_op jit(solution)/shard_map/ppermute | solution.py:420
  18.9 7.9 %copy-start.15 = (bf16[2,288,288]{2,1,0:T(8,128)(2,1)S(1)}, bf16[2,288,288]{2,1,0:T(8,128)(2,1)}, u32[]{:S(2)}) copy-start(bf16[2,288,288]{2,1,0:T(8,128)(2,1)} %constant.35.clone.refs_5_) | copy-start | bytes 995332
  24.7 3.3 %copy-start.19 = (f32[2304,144]{1,0:T(8,128)}, f32[2304,144]{1,0:T(8,128)S(1)}, u32[]{:S(2)}) copy-start(f32[2304,144]{1,0:T(8,128)S(1)} %get-tuple-element.54.refs_1_) | copy-start | bytes 3981316
  24.7 3.6 %collective-permute-start.8 = (bf16[1024,256]{1,0:T(8,128)(2,1)S(1)}, bf16[1024,256]{1,0:T(8,128)(2,1)S(1)}, u32[]{:S(2)}, u32[]{:S(2)}) collective-permute-start(bf16[1024,256]{1,0:T(8,128)(2,1)S(1)} %get-tuple-element.53), channel_id=1, source_target_pairs={{0,16},{2,18},{4,20},{6,22},{8,24},{10,26},{12,28},{14,30},{16,0},... | collective-permute-start | bytes 1572872 | tf_op jit(solution)/shard_map/ppermute | solution.py:404
  26.8 1.2 %copy-start.7 = (bf16[256,512]{1,0:T(8,128)(2,1)}, bf16[256,512]{1,0:T(8,128)(2,1)S(1)}, u32[]{:S(2)}) copy-start(bf16[256,512]{1,0:T(8,128)(2,1)S(1)} %collective-permute-done.3.refs_6_.refs_3_) | copy-start | bytes 786436
  28.0 4.7 %copy-start.17 = (bf16[2,138,276]{2,1,0:T(8,128)(2,1)S(1)}, bf16[2,138,276]{2,1,0:T(8,128)(2,1)}, u32[]{:S(2)}) copy-start(bf16[2,138,276]{2,1,0:T(8,128)(2,1)} %constant.37.clone.refs_2_) | copy-start | bytes 457060
  28.0 21.3 %collective-permute-start.4 = (bf16[576,768]{1,0:T(8,128)(2,1)S(1)}, bf16[576,768]{1,0:T(8,128)(2,1)S(1)}, u32[]{:S(2)}, u32[]{:S(2)}) collective-permute-start(bf16[576,768]{1,0:T(8,128)(2,1)S(1)} %shard_map.148.refs_0_.refs_2_), channel_id=1, source_target_pairs={{0,1},{1,0},{2,3},{3,2},{4,5},{5,4},{6,7},{7,6},{8,9},{9,8},{10,11... | collective-permute-start | bytes 2654216 | tf_op jit(solution)/shard_map/ppermute | solution.py:420
  29.2 12.7 %all-to-all-start = ((bf16[4,256,256]{2,1,0:T(8,128)(2,1)}), bf16[4,256,256]{2,1,0:T(8,128)(2,1)S(1)}, u32[]{:S(2)}, u32[]{:S(2)}) async-start(bf16[4,256,256]{2,1,0:T(8,128)(2,1)} %shard_map.151), calls=%async_computation | async-start | bytes 1048576 | tf_op jit(solution)/shard_map/all_to_all | solution.py:410
  32.7 1.7 %copy-start.20 = (f32[2304,144]{1,0:T(8,128)S(1)}, f32[2304,144]{1,0:T(8,128)}, u32[]{:S(2)}) copy-start(f32[2304,144]{1,0:T(8,128)} %copy-done.19) | copy-start | bytes 3981316
  36.3 1.5 %collective-permute-start.9 = (bf16[256,128]{1,0:T(8,128)(2,1)S(1)}, bf16[256,128]{1,0:T(8,128)(2,1)S(1)}, u32[]{:S(2)}, u32[]{:S(2)}) collective-permute-start(bf16[256,128]{1,0:T(8,128)(2,1)S(1)} %get-tuple-element.56), channel_id=1, source_target_pairs={{0,16},{2,18},{4,20},{6,22},{8,24},{10,26},{12,28},{14,30},{16,0},... | collective-permute-start | bytes 196616 | tf_op jit(solution)/shard_map/ppermute | solution.py:404
  42.7 13.0 %all-to-all-start.1 = ((bf16[8,32,384]{2,1,0:T(8,128)(2,1)}), bf16[8,32,384]{2,1,0:T(8,128)(2,1)S(1)}, u32[]{:S(2)}, u32[]{:S(2)}) async-start(bf16[8,32,384]{2,1,0:T(8,128)(2,1)} %shard_map.153), calls=%async_computation.1 | async-start | bytes 393216 | tf_op jit(solution)/shard_map/all_to_all | solution.py:416
  49.3 1.0 copy-start.6
  50.3 0.9 copy-start.8
  52.6 0.7 copy-start.10
  53.3 0.8 copy-start.21
  55.7 11.9 %copy-start.11 = (bf16[2,72,512]{2,1,0:T(8,128)(2,1)S(1)}, bf16[2,72,512]{2,1,0:T(8,128)(2,1)}, u32[]{:S(2)}) copy-start(bf16[2,72,512]{2,1,0:T(8,128)(2,1)} %copy-done.10) | copy-start | bytes 442372
  55.7 7.4 %collective-permute-start.10 = (bf16[32,256]{1,0:T(8,128)(2,1)S(1)}, bf16[32,256]{1,0:T(8,128)(2,1)S(1)}, u32[]{:S(2)}, u32[]{:S(2)}) collective-permute-start(bf16[32,256]{1,0:T(8,128)(2,1)S(1)} %get-tuple-element.58.refs_0_), channel_id=1, source_target_pairs={{0,2},{2,0},{4,6},{6,4},{8,10},{10,8},{12,14},{14,12},{16,18},{18,... | collective-permute-start | bytes 49160 | tf_op jit(solution)/shard_map/ppermute | solution.py:404
  59.8 24.3 %collective-permute-start.5 = (bf16[2,216,512]{2,1,0:T(8,128)(2,1)S(1)}, bf16[2,216,512]{2,1,0:T(8,128)(2,1)S(1)}, u32[]{:S(2)}, u32[]{:S(2)}) collective-permute-start(bf16[2,216,512]{2,1,0:T(8,128)(2,1)S(1)} %get-tuple-element.47), channel_id=1, source_target_pairs={{0,16},{1,17},{2,18},{3,19},{4,20},{5,21},{6,22},{7,23},{8,24},{9,... | collective-permute-start | bytes 1327112 | tf_op jit(solution)/shard_map/ppermute | solution.py:398
  63.9 12.4 %all-to-all-start.2 = ((bf16[8,32,384]{2,1,0:T(8,128)(2,1)}), bf16[8,32,384]{2,1,0:T(8,128)(2,1)S(1)}, u32[]{:S(2)}, u32[]{:S(2)}) async-start(bf16[8,32,384]{2,1,0:T(8,128)(2,1)} %shard_map.155), calls=%async_computation.2 | async-start | bytes 393216 | tf_op jit(solution)/shard_map/all_to_all | solution.py:416
  67.6 16.5 %collective-permute-start.6 = (bf16[2,72,512]{2,1,0:T(8,128)(2,1)}, bf16[2,72,512]{2,1,0:T(8,128)(2,1)}, u32[]{:S(2)}, u32[]{:S(2)}) collective-permute-start(bf16[2,72,512]{2,1,0:T(8,128)(2,1)} %get-tuple-element.48), channel_id=1, source_target_pairs={{0,3},{1,2},{2,5},{3,4},{4,7},{5,6},{6,9},{7,8},{8,11},{9,10},{10,... | collective-permute-start | bytes 442376 | tf_op jit(solution)/shard_map/ppermute | solution.py:398
  67.6 16.5 %copy-start.2 = (bf16[12,12,4,512]{3,2,1,0:T(4,128)(2,1)S(1)}, bf16[12,12,4,512]{3,2,1,0:T(4,128)(2,1)}, u32[]{:S(2)}) copy-start(bf16[12,12,4,512]{3,2,1,0:T(4,128)(2,1)} %refs_0_.3) | copy-start | bytes 1769476
  67.6 16.5 %copy-start.4 = (bf16[12,12,4,512]{3,2,1,0:T(4,128)(2,1)S(1)}, bf16[12,12,4,512]{3,2,1,0:T(4,128)(2,1)}, u32[]{:S(2)}) copy-start(bf16[12,12,4,512]{3,2,1,0:T(4,128)(2,1)} %refs_1_.7) | copy-start | bytes 1769476
  67.6 16.4 %collective-permute-start.7 = (bf16[2,72,512]{2,1,0:T(8,128)(2,1)S(1)}, bf16[2,72,512]{2,1,0:T(8,128)(2,1)}, u32[]{:S(2)}, u32[]{:S(2)}) collective-permute-start(bf16[2,72,512]{2,1,0:T(8,128)(2,1)S(1)} %copy-done.11), channel_id=1, source_target_pairs={{0,19},{1,18},{2,21},{3,20},{4,23},{5,22},{6,25},{7,24},{8,27},{9,... | collective-permute-start | bytes 442376 | tf_op jit(solution)/shard_map/ppermute | solution.py:398
  77.1 0.6 copy-start.12
  77.7 12.1 %all-to-all-start.3 = ((bf16[4,256,256]{2,1,0:T(8,128)(2,1)}), bf16[4,256,256]{2,1,0:T(8,128)(2,1)S(1)}, u32[]{:S(2)}, u32[]{:S(2)}) async-start(bf16[4,256,256]{2,1,0:T(8,128)(2,1)} %get-tuple-element.60), calls=%async_computation.3 | async-start | bytes 1048576 | tf_op jit(solution)/shard_map/all_to_all | solution.py:410
  81.2 7.1 %collective-permute-start.11 = (bf16[256,128]{1,0:T(8,128)(2,1)}, bf16[256,128]{1,0:T(8,128)(2,1)S(1)}, u32[]{:S(2)}, u32[]{:S(2)}) collective-permute-start(bf16[256,128]{1,0:T(8,128)(2,1)} %copy-done.12), channel_id=1, source_target_pairs={{0,16},{2,18},{4,20},{6,22},{8,24},{10,26},{12,28},{14,30},{16,0},... | collective-permute-start | bytes 196616 | tf_op jit(solution)/shard_map/ppermute | solution.py:404
  84.1 1.0 %copy-start.22 = (bf16[2,216,512]{2,1,0:T(8,128)(2,1)S(1)}, bf16[2,216,512]{2,1,0:T(8,128)(2,1)}, u32[]{:S(2)}) copy-start(bf16[2,216,512]{2,1,0:T(8,128)(2,1)} %copy-done.21) | copy-start | bytes 1327108
  85.1 3.2 %copy-start.13 = (bf16[256,128]{1,0:T(8,128)(2,1)S(1)}, bf16[256,128]{1,0:T(8,128)(2,1)}, u32[]{:S(2)}) copy-start(bf16[256,128]{1,0:T(8,128)(2,1)} %copy-done.12) | copy-start | bytes 196612
  89.8 5.3 %collective-permute-start.15 = (bf16[1024,256]{1,0:T(8,128)(2,1)S(1)}, bf16[1024,256]{1,0:T(8,128)(2,1)S(1)}, u32[]{:S(2)}, u32[]{:S(2)}) collective-permute-start(bf16[1024,256]{1,0:T(8,128)(2,1)S(1)} %bitcast.5), channel_id=1, source_target_pairs={{0,16},{2,18},{4,20},{6,22},{8,24},{10,26},{12,28},{14,30},{16,0},... | collective-permute-start | bytes 1572872 | tf_op jit(solution)/shard_map/ppermute | solution.py:404
  92.9 4.1 %collective-permute-start.14 = (f32[8,512]{1,0:T(8,128)S(1)}, f32[8,512]{1,0:T(8,128)S(1)}, u32[]{:S(2)}, u32[]{:S(2)}) collective-permute-start(f32[8,512]{1,0:T(8,128)S(1)} %shard_map.158.refs_0_), channel_id=1, source_target_pairs={{0,17},{1,16},{16,1},{17,0},{32,49},{33,48},{48,33},{49,32},{64,81... | collective-permute-start | bytes 49160 | tf_op jit(solution)/shard_map/ppermute | solution.py:425
  93.0 4.1 %collective-permute-start.13 = (f32[8,512]{1,0:T(8,128)S(1)}, f32[8,512]{1,0:T(8,128)S(1)}, u32[]{:S(2)}, u32[]{:S(2)}) collective-permute-start(f32[8,512]{1,0:T(8,128)S(1)} %shard_map.158.refs_0_), channel_id=1, source_target_pairs={{0,1},{1,0},{2,3},{3,2},{4,5},{5,4},{6,7},{7,6},{8,9},{9,8},{10,11... | collective-permute-start | bytes 49160 | tf_op jit(solution)/shard_map/ppermute | solution.py:420
  94.3 2.8 %collective-permute-start.12 = (f32[8,512]{1,0:T(8,128)S(1)}, f32[8,512]{1,0:T(8,128)S(1)}, u32[]{:S(2)}, u32[]{:S(2)}) collective-permute-start(f32[8,512]{1,0:T(8,128)S(1)} %shard_map.158.refs_0_), channel_id=1, source_target_pairs={{0,16},{2,18},{4,20},{6,22},{8,24},{10,26},{12,28},{14,30},{16,0},... | collective-permute-start | bytes 49160 | tf_op jit(solution)/shard_map/ppermute | solution.py:404

commit v9 on v8

--- a/solution.py
+++ b/solution.py
@@ -1,3 +1,5 @@
+import functools
+
 import jax
 import jax.numpy as jnp
 import numpy as np
@@ -96,18 +98,23 @@
         copy.wait()
 
 
-def halo_kernel(latent, cot, o_lon, o_lat, o_cor, tiles, h_lon, h_lat, h_cor, in_sems, out_sems):
+def halo_kernel(which, latent, cot, *refs):
+    n = len(which)
+    outs, tiles, helds, in_sems, out_sems = refs[:n], refs[n], refs[n + 1 : 2 * n + 1], refs[-2], refs[-1]
+    lons = (0, 3, 6, 9) if 2 in which else (0, 3)
     arrived, copies = [], []
-    for first in (0, 3, 6, 9):
+    for first in lons:
         for j, grid in enumerate((latent, cot)):
             rows = pl.ds(first, 3)
-            sent(arrived, grid.at[rows], tiles.at[j, rows], in_sems.at[len(arrived)])
-    finish(arrived[:4])
-    for places, held, ref in ((PLACES[1], h_lon, o_lon), (PLACES[3], h_cor, o_cor), (PLACES[2], h_lat, o_lat)):
-        if held is h_lat:
-            finish(arrived[4:])
+            if 2 in which:
+                part = (rows, pl.ds(0, 3))
+                sent(arrived, grid.at[part], tiles.at[(j,) + part], in_sems.at[len(arrived)])
+            else:
+                sent(arrived, grid.at[rows], tiles.at[j, rows], in_sems.at[len(arrived)])
+    finish(arrived)
+    for k, held, ref in zip(which, helds, outs):
         for j in range(2):
-            held[j] = jnp.concatenate([flat(tiles[j, lon, lat]) for lon, lat in places], 0)
+            held[j] = jnp.concatenate([flat(tiles[j, lon, lat]) for lon, lat in PLACES[k]], 0)
             sent(copies, held.at[j], ref.at[j], out_sems.at[len(copies)])
     finish(copies)
 
@@ -437,18 +444,24 @@
 
     part = lambda n: ((2, n, 512), BF)
     halos = [part(216), part(72), part(72)]
-    s_lon, s_lat, s_cor = call(
-        halo_kernel,
-        [],
-        [],
-        [pltpu.VMEM((2,) + latent.shape, BF)]
-        + [pltpu.VMEM(shape, BF) for shape, _ in halos]
-        + [pltpu.SemaphoreType.DMA((8,)), pltpu.SemaphoreType.DMA((6,))],
-        smem=0,
-        mib=60,
-        hbm=[latent, cotangent],
-        hbm_outs=halos,
-    )
+    def halo(which, after):
+        shapes = [halos[k - 1] for k in which]
+        return call(
+            functools.partial(halo_kernel, which),
+            [],
+            [],
+            [pltpu.VMEM((2,) + latent.shape, BF)]
+            + [pltpu.VMEM(shape, BF) for shape, _ in shapes]
+            + [pltpu.SemaphoreType.DMA((8,)), pltpu.SemaphoreType.DMA((4,))],
+            smem=0,
+            mib=60,
+            hbm=[latent, cotangent],
+            hbm_outs=shapes,
+            after=after,
+        )
+
+    s_lat, s_cor = halo((2, 3), [])
+    (s_lon,) = halo((1,), [s_lat])
     in_lon, in_lat, in_cor = moved(s_lon, -1, 0), moved(s_lat, 0, -1), moved(s_cor, -1, -1)
 
     bias, w_copy = call(
@@ -456,7 +469,7 @@
         [((16 * WTOK, WTOK), F32), (w_out.shape, BF)],
         [info, bias_table, order, w_out],
         [pltpu.VMEM((192, 276), F32)] * 2 + [pltpu.VMEM((192, 128), F32)] * 3,
-        us=2,
+        us=30,
     )
     w_other = other_group(w_copy)
 

time: 98.2 us -> 99.9 us (1.017)
  Pallas kernels: 25.5 us -> 27.2 us
  waiting for transfers between devices: 14 us -> 12.3 us
  starting transfers between devices: 50.3 us -> 51.9 us
    pallas_call x16 -> x17, Pallas kernels: 25.5 us -> 27.2 us  [call(): pl.pallas_call(kernel, out_shape=[jax.ShapeDtypeStruct(s, t) for s, t in...]
    ppermute x6, waiting for transfers between devices: 1.84 us -> 0.83 us  [moved(): return lax.ppermute(value, ('lon', 'lat', 'tp'), pairs)]
  transfers between devices with their start and end apart: 20 -> 20, of which waited for: 7 -> 7; matrix products, arithmetic and copies ran while one was open for 0% -> 0% of each run, Pallas kernels for 23% -> 25%
where the time goes in v9:
time: 99.9 us; the launch traced here: 99.2 us
  starting transfers between devices  51.9 us (52%)
  Pallas kernels  27.2 us (27%)
  waiting for transfers between devices  12.3 us (12%)
  local copies, waits for them, and re-layouts  6.7 us (7%)
  between operations  1.01 us (1%)
    pallas_call x17, Pallas kernels, call(): pl.pallas_call(kernel, out_shape=[jax.ShapeDtypeStruct(s, t) for s, t in...  27.2 us
    ppermute x6, starting transfers between devices, moved(): return lax.ppermute(value, ('lon', 'lat', 'tp'), pairs)  21.4 us
    ppermute x6, starting transfers between devices, swapped(): return lax.ppermute(value, ('lon', 'lat'), pairs)  13.4 us
    all_to_all x2, starting transfers between devices, across_z(): return lax.all_to_all(value, 'lon', 0, 0, axis_index_groups=groups)  8.62 us
    all_to_all x2, starting transfers between devices, across_y(): return lax.all_to_all(value, 'lat', 0, 0, axis_index_groups=groups)  6.96 us
    unnamed x46, local copies, waits for them, and re-layouts  6.7 us
    all_to_all x2, waiting for transfers between devices, across_z(): return lax.all_to_all(value, 'lon', 0, 0, axis_index_groups=groups)  4.64 us
    all_to_all x2, waiting for transfers between devices, across_y(): return lax.all_to_all(value, 'lat', 0, 0, axis_index_groups=groups)  4.01 us
  transfers between devices with their start and end apart: 20, of which 7 were waited for; matrix products, arithmetic and copies ran while one was open for 0% of the time, Pallas kernels for 25%

profile of v9, /device:TPU:1, one launch (start us, length us, event | category | flops | bytes accessed | tf_op | source)
XLA Modules:
  0.0 99.2 jit_solution(17107503710411079581)
XLA Ops:
  0.6 1.7 %shard_map.145 = (bf16[2,72,512]{2,1,0:T(8,128)(2,1)}, bf16[2,72,512]{2,1,0:T(8,128)(2,1)}) custom-call(bf16[12,12,4,512]{3,2,1,0:T(4,128)(2,1)} %refs_0_.5, bf16[12,12,4,512]{3,2,1,0:T(4,128)(2,1)} %refs_1_.9), custom_call_target="tpu_custom_call" | custom-call | flops 1000000000 | tf_op jit(solution)/shard_map/pallas_call | solution.py:61
  2.4 6.4 %collective-permute-start.2 = (bf16[2,72,512]{2,1,0:T(8,128)(2,1)}, bf16[2,72,512]{2,1,0:T(8,128)(2,1)S(1)}, u32[]{:S(2)}, u32[]{:S(2)}) collective-permute-start(bf16[2,72,512]{2,1,0:T(8,128)(2,1)} %get-tuple-element.37), channel_id=1, source_target_pairs={{0,255},{1,254},{2,241},{3,240},{4,243},{5,242},{6,245},{7,244},{8... | collective-permute-start | bytes 442376 | tf_op jit(solution)/shard_map/ppermute | solution.py:405
  8.8 0.2 collective-permute-start.1
  9.0 2.0 %shard_map.146 = bf16[2,216,512]{2,1,0:T(8,128)(2,1)} custom-call(bf16[12,12,4,512]{3,2,1,0:T(4,128)(2,1)} %refs_0_.5, bf16[12,12,4,512]{3,2,1,0:T(4,128)(2,1)} %refs_1_.9, bf16[2,72,512]{2,1,0:T(8,128)(2,1)} %get-tuple-element.36.refs_2_), custom_call_target="tpu_custom_call" | custom-call | flops 1000000000 | tf_op jit(solution)/shard_map/pallas_call | solution.py:61
  11.0 5.4 %collective-permute-start = (bf16[2,216,512]{2,1,0:T(8,128)(2,1)}, bf16[2,216,512]{2,1,0:T(8,128)(2,1)S(1)}, u32[]{:S(2)}, u32[]{:S(2)}) collective-permute-start(bf16[2,216,512]{2,1,0:T(8,128)(2,1)} %shard_map.146), channel_id=1, source_target_pairs={{0,240},{1,241},{2,242},{3,243},{4,244},{5,245},{6,246},{7,247},{8... | collective-permute-start | bytes 1327112 | tf_op jit(solution)/shard_map/ppermute | solution.py:405
  16.6 1.8 %shard_map.147 = (f32[2304,144]{1,0:T(8,128)S(1)}, bf16[256,512]{1,0:T(8,128)(2,1)S(1)}) custom-call(s32[2]{0:T(128)S(1)} %pad_add_fusion.refs_0_, f32[2,2,4,3312]{3,2,1,0:T(4,128)S(1)} %copy-done.9, bf16[276,276]{1,0:T(8,128)(2,1)S(1)} %copy-done.18, bf16[256,512]{1,0:T(8,128)(2,1)S(1)} %copy-done.5), custom_call_target="tpu_custom_call" | custom-call | flops 30000001024 | tf_op jit(solution)/shard_map/pallas_call | solution.py:61
  18.5 0.8 collective-permute-done.refs_3_
  19.4 5.9 %shard_map.148 = (f32[1024,256]{1,0:T(8,128)S(1)}, bf16[1024,256]{1,0:T(8,128)(2,1)S(1)}, f32[2304,144]{1,0:T(8,128)S(1)}, bf16[576,256]{1,0:T(8,128)(2,1)S(1)},...) custom-call(s32[2]{0:T(128)S(1)} %pad_add_fusion.refs_0_, ...), custom_call_target="tpu_custom_call" | custom-call | flops 8999999488 | tf_op jit(solution)/shard_map/pallas_call | solution.py:61
  25.2 3.9 %collective-permute-start.8 = (bf16[1024,256]{1,0:T(8,128)(2,1)S(1)}, bf16[1024,256]{1,0:T(8,128)(2,1)S(1)}, u32[]{:S(2)}, u32[]{:S(2)}) collective-permute-start(bf16[1024,256]{1,0:T(8,128)(2,1)S(1)} %get-tuple-element.51), channel_id=1, source_target_pairs={{0,16},{2,18},{4,20},{6,22},{8,24},{10,26},{12,28},{14,30},{16,0},... | collective-permute-start | bytes 1572872 | tf_op jit(solution)/shard_map/ppermute | solution.py:411
  29.1 1.2 %shard_map.149.refs_0_.refs_2_ = bf16[576,768]{1,0:T(8,128)(2,1)S(1)} custom-call(bf16[576,256]{1,0:T(8,128)(2,1)S(1)} %get-tuple-element.39.refs_0_, bf16[576,256]{1,0:T(8,128)(2,1)S(1)} %get-tuple-element.40.refs_1_, bf16[576,256]{1,0:T(8,128)(2,1)S(1)} %get-tuple-element.41.refs_2_, bf16[576,256]{1,0:T(8,128)(2,1)S(1)} %get-tuple-element.42.refs_3_, ...), custom_call_target="tpu_custom_call" | custom-call | flops 2000000000 | tf_op jit(solution)/shard_map/pallas_call | solution.py:61
  30.4 0.2 collective-permute-done.8.refs_1_
  30.7 0.8 shard_map.152
  31.5 3.5 %all-to-all-start = ((bf16[4,256,256]{2,1,0:T(8,128)(2,1)}), bf16[4,256,256]{2,1,0:T(8,128)(2,1)S(1)}, u32[]{:S(2)}, u32[]{:S(2)}) async-start(bf16[4,256,256]{2,1,0:T(8,128)(2,1)} %shard_map.152), calls=%async_computation | async-start | bytes 1048576 | tf_op jit(solution)/shard_map/all_to_all | solution.py:417
  35.0 1.7 %copy-done.20 = f32[2304,144]{1,0:T(8,128)S(1)} copy-done((f32[2304,144]{1,0:T(8,128)S(1)}, f32[2304,144]{1,0:T(8,128)}, u32[]{:S(2)}) %copy-start.20) | copy-done | bytes 1327128
  36.7 2.0 %shard_map.153 = (bf16[256,128]{1,0:T(8,128)(2,1)S(1)}, bf16[256,128]{1,0:T(8,128)(2,1)S(1)}) custom-call(s32[2]{0:T(128)S(1)} %pad_add_fusion.refs_0_, f32[2304,144]{1,0:T(8,128)S(1)} %copy-done.20, bf16[2,138,276]{2,1,0:T(8,128)(2,1)S(1)} %copy-done.17), custom_call_target="tpu_custom_call" | custom-call | flops 2500000000 | tf_op jit(solution)/shard_map/pallas_call | solution.py:61
  38.7 0.6 collective-permute-start.9
  39.3 0.9 collective-permute-done.9.refs_2_
  40.2 4.0 %all-to-all-done.refs_0_ = bf16[4,256,256]{2,1,0:T(8,128)(2,1)S(1)} async-done(((bf16[4,256,256]{2,1,0:T(8,128)(2,1)}), bf16[4,256,256]{2,1,0:T(8,128)(2,1)S(1)}, u32[]{:S(2)}, u32[]{:S(2)}) %all-to-all-start) | async-done | bytes 524320 | tf_op jit(solution)/shard_map/all_to_all | solution.py:417
  44.2 0.8 shard_map.154
  45.0 4.9 %all-to-all-start.1 = ((bf16[8,32,384]{2,1,0:T(8,128)(2,1)}), bf16[8,32,384]{2,1,0:T(8,128)(2,1)S(1)}, u32[]{:S(2)}, u32[]{:S(2)}) async-start(bf16[8,32,384]{2,1,0:T(8,128)(2,1)} %shard_map.154), calls=%async_computation.1 | async-start | bytes 393216 | tf_op jit(solution)/shard_map/all_to_all | solution.py:423
  49.9 1.7 %collective-permute-done.4.refs_1_ = bf16[576,768]{1,0:T(8,128)(2,1)S(1)} collective-permute-done((bf16[576,768]{1,0:T(8,128)(2,1)S(1)}, bf16[576,768]{1,0:T(8,128)(2,1)S(1)}, u32[]{:S(2)}, u32[]{:S(2)}) %collective-permute-start.4) | collective-permute-done | bytes 884768 | tf_op jit(solution)/shard_map/ppermute | solution.py:427
  51.6 0.9 copy-done.6
  52.6 0.9 copy-done.8
  53.5 1.4 %shard_map.150 = (bf16[2,216,512]{2,1,0:T(8,128)(2,1)S(1)}, bf16[2,216,512]{2,1,0:T(8,128)(2,1)S(1)}, bf16[2,72,512]{2,1,0:T(8,128)(2,1)}, bf16[2,72,512]{2,1,0:T(8,128)(2,1)S(1)}, f32[8,128]{1,0:T(8,128)S(1)}) custom-call(bf16[576,768]{1,0:T(8,128)(2,1)S(1)} %shard_map.149.refs_0_.refs_2_, bf16[576,768]{1,0:T(8,128)(2,1)S(1)} %collective-permute-done.4.refs_1_, ...), custom_call_target="tpu_custom_call" | custom-call | flops 30000001024 | tf_op jit(solution)/shard_map/pallas_call | solution.py:61
  54.9 0.7 copy-done.10
  55.6 0.8 copy-done.21
  56.4 2.0 %all-to-all-done.1.refs_0_ = bf16[8,32,384]{2,1,0:T(8,128)(2,1)S(1)} async-done(((bf16[8,32,384]{2,1,0:T(8,128)(2,1)}), bf16[8,32,384]{2,1,0:T(8,128)(2,1)S(1)}, u32[]{:S(2)}, u32[]{:S(2)}) %all-to-all-start.1) | async-done | bytes 196640 | tf_op jit(solution)/shard_map/all_to_all | solution.py:423
  58.5 2.9 %collective-permute-start.10 = (bf16[32,256]{1,0:T(8,128)(2,1)S(1)}, bf16[32,256]{1,0:T(8,128)(2,1)S(1)}, u32[]{:S(2)}, u32[]{:S(2)}) collective-permute-start(bf16[32,256]{1,0:T(8,128)(2,1)S(1)} %get-tuple-element.56.refs_0_), channel_id=1, source_target_pairs={{0,2},{2,0},{4,6},{6,4},{8,10},{10,8},{12,14},{14,12},{16,18},{18,... | collective-permute-start | bytes 49160 | tf_op jit(solution)/shard_map/ppermute | solution.py:411
  61.3 3.4 %collective-permute-start.5 = (bf16[2,216,512]{2,1,0:T(8,128)(2,1)S(1)}, bf16[2,216,512]{2,1,0:T(8,128)(2,1)S(1)}, u32[]{:S(2)}, u32[]{:S(2)}) collective-permute-start(bf16[2,216,512]{2,1,0:T(8,128)(2,1)S(1)} %get-tuple-element.45), channel_id=1, source_target_pairs={{0,16},{1,17},{2,18},{3,19},{4,20},{5,21},{6,22},{7,23},{8,24},{9,... | collective-permute-start | bytes 1327112 | tf_op jit(solution)/shard_map/ppermute | solution.py:405
  64.7 0.7 shard_map.156
  65.4 3.7 %all-to-all-start.2 = ((bf16[8,32,384]{2,1,0:T(8,128)(2,1)}), bf16[8,32,384]{2,1,0:T(8,128)(2,1)S(1)}, u32[]{:S(2)}, u32[]{:S(2)}) async-start(bf16[8,32,384]{2,1,0:T(8,128)(2,1)} %shard_map.156), calls=%async_computation.2 | async-start | bytes 393216 | tf_op jit(solution)/shard_map/all_to_all | solution.py:423
  69.1 0.3 collective-permute-start.6
  69.4 5.7 %collective-permute-start.7 = (bf16[2,72,512]{2,1,0:T(8,128)(2,1)S(1)}, bf16[2,72,512]{2,1,0:T(8,128)(2,1)}, u32[]{:S(2)}, u32[]{:S(2)}) collective-permute-start(bf16[2,72,512]{2,1,0:T(8,128)(2,1)S(1)} %copy-done.11), channel_id=1, source_target_pairs={{0,19},{1,18},{2,21},{3,20},{4,23},{5,22},{6,25},{7,24},{8,27},{9,... | collective-permute-start | bytes 442376 | tf_op jit(solution)/shard_map/ppermute | solution.py:405
  75.1 2.6 %all-to-all-done.2.refs_0_ = bf16[8,32,384]{2,1,0:T(8,128)(2,1)S(1)} async-done(((bf16[8,32,384]{2,1,0:T(8,128)(2,1)}), bf16[8,32,384]{2,1,0:T(8,128)(2,1)S(1)}, u32[]{:S(2)}, u32[]{:S(2)}) %all-to-all-start.2) | async-done | bytes 196640 | tf_op jit(solution)/shard_map/all_to_all | solution.py:423
  77.7 0.8 shard_map.157
  78.5 0.6 copy-done.12
  79.2 3.5 %all-to-all-start.3 = ((bf16[4,256,256]{2,1,0:T(8,128)(2,1)}), bf16[4,256,256]{2,1,0:T(8,128)(2,1)S(1)}, u32[]{:S(2)}, u32[]{:S(2)}) async-start(bf16[4,256,256]{2,1,0:T(8,128)(2,1)} %get-tuple-element.58), calls=%async_computation.3 | async-start | bytes 1048576 | tf_op jit(solution)/shard_map/all_to_all | solution.py:417
  82.6 3.0 %collective-permute-start.11 = (bf16[256,128]{1,0:T(8,128)(2,1)}, bf16[256,128]{1,0:T(8,128)(2,1)S(1)}, u32[]{:S(2)}, u32[]{:S(2)}) collective-permute-start(bf16[256,128]{1,0:T(8,128)(2,1)} %copy-done.12), channel_id=1, source_target_pairs={{0,16},{2,18},{4,20},{6,22},{8,24},{10,26},{12,28},{14,30},{16,0},... | collective-permute-start | bytes 196616 | tf_op jit(solution)/shard_map/ppermute | solution.py:411
  85.7 1.0 %copy-done.22 = bf16[2,216,512]{2,1,0:T(8,128)(2,1)S(1)} copy-done((bf16[2,216,512]{2,1,0:T(8,128)(2,1)S(1)}, bf16[2,216,512]{2,1,0:T(8,128)(2,1)}, u32[]{:S(2)}) %copy-start.22) | copy-done | bytes 442392
  86.7 3.2 %shard_map.151 = (f32[8,128]{1,0:T(8,128)S(1)}, bf16[12,12,4,512]{3,2,1,0:T(4,128)(2,1)}, bf16[12,12,4,512]{3,2,1,0:T(4,128)(2,1)}) custom-call(bf16[12,12,4,512]{3,2,1,0:T(4,128)(2,1)S(1)} %copy-done.2, bf16[12,12,4,512]{3,2,1,0:T(4,128)(2,1)S(1)} %copy-done.4, f32[1,512]{1,0:T(1,128)S(1)} %bitcast.9, bf16[2,216,512]{2,1,0:T(8,128)(2,1)S(1)} %copy-done.22, ...), custom_call_target="tpu_custom_call" | custom-call | flops 30000001024 | tf_op jit(solution)/shard_map/pallas_call | solution.py:61
  89.9 1.5 %shard_map.158 = (f32[2,2,4,3312]{3,2,1,0:T(4,128)}, f32[8,128]{1,0:T(8,128)S(1)}) custom-call(s32[2]{0:T(128)S(1)} %pad_add_fusion.refs_0_, bf16[256,128]{1,0:T(8,128)(2,1)S(1)} %copy-done.13, bf16[256,128]{1,0:T(8,128)(2,1)S(1)} %collective-permute-done.11.refs_2_, f32[8,128]{1,0:T(8,128)S(1)} %get-tuple-element.60.refs_3_), custom_call_target="tpu_custom_call" | custom-call | flops 1000000000 | tf_op jit(solution)/shard_map/pallas_call | solution.py:61
  91.4 2.2 %collective-permute-start.15 = (bf16[1024,256]{1,0:T(8,128)(2,1)S(1)}, bf16[1024,256]{1,0:T(8,128)(2,1)S(1)}, u32[]{:S(2)}, u32[]{:S(2)}) collective-permute-start(bf16[1024,256]{1,0:T(8,128)(2,1)S(1)} %bitcast.5), channel_id=1, source_target_pairs={{0,16},{2,18},{4,20},{6,22},{8,24},{10,26},{12,28},{14,30},{16,0},... | collective-permute-start | bytes 1572872 | tf_op jit(solution)/shard_map/ppermute | solution.py:411
  93.6 0.9 shard_map.159.refs_0_
  94.5 0.6 collective-permute-start.14
  95.1 0.8 collective-permute-start.13
  95.9 0.8 collective-permute-start.12
  96.7 1.9 %shard_map.160 = (f32[8,128]{1,0:T(8,128)S(1)}, f32[3,512,256]{2,1,0:T(8,128)}, f32[256,512]{1,0:T(8,128)}) custom-call(s32[2]{0:T(128)S(1)} %pad_add_fusion.refs_0_, bf16[1024,256]{1,0:T(8,128)(2,1)S(1)} %bitcast.7, bf16[1024,256]{1,0:T(8,128)(2,1)S(1)} %collective-permute-done.15.refs_2_), custom_call_target="tpu_custom_call" | custom-call | flops 2000000000 | tf_op jit(solution)/shard_map/pallas_call | solution.py:61
  98.6 0.6 shard_map.161
  (56 shorter events, 0.4 us)
Async XLA Ops:
  2.4 14.1 %copy-start.5 = (bf16[256,512]{1,0:T(8,128)(2,1)S(1)}, bf16[256,512]{1,0:T(8,128)(2,1)}, u32[]{:S(2)}) copy-start(bf16[256,512]{1,0:T(8,128)(2,1)} %refs_2_.6) | copy-start | bytes 786436
  2.4 14.1 %copy-start.9 = (f32[2,2,4,3312]{3,2,1,0:T(4,128)S(1)}, f32[2,2,4,3312]{3,2,1,0:T(4,128)}, u32[]{:S(2)}) copy-start(f32[2,2,4,3312]{3,2,1,0:T(4,128)} %refs_1_.7) | copy-start | bytes 635908
  2.4 14.1 %copy-start.18 = (bf16[276,276]{1,0:T(8,128)(2,1)S(1)}, bf16[276,276]{1,0:T(8,128)(2,1)}, u32[]{:S(2)}) copy-start(bf16[276,276]{1,0:T(8,128)(2,1)} %constant.36.clone.refs_2_) | copy-start | bytes 457060
  2.4 16.1 %collective-permute-start.2 = (bf16[2,72,512]{2,1,0:T(8,128)(2,1)}, bf16[2,72,512]{2,1,0:T(8,128)(2,1)S(1)}, u32[]{:S(2)}, u32[]{:S(2)}) collective-permute-start(bf16[2,72,512]{2,1,0:T(8,128)(2,1)} %get-tuple-element.37), channel_id=1, source_target_pairs={{0,255},{1,254},{2,241},{3,240},{4,243},{5,242},{6,245},{7,244},{8... | collective-permute-start | bytes 442376 | tf_op jit(solution)/shard_map/ppermute | solution.py:405
  8.8 9.7 %collective-permute-start.1 = (bf16[2,72,512]{2,1,0:T(8,128)(2,1)}, bf16[2,72,512]{2,1,0:T(8,128)(2,1)S(1)}, u32[]{:S(2)}, u32[]{:S(2)}) collective-permute-start(bf16[2,72,512]{2,1,0:T(8,128)(2,1)} %get-tuple-element.36.refs_2_), channel_id=1, source_target_pairs={{0,15},{1,14},{2,1},{3,0},{4,3},{5,2},{6,5},{7,4},{8,7},{9,6},{10,... | collective-permute-start | bytes 442376 | tf_op jit(solution)/shard_map/ppermute | solution.py:405
  11.0 8.3 %collective-permute-start = (bf16[2,216,512]{2,1,0:T(8,128)(2,1)}, bf16[2,216,512]{2,1,0:T(8,128)(2,1)S(1)}, u32[]{:S(2)}, u32[]{:S(2)}) collective-permute-start(bf16[2,216,512]{2,1,0:T(8,128)(2,1)} %shard_map.146), channel_id=1, source_target_pairs={{0,240},{1,241},{2,242},{3,243},{4,244},{5,245},{6,246},{7,247},{8... | collective-permute-start | bytes 1327112 | tf_op jit(solution)/shard_map/ppermute | solution.py:405
  16.5 2.8 %copy-start = (bf16[3,512,256]{2,1,0:T(8,128)(2,1)S(1)}, bf16[3,512,256]{2,1,0:T(8,128)(2,1)}, u32[]{:S(2)}) copy-start(bf16[3,512,256]{2,1,0:T(8,128)(2,1)} %refs_2_.7) | copy-start | bytes 2359300
  16.5 2.8 %copy-start.1 = (bf16[12,12,4,512]{3,2,1,0:T(4,128)(2,1)S(1)}, bf16[12,12,4,512]{3,2,1,0:T(4,128)(2,1)}, u32[]{:S(2)}) copy-start(bf16[12,12,4,512]{3,2,1,0:T(4,128)(2,1)} %refs_0_.5) | copy-start | bytes 1769476
  16.5 2.8 %copy-start.3 = (bf16[12,12,4,512]{3,2,1,0:T(4,128)(2,1)S(1)}, bf16[12,12,4,512]{3,2,1,0:T(4,128)(2,1)}, u32[]{:S(2)}) copy-start(bf16[12,12,4,512]{3,2,1,0:T(4,128)(2,1)} %refs_1_.9) | copy-start | bytes 1769476
  16.5 2.8 %copy-start.14 = (f32[512]{0:T(512)S(1)}, f32[512]{0:T(512)}, u32[]{:S(2)}) copy-start(f32[512]{0:T(512)} %param.12) | copy-start | bytes 6148
  16.6 2.8 %copy-start.16 = (bf16[2,288,288]{2,1,0:T(8,128)(2,1)S(1)}, bf16[2,288,288]{2,1,0:T(8,128)(2,1)}, u32[]{:S(2)}) copy-start(bf16[2,288,288]{2,1,0:T(8,128)(2,1)} %constant.34.clone.refs_6_) | copy-start | bytes 995332
  18.4 10.8 %collective-permute-start.3 = (bf16[256,512]{1,0:T(8,128)(2,1)S(1)}, bf16[256,512]{1,0:T(8,128)(2,1)S(1)}, u32[]{:S(2)}, u32[]{:S(2)}) collective-permute-start(bf16[256,512]{1,0:T(8,128)(2,1)S(1)} %get-tuple-element.43), channel_id=1, source_target_pairs={{0,1},{1,0},{2,3},{3,2},{4,5},{5,4},{6,7},{7,6},{8,9},{9,8},{10,11... | collective-permute-start | bytes 786440 | tf_op jit(solution)/shard_map/ppermute | solution.py:427
  19.4 9.8 %copy-start.15 = (bf16[2,288,288]{2,1,0:T(8,128)(2,1)S(1)}, bf16[2,288,288]{2,1,0:T(8,128)(2,1)}, u32[]{:S(2)}) copy-start(bf16[2,288,288]{2,1,0:T(8,128)(2,1)} %constant.35.clone.refs_5_) | copy-start | bytes 995332
  25.2 5.1 %copy-start.19 = (f32[2304,144]{1,0:T(8,128)}, f32[2304,144]{1,0:T(8,128)S(1)}, u32[]{:S(2)}) copy-start(f32[2304,144]{1,0:T(8,128)S(1)} %get-tuple-element.52.refs_1_) | copy-start | bytes 3981316
  25.2 5.4 %collective-permute-start.8 = (bf16[1024,256]{1,0:T(8,128)(2,1)S(1)}, bf16[1024,256]{1,0:T(8,128)(2,1)S(1)}, u32[]{:S(2)}, u32[]{:S(2)}) collective-permute-start(bf16[1024,256]{1,0:T(8,128)(2,1)S(1)} %get-tuple-element.51), channel_id=1, source_target_pairs={{0,16},{2,18},{4,20},{6,22},{8,24},{10,26},{12,28},{14,30},{16,0},... | collective-permute-start | bytes 1572872 | tf_op jit(solution)/shard_map/ppermute | solution.py:411
  29.1 1.2 %copy-start.7 = (bf16[256,512]{1,0:T(8,128)(2,1)}, bf16[256,512]{1,0:T(8,128)(2,1)S(1)}, u32[]{:S(2)}) copy-start(bf16[256,512]{1,0:T(8,128)(2,1)S(1)} %collective-permute-done.3.refs_6_.refs_3_) | copy-start | bytes 786436
  30.3 4.7 %copy-start.17 = (bf16[2,138,276]{2,1,0:T(8,128)(2,1)S(1)}, bf16[2,138,276]{2,1,0:T(8,128)(2,1)}, u32[]{:S(2)}) copy-start(bf16[2,138,276]{2,1,0:T(8,128)(2,1)} %constant.37.clone.refs_2_) | copy-start | bytes 457060
  30.3 21.3 %collective-permute-start.4 = (bf16[576,768]{1,0:T(8,128)(2,1)S(1)}, bf16[576,768]{1,0:T(8,128)(2,1)S(1)}, u32[]{:S(2)}, u32[]{:S(2)}) collective-permute-start(bf16[576,768]{1,0:T(8,128)(2,1)S(1)} %shard_map.149.refs_0_.refs_2_), channel_id=1, source_target_pairs={{0,1},{1,0},{2,3},{3,2},{4,5},{5,4},{6,7},{7,6},{8,9},{9,8},{10,11... | collective-permute-start | bytes 2654216 | tf_op jit(solution)/shard_map/ppermute | solution.py:427
  31.5 12.7 %all-to-all-start = ((bf16[4,256,256]{2,1,0:T(8,128)(2,1)}), bf16[4,256,256]{2,1,0:T(8,128)(2,1)S(1)}, u32[]{:S(2)}, u32[]{:S(2)}) async-start(bf16[4,256,256]{2,1,0:T(8,128)(2,1)} %shard_map.152), calls=%async_computation | async-start | bytes 1048576 | tf_op jit(solution)/shard_map/all_to_all | solution.py:417
  35.0 1.7 %copy-start.20 = (f32[2304,144]{1,0:T(8,128)S(1)}, f32[2304,144]{1,0:T(8,128)}, u32[]{:S(2)}) copy-start(f32[2304,144]{1,0:T(8,128)} %copy-done.19) | copy-start | bytes 3981316
  38.7 1.5 %collective-permute-start.9 = (bf16[256,128]{1,0:T(8,128)(2,1)S(1)}, bf16[256,128]{1,0:T(8,128)(2,1)S(1)}, u32[]{:S(2)}, u32[]{:S(2)}) collective-permute-start(bf16[256,128]{1,0:T(8,128)(2,1)S(1)} %get-tuple-element.54), channel_id=1, source_target_pairs={{0,16},{2,18},{4,20},{6,22},{8,24},{10,26},{12,28},{14,30},{16,0},... | collective-permute-start | bytes 196616 | tf_op jit(solution)/shard_map/ppermute | solution.py:411
  45.0 13.4 %all-to-all-start.1 = ((bf16[8,32,384]{2,1,0:T(8,128)(2,1)}), bf16[8,32,384]{2,1,0:T(8,128)(2,1)S(1)}, u32[]{:S(2)}, u32[]{:S(2)}) async-start(bf16[8,32,384]{2,1,0:T(8,128)(2,1)} %shard_map.154), calls=%async_computation.1 | async-start | bytes 393216 | tf_op jit(solution)/shard_map/all_to_all | solution.py:423
  51.6 1.0 copy-start.6
  52.6 0.9 copy-start.8
  54.9 0.7 copy-start.10
  55.6 0.8 copy-start.21
  58.4 10.9 %copy-start.11 = (bf16[2,72,512]{2,1,0:T(8,128)(2,1)S(1)}, bf16[2,72,512]{2,1,0:T(8,128)(2,1)}, u32[]{:S(2)}) copy-start(bf16[2,72,512]{2,1,0:T(8,128)(2,1)} %copy-done.10) | copy-start | bytes 442372
  58.5 6.2 %collective-permute-start.10 = (bf16[32,256]{1,0:T(8,128)(2,1)S(1)}, bf16[32,256]{1,0:T(8,128)(2,1)S(1)}, u32[]{:S(2)}, u32[]{:S(2)}) collective-permute-start(bf16[32,256]{1,0:T(8,128)(2,1)S(1)} %get-tuple-element.56.refs_0_), channel_id=1, source_target_pairs={{0,2},{2,0},{4,6},{6,4},{8,10},{10,8},{12,14},{14,12},{16,18},{18,... | collective-permute-start | bytes 49160 | tf_op jit(solution)/shard_map/ppermute | solution.py:411
  61.3 24.4 %collective-permute-start.5 = (bf16[2,216,512]{2,1,0:T(8,128)(2,1)S(1)}, bf16[2,216,512]{2,1,0:T(8,128)(2,1)S(1)}, u32[]{:S(2)}, u32[]{:S(2)}) collective-permute-start(bf16[2,216,512]{2,1,0:T(8,128)(2,1)S(1)} %get-tuple-element.45), channel_id=1, source_target_pairs={{0,16},{1,17},{2,18},{3,19},{4,20},{5,21},{6,22},{7,23},{8,24},{9,... | collective-permute-start | bytes 1327112 | tf_op jit(solution)/shard_map/ppermute | solution.py:405
  65.4 12.3 %all-to-all-start.2 = ((bf16[8,32,384]{2,1,0:T(8,128)(2,1)}), bf16[8,32,384]{2,1,0:T(8,128)(2,1)S(1)}, u32[]{:S(2)}, u32[]{:S(2)}) async-start(bf16[8,32,384]{2,1,0:T(8,128)(2,1)} %shard_map.156), calls=%async_computation.2 | async-start | bytes 393216 | tf_op jit(solution)/shard_map/all_to_all | solution.py:423
  69.1 16.6 %collective-permute-start.6 = (bf16[2,72,512]{2,1,0:T(8,128)(2,1)}, bf16[2,72,512]{2,1,0:T(8,128)(2,1)}, u32[]{:S(2)}, u32[]{:S(2)}) collective-permute-start(bf16[2,72,512]{2,1,0:T(8,128)(2,1)} %get-tuple-element.46), channel_id=1, source_target_pairs={{0,3},{1,2},{2,5},{3,4},{4,7},{5,6},{6,9},{7,8},{8,11},{9,10},{10,... | collective-permute-start | bytes 442376 | tf_op jit(solution)/shard_map/ppermute | solution.py:405
  69.4 16.3 %copy-start.2 = (bf16[12,12,4,512]{3,2,1,0:T(4,128)(2,1)S(1)}, bf16[12,12,4,512]{3,2,1,0:T(4,128)(2,1)}, u32[]{:S(2)}) copy-start(bf16[12,12,4,512]{3,2,1,0:T(4,128)(2,1)} %refs_0_.5) | copy-start | bytes 1769476
  69.4 16.3 %copy-start.4 = (bf16[12,12,4,512]{3,2,1,0:T(4,128)(2,1)S(1)}, bf16[12,12,4,512]{3,2,1,0:T(4,128)(2,1)}, u32[]{:S(2)}) copy-start(bf16[12,12,4,512]{3,2,1,0:T(4,128)(2,1)} %refs_1_.9) | copy-start | bytes 1769476
  69.4 16.3 %collective-permute-start.7 = (bf16[2,72,512]{2,1,0:T(8,128)(2,1)S(1)}, bf16[2,72,512]{2,1,0:T(8,128)(2,1)}, u32[]{:S(2)}, u32[]{:S(2)}) collective-permute-start(bf16[2,72,512]{2,1,0:T(8,128)(2,1)S(1)} %copy-done.11), channel_id=1, source_target_pairs={{0,19},{1,18},{2,21},{3,20},{4,23},{5,22},{6,25},{7,24},{8,27},{9,... | collective-permute-start | bytes 442376 | tf_op jit(solution)/shard_map/ppermute | solution.py:405
  78.5 0.6 copy-start.12
  79.2 12.3 %all-to-all-start.3 = ((bf16[4,256,256]{2,1,0:T(8,128)(2,1)}), bf16[4,256,256]{2,1,0:T(8,128)(2,1)S(1)}, u32[]{:S(2)}, u32[]{:S(2)}) async-start(bf16[4,256,256]{2,1,0:T(8,128)(2,1)} %get-tuple-element.58), calls=%async_computation.3 | async-start | bytes 1048576 | tf_op jit(solution)/shard_map/all_to_all | solution.py:417
  82.6 7.3 %collective-permute-start.11 = (bf16[256,128]{1,0:T(8,128)(2,1)}, bf16[256,128]{1,0:T(8,128)(2,1)S(1)}, u32[]{:S(2)}, u32[]{:S(2)}) collective-permute-start(bf16[256,128]{1,0:T(8,128)(2,1)} %copy-done.12), channel_id=1, source_target_pairs={{0,16},{2,18},{4,20},{6,22},{8,24},{10,26},{12,28},{14,30},{16,0},... | collective-permute-start | bytes 196616 | tf_op jit(solution)/shard_map/ppermute | solution.py:411
  85.7 1.0 %copy-start.22 = (bf16[2,216,512]{2,1,0:T(8,128)(2,1)S(1)}, bf16[2,216,512]{2,1,0:T(8,128)(2,1)}, u32[]{:S(2)}) copy-start(bf16[2,216,512]{2,1,0:T(8,128)(2,1)} %copy-done.21) | copy-start | bytes 1327108
  86.7 3.2 %copy-start.13 = (bf16[256,128]{1,0:T(8,128)(2,1)S(1)}, bf16[256,128]{1,0:T(8,128)(2,1)}, u32[]{:S(2)}) copy-start(bf16[256,128]{1,0:T(8,128)(2,1)} %copy-done.12) | copy-start | bytes 196612
  91.4 5.2 %collective-permute-start.15 = (bf16[1024,256]{1,0:T(8,128)(2,1)S(1)}, bf16[1024,256]{1,0:T(8,128)(2,1)S(1)}, u32[]{:S(2)}, u32[]{:S(2)}) collective-permute-start(bf16[1024,256]{1,0:T(8,128)(2,1)S(1)} %bitcast.5), channel_id=1, source_target_pairs={{0,16},{2,18},{4,20},{6,22},{8,24},{10,26},{12,28},{14,30},{16,0},... | collective-permute-start | bytes 1572872 | tf_op jit(solution)/shard_map/ppermute | solution.py:411
  94.5 4.1 %collective-permute-start.14 = (f32[8,512]{1,0:T(8,128)S(1)}, f32[8,512]{1,0:T(8,128)S(1)}, u32[]{:S(2)}, u32[]{:S(2)}) collective-permute-start(f32[8,512]{1,0:T(8,128)S(1)} %shard_map.159.refs_0_), channel_id=1, source_target_pairs={{0,17},{1,16},{16,1},{17,0},{32,49},{33,48},{48,33},{49,32},{64,81... | collective-permute-start | bytes 49160 | tf_op jit(solution)/shard_map/ppermute | solution.py:432
  95.1 3.5 %collective-permute-start.13 = (f32[8,512]{1,0:T(8,128)S(1)}, f32[8,512]{1,0:T(8,128)S(1)}, u32[]{:S(2)}, u32[]{:S(2)}) collective-permute-start(f32[8,512]{1,0:T(8,128)S(1)} %shard_map.159.refs_0_), channel_id=1, source_target_pairs={{0,1},{1,0},{2,3},{3,2},{4,5},{5,4},{6,7},{7,6},{8,9},{9,8},{10,11... | collective-permute-start | bytes 49160 | tf_op jit(solution)/shard_map/ppermute | solution.py:427
  95.9 2.8 %collective-permute-start.12 = (f32[8,512]{1,0:T(8,128)S(1)}, f32[8,512]{1,0:T(8,128)S(1)}, u32[]{:S(2)}, u32[]{:S(2)}) collective-permute-start(f32[8,512]{1,0:T(8,128)S(1)} %shard_map.159.refs_0_), channel_id=1, source_target_pairs={{0,16},{2,18},{4,20},{6,22},{8,24},{10,26},{12,28},{14,30},{16,0},... | collective-permute-start | bytes 49160 | tf_op jit(solution)/shard_map/ppermute | solution.py:411

commit v10 on v8

--- a/solution.py
+++ b/solution.py
@@ -184,10 +184,10 @@
     for w in range(4):
         rows = slice(w * WTOK, (w + 1) * WTOK)
         four = slice(w * 576, (w + 1) * 576)
-        qs, ds_ = stacked(q[rows]), stacked(down[rows])
-        scores = dot(qs, k[rows], NT) * 0.125 + bias[four, :]
+        qs, ds_ = stacked(q[rows] * BF(0.125)), stacked(down[rows])
+        scores = dot(qs, k[rows], NT) + bias[four, :]
         exps = jnp.exp(scores - jnp.max(scores, -1, keepdims=True))
-        probs = exps / jnp.sum(exps, -1, keepdims=True)
+        probs = exps * (1.0 / jnp.sum(exps, -1, keepdims=True))
         probs_low = probs.astype(BF)
         att_s[rows, :] = unstacked(dot(probs_low, v[rows])).astype(BF)
         dp = dot(ds_, v[rows], NT)
@@ -196,7 +196,7 @@
         o_ds[four, :] = grad
         grad_low = grad.astype(BF)
         gq_s[rows, :] = unstacked(dot(grad_low, k[rows]) * 0.125).astype(BF)
-        gk_s[rows, :] = (dot(grad_low, qs, TN) * 0.125).astype(BF)
+        gk_s[rows, :] = dot(grad_low, qs, TN).astype(BF)
 
     att, gq, gk, gv = att_s[...], gq_s[...], gk_s[...], gv_s[...]
     wo = dot(att, cot, TN)

time: 98.2 us -> 98.2 us (level)
  no operation moved by 1% of the time
where the time goes in v10:
time: 98.2 us; the launch traced here: 97.7 us
  starting transfers between devices  50.3 us (51%)
  Pallas kernels  25.5 us (26%)
  waiting for transfers between devices  14 us (14%)
  local copies, waits for them, and re-layouts  6.7 us (7%)
  between operations  1.03 us (1%)
    pallas_call x16, Pallas kernels, call(): pl.pallas_call(kernel, out_shape=[jax.ShapeDtypeStruct(s, t) for s, t in...  25.5 us
    ppermute x6, starting transfers between devices, moved(): return lax.ppermute(value, ('lon', 'lat', 'tp'), pairs)  20.9 us
    ppermute x6, starting transfers between devices, swapped(): return lax.ppermute(value, ('lon', 'lat'), pairs)  12.7 us
    all_to_all x2, starting transfers between devices, across_z(): return lax.all_to_all(value, 'lon', 0, 0, axis_index_groups=groups)  8.25 us
    all_to_all x2, starting transfers between devices, across_y(): return lax.all_to_all(value, 'lat', 0, 0, axis_index_groups=groups)  6.96 us
    unnamed x46, local copies, waits for them, and re-layouts  6.7 us
    all_to_all x2, waiting for transfers between devices, across_z(): return lax.all_to_all(value, 'lon', 0, 0, axis_index_groups=groups)  4.86 us
    all_to_all x2, waiting for transfers between devices, across_y(): return lax.all_to_all(value, 'lat', 0, 0, axis_index_groups=groups)  4.07 us
  transfers between devices with their start and end apart: 20, of which 7 were waited for; matrix products, arithmetic and copies ran while one was open for 0% of the time, Pallas kernels for 23%

profile of v10, /device:TPU:1, one launch (start us, length us, event | category | flops | bytes accessed | tf_op | source)
XLA Modules:
  0.0 97.7 jit_solution(10795580802374501300)
XLA Ops:
  0.7 2.2 %shard_map.145 = (bf16[2,216,512]{2,1,0:T(8,128)(2,1)}, bf16[2,72,512]{2,1,0:T(8,128)(2,1)}, bf16[2,72,512]{2,1,0:T(8,128)(2,1)}) custom-call(bf16[12,12,4,512]{3,2,1,0:T(4,128)(2,1)} %refs_0_.3, bf16[12,12,4,512]{3,2,1,0:T(4,128)(2,1)} %refs_1_.7), custom_call_target="tpu_custom_call" | custom-call | flops 1000000000 | tf_op jit(solution)/shard_map/pallas_call | solution.py:59
  2.9 3.3 %collective-permute-start = (bf16[2,216,512]{2,1,0:T(8,128)(2,1)}, bf16[2,216,512]{2,1,0:T(8,128)(2,1)S(1)}, u32[]{:S(2)}, u32[]{:S(2)}) collective-permute-start(bf16[2,216,512]{2,1,0:T(8,128)(2,1)} %get-tuple-element.37), channel_id=1, source_target_pairs={{0,240},{1,241},{2,242},{3,243},{4,244},{5,245},{6,246},{7,247},{8... | collective-permute-start | bytes 1327112 | tf_op jit(solution)/shard_map/ppermute | solution.py:398
  6.1 3.2 %collective-permute-start.1 = (bf16[2,72,512]{2,1,0:T(8,128)(2,1)}, bf16[2,72,512]{2,1,0:T(8,128)(2,1)S(1)}, u32[]{:S(2)}, u32[]{:S(2)}) collective-permute-start(bf16[2,72,512]{2,1,0:T(8,128)(2,1)} %get-tuple-element.38), channel_id=1, source_target_pairs={{0,15},{1,14},{2,1},{3,0},{4,3},{5,2},{6,5},{7,4},{8,7},{9,6},{10,... | collective-permute-start | bytes 442376 | tf_op jit(solution)/shard_map/ppermute | solution.py:398
  9.3 5.7 %collective-permute-start.2 = (bf16[2,72,512]{2,1,0:T(8,128)(2,1)}, bf16[2,72,512]{2,1,0:T(8,128)(2,1)S(1)}, u32[]{:S(2)}, u32[]{:S(2)}) collective-permute-start(bf16[2,72,512]{2,1,0:T(8,128)(2,1)} %get-tuple-element.39), channel_id=1, source_target_pairs={{0,255},{1,254},{2,241},{3,240},{4,243},{5,242},{6,245},{7,244},{8... | collective-permute-start | bytes 442376 | tf_op jit(solution)/shard_map/ppermute | solution.py:398
  15.0 0.1 pad_add_fusion.refs_0_
  15.1 1.8 %shard_map.146 = (f32[2304,144]{1,0:T(8,128)S(1)}, bf16[256,512]{1,0:T(8,128)(2,1)S(1)}) custom-call(s32[2]{0:T(128)S(1)} %pad_add_fusion.refs_0_, f32[2,2,4,3312]{3,2,1,0:T(4,128)S(1)} %copy-done.9, bf16[276,276]{1,0:T(8,128)(2,1)S(1)} %copy-done.18, bf16[256,512]{1,0:T(8,128)(2,1)S(1)} %copy-done.5), custom_call_target="tpu_custom_call" | custom-call | flops 2000000000 | tf_op jit(solution)/shard_map/pallas_call | solution.py:59
  16.9 0.1 collective-permute-start.3
  17.0 1.8 %collective-permute-done.2.refs_5_ = bf16[2,72,512]{2,1,0:T(8,128)(2,1)S(1)} collective-permute-done((bf16[2,72,512]{2,1,0:T(8,128)(2,1)}, bf16[2,72,512]{2,1,0:T(8,128)(2,1)S(1)}, u32[]{:S(2)}, u32[]{:S(2)}) %collective-permute-start.2) | collective-permute-done | bytes 147488 | tf_op jit(solution)/shard_map/ppermute | solution.py:398
  18.9 5.8 %shard_map.147 = (f32[1024,256]{1,0:T(8,128)S(1)}, bf16[1024,256]{1,0:T(8,128)(2,1)S(1)}, f32[2304,144]{1,0:T(8,128)S(1)}, bf16[576,256]{1,0:T(8,128)(2,1)S(1)},...) custom-call(s32[2]{0:T(128)S(1)} %pad_add_fusion.refs_0_, ...), custom_call_target="tpu_custom_call" | custom-call | flops 8999999488 | tf_op jit(solution)/shard_map/pallas_call | solution.py:59
  24.7 2.1 %collective-permute-start.8 = (bf16[1024,256]{1,0:T(8,128)(2,1)S(1)}, bf16[1024,256]{1,0:T(8,128)(2,1)S(1)}, u32[]{:S(2)}, u32[]{:S(2)}) collective-permute-start(bf16[1024,256]{1,0:T(8,128)(2,1)S(1)} %get-tuple-element.53), channel_id=1, source_target_pairs={{0,16},{2,18},{4,20},{6,22},{8,24},{10,26},{12,28},{14,30},{16,0},... | collective-permute-start | bytes 1572872 | tf_op jit(solution)/shard_map/ppermute | solution.py:404
  26.8 1.1 %shard_map.148.refs_0_.refs_2_ = bf16[576,768]{1,0:T(8,128)(2,1)S(1)} custom-call(bf16[576,256]{1,0:T(8,128)(2,1)S(1)} %get-tuple-element.41.refs_0_, bf16[576,256]{1,0:T(8,128)(2,1)S(1)} %get-tuple-element.42.refs_1_, bf16[576,256]{1,0:T(8,128)(2,1)S(1)} %get-tuple-element.43.refs_2_, bf16[576,256]{1,0:T(8,128)(2,1)S(1)} %get-tuple-element.44.refs_3_, ...), custom_call_target="tpu_custom_call" | custom-call | flops 2000000000 | tf_op jit(solution)/shard_map/pallas_call | solution.py:59
  28.0 0.1 collective-permute-start.4
  28.1 0.2 collective-permute-done.8.refs_1_
  28.4 0.8 shard_map.151
  29.2 3.5 %all-to-all-start = ((bf16[4,256,256]{2,1,0:T(8,128)(2,1)}), bf16[4,256,256]{2,1,0:T(8,128)(2,1)S(1)}, u32[]{:S(2)}, u32[]{:S(2)}) async-start(bf16[4,256,256]{2,1,0:T(8,128)(2,1)} %shard_map.151), calls=%async_computation | async-start | bytes 1048576 | tf_op jit(solution)/shard_map/all_to_all | solution.py:410
  32.7 1.7 %copy-done.20 = f32[2304,144]{1,0:T(8,128)S(1)} copy-done((f32[2304,144]{1,0:T(8,128)S(1)}, f32[2304,144]{1,0:T(8,128)}, u32[]{:S(2)}) %copy-start.20) | copy-done | bytes 1327128
  34.4 1.9 %shard_map.152 = (bf16[256,128]{1,0:T(8,128)(2,1)S(1)}, bf16[256,128]{1,0:T(8,128)(2,1)S(1)}) custom-call(s32[2]{0:T(128)S(1)} %pad_add_fusion.refs_0_, f32[2304,144]{1,0:T(8,128)S(1)} %copy-done.20, bf16[2,138,276]{2,1,0:T(8,128)(2,1)S(1)} %copy-done.17), custom_call_target="tpu_custom_call" | custom-call | flops 2500000000 | tf_op jit(solution)/shard_map/pallas_call | solution.py:59
  36.3 0.6 collective-permute-start.9
  36.9 0.9 collective-permute-done.9.refs_2_
  37.8 4.1 %all-to-all-done.refs_0_ = bf16[4,256,256]{2,1,0:T(8,128)(2,1)S(1)} async-done(((bf16[4,256,256]{2,1,0:T(8,128)(2,1)}), bf16[4,256,256]{2,1,0:T(8,128)(2,1)S(1)}, u32[]{:S(2)}, u32[]{:S(2)}) %all-to-all-start) | async-done | bytes 524320 | tf_op jit(solution)/shard_map/all_to_all | solution.py:410
  41.9 0.8 shard_map.153
  42.7 4.6 %all-to-all-start.1 = ((bf16[8,32,384]{2,1,0:T(8,128)(2,1)}), bf16[8,32,384]{2,1,0:T(8,128)(2,1)S(1)}, u32[]{:S(2)}, u32[]{:S(2)}) async-start(bf16[8,32,384]{2,1,0:T(8,128)(2,1)} %shard_map.153), calls=%async_computation.1 | async-start | bytes 393216 | tf_op jit(solution)/shard_map/all_to_all | solution.py:416
  47.2 2.1 %collective-permute-done.4.refs_1_ = bf16[576,768]{1,0:T(8,128)(2,1)S(1)} collective-permute-done((bf16[576,768]{1,0:T(8,128)(2,1)S(1)}, bf16[576,768]{1,0:T(8,128)(2,1)S(1)}, u32[]{:S(2)}, u32[]{:S(2)}) %collective-permute-start.4) | collective-permute-done | bytes 884768 | tf_op jit(solution)/shard_map/ppermute | solution.py:420
  49.3 0.9 copy-done.6
  50.3 0.9 copy-done.8
  51.2 1.4 %shard_map.149 = (bf16[2,216,512]{2,1,0:T(8,128)(2,1)S(1)}, bf16[2,216,512]{2,1,0:T(8,128)(2,1)S(1)}, bf16[2,72,512]{2,1,0:T(8,128)(2,1)}, bf16[2,72,512]{2,1,0:T(8,128)(2,1)S(1)}, f32[8,128]{1,0:T(8,128)S(1)}) custom-call(bf16[576,768]{1,0:T(8,128)(2,1)S(1)} %shard_map.148.refs_0_.refs_2_, bf16[576,768]{1,0:T(8,128)(2,1)S(1)} %collective-permute-done.4.refs_1_, ...), custom_call_target="tpu_custom_call" | custom-call | flops 30000001024 | tf_op jit(solution)/shard_map/pallas_call | solution.py:59
  52.6 0.7 copy-done.10
  53.3 0.8 copy-done.21
  54.0 1.7 %all-to-all-done.1.refs_0_ = bf16[8,32,384]{2,1,0:T(8,128)(2,1)S(1)} async-done(((bf16[8,32,384]{2,1,0:T(8,128)(2,1)}), bf16[8,32,384]{2,1,0:T(8,128)(2,1)S(1)}, u32[]{:S(2)}, u32[]{:S(2)}) %all-to-all-start.1) | async-done | bytes 196640 | tf_op jit(solution)/shard_map/all_to_all | solution.py:416
  55.8 4.1 %collective-permute-start.10 = (bf16[32,256]{1,0:T(8,128)(2,1)S(1)}, bf16[32,256]{1,0:T(8,128)(2,1)S(1)}, u32[]{:S(2)}, u32[]{:S(2)}) collective-permute-start(bf16[32,256]{1,0:T(8,128)(2,1)S(1)} %get-tuple-element.58.refs_0_), channel_id=1, source_target_pairs={{0,2},{2,0},{4,6},{6,4},{8,10},{10,8},{12,14},{14,12},{16,18},{18,... | collective-permute-start | bytes 49160 | tf_op jit(solution)/shard_map/ppermute | solution.py:404
  59.8 3.3 %collective-permute-start.5 = (bf16[2,216,512]{2,1,0:T(8,128)(2,1)S(1)}, bf16[2,216,512]{2,1,0:T(8,128)(2,1)S(1)}, u32[]{:S(2)}, u32[]{:S(2)}) collective-permute-start(bf16[2,216,512]{2,1,0:T(8,128)(2,1)S(1)} %get-tuple-element.47), channel_id=1, source_target_pairs={{0,16},{1,17},{2,18},{3,19},{4,20},{5,21},{6,22},{7,23},{8,24},{9,... | collective-permute-start | bytes 1327112 | tf_op jit(solution)/shard_map/ppermute | solution.py:398
  63.2 0.7 shard_map.155
  63.9 3.7 %all-to-all-start.2 = ((bf16[8,32,384]{2,1,0:T(8,128)(2,1)}), bf16[8,32,384]{2,1,0:T(8,128)(2,1)S(1)}, u32[]{:S(2)}, u32[]{:S(2)}) async-start(bf16[8,32,384]{2,1,0:T(8,128)(2,1)} %shard_map.155), calls=%async_computation.2 | async-start | bytes 393216 | tf_op jit(solution)/shard_map/all_to_all | solution.py:416
  67.6 5.4 %collective-permute-start.7 = (bf16[2,72,512]{2,1,0:T(8,128)(2,1)S(1)}, bf16[2,72,512]{2,1,0:T(8,128)(2,1)}, u32[]{:S(2)}, u32[]{:S(2)}) collective-permute-start(bf16[2,72,512]{2,1,0:T(8,128)(2,1)S(1)} %copy-done.11), channel_id=1, source_target_pairs={{0,19},{1,18},{2,21},{3,20},{4,23},{5,22},{6,25},{7,24},{8,27},{9,... | collective-permute-start | bytes 442376 | tf_op jit(solution)/shard_map/ppermute | solution.py:398
  73.1 3.2 %all-to-all-done.2.refs_0_ = bf16[8,32,384]{2,1,0:T(8,128)(2,1)S(1)} async-done(((bf16[8,32,384]{2,1,0:T(8,128)(2,1)}), bf16[8,32,384]{2,1,0:T(8,128)(2,1)S(1)}, u32[]{:S(2)}, u32[]{:S(2)}) %all-to-all-start.2) | async-done | bytes 196640 | tf_op jit(solution)/shard_map/all_to_all | solution.py:416
  76.3 0.8 shard_map.156
  77.1 0.6 copy-done.12
  77.8 3.5 %all-to-all-start.3 = ((bf16[4,256,256]{2,1,0:T(8,128)(2,1)}), bf16[4,256,256]{2,1,0:T(8,128)(2,1)S(1)}, u32[]{:S(2)}, u32[]{:S(2)}) async-start(bf16[4,256,256]{2,1,0:T(8,128)(2,1)} %get-tuple-element.60), calls=%async_computation.3 | async-start | bytes 1048576 | tf_op jit(solution)/shard_map/all_to_all | solution.py:410
  81.2 2.9 %collective-permute-start.11 = (bf16[256,128]{1,0:T(8,128)(2,1)}, bf16[256,128]{1,0:T(8,128)(2,1)S(1)}, u32[]{:S(2)}, u32[]{:S(2)}) collective-permute-start(bf16[256,128]{1,0:T(8,128)(2,1)} %copy-done.12), channel_id=1, source_target_pairs={{0,16},{2,18},{4,20},{6,22},{8,24},{10,26},{12,28},{14,30},{16,0},... | collective-permute-start | bytes 196616 | tf_op jit(solution)/shard_map/ppermute | solution.py:404
  84.1 1.0 %copy-done.22 = bf16[2,216,512]{2,1,0:T(8,128)(2,1)S(1)} copy-done((bf16[2,216,512]{2,1,0:T(8,128)(2,1)S(1)}, bf16[2,216,512]{2,1,0:T(8,128)(2,1)}, u32[]{:S(2)}) %copy-start.22) | copy-done | bytes 442392
  85.1 3.2 %shard_map.150 = (f32[8,128]{1,0:T(8,128)S(1)}, bf16[12,12,4,512]{3,2,1,0:T(4,128)(2,1)}, bf16[12,12,4,512]{3,2,1,0:T(4,128)(2,1)}) custom-call(bf16[12,12,4,512]{3,2,1,0:T(4,128)(2,1)S(1)} %copy-done.2, bf16[12,12,4,512]{3,2,1,0:T(4,128)(2,1)S(1)} %copy-done.4, f32[1,512]{1,0:T(1,128)S(1)} %bitcast.9, bf16[2,216,512]{2,1,0:T(8,128)(2,1)S(1)} %copy-done.22, ...), custom_call_target="tpu_custom_call" | custom-call | flops 30000001024 | tf_op jit(solution)/shard_map/pallas_call | solution.py:59
  88.3 1.5 %shard_map.157 = (f32[2,2,4,3312]{3,2,1,0:T(4,128)}, f32[8,128]{1,0:T(8,128)S(1)}) custom-call(s32[2]{0:T(128)S(1)} %pad_add_fusion.refs_0_, bf16[256,128]{1,0:T(8,128)(2,1)S(1)} %copy-done.13, bf16[256,128]{1,0:T(8,128)(2,1)S(1)} %collective-permute-done.11.refs_2_, f32[8,128]{1,0:T(8,128)S(1)} %get-tuple-element.62.refs_3_), custom_call_target="tpu_custom_call" | custom-call | flops 1000000000 | tf_op jit(solution)/shard_map/pallas_call | solution.py:59
  89.8 2.2 %collective-permute-start.15 = (bf16[1024,256]{1,0:T(8,128)(2,1)S(1)}, bf16[1024,256]{1,0:T(8,128)(2,1)S(1)}, u32[]{:S(2)}, u32[]{:S(2)}) collective-permute-start(bf16[1024,256]{1,0:T(8,128)(2,1)S(1)} %bitcast.5), channel_id=1, source_target_pairs={{0,16},{2,18},{4,20},{6,22},{8,24},{10,26},{12,28},{14,30},{16,0},... | collective-permute-start | bytes 1572872 | tf_op jit(solution)/shard_map/ppermute | solution.py:404
  92.0 0.9 shard_map.158.refs_0_
  93.0 1.3 %collective-permute-start.13 = (f32[8,512]{1,0:T(8,128)S(1)}, f32[8,512]{1,0:T(8,128)S(1)}, u32[]{:S(2)}, u32[]{:S(2)}) collective-permute-start(f32[8,512]{1,0:T(8,128)S(1)} %shard_map.158.refs_0_), channel_id=1, source_target_pairs={{0,1},{1,0},{2,3},{3,2},{4,5},{5,4},{6,7},{7,6},{8,9},{9,8},{10,11... | collective-permute-start | bytes 49160 | tf_op jit(solution)/shard_map/ppermute | solution.py:420
  94.3 0.8 collective-permute-start.12
  95.1 1.9 %shard_map.159 = (f32[8,128]{1,0:T(8,128)S(1)}, f32[3,512,256]{2,1,0:T(8,128)}, f32[256,512]{1,0:T(8,128)}) custom-call(s32[2]{0:T(128)S(1)} %pad_add_fusion.refs_0_, bf16[1024,256]{1,0:T(8,128)(2,1)S(1)} %bitcast.7, bf16[1024,256]{1,0:T(8,128)(2,1)S(1)} %collective-permute-done.15.refs_2_), custom_call_target="tpu_custom_call" | custom-call | flops 2000000000 | tf_op jit(solution)/shard_map/pallas_call | solution.py:59
  97.1 0.6 shard_map.160
  (55 shorter events, 0.2 us)
Async XLA Ops:
  0.6 14.4 %copy-start.18 = (bf16[276,276]{1,0:T(8,128)(2,1)S(1)}, bf16[276,276]{1,0:T(8,128)(2,1)}, u32[]{:S(2)}) copy-start(bf16[276,276]{1,0:T(8,128)(2,1)} %constant.36.clone.refs_2_) | copy-start | bytes 457060
  0.6 14.4 %copy-start.5 = (bf16[256,512]{1,0:T(8,128)(2,1)S(1)}, bf16[256,512]{1,0:T(8,128)(2,1)}, u32[]{:S(2)}) copy-start(bf16[256,512]{1,0:T(8,128)(2,1)} %refs_2_.6) | copy-start | bytes 786436
  0.7 14.4 %copy-start.9 = (f32[2,2,4,3312]{3,2,1,0:T(4,128)S(1)}, f32[2,2,4,3312]{3,2,1,0:T(4,128)}, u32[]{:S(2)}) copy-start(f32[2,2,4,3312]{3,2,1,0:T(4,128)} %refs_1_.5) | copy-start | bytes 635908
  2.9 16.0 %collective-permute-start = (bf16[2,216,512]{2,1,0:T(8,128)(2,1)}, bf16[2,216,512]{2,1,0:T(8,128)(2,1)S(1)}, u32[]{:S(2)}, u32[]{:S(2)}) collective-permute-start(bf16[2,216,512]{2,1,0:T(8,128)(2,1)} %get-tuple-element.37), channel_id=1, source_target_pairs={{0,240},{1,241},{2,242},{3,243},{4,244},{5,245},{6,246},{7,247},{8... | collective-permute-start | bytes 1327112 | tf_op jit(solution)/shard_map/ppermute | solution.py:398
  6.1 10.9 %collective-permute-start.1 = (bf16[2,72,512]{2,1,0:T(8,128)(2,1)}, bf16[2,72,512]{2,1,0:T(8,128)(2,1)S(1)}, u32[]{:S(2)}, u32[]{:S(2)}) collective-permute-start(bf16[2,72,512]{2,1,0:T(8,128)(2,1)} %get-tuple-element.38), channel_id=1, source_target_pairs={{0,15},{1,14},{2,1},{3,0},{4,3},{5,2},{6,5},{7,4},{8,7},{9,6},{10,... | collective-permute-start | bytes 442376 | tf_op jit(solution)/shard_map/ppermute | solution.py:398
  9.3 9.5 %collective-permute-start.2 = (bf16[2,72,512]{2,1,0:T(8,128)(2,1)}, bf16[2,72,512]{2,1,0:T(8,128)(2,1)S(1)}, u32[]{:S(2)}, u32[]{:S(2)}) collective-permute-start(bf16[2,72,512]{2,1,0:T(8,128)(2,1)} %get-tuple-element.39), channel_id=1, source_target_pairs={{0,255},{1,254},{2,241},{3,240},{4,243},{5,242},{6,245},{7,244},{8... | collective-permute-start | bytes 442376 | tf_op jit(solution)/shard_map/ppermute | solution.py:398
  15.1 3.8 %copy-start = (bf16[3,512,256]{2,1,0:T(8,128)(2,1)S(1)}, bf16[3,512,256]{2,1,0:T(8,128)(2,1)}, u32[]{:S(2)}) copy-start(bf16[3,512,256]{2,1,0:T(8,128)(2,1)} %refs_2_.7) | copy-start | bytes 2359300
  15.1 3.8 %copy-start.1 = (bf16[12,12,4,512]{3,2,1,0:T(4,128)(2,1)S(1)}, bf16[12,12,4,512]{3,2,1,0:T(4,128)(2,1)}, u32[]{:S(2)}) copy-start(bf16[12,12,4,512]{3,2,1,0:T(4,128)(2,1)} %refs_0_.3) | copy-start | bytes 1769476
  15.1 3.8 %copy-start.3 = (bf16[12,12,4,512]{3,2,1,0:T(4,128)(2,1)S(1)}, bf16[12,12,4,512]{3,2,1,0:T(4,128)(2,1)}, u32[]{:S(2)}) copy-start(bf16[12,12,4,512]{3,2,1,0:T(4,128)(2,1)} %refs_1_.7) | copy-start | bytes 1769476
  15.1 3.8 %copy-start.14 = (f32[512]{0:T(512)S(1)}, f32[512]{0:T(512)}, u32[]{:S(2)}) copy-start(f32[512]{0:T(512)} %param.12) | copy-start | bytes 6148
  15.1 3.8 %copy-start.16 = (bf16[2,288,288]{2,1,0:T(8,128)(2,1)S(1)}, bf16[2,288,288]{2,1,0:T(8,128)(2,1)}, u32[]{:S(2)}) copy-start(bf16[2,288,288]{2,1,0:T(8,128)(2,1)} %constant.34.clone.refs_6_) | copy-start | bytes 995332
  16.9 9.9 %collective-permute-start.3 = (bf16[256,512]{1,0:T(8,128)(2,1)S(1)}, bf16[256,512]{1,0:T(8,128)(2,1)S(1)}, u32[]{:S(2)}, u32[]{:S(2)}) collective-permute-start(bf16[256,512]{1,0:T(8,128)(2,1)S(1)} %get-tuple-element.45), channel_id=1, source_target_pairs={{0,1},{1,0},{2,3},{3,2},{4,5},{5,4},{6,7},{7,6},{8,9},{9,8},{10,11... | collective-permute-start | bytes 786440 | tf_op jit(solution)/shard_map/ppermute | solution.py:420
  18.9 7.9 %copy-start.15 = (bf16[2,288,288]{2,1,0:T(8,128)(2,1)S(1)}, bf16[2,288,288]{2,1,0:T(8,128)(2,1)}, u32[]{:S(2)}) copy-start(bf16[2,288,288]{2,1,0:T(8,128)(2,1)} %constant.35.clone.refs_5_) | copy-start | bytes 995332
  24.7 3.3 %copy-start.19 = (f32[2304,144]{1,0:T(8,128)}, f32[2304,144]{1,0:T(8,128)S(1)}, u32[]{:S(2)}) copy-start(f32[2304,144]{1,0:T(8,128)S(1)} %get-tuple-element.54.refs_1_) | copy-start | bytes 3981316
  24.7 3.7 %collective-permute-start.8 = (bf16[1024,256]{1,0:T(8,128)(2,1)S(1)}, bf16[1024,256]{1,0:T(8,128)(2,1)S(1)}, u32[]{:S(2)}, u32[]{:S(2)}) collective-permute-start(bf16[1024,256]{1,0:T(8,128)(2,1)S(1)} %get-tuple-element.53), channel_id=1, source_target_pairs={{0,16},{2,18},{4,20},{6,22},{8,24},{10,26},{12,28},{14,30},{16,0},... | collective-permute-start | bytes 1572872 | tf_op jit(solution)/shard_map/ppermute | solution.py:404
  26.8 1.2 %copy-start.7 = (bf16[256,512]{1,0:T(8,128)(2,1)}, bf16[256,512]{1,0:T(8,128)(2,1)S(1)}, u32[]{:S(2)}) copy-start(bf16[256,512]{1,0:T(8,128)(2,1)S(1)} %collective-permute-done.3.refs_6_.refs_3_) | copy-start | bytes 786436
  28.0 4.7 %copy-start.17 = (bf16[2,138,276]{2,1,0:T(8,128)(2,1)S(1)}, bf16[2,138,276]{2,1,0:T(8,128)(2,1)}, u32[]{:S(2)}) copy-start(bf16[2,138,276]{2,1,0:T(8,128)(2,1)} %constant.37.clone.refs_2_) | copy-start | bytes 457060
  28.0 21.3 %collective-permute-start.4 = (bf16[576,768]{1,0:T(8,128)(2,1)S(1)}, bf16[576,768]{1,0:T(8,128)(2,1)S(1)}, u32[]{:S(2)}, u32[]{:S(2)}) collective-permute-start(bf16[576,768]{1,0:T(8,128)(2,1)S(1)} %shard_map.148.refs_0_.refs_2_), channel_id=1, source_target_pairs={{0,1},{1,0},{2,3},{3,2},{4,5},{5,4},{6,7},{7,6},{8,9},{9,8},{10,11... | collective-permute-start | bytes 2654216 | tf_op jit(solution)/shard_map/ppermute | solution.py:420
  29.2 12.7 %all-to-all-start = ((bf16[4,256,256]{2,1,0:T(8,128)(2,1)}), bf16[4,256,256]{2,1,0:T(8,128)(2,1)S(1)}, u32[]{:S(2)}, u32[]{:S(2)}) async-start(bf16[4,256,256]{2,1,0:T(8,128)(2,1)} %shard_map.151), calls=%async_computation | async-start | bytes 1048576 | tf_op jit(solution)/shard_map/all_to_all | solution.py:410
  32.7 1.7 %copy-start.20 = (f32[2304,144]{1,0:T(8,128)S(1)}, f32[2304,144]{1,0:T(8,128)}, u32[]{:S(2)}) copy-start(f32[2304,144]{1,0:T(8,128)} %copy-done.19) | copy-start | bytes 3981316
  36.3 1.5 %collective-permute-start.9 = (bf16[256,128]{1,0:T(8,128)(2,1)S(1)}, bf16[256,128]{1,0:T(8,128)(2,1)S(1)}, u32[]{:S(2)}, u32[]{:S(2)}) collective-permute-start(bf16[256,128]{1,0:T(8,128)(2,1)S(1)} %get-tuple-element.56), channel_id=1, source_target_pairs={{0,16},{2,18},{4,20},{6,22},{8,24},{10,26},{12,28},{14,30},{16,0},... | collective-permute-start | bytes 196616 | tf_op jit(solution)/shard_map/ppermute | solution.py:404
  42.7 13.0 %all-to-all-start.1 = ((bf16[8,32,384]{2,1,0:T(8,128)(2,1)}), bf16[8,32,384]{2,1,0:T(8,128)(2,1)S(1)}, u32[]{:S(2)}, u32[]{:S(2)}) async-start(bf16[8,32,384]{2,1,0:T(8,128)(2,1)} %shard_map.153), calls=%async_computation.1 | async-start | bytes 393216 | tf_op jit(solution)/shard_map/all_to_all | solution.py:416
  49.3 1.0 copy-start.6
  50.3 0.9 copy-start.8
  52.6 0.7 copy-start.10
  53.3 0.8 copy-start.21
  55.7 11.9 %copy-start.11 = (bf16[2,72,512]{2,1,0:T(8,128)(2,1)S(1)}, bf16[2,72,512]{2,1,0:T(8,128)(2,1)}, u32[]{:S(2)}) copy-start(bf16[2,72,512]{2,1,0:T(8,128)(2,1)} %copy-done.10) | copy-start | bytes 442372
  55.8 7.4 %collective-permute-start.10 = (bf16[32,256]{1,0:T(8,128)(2,1)S(1)}, bf16[32,256]{1,0:T(8,128)(2,1)S(1)}, u32[]{:S(2)}, u32[]{:S(2)}) collective-permute-start(bf16[32,256]{1,0:T(8,128)(2,1)S(1)} %get-tuple-element.58.refs_0_), channel_id=1, source_target_pairs={{0,2},{2,0},{4,6},{6,4},{8,10},{10,8},{12,14},{14,12},{16,18},{18,... | collective-permute-start | bytes 49160 | tf_op jit(solution)/shard_map/ppermute | solution.py:404
  59.8 24.3 %collective-permute-start.5 = (bf16[2,216,512]{2,1,0:T(8,128)(2,1)S(1)}, bf16[2,216,512]{2,1,0:T(8,128)(2,1)S(1)}, u32[]{:S(2)}, u32[]{:S(2)}) collective-permute-start(bf16[2,216,512]{2,1,0:T(8,128)(2,1)S(1)} %get-tuple-element.47), channel_id=1, source_target_pairs={{0,16},{1,17},{2,18},{3,19},{4,20},{5,21},{6,22},{7,23},{8,24},{9,... | collective-permute-start | bytes 1327112 | tf_op jit(solution)/shard_map/ppermute | solution.py:398
  63.9 12.4 %all-to-all-start.2 = ((bf16[8,32,384]{2,1,0:T(8,128)(2,1)}), bf16[8,32,384]{2,1,0:T(8,128)(2,1)S(1)}, u32[]{:S(2)}, u32[]{:S(2)}) async-start(bf16[8,32,384]{2,1,0:T(8,128)(2,1)} %shard_map.155), calls=%async_computation.2 | async-start | bytes 393216 | tf_op jit(solution)/shard_map/all_to_all | solution.py:416
  67.6 16.5 %collective-permute-start.6 = (bf16[2,72,512]{2,1,0:T(8,128)(2,1)}, bf16[2,72,512]{2,1,0:T(8,128)(2,1)}, u32[]{:S(2)}, u32[]{:S(2)}) collective-permute-start(bf16[2,72,512]{2,1,0:T(8,128)(2,1)} %get-tuple-element.48), channel_id=1, source_target_pairs={{0,3},{1,2},{2,5},{3,4},{4,7},{5,6},{6,9},{7,8},{8,11},{9,10},{10,... | collective-permute-start | bytes 442376 | tf_op jit(solution)/shard_map/ppermute | solution.py:398
  67.6 16.5 %copy-start.2 = (bf16[12,12,4,512]{3,2,1,0:T(4,128)(2,1)S(1)}, bf16[12,12,4,512]{3,2,1,0:T(4,128)(2,1)}, u32[]{:S(2)}) copy-start(bf16[12,12,4,512]{3,2,1,0:T(4,128)(2,1)} %refs_0_.3) | copy-start | bytes 1769476
  67.6 16.5 %copy-start.4 = (bf16[12,12,4,512]{3,2,1,0:T(4,128)(2,1)S(1)}, bf16[12,12,4,512]{3,2,1,0:T(4,128)(2,1)}, u32[]{:S(2)}) copy-start(bf16[12,12,4,512]{3,2,1,0:T(4,128)(2,1)} %refs_1_.7) | copy-start | bytes 1769476
  67.6 16.4 %collective-permute-start.7 = (bf16[2,72,512]{2,1,0:T(8,128)(2,1)S(1)}, bf16[2,72,512]{2,1,0:T(8,128)(2,1)}, u32[]{:S(2)}, u32[]{:S(2)}) collective-permute-start(bf16[2,72,512]{2,1,0:T(8,128)(2,1)S(1)} %copy-done.11), channel_id=1, source_target_pairs={{0,19},{1,18},{2,21},{3,20},{4,23},{5,22},{6,25},{7,24},{8,27},{9,... | collective-permute-start | bytes 442376 | tf_op jit(solution)/shard_map/ppermute | solution.py:398
  77.1 0.6 copy-start.12
  77.8 12.1 %all-to-all-start.3 = ((bf16[4,256,256]{2,1,0:T(8,128)(2,1)}), bf16[4,256,256]{2,1,0:T(8,128)(2,1)S(1)}, u32[]{:S(2)}, u32[]{:S(2)}) async-start(bf16[4,256,256]{2,1,0:T(8,128)(2,1)} %get-tuple-element.60), calls=%async_computation.3 | async-start | bytes 1048576 | tf_op jit(solution)/shard_map/all_to_all | solution.py:410
  81.2 7.1 %collective-permute-start.11 = (bf16[256,128]{1,0:T(8,128)(2,1)}, bf16[256,128]{1,0:T(8,128)(2,1)S(1)}, u32[]{:S(2)}, u32[]{:S(2)}) collective-permute-start(bf16[256,128]{1,0:T(8,128)(2,1)} %copy-done.12), channel_id=1, source_target_pairs={{0,16},{2,18},{4,20},{6,22},{8,24},{10,26},{12,28},{14,30},{16,0},... | collective-permute-start | bytes 196616 | tf_op jit(solution)/shard_map/ppermute | solution.py:404
  84.1 1.0 %copy-start.22 = (bf16[2,216,512]{2,1,0:T(8,128)(2,1)S(1)}, bf16[2,216,512]{2,1,0:T(8,128)(2,1)}, u32[]{:S(2)}) copy-start(bf16[2,216,512]{2,1,0:T(8,128)(2,1)} %copy-done.21) | copy-start | bytes 1327108
  85.1 3.2 %copy-start.13 = (bf16[256,128]{1,0:T(8,128)(2,1)S(1)}, bf16[256,128]{1,0:T(8,128)(2,1)}, u32[]{:S(2)}) copy-start(bf16[256,128]{1,0:T(8,128)(2,1)} %copy-done.12) | copy-start | bytes 196612
  89.8 5.3 %collective-permute-start.15 = (bf16[1024,256]{1,0:T(8,128)(2,1)S(1)}, bf16[1024,256]{1,0:T(8,128)(2,1)S(1)}, u32[]{:S(2)}, u32[]{:S(2)}) collective-permute-start(bf16[1024,256]{1,0:T(8,128)(2,1)S(1)} %bitcast.5), channel_id=1, source_target_pairs={{0,16},{2,18},{4,20},{6,22},{8,24},{10,26},{12,28},{14,30},{16,0},... | collective-permute-start | bytes 1572872 | tf_op jit(solution)/shard_map/ppermute | solution.py:404
  92.9 4.1 %collective-permute-start.14 = (f32[8,512]{1,0:T(8,128)S(1)}, f32[8,512]{1,0:T(8,128)S(1)}, u32[]{:S(2)}, u32[]{:S(2)}) collective-permute-start(f32[8,512]{1,0:T(8,128)S(1)} %shard_map.158.refs_0_), channel_id=1, source_target_pairs={{0,17},{1,16},{16,1},{17,0},{32,49},{33,48},{48,33},{49,32},{64,81... | collective-permute-start | bytes 49160 | tf_op jit(solution)/shard_map/ppermute | solution.py:425
  93.0 4.1 %collective-permute-start.13 = (f32[8,512]{1,0:T(8,128)S(1)}, f32[8,512]{1,0:T(8,128)S(1)}, u32[]{:S(2)}, u32[]{:S(2)}) collective-permute-start(f32[8,512]{1,0:T(8,128)S(1)} %shard_map.158.refs_0_), channel_id=1, source_target_pairs={{0,1},{1,0},{2,3},{3,2},{4,5},{5,4},{6,7},{7,6},{8,9},{9,8},{10,11... | collective-permute-start | bytes 49160 | tf_op jit(solution)/shard_map/ppermute | solution.py:420
  94.3 2.8 %collective-permute-start.12 = (f32[8,512]{1,0:T(8,128)S(1)}, f32[8,512]{1,0:T(8,128)S(1)}, u32[]{:S(2)}, u32[]{:S(2)}) collective-permute-start(f32[8,512]{1,0:T(8,128)S(1)} %shard_map.158.refs_0_), channel_id=1, source_target_pairs={{0,16},{2,18},{4,20},{6,22},{8,24},{10,26},{12,28},{14,30},{16,0},... | collective-permute-start | bytes 49160 | tf_op jit(solution)/shard_map/ppermute | solution.py:404

commit v11 on v8

--- a/solution.py
+++ b/solution.py
@@ -10,6 +10,8 @@
 F32 = jnp.float32
 WTOK = 144
 OFFS = 23
+PAIRS = 16 * WTOK + 8
+ROOM = 192 + 8
 NT = (((1,), (1,)), ((), ()))
 TN = (((0,), (0,)), ((), ()))
 
@@ -127,9 +129,9 @@
     mid = rest.astype(BF)
     low = (rest - mid.astype(F32)).astype(BF)
     wide = dot(low, order[...]) + dot(mid, order[...]) + dot(high, order[...])
-    t0[...] = wide[:, 0:128]
-    t1[...] = wide[:, 128:256]
-    t2[:, 0:20] = wide[:, 256:276]
+    t0[0:192, :] = wide[:, 0:128]
+    t1[0:192, :] = wide[:, 128:256]
+    t2[0:192, 0:20] = wide[:, 256:276]
     for i in range(16):
         at, rows = pl.ds(i, 12, stride=16), slice(i * 12, i * 12 + 12)
         entries[rows, 0:128] = t0[at, :]
@@ -145,7 +147,7 @@
     last_lev = ((which % 8) >= 4).astype(jnp.int32)
     barred = (last_lat * (edge_t - edge_u) != 0) | (last_lev * (s_t - s_u) != 0)
     for p in range(12):
-        at = jnp.where(barred, -jnp.inf, entries[:, (11 - p) * 12 : (11 - p) * 12 + WTOK])
+        at = jnp.where(barred, -jnp.inf, entries[0:192, (11 - p) * 12 : (11 - p) * 12 + WTOK])
         for i in range(16):
             bias[i * WTOK + p * 12 : i * WTOK + p * 12 + 12, :] = at[i * 12 : i * 12 + 12]
 
@@ -335,7 +337,7 @@
         for i in range(16):
             part[i * 12 : i * 12 + 12, :] = ds[i * WTOK + p * 12 : i * WTOK + p * 12 + 12, :]
         at = slice((11 - p) * 12, (11 - p) * 12 + WTOK)
-        entries[:, at] = entries[:, at] + part[...]
+        entries[:, at] = entries[:, at] + part[0:192, :]
     total = entries[...].astype(BF)
     packed[...] = jnp.zeros_like(packed)
     for s_u in range(2):
@@ -453,16 +455,16 @@
 
     bias, w_copy = call(
         bias_kernel,
-        [((16 * WTOK, WTOK), F32), (w_out.shape, BF)],
+        [((PAIRS, WTOK), F32), (w_out.shape, BF)],
         [info, bias_table, order, w_out],
-        [pltpu.VMEM((192, 276), F32)] * 2 + [pltpu.VMEM((192, 128), F32)] * 3,
+        [pltpu.VMEM((192, 276), F32), pltpu.VMEM((ROOM, 276), F32)] + [pltpu.VMEM((256, 128), F32)] * 3,
         us=2,
     )
     w_other = other_group(w_copy)
 
     keep, send, ds, att, gq, gk, gv = call(
         main_kernel,
-        [((1024, 256), F32), ((1024, 256), BF), ((16 * WTOK, WTOK), F32)] + [((576, 256), BF)] * 4,
+        [((1024, 256), F32), ((1024, 256), BF), ((PAIRS, WTOK), F32)] + [((576, 256), BF)] * 4,
         [info, latent, cotangent, in_lon, in_lat, in_cor, place, gain, w_qkv, w_out, bias],
         [pltpu.VMEM((576, 512), F32)],
         us=9,
@@ -490,7 +492,7 @@
         bias_grad_kernel,
         [((256, 128), BF)] * 2,
         [info, ds, order_halves],
-        [pltpu.VMEM((192, WTOK), F32), pltpu.VMEM((192, 276), F32), pltpu.VMEM((512, 128), F32)]
+        [pltpu.VMEM((ROOM, WTOK), F32), pltpu.VMEM((192, 276), F32), pltpu.VMEM((512, 128), F32)]
         + [pltpu.VMEM((192, 128), F32)] * 6,
         us=2.5,
     )

time: 98.2 us -> 98.2 us (level)
  no operation moved by 1% of the time
where the time goes in v11:
time: 98.2 us; the launch traced here: 97.7 us
  starting transfers between devices  50.3 us (51%)
  Pallas kernels  25.5 us (26%)
  waiting for transfers between devices  14 us (14%)
  local copies, waits for them, and re-layouts  6.71 us (7%)
  between operations  1.03 us (1%)
    pallas_call x16, Pallas kernels, call(): pl.pallas_call(kernel, out_shape=[jax.ShapeDtypeStruct(s, t) for s, t in...  25.5 us
    ppermute x6, starting transfers between devices, moved(): return lax.ppermute(value, ('lon', 'lat', 'tp'), pairs)  20.9 us
    ppermute x6, starting transfers between devices, swapped(): return lax.ppermute(value, ('lon', 'lat'), pairs)  12.7 us
    all_to_all x2, starting transfers between devices, across_z(): return lax.all_to_all(value, 'lon', 0, 0, axis_index_groups=groups)  8.25 us
    all_to_all x2, starting transfers between devices, across_y(): return lax.all_to_all(value, 'lat', 0, 0, axis_index_groups=groups)  6.96 us
    unnamed x46, local copies, waits for them, and re-layouts  6.71 us
    all_to_all x2, waiting for transfers between devices, across_z(): return lax.all_to_all(value, 'lon', 0, 0, axis_index_groups=groups)  4.86 us
    all_to_all x2, waiting for transfers between devices, across_y(): return lax.all_to_all(value, 'lat', 0, 0, axis_index_groups=groups)  4.06 us
  transfers between devices with their start and end apart: 20, of which 7 were waited for; matrix products, arithmetic and copies ran while one was open for 0% of the time, Pallas kernels for 23%

profile of v11, /device:TPU:1, one launch (start us, length us, event | category | flops | bytes accessed | tf_op | source)
XLA Modules:
  0.0 97.7 jit_solution(16361725807595519473)
XLA Ops:
  0.7 2.2 %shard_map.145 = (bf16[2,216,512]{2,1,0:T(8,128)(2,1)}, bf16[2,72,512]{2,1,0:T(8,128)(2,1)}, bf16[2,72,512]{2,1,0:T(8,128)(2,1)}) custom-call(bf16[12,12,4,512]{3,2,1,0:T(4,128)(2,1)} %refs_0_.3, bf16[12,12,4,512]{3,2,1,0:T(4,128)(2,1)} %refs_1_.7), custom_call_target="tpu_custom_call" | custom-call | flops 1000000000 | tf_op jit(solution)/shard_map/pallas_call | solution.py:61
  2.9 3.3 %collective-permute-start = (bf16[2,216,512]{2,1,0:T(8,128)(2,1)}, bf16[2,216,512]{2,1,0:T(8,128)(2,1)S(1)}, u32[]{:S(2)}, u32[]{:S(2)}) collective-permute-start(bf16[2,216,512]{2,1,0:T(8,128)(2,1)} %get-tuple-element.37), channel_id=1, source_target_pairs={{0,240},{1,241},{2,242},{3,243},{4,244},{5,245},{6,246},{7,247},{8... | collective-permute-start | bytes 1327112 | tf_op jit(solution)/shard_map/ppermute | solution.py:400
  6.1 3.2 %collective-permute-start.1 = (bf16[2,72,512]{2,1,0:T(8,128)(2,1)}, bf16[2,72,512]{2,1,0:T(8,128)(2,1)S(1)}, u32[]{:S(2)}, u32[]{:S(2)}) collective-permute-start(bf16[2,72,512]{2,1,0:T(8,128)(2,1)} %get-tuple-element.38), channel_id=1, source_target_pairs={{0,15},{1,14},{2,1},{3,0},{4,3},{5,2},{6,5},{7,4},{8,7},{9,6},{10,... | collective-permute-start | bytes 442376 | tf_op jit(solution)/shard_map/ppermute | solution.py:400
  9.3 5.7 %collective-permute-start.2 = (bf16[2,72,512]{2,1,0:T(8,128)(2,1)}, bf16[2,72,512]{2,1,0:T(8,128)(2,1)S(1)}, u32[]{:S(2)}, u32[]{:S(2)}) collective-permute-start(bf16[2,72,512]{2,1,0:T(8,128)(2,1)} %get-tuple-element.39), channel_id=1, source_target_pairs={{0,255},{1,254},{2,241},{3,240},{4,243},{5,242},{6,245},{7,244},{8... | collective-permute-start | bytes 442376 | tf_op jit(solution)/shard_map/ppermute | solution.py:400
  15.0 0.1 pad_add_fusion.refs_0_
  15.1 1.8 %shard_map.146 = (f32[2312,144]{1,0:T(8,128)S(1)}, bf16[256,512]{1,0:T(8,128)(2,1)S(1)}) custom-call(s32[2]{0:T(128)S(1)} %pad_add_fusion.refs_0_, f32[2,2,4,3312]{3,2,1,0:T(4,128)S(1)} %copy-done.9, bf16[276,276]{1,0:T(8,128)(2,1)S(1)} %copy-done.18, bf16[256,512]{1,0:T(8,128)(2,1)S(1)} %copy-done.5), custom_call_target="tpu_custom_call" | custom-call | flops 2000000000 | tf_op jit(solution)/shard_map/pallas_call | solution.py:61
  16.9 0.1 collective-permute-start.3
  17.0 1.8 %collective-permute-done.2.refs_5_ = bf16[2,72,512]{2,1,0:T(8,128)(2,1)S(1)} collective-permute-done((bf16[2,72,512]{2,1,0:T(8,128)(2,1)}, bf16[2,72,512]{2,1,0:T(8,128)(2,1)S(1)}, u32[]{:S(2)}, u32[]{:S(2)}) %collective-permute-start.2) | collective-permute-done | bytes 147488 | tf_op jit(solution)/shard_map/ppermute | solution.py:400
  18.9 5.8 %shard_map.147 = (f32[1024,256]{1,0:T(8,128)S(1)}, bf16[1024,256]{1,0:T(8,128)(2,1)S(1)}, f32[2312,144]{1,0:T(8,128)S(1)}, bf16[576,256]{1,0:T(8,128)(2,1)S(1)},...) custom-call(s32[2]{0:T(128)S(1)} %pad_add_fusion.refs_0_, ...), custom_call_target="tpu_custom_call" | custom-call | flops 8999999488 | tf_op jit(solution)/shard_map/pallas_call | solution.py:61
  24.7 2.1 %collective-permute-start.8 = (bf16[1024,256]{1,0:T(8,128)(2,1)S(1)}, bf16[1024,256]{1,0:T(8,128)(2,1)S(1)}, u32[]{:S(2)}, u32[]{:S(2)}) collective-permute-start(bf16[1024,256]{1,0:T(8,128)(2,1)S(1)} %get-tuple-element.53), channel_id=1, source_target_pairs={{0,16},{2,18},{4,20},{6,22},{8,24},{10,26},{12,28},{14,30},{16,0},... | collective-permute-start | bytes 1572872 | tf_op jit(solution)/shard_map/ppermute | solution.py:406
  26.8 1.1 %shard_map.148.refs_0_.refs_2_ = bf16[576,768]{1,0:T(8,128)(2,1)S(1)} custom-call(bf16[576,256]{1,0:T(8,128)(2,1)S(1)} %get-tuple-element.41.refs_0_, bf16[576,256]{1,0:T(8,128)(2,1)S(1)} %get-tuple-element.42.refs_1_, bf16[576,256]{1,0:T(8,128)(2,1)S(1)} %get-tuple-element.43.refs_2_, bf16[576,256]{1,0:T(8,128)(2,1)S(1)} %get-tuple-element.44.refs_3_, ...), custom_call_target="tpu_custom_call" | custom-call | flops 2000000000 | tf_op jit(solution)/shard_map/pallas_call | solution.py:61
  28.0 0.1 collective-permute-start.4
  28.1 0.2 collective-permute-done.8.refs_1_
  28.4 0.8 shard_map.151
  29.2 3.5 %all-to-all-start = ((bf16[4,256,256]{2,1,0:T(8,128)(2,1)}), bf16[4,256,256]{2,1,0:T(8,128)(2,1)S(1)}, u32[]{:S(2)}, u32[]{:S(2)}) async-start(bf16[4,256,256]{2,1,0:T(8,128)(2,1)} %shard_map.151), calls=%async_computation | async-start | bytes 1048576 | tf_op jit(solution)/shard_map/all_to_all | solution.py:412
  32.7 1.7 %copy-done.20 = f32[2312,144]{1,0:T(8,128)S(1)} copy-done((f32[2312,144]{1,0:T(8,128)S(1)}, f32[2312,144]{1,0:T(8,128)}, u32[]{:S(2)}) %copy-start.20) | copy-done | bytes 1331736
  34.4 1.9 %shard_map.152 = (bf16[256,128]{1,0:T(8,128)(2,1)S(1)}, bf16[256,128]{1,0:T(8,128)(2,1)S(1)}) custom-call(s32[2]{0:T(128)S(1)} %pad_add_fusion.refs_0_, f32[2312,144]{1,0:T(8,128)S(1)} %copy-done.20, bf16[2,138,276]{2,1,0:T(8,128)(2,1)S(1)} %copy-done.17), custom_call_target="tpu_custom_call" | custom-call | flops 2500000000 | tf_op jit(solution)/shard_map/pallas_call | solution.py:61
  36.3 0.6 collective-permute-start.9
  36.9 0.9 collective-permute-done.9.refs_2_
  37.8 4.1 %all-to-all-done.refs_0_ = bf16[4,256,256]{2,1,0:T(8,128)(2,1)S(1)} async-done(((bf16[4,256,256]{2,1,0:T(8,128)(2,1)}), bf16[4,256,256]{2,1,0:T(8,128)(2,1)S(1)}, u32[]{:S(2)}, u32[]{:S(2)}) %all-to-all-start) | async-done | bytes 524320 | tf_op jit(solution)/shard_map/all_to_all | solution.py:412
  41.9 0.8 shard_map.153
  42.7 4.6 %all-to-all-start.1 = ((bf16[8,32,384]{2,1,0:T(8,128)(2,1)}), bf16[8,32,384]{2,1,0:T(8,128)(2,1)S(1)}, u32[]{:S(2)}, u32[]{:S(2)}) async-start(bf16[8,32,384]{2,1,0:T(8,128)(2,1)} %shard_map.153), calls=%async_computation.1 | async-start | bytes 393216 | tf_op jit(solution)/shard_map/all_to_all | solution.py:418
  47.2 2.1 %collective-permute-done.4.refs_1_ = bf16[576,768]{1,0:T(8,128)(2,1)S(1)} collective-permute-done((bf16[576,768]{1,0:T(8,128)(2,1)S(1)}, bf16[576,768]{1,0:T(8,128)(2,1)S(1)}, u32[]{:S(2)}, u32[]{:S(2)}) %collective-permute-start.4) | collective-permute-done | bytes 884768 | tf_op jit(solution)/shard_map/ppermute | solution.py:422
  49.3 0.9 copy-done.6
  50.3 0.9 copy-done.8
  51.2 1.4 %shard_map.149 = (bf16[2,216,512]{2,1,0:T(8,128)(2,1)S(1)}, bf16[2,216,512]{2,1,0:T(8,128)(2,1)S(1)}, bf16[2,72,512]{2,1,0:T(8,128)(2,1)}, bf16[2,72,512]{2,1,0:T(8,128)(2,1)S(1)}, f32[8,128]{1,0:T(8,128)S(1)}) custom-call(bf16[576,768]{1,0:T(8,128)(2,1)S(1)} %shard_map.148.refs_0_.refs_2_, bf16[576,768]{1,0:T(8,128)(2,1)S(1)} %collective-permute-done.4.refs_1_, ...), custom_call_target="tpu_custom_call" | custom-call | flops 30000001024 | tf_op jit(solution)/shard_map/pallas_call | solution.py:61
  52.6 0.7 copy-done.10
  53.3 0.8 copy-done.21
  54.0 1.7 %all-to-all-done.1.refs_0_ = bf16[8,32,384]{2,1,0:T(8,128)(2,1)S(1)} async-done(((bf16[8,32,384]{2,1,0:T(8,128)(2,1)}), bf16[8,32,384]{2,1,0:T(8,128)(2,1)S(1)}, u32[]{:S(2)}, u32[]{:S(2)}) %all-to-all-start.1) | async-done | bytes 196640 | tf_op jit(solution)/shard_map/all_to_all | solution.py:418
  55.7 4.1 %collective-permute-start.10 = (bf16[32,256]{1,0:T(8,128)(2,1)S(1)}, bf16[32,256]{1,0:T(8,128)(2,1)S(1)}, u32[]{:S(2)}, u32[]{:S(2)}) collective-permute-start(bf16[32,256]{1,0:T(8,128)(2,1)S(1)} %get-tuple-element.58.refs_0_), channel_id=1, source_target_pairs={{0,2},{2,0},{4,6},{6,4},{8,10},{10,8},{12,14},{14,12},{16,18},{18,... | collective-permute-start | bytes 49160 | tf_op jit(solution)/shard_map/ppermute | solution.py:406
  59.8 3.3 %collective-permute-start.5 = (bf16[2,216,512]{2,1,0:T(8,128)(2,1)S(1)}, bf16[2,216,512]{2,1,0:T(8,128)(2,1)S(1)}, u32[]{:S(2)}, u32[]{:S(2)}) collective-permute-start(bf16[2,216,512]{2,1,0:T(8,128)(2,1)S(1)} %get-tuple-element.47), channel_id=1, source_target_pairs={{0,16},{1,17},{2,18},{3,19},{4,20},{5,21},{6,22},{7,23},{8,24},{9,... | collective-permute-start | bytes 1327112 | tf_op jit(solution)/shard_map/ppermute | solution.py:400
  63.2 0.7 shard_map.155
  63.9 3.7 %all-to-all-start.2 = ((bf16[8,32,384]{2,1,0:T(8,128)(2,1)}), bf16[8,32,384]{2,1,0:T(8,128)(2,1)S(1)}, u32[]{:S(2)}, u32[]{:S(2)}) async-start(bf16[8,32,384]{2,1,0:T(8,128)(2,1)} %shard_map.155), calls=%async_computation.2 | async-start | bytes 393216 | tf_op jit(solution)/shard_map/all_to_all | solution.py:418
  67.7 5.4 %collective-permute-start.7 = (bf16[2,72,512]{2,1,0:T(8,128)(2,1)S(1)}, bf16[2,72,512]{2,1,0:T(8,128)(2,1)}, u32[]{:S(2)}, u32[]{:S(2)}) collective-permute-start(bf16[2,72,512]{2,1,0:T(8,128)(2,1)S(1)} %copy-done.11), channel_id=1, source_target_pairs={{0,19},{1,18},{2,21},{3,20},{4,23},{5,22},{6,25},{7,24},{8,27},{9,... | collective-permute-start | bytes 442376 | tf_op jit(solution)/shard_map/ppermute | solution.py:400
  73.1 3.2 %all-to-all-done.2.refs_0_ = bf16[8,32,384]{2,1,0:T(8,128)(2,1)S(1)} async-done(((bf16[8,32,384]{2,1,0:T(8,128)(2,1)}), bf16[8,32,384]{2,1,0:T(8,128)(2,1)S(1)}, u32[]{:S(2)}, u32[]{:S(2)}) %all-to-all-start.2) | async-done | bytes 196640 | tf_op jit(solution)/shard_map/all_to_all | solution.py:418
  76.3 0.8 shard_map.156
  77.1 0.6 copy-done.12
  77.8 3.5 %all-to-all-start.3 = ((bf16[4,256,256]{2,1,0:T(8,128)(2,1)}), bf16[4,256,256]{2,1,0:T(8,128)(2,1)S(1)}, u32[]{:S(2)}, u32[]{:S(2)}) async-start(bf16[4,256,256]{2,1,0:T(8,128)(2,1)} %get-tuple-element.60), calls=%async_computation.3 | async-start | bytes 1048576 | tf_op jit(solution)/shard_map/all_to_all | solution.py:412
  81.2 2.9 %collective-permute-start.11 = (bf16[256,128]{1,0:T(8,128)(2,1)}, bf16[256,128]{1,0:T(8,128)(2,1)S(1)}, u32[]{:S(2)}, u32[]{:S(2)}) collective-permute-start(bf16[256,128]{1,0:T(8,128)(2,1)} %copy-done.12), channel_id=1, source_target_pairs={{0,16},{2,18},{4,20},{6,22},{8,24},{10,26},{12,28},{14,30},{16,0},... | collective-permute-start | bytes 196616 | tf_op jit(solution)/shard_map/ppermute | solution.py:406
  84.1 1.0 %copy-done.22 = bf16[2,216,512]{2,1,0:T(8,128)(2,1)S(1)} copy-done((bf16[2,216,512]{2,1,0:T(8,128)(2,1)S(1)}, bf16[2,216,512]{2,1,0:T(8,128)(2,1)}, u32[]{:S(2)}) %copy-start.22) | copy-done | bytes 442392
  85.1 3.2 %shard_map.150 = (f32[8,128]{1,0:T(8,128)S(1)}, bf16[12,12,4,512]{3,2,1,0:T(4,128)(2,1)}, bf16[12,12,4,512]{3,2,1,0:T(4,128)(2,1)}) custom-call(bf16[12,12,4,512]{3,2,1,0:T(4,128)(2,1)S(1)} %copy-done.2, bf16[12,12,4,512]{3,2,1,0:T(4,128)(2,1)S(1)} %copy-done.4, f32[1,512]{1,0:T(1,128)S(1)} %bitcast.9, bf16[2,216,512]{2,1,0:T(8,128)(2,1)S(1)} %copy-done.22, ...), custom_call_target="tpu_custom_call" | custom-call | flops 30000001024 | tf_op jit(solution)/shard_map/pallas_call | solution.py:61
  88.3 1.5 %shard_map.157 = (f32[2,2,4,3312]{3,2,1,0:T(4,128)}, f32[8,128]{1,0:T(8,128)S(1)}) custom-call(s32[2]{0:T(128)S(1)} %pad_add_fusion.refs_0_, bf16[256,128]{1,0:T(8,128)(2,1)S(1)} %copy-done.13, bf16[256,128]{1,0:T(8,128)(2,1)S(1)} %collective-permute-done.11.refs_2_, f32[8,128]{1,0:T(8,128)S(1)} %get-tuple-element.62.refs_3_), custom_call_target="tpu_custom_call" | custom-call | flops 1000000000 | tf_op jit(solution)/shard_map/pallas_call | solution.py:61
  89.8 2.2 %collective-permute-start.15 = (bf16[1024,256]{1,0:T(8,128)(2,1)S(1)}, bf16[1024,256]{1,0:T(8,128)(2,1)S(1)}, u32[]{:S(2)}, u32[]{:S(2)}) collective-permute-start(bf16[1024,256]{1,0:T(8,128)(2,1)S(1)} %bitcast.5), channel_id=1, source_target_pairs={{0,16},{2,18},{4,20},{6,22},{8,24},{10,26},{12,28},{14,30},{16,0},... | collective-permute-start | bytes 1572872 | tf_op jit(solution)/shard_map/ppermute | solution.py:406
  92.1 0.9 shard_map.158.refs_0_
  93.0 1.3 %collective-permute-start.13 = (f32[8,512]{1,0:T(8,128)S(1)}, f32[8,512]{1,0:T(8,128)S(1)}, u32[]{:S(2)}, u32[]{:S(2)}) collective-permute-start(f32[8,512]{1,0:T(8,128)S(1)} %shard_map.158.refs_0_), channel_id=1, source_target_pairs={{0,1},{1,0},{2,3},{3,2},{4,5},{5,4},{6,7},{7,6},{8,9},{9,8},{10,11... | collective-permute-start | bytes 49160 | tf_op jit(solution)/shard_map/ppermute | solution.py:422
  94.3 0.8 collective-permute-start.12
  95.1 1.9 %shard_map.159 = (f32[8,128]{1,0:T(8,128)S(1)}, f32[3,512,256]{2,1,0:T(8,128)}, f32[256,512]{1,0:T(8,128)}) custom-call(s32[2]{0:T(128)S(1)} %pad_add_fusion.refs_0_, bf16[1024,256]{1,0:T(8,128)(2,1)S(1)} %bitcast.7, bf16[1024,256]{1,0:T(8,128)(2,1)S(1)} %collective-permute-done.15.refs_2_), custom_call_target="tpu_custom_call" | custom-call | flops 2000000000 | tf_op jit(solution)/shard_map/pallas_call | solution.py:61
  97.1 0.6 shard_map.160
  (55 shorter events, 0.2 us)
Async XLA Ops:
  0.6 14.4 %copy-start.18 = (bf16[276,276]{1,0:T(8,128)(2,1)S(1)}, bf16[276,276]{1,0:T(8,128)(2,1)}, u32[]{:S(2)}) copy-start(bf16[276,276]{1,0:T(8,128)(2,1)} %constant.36.clone.refs_2_) | copy-start | bytes 457060
  0.6 14.4 %copy-start.5 = (bf16[256,512]{1,0:T(8,128)(2,1)S(1)}, bf16[256,512]{1,0:T(8,128)(2,1)}, u32[]{:S(2)}) copy-start(bf16[256,512]{1,0:T(8,128)(2,1)} %refs_2_.6) | copy-start | bytes 786436
  0.7 14.4 %copy-start.9 = (f32[2,2,4,3312]{3,2,1,0:T(4,128)S(1)}, f32[2,2,4,3312]{3,2,1,0:T(4,128)}, u32[]{:S(2)}) copy-start(f32[2,2,4,3312]{3,2,1,0:T(4,128)} %refs_1_.5) | copy-start | bytes 635908
  2.9 16.0 %collective-permute-start = (bf16[2,216,512]{2,1,0:T(8,128)(2,1)}, bf16[2,216,512]{2,1,0:T(8,128)(2,1)S(1)}, u32[]{:S(2)}, u32[]{:S(2)}) collective-permute-start(bf16[2,216,512]{2,1,0:T(8,128)(2,1)} %get-tuple-element.37), channel_id=1, source_target_pairs={{0,240},{1,241},{2,242},{3,243},{4,244},{5,245},{6,246},{7,247},{8... | collective-permute-start | bytes 1327112 | tf_op jit(solution)/shard_map/ppermute | solution.py:400
  6.1 10.9 %collective-permute-start.1 = (bf16[2,72,512]{2,1,0:T(8,128)(2,1)}, bf16[2,72,512]{2,1,0:T(8,128)(2,1)S(1)}, u32[]{:S(2)}, u32[]{:S(2)}) collective-permute-start(bf16[2,72,512]{2,1,0:T(8,128)(2,1)} %get-tuple-element.38), channel_id=1, source_target_pairs={{0,15},{1,14},{2,1},{3,0},{4,3},{5,2},{6,5},{7,4},{8,7},{9,6},{10,... | collective-permute-start | bytes 442376 | tf_op jit(solution)/shard_map/ppermute | solution.py:400
  9.3 9.5 %collective-permute-start.2 = (bf16[2,72,512]{2,1,0:T(8,128)(2,1)}, bf16[2,72,512]{2,1,0:T(8,128)(2,1)S(1)}, u32[]{:S(2)}, u32[]{:S(2)}) collective-permute-start(bf16[2,72,512]{2,1,0:T(8,128)(2,1)} %get-tuple-element.39), channel_id=1, source_target_pairs={{0,255},{1,254},{2,241},{3,240},{4,243},{5,242},{6,245},{7,244},{8... | collective-permute-start | bytes 442376 | tf_op jit(solution)/shard_map/ppermute | solution.py:400
  15.1 3.8 %copy-start = (bf16[3,512,256]{2,1,0:T(8,128)(2,1)S(1)}, bf16[3,512,256]{2,1,0:T(8,128)(2,1)}, u32[]{:S(2)}) copy-start(bf16[3,512,256]{2,1,0:T(8,128)(2,1)} %refs_2_.7) | copy-start | bytes 2359300
  15.1 3.8 %copy-start.1 = (bf16[12,12,4,512]{3,2,1,0:T(4,128)(2,1)S(1)}, bf16[12,12,4,512]{3,2,1,0:T(4,128)(2,1)}, u32[]{:S(2)}) copy-start(bf16[12,12,4,512]{3,2,1,0:T(4,128)(2,1)} %refs_0_.3) | copy-start | bytes 1769476
  15.1 3.8 %copy-start.3 = (bf16[12,12,4,512]{3,2,1,0:T(4,128)(2,1)S(1)}, bf16[12,12,4,512]{3,2,1,0:T(4,128)(2,1)}, u32[]{:S(2)}) copy-start(bf16[12,12,4,512]{3,2,1,0:T(4,128)(2,1)} %refs_1_.7) | copy-start | bytes 1769476
  15.1 3.8 %copy-start.14 = (f32[512]{0:T(512)S(1)}, f32[512]{0:T(512)}, u32[]{:S(2)}) copy-start(f32[512]{0:T(512)} %param.12) | copy-start | bytes 6148
  15.1 3.8 %copy-start.16 = (bf16[2,288,288]{2,1,0:T(8,128)(2,1)S(1)}, bf16[2,288,288]{2,1,0:T(8,128)(2,1)}, u32[]{:S(2)}) copy-start(bf16[2,288,288]{2,1,0:T(8,128)(2,1)} %constant.34.clone.refs_6_) | copy-start | bytes 995332
  16.9 9.9 %collective-permute-start.3 = (bf16[256,512]{1,0:T(8,128)(2,1)S(1)}, bf16[256,512]{1,0:T(8,128)(2,1)S(1)}, u32[]{:S(2)}, u32[]{:S(2)}) collective-permute-start(bf16[256,512]{1,0:T(8,128)(2,1)S(1)} %get-tuple-element.45), channel_id=1, source_target_pairs={{0,1},{1,0},{2,3},{3,2},{4,5},{5,4},{6,7},{7,6},{8,9},{9,8},{10,11... | collective-permute-start | bytes 786440 | tf_op jit(solution)/shard_map/ppermute | solution.py:422
  18.9 7.9 %copy-start.15 = (bf16[2,288,288]{2,1,0:T(8,128)(2,1)S(1)}, bf16[2,288,288]{2,1,0:T(8,128)(2,1)}, u32[]{:S(2)}) copy-start(bf16[2,288,288]{2,1,0:T(8,128)(2,1)} %constant.35.clone.refs_5_) | copy-start | bytes 995332
  24.7 3.3 %copy-start.19 = (f32[2312,144]{1,0:T(8,128)}, f32[2312,144]{1,0:T(8,128)S(1)}, u32[]{:S(2)}) copy-start(f32[2312,144]{1,0:T(8,128)S(1)} %get-tuple-element.54.refs_1_) | copy-start | bytes 3995140
  24.7 3.6 %collective-permute-start.8 = (bf16[1024,256]{1,0:T(8,128)(2,1)S(1)}, bf16[1024,256]{1,0:T(8,128)(2,1)S(1)}, u32[]{:S(2)}, u32[]{:S(2)}) collective-permute-start(bf16[1024,256]{1,0:T(8,128)(2,1)S(1)} %get-tuple-element.53), channel_id=1, source_target_pairs={{0,16},{2,18},{4,20},{6,22},{8,24},{10,26},{12,28},{14,30},{16,0},... | collective-permute-start | bytes 1572872 | tf_op jit(solution)/shard_map/ppermute | solution.py:406
  26.8 1.2 %copy-start.7 = (bf16[256,512]{1,0:T(8,128)(2,1)}, bf16[256,512]{1,0:T(8,128)(2,1)S(1)}, u32[]{:S(2)}) copy-start(bf16[256,512]{1,0:T(8,128)(2,1)S(1)} %collective-permute-done.3.refs_6_.refs_3_) | copy-start | bytes 786436
  28.0 4.7 %copy-start.17 = (bf16[2,138,276]{2,1,0:T(8,128)(2,1)S(1)}, bf16[2,138,276]{2,1,0:T(8,128)(2,1)}, u32[]{:S(2)}) copy-start(bf16[2,138,276]{2,1,0:T(8,128)(2,1)} %constant.37.clone.refs_2_) | copy-start | bytes 457060
  28.0 21.3 %collective-permute-start.4 = (bf16[576,768]{1,0:T(8,128)(2,1)S(1)}, bf16[576,768]{1,0:T(8,128)(2,1)S(1)}, u32[]{:S(2)}, u32[]{:S(2)}) collective-permute-start(bf16[576,768]{1,0:T(8,128)(2,1)S(1)} %shard_map.148.refs_0_.refs_2_), channel_id=1, source_target_pairs={{0,1},{1,0},{2,3},{3,2},{4,5},{5,4},{6,7},{7,6},{8,9},{9,8},{10,11... | collective-permute-start | bytes 2654216 | tf_op jit(solution)/shard_map/ppermute | solution.py:422
  29.2 12.7 %all-to-all-start = ((bf16[4,256,256]{2,1,0:T(8,128)(2,1)}), bf16[4,256,256]{2,1,0:T(8,128)(2,1)S(1)}, u32[]{:S(2)}, u32[]{:S(2)}) async-start(bf16[4,256,256]{2,1,0:T(8,128)(2,1)} %shard_map.151), calls=%async_computation | async-start | bytes 1048576 | tf_op jit(solution)/shard_map/all_to_all | solution.py:412
  32.7 1.7 %copy-start.20 = (f32[2312,144]{1,0:T(8,128)S(1)}, f32[2312,144]{1,0:T(8,128)}, u32[]{:S(2)}) copy-start(f32[2312,144]{1,0:T(8,128)} %copy-done.19) | copy-start | bytes 3995140
  36.3 1.5 %collective-permute-start.9 = (bf16[256,128]{1,0:T(8,128)(2,1)S(1)}, bf16[256,128]{1,0:T(8,128)(2,1)S(1)}, u32[]{:S(2)}, u32[]{:S(2)}) collective-permute-start(bf16[256,128]{1,0:T(8,128)(2,1)S(1)} %get-tuple-element.56), channel_id=1, source_target_pairs={{0,16},{2,18},{4,20},{6,22},{8,24},{10,26},{12,28},{14,30},{16,0},... | collective-permute-start | bytes 196616 | tf_op jit(solution)/shard_map/ppermute | solution.py:406
  42.7 13.0 %all-to-all-start.1 = ((bf16[8,32,384]{2,1,0:T(8,128)(2,1)}), bf16[8,32,384]{2,1,0:T(8,128)(2,1)S(1)}, u32[]{:S(2)}, u32[]{:S(2)}) async-start(bf16[8,32,384]{2,1,0:T(8,128)(2,1)} %shard_map.153), calls=%async_computation.1 | async-start | bytes 393216 | tf_op jit(solution)/shard_map/all_to_all | solution.py:418
  49.3 1.0 copy-start.6
  50.3 0.9 copy-start.8
  52.6 0.7 copy-start.10
  53.3 0.8 copy-start.21
  55.7 11.9 %copy-start.11 = (bf16[2,72,512]{2,1,0:T(8,128)(2,1)S(1)}, bf16[2,72,512]{2,1,0:T(8,128)(2,1)}, u32[]{:S(2)}) copy-start(bf16[2,72,512]{2,1,0:T(8,128)(2,1)} %copy-done.10) | copy-start | bytes 442372
  55.7 7.4 %collective-permute-start.10 = (bf16[32,256]{1,0:T(8,128)(2,1)S(1)}, bf16[32,256]{1,0:T(8,128)(2,1)S(1)}, u32[]{:S(2)}, u32[]{:S(2)}) collective-permute-start(bf16[32,256]{1,0:T(8,128)(2,1)S(1)} %get-tuple-element.58.refs_0_), channel_id=1, source_target_pairs={{0,2},{2,0},{4,6},{6,4},{8,10},{10,8},{12,14},{14,12},{16,18},{18,... | collective-permute-start | bytes 49160 | tf_op jit(solution)/shard_map/ppermute | solution.py:406
  59.8 24.3 %collective-permute-start.5 = (bf16[2,216,512]{2,1,0:T(8,128)(2,1)S(1)}, bf16[2,216,512]{2,1,0:T(8,128)(2,1)S(1)}, u32[]{:S(2)}, u32[]{:S(2)}) collective-permute-start(bf16[2,216,512]{2,1,0:T(8,128)(2,1)S(1)} %get-tuple-element.47), channel_id=1, source_target_pairs={{0,16},{1,17},{2,18},{3,19},{4,20},{5,21},{6,22},{7,23},{8,24},{9,... | collective-permute-start | bytes 1327112 | tf_op jit(solution)/shard_map/ppermute | solution.py:400
  63.9 12.4 %all-to-all-start.2 = ((bf16[8,32,384]{2,1,0:T(8,128)(2,1)}), bf16[8,32,384]{2,1,0:T(8,128)(2,1)S(1)}, u32[]{:S(2)}, u32[]{:S(2)}) async-start(bf16[8,32,384]{2,1,0:T(8,128)(2,1)} %shard_map.155), calls=%async_computation.2 | async-start | bytes 393216 | tf_op jit(solution)/shard_map/all_to_all | solution.py:418
  67.6 16.5 %collective-permute-start.6 = (bf16[2,72,512]{2,1,0:T(8,128)(2,1)}, bf16[2,72,512]{2,1,0:T(8,128)(2,1)}, u32[]{:S(2)}, u32[]{:S(2)}) collective-permute-start(bf16[2,72,512]{2,1,0:T(8,128)(2,1)} %get-tuple-element.48), channel_id=1, source_target_pairs={{0,3},{1,2},{2,5},{3,4},{4,7},{5,6},{6,9},{7,8},{8,11},{9,10},{10,... | collective-permute-start | bytes 442376 | tf_op jit(solution)/shard_map/ppermute | solution.py:400
  67.6 16.5 %copy-start.2 = (bf16[12,12,4,512]{3,2,1,0:T(4,128)(2,1)S(1)}, bf16[12,12,4,512]{3,2,1,0:T(4,128)(2,1)}, u32[]{:S(2)}) copy-start(bf16[12,12,4,512]{3,2,1,0:T(4,128)(2,1)} %refs_0_.3) | copy-start | bytes 1769476
  67.6 16.5 %copy-start.4 = (bf16[12,12,4,512]{3,2,1,0:T(4,128)(2,1)S(1)}, bf16[12,12,4,512]{3,2,1,0:T(4,128)(2,1)}, u32[]{:S(2)}) copy-start(bf16[12,12,4,512]{3,2,1,0:T(4,128)(2,1)} %refs_1_.7) | copy-start | bytes 1769476
  67.7 16.4 %collective-permute-start.7 = (bf16[2,72,512]{2,1,0:T(8,128)(2,1)S(1)}, bf16[2,72,512]{2,1,0:T(8,128)(2,1)}, u32[]{:S(2)}, u32[]{:S(2)}) collective-permute-start(bf16[2,72,512]{2,1,0:T(8,128)(2,1)S(1)} %copy-done.11), channel_id=1, source_target_pairs={{0,19},{1,18},{2,21},{3,20},{4,23},{5,22},{6,25},{7,24},{8,27},{9,... | collective-permute-start | bytes 442376 | tf_op jit(solution)/shard_map/ppermute | solution.py:400
  77.1 0.6 copy-start.12
  77.8 12.1 %all-to-all-start.3 = ((bf16[4,256,256]{2,1,0:T(8,128)(2,1)}), bf16[4,256,256]{2,1,0:T(8,128)(2,1)S(1)}, u32[]{:S(2)}, u32[]{:S(2)}) async-start(bf16[4,256,256]{2,1,0:T(8,128)(2,1)} %get-tuple-element.60), calls=%async_computation.3 | async-start | bytes 1048576 | tf_op jit(solution)/shard_map/all_to_all | solution.py:412
  81.2 7.1 %collective-permute-start.11 = (bf16[256,128]{1,0:T(8,128)(2,1)}, bf16[256,128]{1,0:T(8,128)(2,1)S(1)}, u32[]{:S(2)}, u32[]{:S(2)}) collective-permute-start(bf16[256,128]{1,0:T(8,128)(2,1)} %copy-done.12), channel_id=1, source_target_pairs={{0,16},{2,18},{4,20},{6,22},{8,24},{10,26},{12,28},{14,30},{16,0},... | collective-permute-start | bytes 196616 | tf_op jit(solution)/shard_map/ppermute | solution.py:406
  84.1 1.0 %copy-start.22 = (bf16[2,216,512]{2,1,0:T(8,128)(2,1)S(1)}, bf16[2,216,512]{2,1,0:T(8,128)(2,1)}, u32[]{:S(2)}) copy-start(bf16[2,216,512]{2,1,0:T(8,128)(2,1)} %copy-done.21) | copy-start | bytes 1327108
  85.1 3.2 %copy-start.13 = (bf16[256,128]{1,0:T(8,128)(2,1)S(1)}, bf16[256,128]{1,0:T(8,128)(2,1)}, u32[]{:S(2)}) copy-start(bf16[256,128]{1,0:T(8,128)(2,1)} %copy-done.12) | copy-start | bytes 196612
  89.8 5.3 %collective-permute-start.15 = (bf16[1024,256]{1,0:T(8,128)(2,1)S(1)}, bf16[1024,256]{1,0:T(8,128)(2,1)S(1)}, u32[]{:S(2)}, u32[]{:S(2)}) collective-permute-start(bf16[1024,256]{1,0:T(8,128)(2,1)S(1)} %bitcast.5), channel_id=1, source_target_pairs={{0,16},{2,18},{4,20},{6,22},{8,24},{10,26},{12,28},{14,30},{16,0},... | collective-permute-start | bytes 1572872 | tf_op jit(solution)/shard_map/ppermute | solution.py:406
  92.9 4.1 %collective-permute-start.14 = (f32[8,512]{1,0:T(8,128)S(1)}, f32[8,512]{1,0:T(8,128)S(1)}, u32[]{:S(2)}, u32[]{:S(2)}) collective-permute-start(f32[8,512]{1,0:T(8,128)S(1)} %shard_map.158.refs_0_), channel_id=1, source_target_pairs={{0,17},{1,16},{16,1},{17,0},{32,49},{33,48},{48,33},{49,32},{64,81... | collective-permute-start | bytes 49160 | tf_op jit(solution)/shard_map/ppermute | solution.py:427
  93.0 4.1 %collective-permute-start.13 = (f32[8,512]{1,0:T(8,128)S(1)}, f32[8,512]{1,0:T(8,128)S(1)}, u32[]{:S(2)}, u32[]{:S(2)}) collective-permute-start(f32[8,512]{1,0:T(8,128)S(1)} %shard_map.158.refs_0_), channel_id=1, source_target_pairs={{0,1},{1,0},{2,3},{3,2},{4,5},{5,4},{6,7},{7,6},{8,9},{9,8},{10,11... | collective-permute-start | bytes 49160 | tf_op jit(solution)/shard_map/ppermute | solution.py:422
  94.3 2.8 %collective-permute-start.12 = (f32[8,512]{1,0:T(8,128)S(1)}, f32[8,512]{1,0:T(8,128)S(1)}, u32[]{:S(2)}, u32[]{:S(2)}) collective-permute-start(f32[8,512]{1,0:T(8,128)S(1)} %shard_map.158.refs_0_), channel_id=1, source_target_pairs={{0,16},{2,18},{4,20},{6,22},{8,24},{10,26},{12,28},{14,30},{16,0},... | collective-permute-start | bytes 49160 | tf_op jit(solution)/shard_map/ppermute | solution.py:406
